TPU v7x, 32 devices: a whole 2x2x4 slice. The times are simulated.
32 devices in a mesh: groups: 2 (over y), tensor: 8 (over z, x), tokens: 2 (over core).
Axes of the slice: x: 2, y: 2, z: 4, core: 2. Of those that a mesh axis runs over, the one named last changes fastest.
Arguments:
- att_queries: bfloat16 [1024, 16384], P(('groups', 'tokens'), 'tensor'), parts along dimension 0, may hold values from -4.5 to 4.5
- att_keys: bfloat16 [1024, 8, 128], P(('groups', 'tokens')), parts along dimension 0, may hold values from -4.5 to 4.5
- att_values: bfloat16 [1024, 8, 128], P(('groups', 'tokens')), parts along dimension 0, may hold values from -4 to 4
- out_weight: bfloat16 [16384, 16384], P('tensor', 'tokens'), may hold values from -0.0625 to 0.0625
- residual: bfloat16 [1024, 16384], P(('groups', 'tokens'), 'tensor'), parts along dimension 0, may hold values from -4 to 4
- norm_gain: bfloat16 [16384], P('tensor'), may hold values from 0.25 to 1.75
- next_weight: bfloat16 [16384, 16384], P('tokens', 'tensor'), may hold values from -0.046875 to 0.046875
Outputs:
- resid_out: bfloat16 [1024, 16384], P(('groups', 'tokens'), 'tensor'), parts along dimension 0
- next_queries: bfloat16 [1024, 16384], P(('groups', 'tokens'), 'tensor'), parts along dimension 0
There are 2 independent parts, one for each index of `groups`. A program takes and returns all parts, laid end to end along the dimension named above; an argument that names none is the same for every part. Nothing has to cross between parts.
All inputs are finite; a program needn't handle non-finite values. Where the computation divides by a largest or mean magnitude, that divisor is 1e-20 or more.
Results may differ from a plain program's by a relative error of at most 0.013.
Values may be sent and summed in bfloat16 or wider, within the bound.
No kernel may reach another device: no remote copies, remote signals or barrier semaphores. Data moves between devices by JAX's collectives and lax.ppermute only.
A program may use at most 384 MiB of HBM per device.

v0:
```python
import math

import jax
import jax.numpy as jnp
from jax import lax
from jax.sharding import PartitionSpec as P

D = 16384
H = 128
KVH = 8
HD = 128
G = 128


EPS_GROUP = 1e-06
EPS_NORM = 1e-05


def group_code(matrix):
    lead = matrix.shape[:-1]
    grouped = matrix.reshape(lead + (matrix.shape[-1] // G, G))
    scales = (jnp.max(jnp.abs(grouped), axis=-1, keepdims=True) + EPS_GROUP).astype(jnp.bfloat16)
    coded = (grouped / scales.astype(jnp.float32)).astype(jnp.bfloat16)
    return (coded, scales)


def decode_groups(coded, scales):
    return (coded.astype(jnp.float32) * scales.astype(jnp.float32)).astype(jnp.bfloat16)


def on_device(att_queries, att_keys, att_values, out_weight, residual, norm_gain, next_weight):
    tok_rows = att_queries.shape[0]
    heads_here = att_queries.shape[1] // HD
    group_heads = H // KVH
    kv_head = lax.axis_index("tensor") * heads_here // group_heads
    own_keys = lax.dynamic_index_in_dim(att_keys, kv_head, 1, keepdims=False)
    own_values = lax.dynamic_index_in_dim(att_values, kv_head, 1, keepdims=False)
    query_heads = att_queries.reshape(tok_rows, heads_here, HD)
    query_pos = lax.axis_index("tokens") * tok_rows + jnp.arange(tok_rows, dtype=jnp.int32)
    inv_root = 1.0 / math.sqrt(HD)
    run_max = jnp.full((heads_here, tok_rows), -1e30, jnp.float32)
    piece_keys = lax.all_gather(own_keys, "tokens", axis=0, tiled=True)
    piece_values = lax.all_gather(own_values, "tokens", axis=0, tiled=True)
    scores = (
        jnp.einsum("qhd,kd->hqk", query_heads, piece_keys, preferred_element_type=jnp.float32)
        * inv_root
    )
    key_pos = jnp.arange(piece_keys.shape[0], dtype=jnp.int32)
    visible = (key_pos[None, :] <= query_pos[:, None])[None]
    scores = jnp.where(visible, scores, -1e30)
    new_max = jnp.maximum(run_max, jnp.max(scores, axis=-1))
    weights = jnp.where(visible, jnp.exp(scores - new_max[..., None]), 0.0)
    new_sum = jnp.sum(weights, axis=-1)
    update = jnp.einsum(
        "hqk,kd->hqd",
        weights.astype(jnp.bfloat16),
        piece_values,
        preferred_element_type=jnp.float32,
    )
    head_rows = (update / new_sum[..., None]).astype(jnp.bfloat16)
    attn_rows = jnp.transpose(head_rows, (1, 0, 2)).reshape(tok_rows, heads_here * HD)
    partial_value = jnp.dot(
        attn_rows,
        lax.all_gather(out_weight, "tokens", axis=1, tiled=True),
        preferred_element_type=jnp.float32,
    )
    coded, scales = group_code(partial_value)
    coded_in = lax.all_to_all(coded[None], "tensor", split_axis=2, concat_axis=0, tiled=True)
    scales_in = lax.all_to_all(scales[None], "tensor", split_axis=2, concat_axis=0, tiled=True)
    attn_out = jnp.sum(coded_in.astype(jnp.float32) * scales_in.astype(jnp.float32), axis=0)
    mixed = residual.astype(jnp.float32) + attn_out.reshape(tok_rows, residual.shape[1])
    resid_out = mixed.astype(jnp.bfloat16)
    local_squares = jnp.sum(mixed * mixed, axis=1)
    total_squares = lax.psum(local_squares, "tensor")
    normed = mixed / jnp.sqrt(total_squares / D + EPS_NORM)[:, None] * norm_gain.astype(jnp.float32)
    coded_n, scale_n = group_code(normed)
    full_weight = lax.all_gather(next_weight, "tokens", axis=0, tiled=True)
    piece_coded = lax.all_gather(coded_n, "tensor", axis=1, tiled=True)
    piece_scales = lax.all_gather(scale_n, "tensor", axis=1, tiled=True)
    rows_here = piece_coded.shape[1] * G
    flat = decode_groups(piece_coded, piece_scales).reshape(tok_rows, rows_here)
    query_sum = jnp.dot(flat, full_weight, preferred_element_type=jnp.float32)
    next_queries = query_sum.astype(jnp.bfloat16)
    return (resid_out, next_queries)


def solution(mesh):
    in_specs = (
        P(("groups", "tokens"), "tensor"),
        P(("groups", "tokens"), None, None),
        P(("groups", "tokens"), None, None),
        P("tensor", "tokens"),
        P(("groups", "tokens"), "tensor"),
        P("tensor"),
        P("tokens", "tensor"),
    )
    out_specs = (P(("groups", "tokens"), "tensor"), P(("groups", "tokens"), "tensor"))
    return jax.shard_map(
        on_device, mesh=mesh, in_specs=in_specs, out_specs=out_specs, check_vma=False
    )
```

profile of v0, /device:TPU:0, one launch (start us, length us, event | category | flops | bytes accessed | tf_op | source)
XLA Modules:
  0.0 736.3 jit_solution(18225961423647260590)
XLA Ops:
  7.9 1.2 constant_dynamic-slice_fusion.1
  9.1 1.2 constant_dynamic-slice_fusion
  10.4 2.0 all-gather
  12.5 1.9 all-gather.1
  14.4 1.4 fusion.5
  15.9 2.0 fusion.6
  17.9 2.4 fusion.14
  20.3 87.1 %all-gather.7.cloned.1.call-done = bf16[2048,16384]{1,0:T(8,128)(2,1)} async-done(((bf16[2048,8192]{1,0:T(8,128)(2,1)}), bf16[2048,16384]{1,0:T(8,128)(2,1)}) %all-gather.7.cloned.1.call-update) | async-done | bytes 67108880 | tf_op jit(solution)/shard_map/all_gather | solution.py:64
  107.4 86.6 %copy.53 = bf16[16384,2048]{1,0:T(8,128)(2,1)} copy(bf16[16384,2048]{0,1:T(8,128)(2,1)} %bitcast.9) | data formatting | bytes 134217728 | tf_op jit(solution)/shard_map/dot_general | solution.py:62
  194.0 33.0 %abs_reduce_fusion = (f32[256,128]{0,1:T(8,128)S(1)}, f32[256,128,128]{0,2,1:T(8,128)}) fusion(bf16[256,2048,1]{0,1,2:T(8,128)(2,1)S(1)} %bitcast.88, bf16[128,128,2048]{2,1,0:T(8,128)(2,1)} %bitcast.10), kind=kOutput, calls=%fused_computation.4 | convolution fusion | flops 17188225024 | bytes 85065728 | tf_op jit(solution)/shard_map/dot_general | solution.py:62
  229.3 5.8 all-to-all-start.1
  235.1 9.5 %fusion.4 = bf16[1,256,128,128]{1,3,0,2:T(8,128)(2,1)} fusion(f32[256,128,128]{0,2,1:T(8,128)} %get-tuple-element.9, f32[256,128]{0,1:T(8,128)S(1)} %get-tuple-element.5), kind=kLoop, calls=%fused_computation.10 | loop fusion | flops 8388608 | bytes 25296896 | tf_op jit(solution)/shard_map/broadcast_in_dim | solution.py:68
  244.6 6.1 all-to-all-start
  251.2 182.6 %all-to-all-done = bf16[1,256,128,128]{1,3,0,2:T(8,128)(2,1)} async-done(((bf16[1,256,128,128]{1,3,0,2:T(8,128)(2,1)}), bf16[1,256,128,128]{1,3,0,2:T(8,128)(2,1)}, u32[]{:S(2)}, u32[]{:S(2)}) %all-to-all-start) | async-done | bytes 8388640 | tf_op jit(solution)/shard_map/all_to_all | solution.py:68
  433.8 7.2 fusion
  441.0 1.9 copy.58
  443.3 19.5 %psum.7 = f32[256]{0:T(256)S(1)} all-reduce(f32[256]{0:T(256)S(1)} %multiply_reduce_fusion), channel_id=1, replica_groups=mesh['groups'=2,'tensor'=8,'tokens'=2] {'tensor'}, use_global_device_ids=true, to_apply=%region_5.6 | all-reduce | flops 256 | bytes 2048 | tf_op jit(solution)/shard_map/psum | solution.py:74
  462.8 1.5 multiply_bitcast_fusion
  465.5 1.7 divide_convert_fusion.1
  467.9 30.9 %all-gather.2 = bf16[256,128]{0,1:T(8,128)(2,1)S(1)} all-gather(bf16[256,16]{0,1:T(8,128)(2,1)S(1)} %add_convert_fusion.1), channel_id=4, replica_groups=mesh['groups'=2,'tensor'=8,'tokens'=2] {'tensor'}, dimensions={1}, use_global_device_ids=true | all-gather | bytes 73728 | tf_op jit(solution)/shard_map/all_gather | solution.py:79
  498.9 91.8 %all-gather.9.cloned.1.call-done = bf16[256,128,128]{2,1,0:T(8,128)(2,1)} async-done(((bf16[256,16,128]{2,1,0:T(8,128)(2,1)}), bf16[256,128,128]{2,1,0:T(8,128)(2,1)}) %all-gather.9.cloned.1.call-update) | async-done | bytes 8388624 | tf_op jit(solution)/shard_map/all_gather | solution.py:78
  590.7 8.8 %multiply_convert_fusion = bf16[256,128,128]{2,1,0:T(8,128)(2,1)} fusion(bf16[256,128,128]{2,1,0:T(8,128)(2,1)} %all-gather.9.cloned.1.call-done, f32[256,128]{1,0:T(8,128)S(1)} %copy.61), kind=kLoop, calls=%fused_computation.2 | loop fusion | flops 12582912 | bytes 16908288 | tf_op jit(solution)/shard_map/convert_element_type | solution.py:28
  599.4 86.1 %all-gather.11.cloned.1.call-done = bf16[16384,2048]{1,0:T(8,128)(2,1)} async-done(((bf16[8192,2048]{1,0:T(8,128)(2,1)}), bf16[16384,2048]{1,0:T(8,128)(2,1)}) %all-gather.11.cloned.1.call-update) | async-done | bytes 67108880 | tf_op jit(solution)/shard_map/all_gather | solution.py:77
  685.5 44.3 %fusion.11 = bf16[256,2048]{1,0:T(8,128)(2,1)} fusion(bf16[16384,2048]{1,0:T(8,128)(2,1)} %all-gather.11.cloned.1.call-done, bf16[32,8,128,128]{3,2,1,0:T(8,128)(2,1)} %bitcast.82), kind=kOutput, calls=%fused_computation.16 | convolution fusion | flops 17180393472 | bytes 76546048 | tf_op jit(solution)/shard_map/dot_general | solution.py:82
  (37 shorter events, 6.1 us)
Async XLA Ops:
  7.2 7.3 copy-start
  7.2 100.2 %all-gather.7.cloned.1.call-start = ((), (), s32[]{:S(2)}) async-start(), calls=%async_computation.2 | async-start | bytes 100663296 | tf_op jit(solution)/shard_map/all_gather | solution.py:64
  229.3 15.3 %all-to-all-start.1 = ((bf16[8,2,2048]{2,1,0:T(2,128)(2,1)}), bf16[8,2,2048]{2,1,0:T(2,128)(2,1)S(1)}, u32[]{:S(2)}, u32[]{:S(2)}) async-start(bf16[8,2,2048]{2,1,0:T(2,128)(2,1)} %reshape.124), calls=%async_computation.1 | async-start | bytes 131072 | tf_op jit(solution)/shard_map/all_to_all | solution.py:69
  244.6 6.4 copy-start.3
  244.6 189.2 %all-to-all-start = ((bf16[1,256,128,128]{1,3,0,2:T(8,128)(2,1)}), bf16[1,256,128,128]{1,3,0,2:T(8,128)(2,1)}, u32[]{:S(2)}, u32[]{:S(2)}) async-start(bf16[1,256,128,128]{1,3,0,2:T(8,128)(2,1)} %fusion.4), calls=%async_computation | async-start | bytes 16777216 | tf_op jit(solution)/shard_map/all_to_all | solution.py:68
  250.7 192.2 %copy-start.2 = (bf16[256,2048]{1,0:T(8,128)(2,1)S(1)}, bf16[256,2048]{1,0:T(8,128)(2,1)}, u32[]{:S(2)}) copy-start(bf16[256,2048]{1,0:T(8,128)(2,1)} %param.11) | copy-start | bytes 3145732
  250.7 339.9 %all-gather.9.cloned.1.call-start = ((), (), s32[]{:S(2)}) async-start(), calls=%async_computation.3 | async-start | bytes 9437184 | tf_op jit(solution)/shard_map/all_gather | solution.py:78
  467.2 218.4 %all-gather.11.cloned.1.call-start = ((), (), s32[]{:S(2)}) async-start(), calls=%async_computation.4 | async-start | bytes 100663296 | tf_op jit(solution)/shard_map/all_gather | solution.py:77
  685.5 44.3 %copy-start.1 = (bf16[256,2048]{1,0:T(8,128)(2,1)S(1)}, bf16[256,2048]{1,0:T(8,128)(2,1)}, u32[]{:S(2)}) copy-start(bf16[256,2048]{1,0:T(8,128)(2,1)} %param.7) | copy-start | bytes 3145732
Sparse Core Ops, SparseCore 0:
  9.6 97.7 all-gather.6
  467.3 123.3 all-gather.8
  592.2 93.2 all-gather.10
where the time goes:
time: 739 us; the launch traced here: 736 us
  waiting for transfers between devices  449 us (61%)
  local copies, waits for them, and re-layouts  93.1 us (13%)
  matrix products  81.1 us (11%)
  blocking collectives  54.2 us (7%)
  other arithmetic  32.9 us (4%)
  between operations  13.9 us (2%)
  starting transfers between devices  12.2 us (2%)
    all_to_all x1, waiting for transfers between devices, on_device(): lax.all_to_all(coded[None], 'tensor', split_axis=2, concat_axis=0, tiled=...  183 us
    all_gather x1, waiting for transfers between devices, on_device(): piece_coded = lax.all_gather(coded_n, 'tensor', axis=1, tiled=True)  91.8 us
    all_gather x1, waiting for transfers between devices, on_device(): lax.all_gather(out_weight, 'tokens', axis=1, tiled=True)  87.1 us
    dot_general x1, local copies, waits for them, and re-layouts, on_device(): jnp.dot(attn_rows, lax.all_gather(out_weight, 'tokens', axis=1, tiled=Tru...  86.6 us
    all_gather x1, waiting for transfers between devices, on_device(): full_weight = lax.all_gather(next_weight, 'tokens', axis=0, tiled=True)  86.1 us
    dot_general x1, matrix products, on_device(): query_sum = jnp.dot(flat, full_weight, preferred_element_type=jnp.float32)  44.3 us
    dot_general x1, matrix products, on_device(): jnp.dot(attn_rows, lax.all_gather(out_weight, 'tokens', axis=1, tiled=Tru...  33 us
    all_gather x1, blocking collectives, on_device(): piece_scales = lax.all_gather(scale_n, 'tensor', axis=1, tiled=True)  30.9 us
  transfers between devices with their start and end apart: 5, of which 4 were waited for; matrix products, arithmetic and copies ran while one was open for 4% of the time, Pallas kernels for 0%

commit v1 on v0

v1 whole, which is shorter than its diff:
```python
import functools
import math

import jax
import jax.numpy as jnp
import numpy as np
from jax import lax
from jax.experimental import pallas as pl
from jax.experimental.pallas import tpu as pltpu
from jax.sharding import PartitionSpec as P

D = 16384
H = 128
KVH = 8
HD = 128
EPS_NORM = 1e-05
BF16 = jnp.bfloat16
F32 = jnp.float32
RING_LIMIT = 16
MIB = 1024 * 1024


def dot(a, b):
    return jnp.dot(a, b, preferred_element_type=F32)


def attention_kernel(heads, core_ref, q_ref, k_ref, v_ref, pk_ref, pv_ref, o_ref):
    rows = q_ref.shape[0]
    inv_root = 1.0 / math.sqrt(HD)
    query_pos = lax.broadcasted_iota(jnp.int32, (rows, rows), 0)
    key_pos = lax.broadcasted_iota(jnp.int32, (rows, rows), 1)
    visible = key_pos <= query_pos
    peer_visible = core_ref[0] == 1
    contract = (((1,), (1,)), ((), ()))
    for head in range(heads):
        columns = slice(head * HD, (head + 1) * HD)
        query = q_ref[:, columns]
        own = lax.dot_general(query, k_ref[...], contract, preferred_element_type=F32) * inv_root
        far = lax.dot_general(query, pk_ref[...], contract, preferred_element_type=F32) * inv_root
        own = jnp.where(visible, own, -1e30)
        far = jnp.where(peer_visible, far, -1e30)
        top = jnp.maximum(jnp.max(own, axis=1, keepdims=True), jnp.max(far, axis=1, keepdims=True))
        own = jnp.exp(own - top)
        far = jnp.exp(far - top)
        total = jnp.sum(own, axis=1, keepdims=True) + jnp.sum(far, axis=1, keepdims=True)
        mixed = dot(own.astype(BF16), v_ref[...]) + dot(far.astype(BF16), pv_ref[...])
        o_ref[:, columns] = (mixed / total).astype(BF16)


def attention(core, queries, keys, values, peer_keys, peer_values):
    rows, width = queries.shape
    heads = min(4, width // HD)
    whole = pl.BlockSpec((rows, HD), lambda h, s: (0, 0))
    part = pl.BlockSpec((rows, heads * HD), lambda h, s: (0, h))
    return pl.pallas_call(
        functools.partial(attention_kernel, heads),
        grid_spec=pltpu.PrefetchScalarGridSpec(
            num_scalar_prefetch=1,
            grid=(width // (heads * HD),),
            in_specs=[part, whole, whole, whole, whole],
            out_specs=part,
        ),
        out_shape=jax.ShapeDtypeStruct((rows, width), BF16),
        compiler_params=pltpu.CompilerParams(vmem_limit_bytes=24 * MIB),
        cost_estimate=pl.CostEstimate(
            flops=8 * rows * rows * width, bytes_accessed=4 * rows * width, transcendentals=2 * rows * rows * width // HD
        ),
        name="attention",
    )(core, queries, keys, values, peer_keys, peer_values)


def project_kernel(info_ref, x_ref, w_ref, own_ref, peer_ref):
    rows = own_ref.shape[0]
    result = dot(x_ref[...], w_ref[...]).astype(BF16)
    own_ref[...] = result[:rows]
    peer_ref[...] = result[rows:]


def project(info, pair, both, weight, width):
    depth = both.shape[1]
    rows = both.shape[0] // 2
    tile = min(512, width)
    tiles = width // tile
    out = pl.BlockSpec((rows, tile), lambda j, s: (0, j))
    return pl.pallas_call(
        project_kernel,
        grid_spec=pltpu.PrefetchScalarGridSpec(
            num_scalar_prefetch=1,
            grid=(tiles,),
            in_specs=[
                pl.BlockSpec((2 * rows, depth), lambda j, s: (0, 0)),
                pl.BlockSpec((depth, tile), lambda j, s: (0, s[pair] * tiles + j)),
            ],
            out_specs=[out, out],
        ),
        out_shape=[jax.ShapeDtypeStruct((rows, width), BF16)] * 2,
        compiler_params=pltpu.CompilerParams(vmem_limit_bytes=24 * MIB),
        cost_estimate=pl.CostEstimate(
            flops=4 * rows * depth * width, bytes_accessed=2 * depth * width, transcendentals=0
        ),
        name="project",
    )(info, both, weight)


def query_kernel(pieces, pair, half, first, info_ref, *refs):
    one, other, far = refs[:pieces], refs[pieces : 2 * pieces], refs[2 * pieces : 3 * pieces]
    w_ref = refs[3 * pieces]
    acc_refs = refs[3 * pieces + 1 : -3]
    own_ref, peer_ref, x_ref = refs[-3:]
    rows = own_ref.shape[0]
    width = one[0].shape[1]

    @pl.when(pl.program_id(0) == 0)
    def _():
        for piece in range(pieces):
            columns = slice(piece * width, (piece + 1) * width)

            @pl.when(info_ref[half + pair] == 1)
            def _():
                x_ref[:rows, columns] = one[piece][...]

            @pl.when(info_ref[half + pair] == 0)
            def _():
                x_ref[:rows, columns] = other[piece][...]

            x_ref[rows:, columns] = far[piece][...]

    result = dot(x_ref[...], w_ref[...])
    if first:
        own_ref[...] = result[:rows]
        peer_ref[...] = result[rows:].astype(peer_ref.dtype)
    else:
        own_ref[...] = acc_refs[0][...] + result[:rows]
        peer_ref[...] = (acc_refs[1][...] + result[rows:]).astype(peer_ref.dtype)


def query_block(info, pair, half, one, other, far, weight, acc, last):
    pieces = len(one)
    rows, piece_width = one[0].shape
    depth = pieces * piece_width
    width = weight.shape[1]
    tile = min(512, width)
    whole = pl.BlockSpec((rows, piece_width), lambda j, s: (0, 0))
    out = pl.BlockSpec((rows, tile), lambda j, s: (0, j))
    first = acc is None
    acc = () if first else acc
    return pl.pallas_call(
        functools.partial(query_kernel, pieces, pair, half, first),
        grid_spec=pltpu.PrefetchScalarGridSpec(
            num_scalar_prefetch=1,
            grid=(width // tile,),
            in_specs=[whole] * (3 * pieces)
            + [pl.BlockSpec((depth, tile), lambda j, s: (s[pair], j))]
            + [out] * len(acc),
            out_specs=[out, out],
            scratch_shapes=[pltpu.VMEM((2 * rows, depth), BF16)],
        ),
        out_shape=[
            jax.ShapeDtypeStruct((rows, width), F32),
            jax.ShapeDtypeStruct((rows, width), BF16 if last else F32),
        ],
        compiler_params=pltpu.CompilerParams(vmem_limit_bytes=32 * MIB),
        cost_estimate=pl.CostEstimate(
            flops=4 * rows * depth * width, bytes_accessed=2 * depth * width + 16 * rows * width, transcendentals=0
        ),
        name="next_query",
    )(info, *one, *other, *far, weight, *acc)


def ring_of(n):
    return [2 * p for p in range(n // 2)] + [2 * p + 1 for p in reversed(range(n // 2))]


def on_ring(n, att_queries, att_keys, att_values, out_weight, residual, norm_gain, next_weight):
    half = n // 2
    ring = ring_of(n)
    place = {chip: p for p, chip in enumerate(ring)}
    up = [(ring[p], ring[(p + 1) % n]) for p in range(n)]
    down = [(b, a) for a, b in up]
    swap = [(0, 1), (1, 0)]
    chip = lax.axis_index("tensor")
    core = lax.axis_index("tokens")
    rows, width = att_queries.shape
    pieces = 2 if width >= 256 else 1
    piece_width = residual.shape[1] // pieces

    table = np.zeros((n, 2, n), np.int32)
    for c in range(n):
        for k in range(half):
            near, far = ring[(place[c] + k) % n], ring[(place[c] + k + half) % n]
            for h in range(2):
                mine = near // half == h
                assert mine != (far // half == h)
                table[c, h, k] = (near if mine else far) - h * half
                table[c, h, half + k] = mine
    info = lax.dynamic_index_in_dim(jnp.asarray(table.reshape(2 * n, n)), chip * 2 + core, 0, keepdims=False)
    near_mine = [info[half + k] == 1 for k in range(half)]

    heads_here = width // HD
    kv_head = chip * heads_here // (H // KVH)
    own_keys = lax.dynamic_index_in_dim(att_keys, kv_head, 1, keepdims=False)
    own_values = lax.dynamic_index_in_dim(att_values, kv_head, 1, keepdims=False)
    peer_keys = lax.ppermute(own_keys, "tokens", swap)
    peer_values = lax.ppermute(own_values, "tokens", swap)
    attended = attention(core[None], att_queries, own_keys, own_values, peer_keys, peer_values)
    both = jnp.concatenate([attended, lax.ppermute(attended, "tokens", swap)], axis=0)

    mine, swapped = {}, {}
    order = [0] + [k for j in range(1, half) for k in (half - j, j) if k not in range(0, 1)]
    order = list(dict.fromkeys(order))
    for k in order:
        mine[k], outgoing = project(info, k, both, out_weight, residual.shape[1])
        swapped[k] = lax.ppermute(outgoing, "tokens", swap)

    def columns_of(array, piece):
        return array[:, piece * piece_width : (piece + 1) * piece_width]

    def block(q, piece):
        k = q % half
        near = near_mine[k] if q == k else jnp.logical_not(near_mine[k])
        return jnp.where(near, columns_of(mine[k], piece), columns_of(swapped[k], piece)).astype(F32)

    hops = [(half, half - 1) if piece % 2 == 0 else (half - 1, half) for piece in range(pieces)]
    arrived = {}
    for step in range(1, half + 1):
        for piece in range(pieces):
            for way, pairs in ((0, up), (1, down)):
                length = hops[piece][way]
                if step > length:
                    continue
                q = length - step + 1
                value = block(q if way == 0 else -q, piece)
                if step > 1:
                    value = value + arrived[piece, way].astype(F32)
                arrived[piece, way] = lax.ppermute(value.astype(BF16), "tensor", pairs)

    resid, scaled = [], []
    squares = jnp.zeros((rows,), F32)
    for piece in range(pieces):
        mixed = columns_of(residual, piece).astype(F32) + block(0, piece)
        for way in range(2):
            if hops[piece][way]:
                mixed = mixed + arrived[piece, way].astype(F32)
        resid.append(mixed.astype(BF16))
        gain = norm_gain[piece * piece_width : (piece + 1) * piece_width].astype(F32)
        scaled.append((mixed * gain).astype(BF16))
        squares = squares + jnp.sum(mixed * mixed, axis=1)
    resid_out = jnp.concatenate(resid, axis=1)

    held = {(piece, 0): scaled[piece] for piece in range(pieces)}
    for step in range(1, half + 1):
        for piece in range(pieces):
            for way, pairs in ((0, up), (1, down)):
                if step > hops[piece][way]:
                    continue
                sign = -1 if way == 0 else 1
                source = (piece, sign * (step - 1))
                target = sign * step
                value = lax.ppermute(held[source], "tensor", pairs)
                held[piece, target] = value
                if abs(target) == half:
                    held[piece, half] = held[piece, -half] = value
    distance = half
    while distance >= 1:
        shifted = [(ring[p], ring[(p + distance) % n]) for p in range(n)]
        squares = squares + lax.ppermute(squares, "tensor", shifted)
        distance //= 2

    acc = None
    when = sorted(range(half), key=lambda k: max(k, half - k))
    for k in when:
        one = [held[piece, k] for piece in range(pieces)]
        other = [held[piece, k - half] for piece in range(pieces)]
        far = [
            lax.ppermute(jnp.where(near_mine[k], other[piece], one[piece]), "tokens", swap) for piece in range(pieces)
        ]
        acc = query_block(info, k, half, one, other, far, next_weight, acc, k == when[-1])
    query_sum = acc[0] + lax.ppermute(acc[1], "tokens", swap).astype(F32)
    factor = 1.0 / jnp.sqrt(squares / D + EPS_NORM)
    return (resid_out, (query_sum * factor[:, None]).astype(BF16))


def on_mesh(n, att_queries, att_keys, att_values, out_weight, residual, norm_gain, next_weight):
    rows, width = att_queries.shape
    swap = [(0, 1), (1, 0)]
    chip = lax.axis_index("tensor")
    core = lax.axis_index("tokens")
    kv_head = chip * (width // HD) // (H // KVH)
    own_keys = lax.dynamic_index_in_dim(att_keys, kv_head, 1, keepdims=False)
    own_values = lax.dynamic_index_in_dim(att_values, kv_head, 1, keepdims=False)
    peer_keys = lax.ppermute(own_keys, "tokens", swap)
    peer_values = lax.ppermute(own_values, "tokens", swap)
    attended = attention(core[None], att_queries, own_keys, own_values, peer_keys, peer_values)
    both = lax.all_gather(attended, "tokens", axis=0, tiled=True)
    partial = dot(both, out_weight).astype(BF16)
    partial = lax.all_to_all(partial, "tokens", split_axis=0, concat_axis=1, tiled=True)
    attn_out = lax.psum_scatter(partial.astype(F32), "tensor", scatter_dimension=1, tiled=True)
    mixed = residual.astype(F32) + attn_out
    total_squares = lax.psum(jnp.sum(mixed * mixed, axis=1), "tensor")
    factor = 1.0 / jnp.sqrt(total_squares / D + EPS_NORM)
    normed = (mixed * factor[:, None] * norm_gain.astype(F32)).astype(BF16)
    gathered = lax.all_gather(normed, "tensor", axis=1, tiled=True)
    halves = lax.all_to_all(gathered, "tokens", split_axis=1, concat_axis=0, tiled=True)
    query_sum = lax.psum_scatter(dot(halves, next_weight), "tokens", scatter_dimension=0, tiled=True)
    return (mixed.astype(BF16), query_sum.astype(BF16))


def solution(mesh):
    n = mesh.shape["tensor"]
    in_specs = (
        P(("groups", "tokens"), "tensor"),
        P(("groups", "tokens"), None, None),
        P(("groups", "tokens"), None, None),
        P("tensor", "tokens"),
        P(("groups", "tokens"), "tensor"),
        P("tensor"),
        P("tokens", "tensor"),
    )
    out_specs = (P(("groups", "tokens"), "tensor"), P(("groups", "tokens"), "tensor"))
    body = functools.partial(on_ring if n <= RING_LIMIT else on_mesh, n)
    return jax.shard_map(body, mesh=mesh, in_specs=in_specs, out_specs=out_specs, check_vma=False)
```

time: 739 us -> 320 us (0.43)
  waiting for transfers between devices: 449 us -> 174 us
  local copies, waits for them, and re-layouts: 93.1 us -> 4.94 us
  matrix products: 81.1 us -> 0 us
  Pallas kernels: 0 us -> 71.4 us
  blocking collectives: 54.2 us -> 0 us
  starting transfers between devices: 12.2 us -> 41 us
  between operations: 13.9 us -> 3.43 us
  other arithmetic: 32.9 us -> 24.4 us
    all_gather x3 -> x0, waiting for transfers between devices: 265 us -> none  [the longest x1 91.8 us: on_device(): piece_coded = lax.all_gather(coded_n, 'tensor', axis=1, tiled=True)]
    all_to_all x2 -> x0, waiting for transfers between devices: 183 us -> none  [the longest x1 183 us: on_device(): lax.all_to_all(coded[None], 'tensor', split_axis=2, concat_axis=0, tiled=...]
    ppermute x0 -> x47, waiting for transfers between devices: none -> 174 us  [the longest x14 92.8 us: on_ring(): arrived[piece, way] = lax.ppermute(value.astype(BF16), 'tensor', pairs)]
    dot_general x1 -> x0, local copies, waits for them, and re-layouts: 86.6 us -> none  [on_device(): jnp.dot(attn_rows, lax.all_gather(out_weight, 'tokens', axis=1, tiled=Tru...]
    dot_general x4 -> x0, matrix products: 81.1 us -> none  [the longest x1 44.3 us: on_device(): query_sum = jnp.dot(flat, full_weight, preferred_element_type=jnp.float32)]
    pallas_call x0 -> x9, Pallas kernels: none -> 71.4 us  [the longest x4 33.8 us: project(): pl.pallas_call(project_kernel, grid_spec=pltpu.PrefetchScalarGridSpec(num...]
    ppermute x0 -> x47, starting transfers between devices: none -> 41 us  [the longest x14 19.8 us: on_ring(): arrived[piece, way] = lax.ppermute(value.astype(BF16), 'tensor', pairs)]
    all_gather x3 -> x0, blocking collectives: 34.8 us -> none  [the longest x1 30.9 us: on_device(): piece_scales = lax.all_gather(scale_n, 'tensor', axis=1, tiled=True)]
  transfers between devices with their start and end apart: 5 -> 47, of which waited for: 4 -> 23; matrix products, arithmetic and copies ran while one was open for 4% -> 6% of each run, Pallas kernels for 0% -> 15%
where the time goes in v1:
time: 320 us; the launch traced here: 319 us
  waiting for transfers between devices  174 us (54%)
  Pallas kernels  71.4 us (22%)
  starting transfers between devices  41 us (13%)
  other arithmetic  24.4 us (8%)
  local copies, waits for them, and re-layouts  4.94 us (2%)
  between operations  3.43 us (1%)
    ppermute x14, waiting for transfers between devices, on_ring(): arrived[piece, way] = lax.ppermute(value.astype(BF16), 'tensor', pairs)  92.8 us
    ppermute x14, waiting for transfers between devices, on_ring(): value = lax.ppermute(held[source], 'tensor', pairs)  66.9 us
    pallas_call x4, Pallas kernels, project(): pl.pallas_call(project_kernel, grid_spec=pltpu.PrefetchScalarGridSpec(num...  33.8 us
    pallas_call x4, Pallas kernels, query_block(): pl.pallas_call(functools.partial(query_kernel, pieces, pair, half, first)...  31.9 us
    ppermute x14, starting transfers between devices, on_ring(): arrived[piece, way] = lax.ppermute(value.astype(BF16), 'tensor', pairs)  19.8 us
    ppermute x14, starting transfers between devices, on_ring(): value = lax.ppermute(held[source], 'tensor', pairs)  15.3 us
    convert_element_type x5, other arithmetic, on_ring(): arrived[piece, way] = lax.ppermute(value.astype(BF16), 'tensor', pairs)  11.5 us
    ppermute x3, waiting for transfers between devices, on_ring(): squares = squares + lax.ppermute(squares, 'tensor', shifted)  10.8 us
  transfers between devices with their start and end apart: 47, of which 23 were waited for; matrix products, arithmetic and copies ran while one was open for 6% of the time, Pallas kernels for 15%

profile of v1, /device:TPU:0, one launch (start us, length us, event | category | flops | bytes accessed | tf_op | source)
XLA Modules:
  0.0 318.7 jit_solution(15418038299832908947)
XLA Ops:
  16.1 8.4 %project.4 = (bf16[256,2048]{1,0:T(8,128)(2,1)S(1)}, bf16[256,2048]{1,0:T(8,128)(2,1)}) custom-call(s32[8]{0:T(128)S(1)} %get-tuple-element.54.info_ref, bf16[512,2048]{1,0:T(8,128)(2,1)S(1)} %pad_maximum_fusion.x_ref, bf16[2048,8192]{1,0:T(8,128)(2,1)} %w_ref.7), custom_call_target="tpu_custom_call" | custom-call | flops 4294967296 | bytes 8388608 | tf_op jit(solution)/shard_map/project/pallas_call | solution.py:85
  24.6 8.5 %project.5 = (bf16[256,2048]{1,0:T(8,128)(2,1)S(1)}, bf16[256,2048]{1,0:T(8,128)(2,1)}) custom-call(s32[8]{0:T(128)S(1)} %get-tuple-element.54.info_ref, bf16[512,2048]{1,0:T(8,128)(2,1)S(1)} %pad_maximum_fusion.x_ref, bf16[2048,8192]{1,0:T(8,128)(2,1)} %w_ref.7), custom_call_target="tpu_custom_call" | custom-call | flops 4294967296 | bytes 8388608 | tf_op jit(solution)/shard_map/project/pallas_call | solution.py:85
  33.5 8.5 %project.7 = (bf16[256,2048]{1,0:T(8,128)(2,1)S(1)}, bf16[256,2048]{1,0:T(8,128)(2,1)}) custom-call(s32[8]{0:T(128)S(1)} %get-tuple-element.54.info_ref, bf16[512,2048]{1,0:T(8,128)(2,1)S(1)} %pad_maximum_fusion.x_ref, bf16[2048,8192]{1,0:T(8,128)(2,1)} %w_ref.7), custom_call_target="tpu_custom_call" | custom-call | flops 4294967296 | bytes 8388608 | tf_op jit(solution)/shard_map/project/pallas_call | solution.py:85
  44.5 8.4 %project.6 = (bf16[256,2048]{1,0:T(8,128)(2,1)S(1)}, bf16[256,2048]{1,0:T(8,128)(2,1)}) custom-call(s32[8]{0:T(128)S(1)} %get-tuple-element.54.info_ref, bf16[512,2048]{1,0:T(8,128)(2,1)S(1)} %pad_maximum_fusion.x_ref, bf16[2048,8192]{1,0:T(8,128)(2,1)} %w_ref.7), custom_call_target="tpu_custom_call" | custom-call | flops 4294967296 | bytes 8388608 | tf_op jit(solution)/shard_map/project/pallas_call | solution.py:85
  64.6 6.7 %collective-permute-done.7 = bf16[256,1024]{1,0:T(8,128)(2,1)S(1)} collective-permute-done((bf16[256,1024]{1,0:T(8,128)(2,1)S(1)}, bf16[256,1024]{1,0:T(8,128)(2,1)S(1)}, u32[]{:S(2)}, u32[]{:S(2)}) %collective-permute-start.7) | collective-permute-done | bytes 524320 | tf_op jit(solution)/shard_map/ppermute | solution.py:235
  76.3 6.3 %collective-permute-done.14 = bf16[256,1024]{1,0:T(8,128)(2,1)} collective-permute-done((bf16[256,1024]{1,0:T(8,128)(2,1)}, bf16[256,1024]{1,0:T(8,128)(2,1)}, u32[]{:S(2)}, u32[]{:S(2)}) %collective-permute-start.14) | collective-permute-done | bytes 524320 | tf_op jit(solution)/shard_map/ppermute | solution.py:235
  82.6 10.8 %collective-permute-done.8 = bf16[256,1024]{1,0:T(8,128)(2,1)} collective-permute-done((bf16[256,1024]{1,0:T(8,128)(2,1)}, bf16[256,1024]{1,0:T(8,128)(2,1)}, u32[]{:S(2)}, u32[]{:S(2)}) %collective-permute-start.8) | collective-permute-done | bytes 524320 | tf_op jit(solution)/shard_map/ppermute | solution.py:235
  100.1 11.4 %collective-permute-done.15 = bf16[256,1024]{1,0:T(8,128)(2,1)S(1)} collective-permute-done((bf16[256,1024]{1,0:T(8,128)(2,1)S(1)}, bf16[256,1024]{1,0:T(8,128)(2,1)S(1)}, u32[]{:S(2)}, u32[]{:S(2)}) %collective-permute-start.15) | collective-permute-done | bytes 524320 | tf_op jit(solution)/shard_map/ppermute | solution.py:235
  111.5 10.0 %collective-permute-done.9 = bf16[256,1024]{1,0:T(8,128)(2,1)S(1)} collective-permute-done((bf16[256,1024]{1,0:T(8,128)(2,1)S(1)}, bf16[256,1024]{1,0:T(8,128)(2,1)S(1)}, u32[]{:S(2)}, u32[]{:S(2)}) %collective-permute-start.9) | collective-permute-done | bytes 524320 | tf_op jit(solution)/shard_map/ppermute | solution.py:235
  127.5 11.9 %collective-permute-done.18 = bf16[256,1024]{1,0:T(8,128)(2,1)S(1)} collective-permute-done((bf16[256,1024]{1,0:T(8,128)(2,1)S(1)}, bf16[256,1024]{1,0:T(8,128)(2,1)S(1)}, u32[]{:S(2)}, u32[]{:S(2)}) %collective-permute-start.18) | collective-permute-done | bytes 524320 | tf_op jit(solution)/shard_map/ppermute | solution.py:235
  144.3 6.3 %collective-permute-done.12 = bf16[256,1024]{1,0:T(8,128)(2,1)S(1)} collective-permute-done((bf16[256,1024]{1,0:T(8,128)(2,1)}, bf16[256,1024]{1,0:T(8,128)(2,1)S(1)}, u32[]{:S(2)}, u32[]{:S(2)}) %collective-permute-start.12) | collective-permute-done | bytes 524320 | tf_op jit(solution)/shard_map/ppermute | solution.py:235
  150.6 9.0 %collective-permute-done.19 = bf16[256,1024]{1,0:T(8,128)(2,1)S(1)} collective-permute-done((bf16[256,1024]{1,0:T(8,128)(2,1)S(1)}, bf16[256,1024]{1,0:T(8,128)(2,1)S(1)}, u32[]{:S(2)}, u32[]{:S(2)}) %collective-permute-start.19) | collective-permute-done | bytes 524320 | tf_op jit(solution)/shard_map/ppermute | solution.py:235
  164.2 12.2 %collective-permute-done.13 = bf16[256,1024]{1,0:T(8,128)(2,1)S(1)} collective-permute-done((bf16[256,1024]{1,0:T(8,128)(2,1)S(1)}, bf16[256,1024]{1,0:T(8,128)(2,1)S(1)}, u32[]{:S(2)}, u32[]{:S(2)}) %collective-permute-start.13) | collective-permute-done | bytes 524320 | tf_op jit(solution)/shard_map/ppermute | solution.py:235
  176.4 8.1 %collective-permute-done.20 = bf16[256,1024]{1,0:T(8,128)(2,1)S(1)} collective-permute-done((bf16[256,1024]{1,0:T(8,128)(2,1)S(1)}, bf16[256,1024]{1,0:T(8,128)(2,1)S(1)}, u32[]{:S(2)}, u32[]{:S(2)}) %collective-permute-start.20) | collective-permute-done | bytes 524320 | tf_op jit(solution)/shard_map/ppermute | solution.py:235
  191.0 11.3 %collective-permute-done.34.refs_3_ = bf16[256,1024]{1,0:T(8,128)(2,1)S(1)} collective-permute-done((bf16[256,1024]{1,0:T(8,128)(2,1)S(1)}, bf16[256,1024]{1,0:T(8,128)(2,1)S(1)}, u32[]{:S(2)}, u32[]{:S(2)}) %collective-permute-start.34) | collective-permute-done | bytes 524320 | tf_op jit(solution)/shard_map/ppermute | solution.py:259
  204.3 9.2 %collective-permute-done.21.refs_2_ = bf16[256,1024]{1,0:T(8,128)(2,1)S(1)} collective-permute-done((bf16[256,1024]{1,0:T(8,128)(2,1)S(1)}, bf16[256,1024]{1,0:T(8,128)(2,1)S(1)}, u32[]{:S(2)}, u32[]{:S(2)}) %collective-permute-start.21) | collective-permute-done | bytes 524320 | tf_op jit(solution)/shard_map/ppermute | solution.py:259
  215.6 9.2 %collective-permute-done.37.refs_3_ = bf16[256,1024]{1,0:T(8,128)(2,1)S(1)} collective-permute-done((bf16[256,1024]{1,0:T(8,128)(2,1)S(1)}, bf16[256,1024]{1,0:T(8,128)(2,1)S(1)}, u32[]{:S(2)}, u32[]{:S(2)}) %collective-permute-start.37) | collective-permute-done | bytes 524320 | tf_op jit(solution)/shard_map/ppermute | solution.py:259
  226.2 9.8 %collective-permute-done.22.refs_2_ = bf16[256,1024]{1,0:T(8,128)(2,1)S(1)} collective-permute-done((bf16[256,1024]{1,0:T(8,128)(2,1)S(1)}, bf16[256,1024]{1,0:T(8,128)(2,1)S(1)}, u32[]{:S(2)}, u32[]{:S(2)}) %collective-permute-start.22) | collective-permute-done | bytes 524320 | tf_op jit(solution)/shard_map/ppermute | solution.py:259
  238.2 9.0 %collective-permute-done.38.refs_3_ = bf16[256,1024]{1,0:T(8,128)(2,1)S(1)} collective-permute-done((bf16[256,1024]{1,0:T(8,128)(2,1)S(1)}, bf16[256,1024]{1,0:T(8,128)(2,1)S(1)}, u32[]{:S(2)}, u32[]{:S(2)}) %collective-permute-start.38) | collective-permute-done | bytes 524320 | tf_op jit(solution)/shard_map/ppermute | solution.py:259
  256.3 7.9 %next_query.4 = (f32[256,2048]{1,0:T(8,128)S(1)}, f32[256,2048]{1,0:T(8,128)S(1)}) custom-call(s32[8]{0:T(128)S(1)} %get-tuple-element.54.info_ref, bf16[256,1024]{1,0:T(8,128)(2,1)S(1)} %collective-permute-done.32.refs_0_, bf16[256,1024]{1,0:T(8,128)(2,1)S(1)} %collective-permute-done.26.refs_1_, bf16[256,1024]{1,0:T(8,128)(2,1)S(1)} %collective-permute-done.22.refs_2_, ...), custom_call_target="tpu_custom_call" | custom-call | flops 4294967296 | bytes 16777216 | tf_op jit(solution)/shard_map/next_query/pallas_call | solution.py:147
  264.7 9.5 %collective-permute-done.28.refs_3_ = bf16[256,1024]{1,0:T(8,128)(2,1)S(1)} collective-permute-done((bf16[256,1024]{1,0:T(8,128)(2,1)S(1)}, bf16[256,1024]{1,0:T(8,128)(2,1)S(1)}, u32[]{:S(2)}, u32[]{:S(2)}) %collective-permute-start.28) | collective-permute-done | bytes 524320 | tf_op jit(solution)/shard_map/ppermute | solution.py:259
  278.9 8.0 %next_query.5 = (f32[256,2048]{1,0:T(8,128)S(1)}, f32[256,2048]{1,0:T(8,128)S(1)}) custom-call(s32[8]{0:T(128)S(1)} %get-tuple-element.54.info_ref, bf16[256,1024]{1,0:T(8,128)(2,1)S(1)} %collective-permute-done.31.refs_0_, bf16[256,1024]{1,0:T(8,128)(2,1)S(1)} %collective-permute-done.25.refs_1_, bf16[256,1024]{1,0:T(8,128)(2,1)S(1)} %collective-permute-done.23.refs_2_, ...), custom_call_target="tpu_custom_call" | custom-call | flops 4294967296 | bytes 16777216 | tf_op jit(solution)/shard_map/next_query/pallas_call | solution.py:147
  286.9 8.0 %next_query.6 = (f32[256,2048]{1,0:T(8,128)S(1)}, f32[256,2048]{1,0:T(8,128)S(1)}) custom-call(s32[8]{0:T(128)S(1)} %get-tuple-element.54.info_ref, bf16[256,1024]{1,0:T(8,128)(2,1)S(1)} %collective-permute-done.33.refs_0_, bf16[256,1024]{1,0:T(8,128)(2,1)S(1)} %collective-permute-done.27.refs_1_, bf16[256,1024]{1,0:T(8,128)(2,1)S(1)} %collective-permute-done.21.refs_2_, ...), custom_call_target="tpu_custom_call" | custom-call | flops 4294967296 | bytes 16777216 | tf_op jit(solution)/shard_map/next_query/pallas_call | solution.py:147
  295.0 8.0 %next_query.7 = (f32[256,2048]{1,0:T(8,128)S(1)}, bf16[256,2048]{1,0:T(8,128)(2,1)S(1)}) custom-call(s32[8]{0:T(128)S(1)} %get-tuple-element.54.info_ref, bf16[256,1024]{1,0:T(8,128)(2,1)S(1)} %get-tuple-element.52.refs_0_, bf16[256,1024]{1,0:T(8,128)(2,1)S(1)} %get-tuple-element.50.refs_1_, bf16[256,1024]{1,0:T(8,128)(2,1)S(1)} %collective-permute-done.24.refs_2_, ...), custom_call_target="tpu_custom_call" | custom-call | flops 4294967296 | bytes 16777216 | tf_op jit(solution)/shard_map/next_query/pallas_call | solution.py:147
  (136 shorter events, 98.8 us)
Async XLA Ops:
  24.5 28.8 %collective-permute-start.3 = (bf16[256,2048]{1,0:T(8,128)(2,1)}, bf16[256,2048]{1,0:T(8,128)(2,1)}, u32[]{:S(2)}, u32[]{:S(2)}) collective-permute-start(bf16[256,2048]{1,0:T(8,128)(2,1)} %get-tuple-element.19), channel_id=1, source_target_pairs={{0,1},{1,0},{2,3},{3,2},{4,5},{5,4},{6,7},{7,6},{8,9},{9,8},{10,11... | collective-permute-start | bytes 3145736 | tf_op jit(solution)/shard_map/ppermute | solution.py:213
  33.1 25.6 %collective-permute-start.4 = (bf16[256,2048]{1,0:T(8,128)(2,1)}, bf16[256,2048]{1,0:T(8,128)(2,1)}, u32[]{:S(2)}, u32[]{:S(2)}) collective-permute-start(bf16[256,2048]{1,0:T(8,128)(2,1)} %get-tuple-element.21), channel_id=1, source_target_pairs={{0,1},{1,0},{2,3},{3,2},{4,5},{5,4},{6,7},{7,6},{8,9},{9,8},{10,11... | collective-permute-start | bytes 3145736 | tf_op jit(solution)/shard_map/ppermute | solution.py:213
  53.0 23.3 %collective-permute-start.5 = (bf16[256,2048]{1,0:T(8,128)(2,1)}, bf16[256,2048]{1,0:T(8,128)(2,1)}, u32[]{:S(2)}, u32[]{:S(2)}) collective-permute-start(bf16[256,2048]{1,0:T(8,128)(2,1)} %get-tuple-element.23), channel_id=1, source_target_pairs={{0,1},{1,0},{2,3},{3,2},{4,5},{5,4},{6,7},{7,6},{8,9},{9,8},{10,11... | collective-permute-start | bytes 3145736 | tf_op jit(solution)/shard_map/ppermute | solution.py:213
  62.5 20.0 %collective-permute-start.14 = (bf16[256,1024]{1,0:T(8,128)(2,1)}, bf16[256,1024]{1,0:T(8,128)(2,1)}, u32[]{:S(2)}, u32[]{:S(2)}) collective-permute-start(bf16[256,1024]{1,0:T(8,128)(2,1)} %broadcast_select_fusion.5), channel_id=1, source_target_pairs={{0,4},{4,8},{8,12},{12,14},{14,10},{10,6},{6,2},{2,0},{1,5},{5,9},... | collective-permute-start | bytes 1572872 | tf_op jit(solution)/shard_map/ppermute | solution.py:235
  73.4 20.0 %collective-permute-start.8 = (bf16[256,1024]{1,0:T(8,128)(2,1)}, bf16[256,1024]{1,0:T(8,128)(2,1)}, u32[]{:S(2)}, u32[]{:S(2)}) collective-permute-start(bf16[256,1024]{1,0:T(8,128)(2,1)} %add_convert_fusion.9), channel_id=1, source_target_pairs={{0,4},{4,8},{8,12},{12,14},{14,10},{10,6},{6,2},{2,0},{1,5},{5,9},... | collective-permute-start | bytes 1572872 | tf_op jit(solution)/shard_map/ppermute | solution.py:235
  76.2 23.9 %collective-permute-start.17 = (bf16[256,1024]{1,0:T(8,128)(2,1)}, bf16[256,1024]{1,0:T(8,128)(2,1)S(1)}, u32[]{:S(2)}, u32[]{:S(2)}) collective-permute-start(bf16[256,1024]{1,0:T(8,128)(2,1)} %get-tuple-element.47), channel_id=1, source_target_pairs={{4,0},{8,4},{12,8},{14,12},{10,14},{6,10},{2,6},{0,2},{5,1},{9,5},... | collective-permute-start | bytes 1572872 | tf_op jit(solution)/shard_map/ppermute | solution.py:235
  98.5 23.0 %collective-permute-start.9 = (bf16[256,1024]{1,0:T(8,128)(2,1)S(1)}, bf16[256,1024]{1,0:T(8,128)(2,1)S(1)}, u32[]{:S(2)}, u32[]{:S(2)}) collective-permute-start(bf16[256,1024]{1,0:T(8,128)(2,1)S(1)} %get-tuple-element.43), channel_id=1, source_target_pairs={{0,4},{4,8},{8,12},{12,14},{14,10},{10,6},{6,2},{2,0},{1,5},{5,9},... | collective-permute-start | bytes 1572872 | tf_op jit(solution)/shard_map/ppermute | solution.py:235
  125.9 24.7 %collective-permute-start.12 = (bf16[256,1024]{1,0:T(8,128)(2,1)}, bf16[256,1024]{1,0:T(8,128)(2,1)S(1)}, u32[]{:S(2)}, u32[]{:S(2)}) collective-permute-start(bf16[256,1024]{1,0:T(8,128)(2,1)} %get-tuple-element.44), channel_id=1, source_target_pairs={{4,0},{8,4},{12,8},{14,12},{10,14},{6,10},{2,6},{0,2},{5,1},{9,5},... | collective-permute-start | bytes 1572872 | tf_op jit(solution)/shard_map/ppermute | solution.py:235
  140.7 19.0 %collective-permute-start.19 = (bf16[256,1024]{1,0:T(8,128)(2,1)S(1)}, bf16[256,1024]{1,0:T(8,128)(2,1)S(1)}, u32[]{:S(2)}, u32[]{:S(2)}) collective-permute-start(bf16[256,1024]{1,0:T(8,128)(2,1)S(1)} %add_convert_fusion.1), channel_id=1, source_target_pairs={{4,0},{8,4},{12,8},{14,12},{10,14},{6,10},{2,6},{0,2},{5,1},{9,5},... | collective-permute-start | bytes 1572872 | tf_op jit(solution)/shard_map/ppermute | solution.py:235
  142.1 22.0 %collective-permute-start.10 = (bf16[256,1024]{1,0:T(8,128)(2,1)}, bf16[256,1024]{1,0:T(8,128)(2,1)S(1)}, u32[]{:S(2)}, u32[]{:S(2)}) collective-permute-start(bf16[256,1024]{1,0:T(8,128)(2,1)} %get-tuple-element.40), channel_id=1, source_target_pairs={{0,4},{4,8},{8,12},{12,14},{14,10},{10,6},{6,2},{2,0},{1,5},{5,9},... | collective-permute-start | bytes 1572872 | tf_op jit(solution)/shard_map/ppermute | solution.py:235
  142.8 21.4 %collective-permute-start.16 = (bf16[256,1024]{1,0:T(8,128)(2,1)}, bf16[256,1024]{1,0:T(8,128)(2,1)S(1)}, u32[]{:S(2)}, u32[]{:S(2)}) collective-permute-start(bf16[256,1024]{1,0:T(8,128)(2,1)} %get-tuple-element.42), channel_id=1, source_target_pairs={{0,4},{4,8},{8,12},{12,14},{14,10},{10,6},{6,2},{2,0},{1,5},{5,9},... | collective-permute-start | bytes 1572872 | tf_op jit(solution)/shard_map/ppermute | solution.py:235
  162.6 21.9 %collective-permute-start.20 = (bf16[256,1024]{1,0:T(8,128)(2,1)S(1)}, bf16[256,1024]{1,0:T(8,128)(2,1)S(1)}, u32[]{:S(2)}, u32[]{:S(2)}) collective-permute-start(bf16[256,1024]{1,0:T(8,128)(2,1)S(1)} %get-tuple-element.49), channel_id=1, source_target_pairs={{4,0},{8,4},{12,8},{14,12},{10,14},{6,10},{2,6},{0,2},{5,1},{9,5},... | collective-permute-start | bytes 1572872 | tf_op jit(solution)/shard_map/ppermute | solution.py:235
  188.9 24.6 %collective-permute-start.21 = (bf16[256,1024]{1,0:T(8,128)(2,1)S(1)}, bf16[256,1024]{1,0:T(8,128)(2,1)S(1)}, u32[]{:S(2)}, u32[]{:S(2)}) collective-permute-start(bf16[256,1024]{1,0:T(8,128)(2,1)S(1)} %get-tuple-element.52.refs_0_), channel_id=1, source_target_pairs={{0,4},{4,8},{8,12},{12,14},{14,10},{10,6},{6,2},{2,0},{1,5},{5,9},... | collective-permute-start | bytes 1572872 | tf_op jit(solution)/shard_map/ppermute | solution.py:259
  189.8 25.1 %collective-permute-start.31 = (bf16[256,1024]{1,0:T(8,128)(2,1)S(1)}, bf16[256,1024]{1,0:T(8,128)(2,1)S(1)}, u32[]{:S(2)}, u32[]{:S(2)}) collective-permute-start(bf16[256,1024]{1,0:T(8,128)(2,1)S(1)} %get-tuple-element.52.refs_0_), channel_id=1, source_target_pairs={{4,0},{8,4},{12,8},{14,12},{10,14},{6,10},{2,6},{0,2},{5,1},{9,5},... | collective-permute-start | bytes 1572872 | tf_op jit(solution)/shard_map/ppermute | solution.py:259
  202.3 22.5 %collective-permute-start.37 = (bf16[256,1024]{1,0:T(8,128)(2,1)S(1)}, bf16[256,1024]{1,0:T(8,128)(2,1)S(1)}, u32[]{:S(2)}, u32[]{:S(2)}) collective-permute-start(bf16[256,1024]{1,0:T(8,128)(2,1)S(1)} %collective-permute-done.34.refs_3_), channel_id=1, source_target_pairs={{0,4},{4,8},{8,12},{12,14},{14,10},{10,6},{6,2},{2,0},{1,5},{5,9},... | collective-permute-start | bytes 1572872 | tf_op jit(solution)/shard_map/ppermute | solution.py:259
  203.6 22.5 %collective-permute-start.26 = (bf16[256,1024]{1,0:T(8,128)(2,1)S(1)}, bf16[256,1024]{1,0:T(8,128)(2,1)S(1)}, u32[]{:S(2)}, u32[]{:S(2)}) collective-permute-start(bf16[256,1024]{1,0:T(8,128)(2,1)S(1)} %collective-permute-done.25.refs_1_), channel_id=1, source_target_pairs={{4,0},{8,4},{12,8},{14,12},{10,14},{6,10},{2,6},{0,2},{5,1},{9,5},... | collective-permute-start | bytes 1572872 | tf_op jit(solution)/shard_map/ppermute | solution.py:259
  213.5 22.5 %collective-permute-start.22 = (bf16[256,1024]{1,0:T(8,128)(2,1)S(1)}, bf16[256,1024]{1,0:T(8,128)(2,1)S(1)}, u32[]{:S(2)}, u32[]{:S(2)}) collective-permute-start(bf16[256,1024]{1,0:T(8,128)(2,1)S(1)} %collective-permute-done.21.refs_2_), channel_id=1, source_target_pairs={{0,4},{4,8},{8,12},{12,14},{14,10},{10,6},{6,2},{2,0},{1,5},{5,9},... | collective-permute-start | bytes 1572872 | tf_op jit(solution)/shard_map/ppermute | solution.py:259
  214.9 22.5 %collective-permute-start.32 = (bf16[256,1024]{1,0:T(8,128)(2,1)S(1)}, bf16[256,1024]{1,0:T(8,128)(2,1)S(1)}, u32[]{:S(2)}, u32[]{:S(2)}) collective-permute-start(bf16[256,1024]{1,0:T(8,128)(2,1)S(1)} %collective-permute-done.31.refs_0_), channel_id=1, source_target_pairs={{4,0},{8,4},{12,8},{14,12},{10,14},{6,10},{2,6},{0,2},{5,1},{9,5},... | collective-permute-start | bytes 1572872 | tf_op jit(solution)/shard_map/ppermute | solution.py:259
  224.8 22.5 %collective-permute-start.38 = (bf16[256,1024]{1,0:T(8,128)(2,1)S(1)}, bf16[256,1024]{1,0:T(8,128)(2,1)S(1)}, u32[]{:S(2)}, u32[]{:S(2)}) collective-permute-start(bf16[256,1024]{1,0:T(8,128)(2,1)S(1)} %collective-permute-done.37.refs_3_), channel_id=1, source_target_pairs={{0,4},{4,8},{8,12},{12,14},{14,10},{10,6},{6,2},{2,0},{1,5},{5,9},... | collective-permute-start | bytes 1572872 | tf_op jit(solution)/shard_map/ppermute | solution.py:259
  226.2 28.4 %collective-permute-start.42 = (bf16[256,1024]{1,0:T(8,128)(2,1)S(1)}, bf16[256,1024]{1,0:T(8,128)(2,1)S(1)}, u32[]{:S(2)}, u32[]{:S(2)}) collective-permute-start(bf16[256,1024]{1,0:T(8,128)(2,1)S(1)} %broadcast_select_fusion.6), channel_id=1, source_target_pairs={{0,1},{1,0},{2,3},{3,2},{4,5},{5,4},{6,7},{7,6},{8,9},{9,8},{10,11... | collective-permute-start | bytes 1572872 | tf_op jit(solution)/shard_map/ppermute | solution.py:275
  253.8 24.5 %collective-permute-start.40 = (bf16[256,1024]{1,0:T(8,128)(2,1)S(1)}, bf16[256,1024]{1,0:T(8,128)(2,1)S(1)}, u32[]{:S(2)}, u32[]{:S(2)}) collective-permute-start(bf16[256,1024]{1,0:T(8,128)(2,1)S(1)} %broadcast_select_fusion.8), channel_id=1, source_target_pairs={{0,1},{1,0},{2,3},{3,2},{4,5},{5,4},{6,7},{7,6},{8,9},{9,8},{10,11... | collective-permute-start | bytes 1572872 | tf_op jit(solution)/shard_map/ppermute | solution.py:275
  253.9 25.0 %collective-permute-start.39 = (bf16[256,1024]{1,0:T(8,128)(2,1)S(1)}, bf16[256,1024]{1,0:T(8,128)(2,1)S(1)}, u32[]{:S(2)}, u32[]{:S(2)}) collective-permute-start(bf16[256,1024]{1,0:T(8,128)(2,1)S(1)} %broadcast_select_fusion.9), channel_id=1, source_target_pairs={{0,1},{1,0},{2,3},{3,2},{4,5},{5,4},{6,7},{7,6},{8,9},{9,8},{10,11... | collective-permute-start | bytes 1572872 | tf_op jit(solution)/shard_map/ppermute | solution.py:275
  254.5 32.4 %collective-permute-start.36 = (bf16[256,1024]{1,0:T(8,128)(2,1)S(1)}, bf16[256,1024]{1,0:T(8,128)(2,1)S(1)}, u32[]{:S(2)}, u32[]{:S(2)}) collective-permute-start(bf16[256,1024]{1,0:T(8,128)(2,1)S(1)} %broadcast_select_fusion.3), channel_id=1, source_target_pairs={{0,1},{1,0},{2,3},{3,2},{4,5},{5,4},{6,7},{7,6},{8,9},{9,8},{10,11... | collective-permute-start | bytes 1572872 | tf_op jit(solution)/shard_map/ppermute | solution.py:275
  254.6 19.6 %collective-permute-start.28 = (bf16[256,1024]{1,0:T(8,128)(2,1)S(1)}, bf16[256,1024]{1,0:T(8,128)(2,1)S(1)}, u32[]{:S(2)}, u32[]{:S(2)}) collective-permute-start(bf16[256,1024]{1,0:T(8,128)(2,1)S(1)} %collective-permute-done.27.refs_1_), channel_id=1, source_target_pairs={{4,0},{8,4},{12,8},{14,12},{10,14},{6,10},{2,6},{0,2},{5,1},{9,5},... | collective-permute-start | bytes 1572872 | tf_op jit(solution)/shard_map/ppermute | solution.py:259
  (35 other events, 470.3 us)

commit v2 on v1

--- a/solution.py
+++ b/solution.py
@@ -24,7 +24,8 @@
     return jnp.dot(a, b, preferred_element_type=F32)
 
 
-def attention_kernel(heads, core_ref, q_ref, k_ref, v_ref, pk_ref, pv_ref, o_ref):
+def attention_kernel(heads, core_ref, q_ref, k_ref, v_ref, pk_ref, pv_ref, *refs):
+    o_ref = refs[-1]
     rows = q_ref.shape[0]
     inv_root = 1.0 / math.sqrt(HD)
     query_pos = lax.broadcasted_iota(jnp.int32, (rows, rows), 0)
@@ -47,17 +48,21 @@
         o_ref[:, columns] = (mixed / total).astype(BF16)
 
 
-def attention(core, queries, keys, values, peer_keys, peer_values):
+def attention(core, queries, keys, values, peer_keys, peer_values, after=()):
+    queries, index, count = queries
     rows, width = queries.shape
+    width = width // count
     heads = min(4, width // HD)
+    first = index * width // (heads * HD)
     whole = pl.BlockSpec((rows, HD), lambda h, s: (0, 0))
+    wanted = pl.BlockSpec((rows, heads * HD), lambda h, s: (0, first + h))
     part = pl.BlockSpec((rows, heads * HD), lambda h, s: (0, h))
     return pl.pallas_call(
         functools.partial(attention_kernel, heads),
         grid_spec=pltpu.PrefetchScalarGridSpec(
             num_scalar_prefetch=1,
             grid=(width // (heads * HD),),
-            in_specs=[part, whole, whole, whole, whole],
+            in_specs=[wanted, whole, whole, whole, whole] + [pl.BlockSpec(memory_space=pl.ANY)] * len(after),
             out_specs=part,
         ),
         out_shape=jax.ShapeDtypeStruct((rows, width), BF16),
@@ -66,52 +71,77 @@
             flops=8 * rows * rows * width, bytes_accessed=4 * rows * width, transcendentals=2 * rows * rows * width // HD
         ),
         name="attention",
-    )(core, queries, keys, values, peer_keys, peer_values)
-
-
-def project_kernel(info_ref, x_ref, w_ref, own_ref, peer_ref):
+    )(core, queries, keys, values, peer_keys, peer_values, *after)
+
+
+def project_kernel(parts, info_ref, *refs):
+    own, peer = refs[:parts], refs[parts : 2 * parts]
+    w_ref = refs[2 * parts]
+    own_ref, peer_ref, x_ref, sum_ref = refs[-4:]
     rows = own_ref.shape[0]
-    result = dot(x_ref[...], w_ref[...]).astype(BF16)
-    own_ref[...] = result[:rows]
-    peer_ref[...] = result[rows:]
-
-
-def project(info, pair, both, weight, width):
-    depth = both.shape[1]
-    rows = both.shape[0] // 2
-    tile = min(512, width)
-    tiles = width // tile
-    out = pl.BlockSpec((rows, tile), lambda j, s: (0, j))
+    width = own[0].shape[1]
+    depth = w_ref.shape[0]
+    step = pl.program_id(0)
+
+    @pl.when(step == 0)
+    def _():
+        for part in range(parts):
+            columns = slice(part * width, (part + 1) * width)
+            x_ref[:rows, columns] = own[part][...]
+            x_ref[rows:, columns] = peer[part][...]
+
+    chunk = x_ref[:, pl.ds(pl.multiple_of(step * depth, depth), depth)]
+    result = dot(chunk, w_ref[...])
+
+    @pl.when(step == 0)
+    def _():
+        sum_ref[...] = result
+
+    @pl.when(step > 0)
+    def _():
+        total = (sum_ref[...] + result).astype(BF16)
+        own_ref[...] = total[:rows]
+        peer_ref[...] = total[rows:]
+
+
+def project(info, pair, pieces, piece, own, peer, weight, width, after):
+    rows, part_width = own[0].shape
+    parts = len(own)
+    depth = parts * part_width
+    whole = pl.BlockSpec((rows, part_width), lambda j, s: (0, 0))
+    out = pl.BlockSpec((rows, width), lambda j, s: (0, 0))
     return pl.pallas_call(
-        project_kernel,
+        functools.partial(project_kernel, parts),
         grid_spec=pltpu.PrefetchScalarGridSpec(
             num_scalar_prefetch=1,
-            grid=(tiles,),
-            in_specs=[
-                pl.BlockSpec((2 * rows, depth), lambda j, s: (0, 0)),
-                pl.BlockSpec((depth, tile), lambda j, s: (0, s[pair] * tiles + j)),
-            ],
+            grid=(2,),
+            in_specs=[whole] * (2 * parts)
+            + [pl.BlockSpec((depth // 2, width), lambda j, s: (j, s[pair] * pieces + piece))]
+            + [pl.BlockSpec(memory_space=pl.ANY)] * len(after),
             out_specs=[out, out],
+            scratch_shapes=[pltpu.VMEM((2 * rows, depth), BF16), pltpu.VMEM((2 * rows, width), F32)],
         ),
         out_shape=[jax.ShapeDtypeStruct((rows, width), BF16)] * 2,
-        compiler_params=pltpu.CompilerParams(vmem_limit_bytes=24 * MIB),
+        compiler_params=pltpu.CompilerParams(vmem_limit_bytes=20 * MIB),
         cost_estimate=pl.CostEstimate(
             flops=4 * rows * depth * width, bytes_accessed=2 * depth * width, transcendentals=0
         ),
         name="project",
-    )(info, both, weight)
+    )(info, *own, *peer, weight, *after)
 
 
 def query_kernel(pieces, pair, half, first, info_ref, *refs):
     one, other, far = refs[:pieces], refs[pieces : 2 * pieces], refs[2 * pieces : 3 * pieces]
     w_ref = refs[3 * pieces]
-    acc_refs = refs[3 * pieces + 1 : -3]
-    own_ref, peer_ref, x_ref = refs[-3:]
+    acc_refs = () if first else refs[3 * pieces + 1 : 3 * pieces + 3]
+    own_ref, peer_ref, info_out, x_ref = refs[-4:]
     rows = own_ref.shape[0]
     width = one[0].shape[1]
 
     @pl.when(pl.program_id(0) == 0)
     def _():
+        for index in range(2 * half):
+            info_out[index] = info_ref[index]
         for piece in range(pieces):
             columns = slice(piece * width, (piece + 1) * width)
 
@@ -134,12 +164,12 @@
         peer_ref[...] = (acc_refs[1][...] + result[rows:]).astype(peer_ref.dtype)
 
 
-def query_block(info, pair, half, one, other, far, weight, acc, last):
+def query_block(info, pair, half, one, other, far, weight, acc, last, after):
     pieces = len(one)
     rows, piece_width = one[0].shape
     depth = pieces * piece_width
     width = weight.shape[1]
-    tile = min(512, width)
+    tile = min(1024, width)
     whole = pl.BlockSpec((rows, piece_width), lambda j, s: (0, 0))
     out = pl.BlockSpec((rows, tile), lambda j, s: (0, j))
     first = acc is None
@@ -151,20 +181,22 @@
             grid=(width // tile,),
             in_specs=[whole] * (3 * pieces)
             + [pl.BlockSpec((depth, tile), lambda j, s: (s[pair], j))]
-            + [out] * len(acc),
-            out_specs=[out, out],
+            + [out] * len(acc)
+            + [pl.BlockSpec(memory_space=pl.ANY)] * len(after),
+            out_specs=[out, out, pl.BlockSpec(memory_space=pltpu.SMEM)],
             scratch_shapes=[pltpu.VMEM((2 * rows, depth), BF16)],
         ),
         out_shape=[
             jax.ShapeDtypeStruct((rows, width), F32),
             jax.ShapeDtypeStruct((rows, width), BF16 if last else F32),
+            jax.ShapeDtypeStruct(info.shape, jnp.int32),
         ],
-        compiler_params=pltpu.CompilerParams(vmem_limit_bytes=32 * MIB),
+        compiler_params=pltpu.CompilerParams(vmem_limit_bytes=30 * MIB),
         cost_estimate=pl.CostEstimate(
             flops=4 * rows * depth * width, bytes_accessed=2 * depth * width + 16 * rows * width, transcendentals=0
         ),
         name="next_query",
-    )(info, *one, *other, *far, weight, *acc)
+    )(info, *one, *other, *far, weight, *acc, *after)
 
 
 def ring_of(n):
@@ -194,7 +226,8 @@
                 table[c, h, k] = (near if mine else far) - h * half
                 table[c, h, half + k] = mine
     info = lax.dynamic_index_in_dim(jnp.asarray(table.reshape(2 * n, n)), chip * 2 + core, 0, keepdims=False)
-    near_mine = [info[half + k] == 1 for k in range(half)]
+    def is_near(index, k):
+        return index[half + k] == 1
 
     heads_here = width // HD
     kv_head = chip * heads_here // (H // KVH)
@@ -202,37 +235,52 @@
     own_values = lax.dynamic_index_in_dim(att_values, kv_head, 1, keepdims=False)
     peer_keys = lax.ppermute(own_keys, "tokens", swap)
     peer_values = lax.ppermute(own_values, "tokens", swap)
-    attended = attention(core[None], att_queries, own_keys, own_values, peer_keys, peer_values)
-    both = jnp.concatenate([attended, lax.ppermute(attended, "tokens", swap)], axis=0)
-
-    mine, swapped = {}, {}
-    order = [0] + [k for j in range(1, half) for k in (half - j, j) if k not in range(0, 1)]
-    order = list(dict.fromkeys(order))
-    for k in order:
-        mine[k], outgoing = project(info, k, both, out_weight, residual.shape[1])
-        swapped[k] = lax.ppermute(outgoing, "tokens", swap)
+    attended, attended_peer = [], []
+    for part in range(2):
+        queries = (att_queries, part, 2)
+        attended.append(attention(core[None], queries, own_keys, own_values, peer_keys, peer_values, attended))
+        attended_peer.append(lax.ppermute(attended[-1], "tokens", swap))
 
     def columns_of(array, piece):
         return array[:, piece * piece_width : (piece + 1) * piece_width]
 
+    hops = [(half, half - 1) if piece % 2 == 0 else (half - 1, half) for piece in range(pieces)]
+    chains = [(piece, way) for way in range(2) for piece in range(pieces)]
+    chains = sorted(chains, key=lambda c: (c[0] + c[1]) % 2)
+    events = [
+        (piece, way, step) for step in range(1, half + 1) for piece, way in chains if step <= hops[piece][way]
+    ]
+
+    def place_of(piece, way, step):
+        q = hops[piece][way] - step + 1
+        return q if way == 0 else -q
+
+    order = list(dict.fromkeys([(place_of(*event) % half, event[0]) for event in events] + [(0, p) for p in range(pieces)]))
+    made = {}
+
+    def make(after):
+        if len(made) < len(order):
+            k, piece = order[len(made)]
+            mine, outgoing = project(
+                info, k, pieces, piece, attended, attended_peer, out_weight, piece_width, after
+            )
+            made[k, piece] = (mine, lax.ppermute(outgoing, "tokens", swap))
+
     def block(q, piece):
-        k = q % half
-        near = near_mine[k] if q == k else jnp.logical_not(near_mine[k])
-        return jnp.where(near, columns_of(mine[k], piece), columns_of(swapped[k], piece)).astype(F32)
-
-    hops = [(half, half - 1) if piece % 2 == 0 else (half - 1, half) for piece in range(pieces)]
+        mine, swapped = made[q % half, piece]
+        near = is_near(info, q % half) if q == q % half else jnp.logical_not(is_near(info, q % half))
+        return jnp.where(near, mine, swapped).astype(F32)
+
     arrived = {}
-    for step in range(1, half + 1):
-        for piece in range(pieces):
-            for way, pairs in ((0, up), (1, down)):
-                length = hops[piece][way]
-                if step > length:
-                    continue
-                q = length - step + 1
-                value = block(q if way == 0 else -q, piece)
-                if step > 1:
-                    value = value + arrived[piece, way].astype(F32)
-                arrived[piece, way] = lax.ppermute(value.astype(BF16), "tensor", pairs)
+    make(())
+    make(())
+    for piece, way, step in events:
+        value = block(place_of(piece, way, step), piece)
+        if step > 1:
+            value = value + arrived[piece, way].astype(F32)
+        value = value.astype(BF16)
+        arrived[piece, way] = lax.ppermute(value, "tensor", up if way == 0 else down)
+        make((value,))
 
     resid, scaled = [], []
     squares = jnp.zeros((rows,), F32)
@@ -261,20 +309,25 @@
                 if abs(target) == half:
                     held[piece, half] = held[piece, -half] = value
     distance = half
+    totals = []
     while distance >= 1:
         shifted = [(ring[p], ring[(p + distance) % n]) for p in range(n)]
         squares = squares + lax.ppermute(squares, "tensor", shifted)
+        totals.append(squares)
         distance //= 2
 
     acc = None
     when = sorted(range(half), key=lambda k: max(k, half - k))
-    for k in when:
+    indices = [info, info]
+    for count, k in enumerate(when):
         one = [held[piece, k] for piece in range(pieces)]
         other = [held[piece, k - half] for piece in range(pieces)]
-        far = [
-            lax.ppermute(jnp.where(near_mine[k], other[piece], one[piece]), "tokens", swap) for piece in range(pieces)
-        ]
-        acc = query_block(info, k, half, one, other, far, next_weight, acc, k == when[-1])
+        near = is_near(indices[-2] if count > 1 else indices[-1], k)
+        far = [lax.ppermute(jnp.where(near, other[piece], one[piece]), "tokens", swap) for piece in range(pieces)]
+        *acc, index = query_block(
+            info, k, half, one, other, far, next_weight, acc, k == when[-1], totals[max(count - 1, 0) : count]
+        )
+        indices.append(index)
     query_sum = acc[0] + lax.ppermute(acc[1], "tokens", swap).astype(F32)
     factor = 1.0 / jnp.sqrt(squares / D + EPS_NORM)
     return (resid_out, (query_sum * factor[:, None]).astype(BF16))
@@ -290,7 +343,7 @@
     own_values = lax.dynamic_index_in_dim(att_values, kv_head, 1, keepdims=False)
     peer_keys = lax.ppermute(own_keys, "tokens", swap)
     peer_values = lax.ppermute(own_values, "tokens", swap)
-    attended = attention(core[None], att_queries, own_keys, own_values, peer_keys, peer_values)
+    attended = attention(core[None], (att_queries, 0, 1), own_keys, own_values, peer_keys, peer_values)
     both = lax.all_gather(attended, "tokens", axis=0, tiled=True)
     partial = dot(both, out_weight).astype(BF16)
     partial = lax.all_to_all(partial, "tokens", split_axis=0, concat_axis=1, tiled=True)

time: 320 us -> 282 us (0.88)
  waiting for transfers between devices: 174 us -> 130 us
  Pallas kernels: 71.4 us -> 82.7 us
  other arithmetic: 24.4 us -> 16.9 us
  starting transfers between devices: 41 us -> 37.2 us
  local copies, waits for them, and re-layouts: 4.94 us -> 8.6 us
    ppermute x27 -> x32, waiting for transfers between devices: 94.7 us -> 58.8 us  [the longest x14 57.5 us: on_ring(): lax.ppermute(value, 'tensor', up if way == 0 else down)]
    ppermute x14, waiting for transfers between devices: 66.9 us -> 52.2 us  [on_ring(): value = lax.ppermute(held[source], 'tensor', pairs)]
    pallas_call x4 -> x8, Pallas kernels: 33.8 us -> 43.3 us  [project(): pl.pallas_call(functools.partial(project_kernel, parts), grid_spec=pltpu....]
    ppermute x3, waiting for transfers between devices: 10.8 us -> 16.7 us  [on_ring(): squares = squares + lax.ppermute(squares, 'tensor', shifted)]
    ppermute x27 -> x32, starting transfers between devices: 22.4 us -> 19.1 us  [the longest x14 15.4 us: on_ring(): lax.ppermute(value, 'tensor', up if way == 0 else down)]
    convert_element_type x5 -> x8, other arithmetic: 11.5 us -> 8.99 us  [on_ring(): value = value.astype(BF16)]
    select_n x11 -> x12, other arithmetic: 6.76 us -> 4.43 us  [the longest x4 3.98 us: block(): return jnp.where(near, mine, swapped).astype(F32)]
  transfers between devices with their start and end apart: 47 -> 52, of which waited for: 23 -> 24; matrix products, arithmetic and copies ran while one was open for 6% -> 6% of each run, Pallas kernels for 15% -> 22%
where the time goes in v2:
time: 282 us; the launch traced here: 281 us
  waiting for transfers between devices  130 us (46%)
  Pallas kernels  82.7 us (29%)
  starting transfers between devices  37.2 us (13%)
  other arithmetic  16.9 us (6%)
  local copies, waits for them, and re-layouts  8.6 us (3%)
  between operations  5.78 us (2%)
    ppermute x14, waiting for transfers between devices, on_ring(): lax.ppermute(value, 'tensor', up if way == 0 else down)  57.5 us
    ppermute x14, waiting for transfers between devices, on_ring(): value = lax.ppermute(held[source], 'tensor', pairs)  52.2 us
    pallas_call x8, Pallas kernels, project(): pl.pallas_call(functools.partial(project_kernel, parts), grid_spec=pltpu....  43.3 us
    pallas_call x4, Pallas kernels, query_block(): pl.pallas_call(functools.partial(query_kernel, pieces, pair, half, first)...  33.7 us
    ppermute x3, waiting for transfers between devices, on_ring(): squares = squares + lax.ppermute(squares, 'tensor', shifted)  16.7 us
    ppermute x14, starting transfers between devices, on_ring(): lax.ppermute(value, 'tensor', up if way == 0 else down)  15.4 us
    ppermute x14, starting transfers between devices, on_ring(): value = lax.ppermute(held[source], 'tensor', pairs)  14.6 us
    convert_element_type x8, other arithmetic, on_ring(): value = value.astype(BF16)  8.99 us
  transfers between devices with their start and end apart: 52, of which 24 were waited for; matrix products, arithmetic and copies ran while one was open for 6% of the time, Pallas kernels for 22%

profile of v2, /device:TPU:0, one launch (start us, length us, event | category | flops | bytes accessed | tf_op | source)
XLA Modules:
  0.0 281.2 jit_solution(6166227696723470513)
XLA Ops:
  14.0 5.1 %project.8 = (bf16[256,1024]{1,0:T(8,128)(2,1)S(1)}, bf16[256,1024]{1,0:T(8,128)(2,1)S(1)}) custom-call(s32[8]{0:T(128)S(1)} %get-tuple-element.71.info_ref, bf16[256,1024]{1,0:T(8,128)(2,1)S(1)} %attention.2.refs_0_, bf16[256,1024]{1,0:T(8,128)(2,1)S(1)} %attention.3.refs_1_, bf16[256,1024]{1,0:T(8,128)(2,1)S(1)} %collective-permute-done.2.refs_2_, ...), custom_call_target="tpu_custom_call" | custom-call | flops 2147483648 | bytes 4194304 | tf_op jit(solution)/shard_map/project/pallas_call | solution.py:113
  22.4 5.1 %project.13 = (bf16[256,1024]{1,0:T(8,128)(2,1)S(1)}, bf16[256,1024]{1,0:T(8,128)(2,1)S(1)}) custom-call(s32[8]{0:T(128)S(1)} %get-tuple-element.71.info_ref, bf16[256,1024]{1,0:T(8,128)(2,1)S(1)} %attention.2.refs_0_, bf16[256,1024]{1,0:T(8,128)(2,1)S(1)} %attention.3.refs_1_, bf16[256,1024]{1,0:T(8,128)(2,1)S(1)} %collective-permute-done.2.refs_2_, ...), custom_call_target="tpu_custom_call" | custom-call | flops 2147483648 | bytes 4194304 | tf_op jit(solution)/shard_map/project/pallas_call | solution.py:113
  28.3 5.1 %project.9 = (bf16[256,1024]{1,0:T(8,128)(2,1)S(1)}, bf16[256,1024]{1,0:T(8,128)(2,1)S(1)}) custom-call(s32[8]{0:T(128)S(1)} %get-tuple-element.71.info_ref, bf16[256,1024]{1,0:T(8,128)(2,1)S(1)} %attention.2.refs_0_, bf16[256,1024]{1,0:T(8,128)(2,1)S(1)} %attention.3.refs_1_, bf16[256,1024]{1,0:T(8,128)(2,1)S(1)} %collective-permute-done.2.refs_2_, ...), custom_call_target="tpu_custom_call" | custom-call | flops 2147483648 | bytes 4194304 | tf_op jit(solution)/shard_map/project/pallas_call | solution.py:113
  37.8 5.1 %project.14 = (bf16[256,1024]{1,0:T(8,128)(2,1)S(1)}, bf16[256,1024]{1,0:T(8,128)(2,1)S(1)}) custom-call(s32[8]{0:T(128)S(1)} %get-tuple-element.71.info_ref, bf16[256,1024]{1,0:T(8,128)(2,1)S(1)} %attention.2.refs_0_, bf16[256,1024]{1,0:T(8,128)(2,1)S(1)} %attention.3.refs_1_, bf16[256,1024]{1,0:T(8,128)(2,1)S(1)} %collective-permute-done.2.refs_2_, ...), custom_call_target="tpu_custom_call" | custom-call | flops 2147483648 | bytes 4194304 | tf_op jit(solution)/shard_map/project/pallas_call | solution.py:113
  43.2 5.9 %project.10 = (bf16[256,1024]{1,0:T(8,128)(2,1)S(1)}, bf16[256,1024]{1,0:T(8,128)(2,1)}) custom-call(s32[8]{0:T(128)S(1)} %get-tuple-element.71.info_ref, bf16[256,1024]{1,0:T(8,128)(2,1)S(1)} %attention.2.refs_0_, bf16[256,1024]{1,0:T(8,128)(2,1)S(1)} %attention.3.refs_1_, bf16[256,1024]{1,0:T(8,128)(2,1)S(1)} %collective-permute-done.2.refs_2_, ...), custom_call_target="tpu_custom_call" | custom-call | flops 2147483648 | bytes 4194304 | tf_op jit(solution)/shard_map/project/pallas_call | solution.py:113
  51.9 5.9 %project.15 = (bf16[256,1024]{1,0:T(8,128)(2,1)S(1)}, bf16[256,1024]{1,0:T(8,128)(2,1)}) custom-call(s32[8]{0:T(128)S(1)} %get-tuple-element.71.info_ref, bf16[256,1024]{1,0:T(8,128)(2,1)S(1)} %attention.2.refs_0_, bf16[256,1024]{1,0:T(8,128)(2,1)S(1)} %attention.3.refs_1_, bf16[256,1024]{1,0:T(8,128)(2,1)S(1)} %collective-permute-done.2.refs_2_, ...), custom_call_target="tpu_custom_call" | custom-call | flops 2147483648 | bytes 4194304 | tf_op jit(solution)/shard_map/project/pallas_call | solution.py:113
  62.6 5.1 %project.11 = (bf16[256,1024]{1,0:T(8,128)(2,1)S(1)}, bf16[256,1024]{1,0:T(8,128)(2,1)S(1)}) custom-call(s32[8]{0:T(128)S(1)} %get-tuple-element.71.info_ref, bf16[256,1024]{1,0:T(8,128)(2,1)S(1)} %attention.2.refs_0_, bf16[256,1024]{1,0:T(8,128)(2,1)S(1)} %attention.3.refs_1_, bf16[256,1024]{1,0:T(8,128)(2,1)S(1)} %collective-permute-done.2.refs_2_, ...), custom_call_target="tpu_custom_call" | custom-call | flops 2147483648 | bytes 4194304 | tf_op jit(solution)/shard_map/project/pallas_call | solution.py:113
  74.7 9.6 %collective-permute-done.21 = bf16[256,1024]{1,0:T(8,128)(2,1)S(1)} collective-permute-done((bf16[256,1024]{1,0:T(8,128)(2,1)S(1)}, bf16[256,1024]{1,0:T(8,128)(2,1)S(1)}, u32[]{:S(2)}, u32[]{:S(2)}) %collective-permute-start.21) | collective-permute-done | bytes 524320 | tf_op jit(solution)/shard_map/ppermute | solution.py:282
  85.5 5.9 %project.12 = (bf16[256,1024]{1,0:T(8,128)(2,1)S(1)}, bf16[256,1024]{1,0:T(8,128)(2,1)}) custom-call(s32[8]{0:T(128)S(1)} %get-tuple-element.71.info_ref, bf16[256,1024]{1,0:T(8,128)(2,1)S(1)} %attention.2.refs_0_, bf16[256,1024]{1,0:T(8,128)(2,1)S(1)} %attention.3.refs_1_, bf16[256,1024]{1,0:T(8,128)(2,1)S(1)} %collective-permute-done.2.refs_2_, ...), custom_call_target="tpu_custom_call" | custom-call | flops 2147483648 | bytes 4194304 | tf_op jit(solution)/shard_map/project/pallas_call | solution.py:113
  101.1 6.0 %collective-permute-done.23 = bf16[256,1024]{1,0:T(8,128)(2,1)} collective-permute-done((bf16[256,1024]{1,0:T(8,128)(2,1)S(1)}, bf16[256,1024]{1,0:T(8,128)(2,1)}, u32[]{:S(2)}, u32[]{:S(2)}) %collective-permute-start.23) | collective-permute-done | bytes 524320 | tf_op jit(solution)/shard_map/ppermute | solution.py:282
  108.8 9.5 %collective-permute-done.17 = bf16[256,1024]{1,0:T(8,128)(2,1)} collective-permute-done((bf16[256,1024]{1,0:T(8,128)(2,1)}, bf16[256,1024]{1,0:T(8,128)(2,1)}, u32[]{:S(2)}, u32[]{:S(2)}) %collective-permute-start.17) | collective-permute-done | bytes 524320 | tf_op jit(solution)/shard_map/ppermute | solution.py:282
  130.0 10.7 %collective-permute-done.18 = bf16[256,1024]{1,0:T(8,128)(2,1)S(1)} collective-permute-done((bf16[256,1024]{1,0:T(8,128)(2,1)S(1)}, bf16[256,1024]{1,0:T(8,128)(2,1)S(1)}, u32[]{:S(2)}, u32[]{:S(2)}) %collective-permute-start.18) | collective-permute-done | bytes 524320 | tf_op jit(solution)/shard_map/ppermute | solution.py:282
  140.7 10.8 %collective-permute-done.25 = bf16[256,1024]{1,0:T(8,128)(2,1)S(1)} collective-permute-done((bf16[256,1024]{1,0:T(8,128)(2,1)S(1)}, bf16[256,1024]{1,0:T(8,128)(2,1)S(1)}, u32[]{:S(2)}, u32[]{:S(2)}) %collective-permute-start.25) | collective-permute-done | bytes 524320 | tf_op jit(solution)/shard_map/ppermute | solution.py:282
  156.8 10.5 %collective-permute-done.26.refs_2_ = bf16[256,1024]{1,0:T(8,128)(2,1)S(1)} collective-permute-done((bf16[256,1024]{1,0:T(8,128)(2,1)S(1)}, bf16[256,1024]{1,0:T(8,128)(2,1)S(1)}, u32[]{:S(2)}, u32[]{:S(2)}) %collective-permute-start.26) | collective-permute-done | bytes 524320 | tf_op jit(solution)/shard_map/ppermute | solution.py:307
  169.4 11.1 %collective-permute-done.30.refs_1_ = bf16[256,1024]{1,0:T(8,128)(2,1)S(1)} collective-permute-done((bf16[256,1024]{1,0:T(8,128)(2,1)S(1)}, bf16[256,1024]{1,0:T(8,128)(2,1)S(1)}, u32[]{:S(2)}, u32[]{:S(2)}) %collective-permute-start.30) | collective-permute-done | bytes 524320 | tf_op jit(solution)/shard_map/ppermute | solution.py:307
  182.6 7.2 %collective-permute-done.27.refs_2_ = bf16[256,1024]{1,0:T(8,128)(2,1)S(1)} collective-permute-done((bf16[256,1024]{1,0:T(8,128)(2,1)S(1)}, bf16[256,1024]{1,0:T(8,128)(2,1)S(1)}, u32[]{:S(2)}, u32[]{:S(2)}) %collective-permute-start.27) | collective-permute-done | bytes 524320 | tf_op jit(solution)/shard_map/ppermute | solution.py:307
  191.9 10.0 %collective-permute-done.31.refs_1_ = bf16[256,1024]{1,0:T(8,128)(2,1)S(1)} collective-permute-done((bf16[256,1024]{1,0:T(8,128)(2,1)S(1)}, bf16[256,1024]{1,0:T(8,128)(2,1)S(1)}, u32[]{:S(2)}, u32[]{:S(2)}) %collective-permute-start.31) | collective-permute-done | bytes 524320 | tf_op jit(solution)/shard_map/ppermute | solution.py:307
  204.9 12.3 %collective-permute-done.43 = f32[256]{0:T(256)S(1)} collective-permute-done((f32[256]{0:T(256)S(1)}, f32[256]{0:T(256)S(1)}, u32[]{:S(2)}, u32[]{:S(2)}) %collective-permute-start.43) | collective-permute-done | bytes 1056 | tf_op jit(solution)/shard_map/ppermute | solution.py:315
  217.1 4.5 %collective-permute-done.49 = f32[256]{0:T(256)S(1)} collective-permute-done((f32[256]{0:T(256)S(1)}, f32[256]{0:T(256)S(1)}, u32[]{:S(2)}, u32[]{:S(2)}) %collective-permute-start.49) | collective-permute-done | bytes 1056 | tf_op jit(solution)/shard_map/ppermute | solution.py:315
  225.7 8.5 %next_query.4 = (f32[256,2048]{1,0:T(8,128)S(1)}, f32[256,2048]{1,0:T(8,128)S(1)}, s32[8]{0:T(128)S(1)}) custom-call(s32[8]{0:T(128)S(1)} %get-tuple-element.71.info_ref, bf16[256,1024]{1,0:T(8,128)(2,1)S(1)} %collective-permute-done.38.refs_0_, bf16[256,1024]{1,0:T(8,128)(2,1)S(1)} %collective-permute-done.31.refs_1_, ...), custom_call_target="tpu_custom_call" | custom-call | flops 4294967296 | bytes 16777216 | tf_op jit(solution)/shard_map/next_query/pallas_call | solution.py:177
  236.8 8.1 %collective-permute-done.46.refs_0_ = bf16[256,1024]{1,0:T(8,128)(2,1)S(1)} collective-permute-done((bf16[256,1024]{1,0:T(8,128)(2,1)S(1)}, bf16[256,1024]{1,0:T(8,128)(2,1)S(1)}, u32[]{:S(2)}, u32[]{:S(2)}) %collective-permute-start.46) | collective-permute-done | bytes 524320 | tf_op jit(solution)/shard_map/ppermute | solution.py:307
  247.4 8.5 %next_query.5 = (f32[256,2048]{1,0:T(8,128)S(1)}, f32[256,2048]{1,0:T(8,128)S(1)}, s32[8]{0:T(128)S(1)}) custom-call(s32[8]{0:T(128)S(1)} %get-tuple-element.71.info_ref, bf16[256,1024]{1,0:T(8,128)(2,1)S(1)} %collective-permute-done.34.refs_0_, bf16[256,1024]{1,0:T(8,128)(2,1)S(1)} %collective-permute-done.30.refs_1_, ...), custom_call_target="tpu_custom_call" | custom-call | flops 4294967296 | bytes 16777216 | tf_op jit(solution)/shard_map/next_query/pallas_call | solution.py:177
  260.3 8.4 %next_query.6 = (f32[256,2048]{1,0:T(8,128)S(1)}, f32[256,2048]{1,0:T(8,128)S(1)}, s32[8]{0:T(128)}) custom-call(s32[8]{0:T(128)S(1)} %get-tuple-element.71.info_ref, bf16[256,1024]{1,0:T(8,128)(2,1)S(1)} %collective-permute-done.46.refs_0_, bf16[256,1024]{1,0:T(8,128)(2,1)S(1)} %collective-permute-done.32.refs_1_, ...), custom_call_target="tpu_custom_call" | custom-call | flops 4294967296 | bytes 16777216 | tf_op jit(solution)/shard_map/next_query/pallas_call | solution.py:177
  268.8 8.3 %next_query.7 = (f32[256,2048]{1,0:T(8,128)S(1)}, bf16[256,2048]{1,0:T(8,128)(2,1)S(1)}, s32[8]{0:T(128)}) custom-call(s32[8]{0:T(128)S(1)} %get-tuple-element.71.info_ref, bf16[256,1024]{1,0:T(8,128)(2,1)S(1)} %get-tuple-element.62.refs_0_, bf16[256,1024]{1,0:T(8,128)(2,1)S(1)} %get-tuple-element.60.refs_1_, ...), custom_call_target="tpu_custom_call" | custom-call | flops 4294967296 | bytes 16777216 | tf_op jit(solution)/shard_map/next_query/pallas_call | solution.py:177
  (182 shorter events, 88.1 us)
Async XLA Ops:
  34.0 17.7 %collective-permute-start.12 = (bf16[256,1024]{1,0:T(8,128)(2,1)S(1)}, bf16[256,1024]{1,0:T(8,128)(2,1)S(1)}, u32[]{:S(2)}, u32[]{:S(2)}) collective-permute-start(bf16[256,1024]{1,0:T(8,128)(2,1)S(1)} %broadcast_select_fusion.10.refs_5_), channel_id=1, source_target_pairs={{0,4},{4,8},{8,12},{12,14},{14,10},{10,6},{6,2},{2,0},{1,5},{5,9},... | collective-permute-start | bytes 1572872 | tf_op jit(solution)/shard_map/ppermute | solution.py:282
  50.3 17.7 %collective-permute-start.20 = (bf16[256,1024]{1,0:T(8,128)(2,1)}, bf16[256,1024]{1,0:T(8,128)(2,1)}, u32[]{:S(2)}, u32[]{:S(2)}) collective-permute-start(bf16[256,1024]{1,0:T(8,128)(2,1)} %broadcast_select_fusion.6.refs_5_), channel_id=1, source_target_pairs={{0,4},{4,8},{8,12},{12,14},{14,10},{10,6},{6,2},{2,0},{1,5},{5,9},... | collective-permute-start | bytes 1572872 | tf_op jit(solution)/shard_map/ppermute | solution.py:282
  70.9 21.5 %collective-permute-start.16 = (bf16[256,1024]{1,0:T(8,128)(2,1)}, bf16[256,1024]{1,0:T(8,128)(2,1)}, u32[]{:S(2)}, u32[]{:S(2)}) collective-permute-start(bf16[256,1024]{1,0:T(8,128)(2,1)} %broadcast_select_fusion.7.refs_5_), channel_id=1, source_target_pairs={{4,0},{8,4},{12,8},{14,12},{10,14},{6,10},{2,6},{0,2},{5,1},{9,5},... | collective-permute-start | bytes 1572872 | tf_op jit(solution)/shard_map/ppermute | solution.py:282
  71.6 23.3 %collective-permute-start.13 = (bf16[256,1024]{1,0:T(8,128)(2,1)S(1)}, bf16[256,1024]{1,0:T(8,128)(2,1)}, u32[]{:S(2)}, u32[]{:S(2)}) collective-permute-start(bf16[256,1024]{1,0:T(8,128)(2,1)S(1)} %add_convert_fusion.8.refs_5_), channel_id=1, source_target_pairs={{0,4},{4,8},{8,12},{12,14},{14,10},{10,6},{6,2},{2,0},{1,5},{5,9},... | collective-permute-start | bytes 1572872 | tf_op jit(solution)/shard_map/ppermute | solution.py:282
  97.8 20.5 %collective-permute-start.17 = (bf16[256,1024]{1,0:T(8,128)(2,1)}, bf16[256,1024]{1,0:T(8,128)(2,1)}, u32[]{:S(2)}, u32[]{:S(2)}) collective-permute-start(bf16[256,1024]{1,0:T(8,128)(2,1)} %get-tuple-element.67), channel_id=1, source_target_pairs={{4,0},{8,4},{12,8},{14,12},{10,14},{6,10},{2,6},{0,2},{5,1},{9,5},... | collective-permute-start | bytes 1572872 | tf_op jit(solution)/shard_map/ppermute | solution.py:282
  98.1 31.8 %collective-permute-start.22 = (bf16[256,1024]{1,0:T(8,128)(2,1)}, bf16[256,1024]{1,0:T(8,128)(2,1)S(1)}, u32[]{:S(2)}, u32[]{:S(2)}) collective-permute-start(bf16[256,1024]{1,0:T(8,128)(2,1)} %get-tuple-element.68), channel_id=1, source_target_pairs={{0,4},{4,8},{8,12},{12,14},{14,10},{10,6},{6,2},{2,0},{1,5},{5,9},... | collective-permute-start | bytes 1572872 | tf_op jit(solution)/shard_map/ppermute | solution.py:282
  99.8 23.0 %collective-permute-start.14 = (bf16[256,1024]{1,0:T(8,128)(2,1)}, bf16[256,1024]{1,0:T(8,128)(2,1)S(1)}, u32[]{:S(2)}, u32[]{:S(2)}) collective-permute-start(bf16[256,1024]{1,0:T(8,128)(2,1)} %get-tuple-element.66), channel_id=1, source_target_pairs={{0,4},{4,8},{8,12},{12,14},{14,10},{10,6},{6,2},{2,0},{1,5},{5,9},... | collective-permute-start | bytes 1572872 | tf_op jit(solution)/shard_map/ppermute | solution.py:282
  108.4 21.0 %collective-permute-start.24 = (bf16[256,1024]{1,0:T(8,128)(2,1)S(1)}, bf16[256,1024]{1,0:T(8,128)(2,1)S(1)}, u32[]{:S(2)}, u32[]{:S(2)}) collective-permute-start(bf16[256,1024]{1,0:T(8,128)(2,1)S(1)} %add_convert_fusion.1), channel_id=1, source_target_pairs={{4,0},{8,4},{12,8},{14,12},{10,14},{6,10},{2,6},{0,2},{5,1},{9,5},... | collective-permute-start | bytes 1572872 | tf_op jit(solution)/shard_map/ppermute | solution.py:282
  119.7 21.0 %collective-permute-start.18 = (bf16[256,1024]{1,0:T(8,128)(2,1)S(1)}, bf16[256,1024]{1,0:T(8,128)(2,1)S(1)}, u32[]{:S(2)}, u32[]{:S(2)}) collective-permute-start(bf16[256,1024]{1,0:T(8,128)(2,1)S(1)} %add_convert_fusion.4), channel_id=1, source_target_pairs={{4,0},{8,4},{12,8},{14,12},{10,14},{6,10},{2,6},{0,2},{5,1},{9,5},... | collective-permute-start | bytes 1572872 | tf_op jit(solution)/shard_map/ppermute | solution.py:282
  123.1 17.6 %collective-permute-start.15 = (bf16[256,1024]{1,0:T(8,128)(2,1)S(1)}, bf16[256,1024]{1,0:T(8,128)(2,1)S(1)}, u32[]{:S(2)}, u32[]{:S(2)}) collective-permute-start(bf16[256,1024]{1,0:T(8,128)(2,1)S(1)} %add_convert_fusion.6), channel_id=1, source_target_pairs={{0,4},{4,8},{8,12},{12,14},{14,10},{10,6},{6,2},{2,0},{1,5},{5,9},... | collective-permute-start | bytes 1572872 | tf_op jit(solution)/shard_map/ppermute | solution.py:282
  129.7 21.8 %collective-permute-start.25 = (bf16[256,1024]{1,0:T(8,128)(2,1)S(1)}, bf16[256,1024]{1,0:T(8,128)(2,1)S(1)}, u32[]{:S(2)}, u32[]{:S(2)}) collective-permute-start(bf16[256,1024]{1,0:T(8,128)(2,1)S(1)} %add_convert_fusion), channel_id=1, source_target_pairs={{4,0},{8,4},{12,8},{14,12},{10,14},{6,10},{2,6},{0,2},{5,1},{9,5},... | collective-permute-start | bytes 1572872 | tf_op jit(solution)/shard_map/ppermute | solution.py:282
  153.9 15.4 %collective-permute-start.34 = (bf16[256,1024]{1,0:T(8,128)(2,1)S(1)}, bf16[256,1024]{1,0:T(8,128)(2,1)S(1)}, u32[]{:S(2)}, u32[]{:S(2)}) collective-permute-start(bf16[256,1024]{1,0:T(8,128)(2,1)S(1)} %get-tuple-element.62.refs_0_), channel_id=1, source_target_pairs={{4,0},{8,4},{12,8},{14,12},{10,14},{6,10},{2,6},{0,2},{5,1},{9,5},... | collective-permute-start | bytes 1572872 | tf_op jit(solution)/shard_map/ppermute | solution.py:307
  154.7 25.8 %collective-permute-start.30 = (bf16[256,1024]{1,0:T(8,128)(2,1)S(1)}, bf16[256,1024]{1,0:T(8,128)(2,1)S(1)}, u32[]{:S(2)}, u32[]{:S(2)}) collective-permute-start(bf16[256,1024]{1,0:T(8,128)(2,1)S(1)} %get-tuple-element.60.refs_1_), channel_id=1, source_target_pairs={{4,0},{8,4},{12,8},{14,12},{10,14},{6,10},{2,6},{0,2},{5,1},{9,5},... | collective-permute-start | bytes 1572872 | tf_op jit(solution)/shard_map/ppermute | solution.py:307
  155.1 25.5 %collective-permute-start.35 = (bf16[256,1024]{1,0:T(8,128)(2,1)S(1)}, bf16[256,1024]{1,0:T(8,128)(2,1)S(1)}, u32[]{:S(2)}, u32[]{:S(2)}) collective-permute-start(bf16[256,1024]{1,0:T(8,128)(2,1)S(1)} %get-tuple-element.60.refs_1_), channel_id=1, source_target_pairs={{0,4},{4,8},{8,12},{12,14},{14,10},{10,6},{6,2},{2,0},{1,5},{5,9},... | collective-permute-start | bytes 1572872 | tf_op jit(solution)/shard_map/ppermute | solution.py:307
  167.4 22.5 %collective-permute-start.27 = (bf16[256,1024]{1,0:T(8,128)(2,1)S(1)}, bf16[256,1024]{1,0:T(8,128)(2,1)S(1)}, u32[]{:S(2)}, u32[]{:S(2)}) collective-permute-start(bf16[256,1024]{1,0:T(8,128)(2,1)S(1)} %collective-permute-done.26.refs_2_), channel_id=1, source_target_pairs={{0,4},{4,8},{8,12},{12,14},{14,10},{10,6},{6,2},{2,0},{1,5},{5,9},... | collective-permute-start | bytes 1572872 | tf_op jit(solution)/shard_map/ppermute | solution.py:307
  169.3 22.5 %collective-permute-start.38 = (bf16[256,1024]{1,0:T(8,128)(2,1)S(1)}, bf16[256,1024]{1,0:T(8,128)(2,1)S(1)}, u32[]{:S(2)}, u32[]{:S(2)}) collective-permute-start(bf16[256,1024]{1,0:T(8,128)(2,1)S(1)} %collective-permute-done.34.refs_0_), channel_id=1, source_target_pairs={{4,0},{8,4},{12,8},{14,12},{10,14},{6,10},{2,6},{0,2},{5,1},{9,5},... | collective-permute-start | bytes 1572872 | tf_op jit(solution)/shard_map/ppermute | solution.py:307
  180.5 21.4 %collective-permute-start.31 = (bf16[256,1024]{1,0:T(8,128)(2,1)S(1)}, bf16[256,1024]{1,0:T(8,128)(2,1)S(1)}, u32[]{:S(2)}, u32[]{:S(2)}) collective-permute-start(bf16[256,1024]{1,0:T(8,128)(2,1)S(1)} %collective-permute-done.30.refs_1_), channel_id=1, source_target_pairs={{4,0},{8,4},{12,8},{14,12},{10,14},{6,10},{2,6},{0,2},{5,1},{9,5},... | collective-permute-start | bytes 1572872 | tf_op jit(solution)/shard_map/ppermute | solution.py:307
  180.5 21.3 %collective-permute-start.36 = (bf16[256,1024]{1,0:T(8,128)(2,1)S(1)}, bf16[256,1024]{1,0:T(8,128)(2,1)S(1)}, u32[]{:S(2)}, u32[]{:S(2)}) collective-permute-start(bf16[256,1024]{1,0:T(8,128)(2,1)S(1)} %collective-permute-done.35.refs_3_), channel_id=1, source_target_pairs={{0,4},{4,8},{8,12},{12,14},{14,10},{10,6},{6,2},{2,0},{1,5},{5,9},... | collective-permute-start | bytes 1572872 | tf_op jit(solution)/shard_map/ppermute | solution.py:307
  191.8 31.9 %collective-permute-start.39 = (bf16[256,1024]{1,0:T(8,128)(2,1)S(1)}, bf16[256,1024]{1,0:T(8,128)(2,1)S(1)}, u32[]{:S(2)}, u32[]{:S(2)}) collective-permute-start(bf16[256,1024]{1,0:T(8,128)(2,1)S(1)} %broadcast_select_fusion.9), channel_id=1, source_target_pairs={{0,1},{1,0},{2,3},{3,2},{4,5},{5,4},{6,7},{7,6},{8,9},{9,8},{10,11... | collective-permute-start | bytes 1572872 | tf_op jit(solution)/shard_map/ppermute | solution.py:326
  201.9 21.7 %collective-permute-start.40 = (bf16[256,1024]{1,0:T(8,128)(2,1)S(1)}, bf16[256,1024]{1,0:T(8,128)(2,1)S(1)}, u32[]{:S(2)}, u32[]{:S(2)}) collective-permute-start(bf16[256,1024]{1,0:T(8,128)(2,1)S(1)} %broadcast_select_fusion.8), channel_id=1, source_target_pairs={{0,1},{1,0},{2,3},{3,2},{4,5},{5,4},{6,7},{7,6},{8,9},{9,8},{10,11... | collective-permute-start | bytes 1572872 | tf_op jit(solution)/shard_map/ppermute | solution.py:326
  202.0 33.4 %collective-permute-start.28 = (bf16[256,1024]{1,0:T(8,128)(2,1)S(1)}, bf16[256,1024]{1,0:T(8,128)(2,1)S(1)}, u32[]{:S(2)}, u32[]{:S(2)}) collective-permute-start(bf16[256,1024]{1,0:T(8,128)(2,1)S(1)} %collective-permute-done.27.refs_2_), channel_id=1, source_target_pairs={{0,4},{4,8},{8,12},{12,14},{14,10},{10,6},{6,2},{2,0},{1,5},{5,9},... | collective-permute-start | bytes 1572872 | tf_op jit(solution)/shard_map/ppermute | solution.py:307
  221.6 38.7 %collective-permute-start.50 = (f32[256]{0:T(256)S(1)}, f32[256]{0:T(256)S(1)}, u32[]{:S(2)}, u32[]{:S(2)}) collective-permute-start(f32[256]{0:T(256)S(1)} %add.103.refs_9_), channel_id=1, source_target_pairs={{0,4},{4,8},{8,12},{12,14},{14,10},{10,6},{6,2},{2,0},{1,5},{5,9},... | collective-permute-start | bytes 3080 | tf_op jit(solution)/shard_map/ppermute | solution.py:315
  221.6 23.4 %collective-permute-start.32 = (bf16[256,1024]{1,0:T(8,128)(2,1)S(1)}, bf16[256,1024]{1,0:T(8,128)(2,1)S(1)}, u32[]{:S(2)}, u32[]{:S(2)}) collective-permute-start(bf16[256,1024]{1,0:T(8,128)(2,1)S(1)} %collective-permute-done.31.refs_1_), channel_id=1, source_target_pairs={{4,0},{8,4},{12,8},{14,12},{10,14},{6,10},{2,6},{0,2},{5,1},{9,5},... | collective-permute-start | bytes 1572872 | tf_op jit(solution)/shard_map/ppermute | solution.py:307
  223.7 21.2 %collective-permute-start.46 = (bf16[256,1024]{1,0:T(8,128)(2,1)S(1)}, bf16[256,1024]{1,0:T(8,128)(2,1)S(1)}, u32[]{:S(2)}, u32[]{:S(2)}) collective-permute-start(bf16[256,1024]{1,0:T(8,128)(2,1)S(1)} %collective-permute-done.38.refs_0_), channel_id=1, source_target_pairs={{4,0},{8,4},{12,8},{14,12},{10,14},{6,10},{2,6},{0,2},{5,1},{9,5},... | collective-permute-start | bytes 1572872 | tf_op jit(solution)/shard_map/ppermute | solution.py:307
  (53 other events, 589.1 us)

commit v3 on v2

--- a/solution.py
+++ b/solution.py
@@ -74,67 +74,47 @@
     )(core, queries, keys, values, peer_keys, peer_values, *after)
 
 
-def project_kernel(parts, info_ref, *refs):
-    own, peer = refs[:parts], refs[parts : 2 * parts]
-    w_ref = refs[2 * parts]
-    own_ref, peer_ref, x_ref, sum_ref = refs[-4:]
+def project_kernel(info_ref, x_ref, w_ref, *refs):
+    own_ref, peer_ref = refs[-2:]
     rows = own_ref.shape[0]
-    width = own[0].shape[1]
-    depth = w_ref.shape[0]
-    step = pl.program_id(0)
-
-    @pl.when(step == 0)
-    def _():
-        for part in range(parts):
-            columns = slice(part * width, (part + 1) * width)
-            x_ref[:rows, columns] = own[part][...]
-            x_ref[rows:, columns] = peer[part][...]
-
-    chunk = x_ref[:, pl.ds(pl.multiple_of(step * depth, depth), depth)]
-    result = dot(chunk, w_ref[...])
-
-    @pl.when(step == 0)
-    def _():
-        sum_ref[...] = result
-
-    @pl.when(step > 0)
-    def _():
-        total = (sum_ref[...] + result).astype(BF16)
-        own_ref[...] = total[:rows]
-        peer_ref[...] = total[rows:]
-
-
-def project(info, pair, pieces, piece, own, peer, weight, width, after):
-    rows, part_width = own[0].shape
-    parts = len(own)
-    depth = parts * part_width
-    whole = pl.BlockSpec((rows, part_width), lambda j, s: (0, 0))
-    out = pl.BlockSpec((rows, width), lambda j, s: (0, 0))
+    result = dot(x_ref[...], w_ref[...]).astype(BF16)
+    own_ref[...] = result[:rows]
+    peer_ref[...] = result[rows:]
+
+
+def project(info, pair, pieces, piece, both, weight, width, after):
+    rows, depth = both.shape
+    rows = rows // 2
+    tile = min(512, width)
+    tiles = width // tile
+    out = pl.BlockSpec((rows, tile), lambda j, s: (0, j))
     return pl.pallas_call(
-        functools.partial(project_kernel, parts),
+        project_kernel,
         grid_spec=pltpu.PrefetchScalarGridSpec(
             num_scalar_prefetch=1,
-            grid=(2,),
-            in_specs=[whole] * (2 * parts)
-            + [pl.BlockSpec((depth // 2, width), lambda j, s: (j, s[pair] * pieces + piece))]
+            grid=(tiles,),
+            in_specs=[
+                pl.BlockSpec(memory_space=pltpu.VMEM),
+                pl.BlockSpec((depth, tile), lambda j, s: (0, (s[pair] * pieces + piece) * tiles + j)),
+            ]
             + [pl.BlockSpec(memory_space=pl.ANY)] * len(after),
             out_specs=[out, out],
-            scratch_shapes=[pltpu.VMEM((2 * rows, depth), BF16), pltpu.VMEM((2 * rows, width), F32)],
         ),
         out_shape=[jax.ShapeDtypeStruct((rows, width), BF16)] * 2,
-        compiler_params=pltpu.CompilerParams(vmem_limit_bytes=20 * MIB),
+        compiler_params=pltpu.CompilerParams(vmem_limit_bytes=34 * MIB),
         cost_estimate=pl.CostEstimate(
             flops=4 * rows * depth * width, bytes_accessed=2 * depth * width, transcendentals=0
         ),
         name="project",
-    )(info, *own, *peer, weight, *after)
-
-
-def query_kernel(pieces, pair, half, first, info_ref, *refs):
+    )(info, both, weight, *after)
+
+
+def query_kernel(pieces, pair, half, first, count, info_ref, *refs):
     one, other, far = refs[:pieces], refs[pieces : 2 * pieces], refs[2 * pieces : 3 * pieces]
     w_ref = refs[3 * pieces]
     acc_refs = () if first else refs[3 * pieces + 1 : 3 * pieces + 3]
-    own_ref, peer_ref, info_out, x_ref = refs[-4:]
+    squares = refs[len(refs) - 5 - count : len(refs) - 5]
+    own_ref, peer_ref, info_out, squares_out, x_ref = refs[-5:]
     rows = own_ref.shape[0]
     width = one[0].shape[1]
 
@@ -142,6 +122,10 @@
     def _():
         for index in range(2 * half):
             info_out[index] = info_ref[index]
+        total = squares[0][...]
+        for more in squares[1:]:
+            total = total + more[...]
+        squares_out[...] = total
         for piece in range(pieces):
             columns = slice(piece * width, (piece + 1) * width)
 
@@ -164,39 +148,40 @@
         peer_ref[...] = (acc_refs[1][...] + result[rows:]).astype(peer_ref.dtype)
 
 
-def query_block(info, pair, half, one, other, far, weight, acc, last, after):
+def query_block(info, pair, half, one, other, far, weight, acc, last, squares):
     pieces = len(one)
     rows, piece_width = one[0].shape
     depth = pieces * piece_width
     width = weight.shape[1]
-    tile = min(1024, width)
-    whole = pl.BlockSpec((rows, piece_width), lambda j, s: (0, 0))
+    tile = min(512, width)
+    whole = pl.BlockSpec(memory_space=pltpu.VMEM)
     out = pl.BlockSpec((rows, tile), lambda j, s: (0, j))
     first = acc is None
     acc = () if first else acc
     return pl.pallas_call(
-        functools.partial(query_kernel, pieces, pair, half, first),
+        functools.partial(query_kernel, pieces, pair, half, first, len(squares)),
         grid_spec=pltpu.PrefetchScalarGridSpec(
             num_scalar_prefetch=1,
             grid=(width // tile,),
             in_specs=[whole] * (3 * pieces)
             + [pl.BlockSpec((depth, tile), lambda j, s: (s[pair], j))]
             + [out] * len(acc)
-            + [pl.BlockSpec(memory_space=pl.ANY)] * len(after),
-            out_specs=[out, out, pl.BlockSpec(memory_space=pltpu.SMEM)],
+            + [whole] * len(squares),
+            out_specs=[out, out, pl.BlockSpec(memory_space=pltpu.SMEM), whole],
             scratch_shapes=[pltpu.VMEM((2 * rows, depth), BF16)],
         ),
         out_shape=[
             jax.ShapeDtypeStruct((rows, width), F32),
             jax.ShapeDtypeStruct((rows, width), BF16 if last else F32),
             jax.ShapeDtypeStruct(info.shape, jnp.int32),
+            jax.ShapeDtypeStruct(squares[0].shape, F32),
         ],
-        compiler_params=pltpu.CompilerParams(vmem_limit_bytes=30 * MIB),
+        compiler_params=pltpu.CompilerParams(vmem_limit_bytes=34 * MIB),
         cost_estimate=pl.CostEstimate(
             flops=4 * rows * depth * width, bytes_accessed=2 * depth * width + 16 * rows * width, transcendentals=0
         ),
         name="next_query",
-    )(info, *one, *other, *far, weight, *acc, *after)
+    )(info, *one, *other, *far, weight, *acc, *squares)
 
 
 def ring_of(n):
@@ -241,6 +226,10 @@
         attended.append(attention(core[None], queries, own_keys, own_values, peer_keys, peer_values, attended))
         attended_peer.append(lax.ppermute(attended[-1], "tokens", swap))
 
+    both = jnp.concatenate(
+        [jnp.concatenate(attended, axis=1), jnp.concatenate(attended_peer, axis=1)], axis=0
+    )
+
     def columns_of(array, piece):
         return array[:, piece * piece_width : (piece + 1) * piece_width]
 
@@ -261,9 +250,7 @@
     def make(after):
         if len(made) < len(order):
             k, piece = order[len(made)]
-            mine, outgoing = project(
-                info, k, pieces, piece, attended, attended_peer, out_weight, piece_width, after
-            )
+            mine, outgoing = project(info, k, pieces, piece, both, out_weight, piece_width, after)
             made[k, piece] = (mine, lax.ppermute(outgoing, "tokens", swap))
 
     def block(q, piece):
@@ -271,7 +258,7 @@
         near = is_near(info, q % half) if q == q % half else jnp.logical_not(is_near(info, q % half))
         return jnp.where(near, mine, swapped).astype(F32)
 
-    arrived = {}
+    arrived, landed = {}, []
     make(())
     make(())
     for piece, way, step in events:
@@ -280,7 +267,8 @@
             value = value + arrived[piece, way].astype(F32)
         value = value.astype(BF16)
         arrived[piece, way] = lax.ppermute(value, "tensor", up if way == 0 else down)
-        make((value,))
+        landed.append(arrived[piece, way])
+        make((value, *landed[-3:-2]))
 
     resid, scaled = [], []
     squares = jnp.zeros((rows,), F32)
@@ -308,14 +296,8 @@
                 held[piece, target] = value
                 if abs(target) == half:
                     held[piece, half] = held[piece, -half] = value
-    distance = half
-    totals = []
-    while distance >= 1:
-        shifted = [(ring[p], ring[(p + distance) % n]) for p in range(n)]
-        squares = squares + lax.ppermute(squares, "tensor", shifted)
-        totals.append(squares)
-        distance //= 2
-
+    squares = squares[None]
+    reach = half
     acc = None
     when = sorted(range(half), key=lambda k: max(k, half - k))
     indices = [info, info]
@@ -324,10 +306,18 @@
         other = [held[piece, k - half] for piece in range(pieces)]
         near = is_near(indices[-2] if count > 1 else indices[-1], k)
         far = [lax.ppermute(jnp.where(near, other[piece], one[piece]), "tokens", swap) for piece in range(pieces)]
-        *acc, index = query_block(
-            info, k, half, one, other, far, next_weight, acc, k == when[-1], totals[max(count - 1, 0) : count]
+        sums = [squares]
+        if reach >= 1 and count != half - 2:
+            sums.append(lax.ppermute(squares, "tensor", [(ring[p], ring[(p + reach) % n]) for p in range(n)]))
+            reach //= 2
+        *acc, index, squares = query_block(
+            info, k, half, one, other, far, next_weight, acc, k == when[-1], sums
         )
         indices.append(index)
+    while reach >= 1:
+        squares = squares + lax.ppermute(squares, "tensor", [(ring[p], ring[(p + reach) % n]) for p in range(n)])
+        reach //= 2
+    squares = squares[0]
     query_sum = acc[0] + lax.ppermute(acc[1], "tokens", swap).astype(F32)
     factor = 1.0 / jnp.sqrt(squares / D + EPS_NORM)
     return (resid_out, (query_sum * factor[:, None]).astype(BF16))

time: 282 us -> 283 us (level)
  starting transfers between devices: 37.2 us -> 46.3 us
  waiting for transfers between devices: 130 us -> 121 us
  other arithmetic: 16.9 us -> 20.3 us
  Pallas kernels: 82.7 us -> 79.8 us
    ppermute x14, waiting for transfers between devices: 52.2 us -> 41.7 us  [on_ring(): value = lax.ppermute(held[source], 'tensor', pairs)]
    ppermute x3, starting transfers between devices: 2.27 us -> 6.91 us  [on_ring(): lax.ppermute(squares, 'tensor', [(ring[p], ring[(p + reach) % n]) for p i...]
    ppermute x14, starting transfers between devices: 15.4 us -> 18.7 us  [on_ring(): lax.ppermute(value, 'tensor', up if way == 0 else down)]
    pallas_call x12, Pallas kernels: 77 us -> 74 us  [the longest x8 39.8 us: project(): pl.pallas_call(project_kernel, grid_spec=pltpu.PrefetchScalarGridSpec(num...]
    convert_element_type x8, other arithmetic: 8.99 us -> 11.8 us  [on_ring(): value = value.astype(BF16)]
    ppermute x14, waiting for transfers between devices: 57.5 us -> 60.3 us  [on_ring(): lax.ppermute(value, 'tensor', up if way == 0 else down)]
  transfers between devices with their start and end apart: 52 -> 52, of which waited for: 24 -> 26; matrix products, arithmetic and copies ran while one was open for 6% -> 7% of each run, Pallas kernels for 22% -> 20%
where the time goes in v3:
time: 283 us; the launch traced here: 282 us
  waiting for transfers between devices  121 us (43%)
  Pallas kernels  79.8 us (28%)
  starting transfers between devices  46.3 us (16%)
  other arithmetic  20.3 us (7%)
  local copies, waits for them, and re-layouts  9.3 us (3%)
  between operations  5.59 us (2%)
    ppermute x14, waiting for transfers between devices, on_ring(): lax.ppermute(value, 'tensor', up if way == 0 else down)  60.3 us
    ppermute x14, waiting for transfers between devices, on_ring(): value = lax.ppermute(held[source], 'tensor', pairs)  41.7 us
    pallas_call x8, Pallas kernels, project(): pl.pallas_call(project_kernel, grid_spec=pltpu.PrefetchScalarGridSpec(num...  39.8 us
    pallas_call x4, Pallas kernels, query_block(): pl.pallas_call(functools.partial(query_kernel, pieces, pair, half, first,...  34.2 us
    ppermute x14, starting transfers between devices, on_ring(): lax.ppermute(value, 'tensor', up if way == 0 else down)  18.7 us
    ppermute x14, starting transfers between devices, on_ring(): value = lax.ppermute(held[source], 'tensor', pairs)  17.1 us
    ppermute x3, waiting for transfers between devices, on_ring(): lax.ppermute(squares, 'tensor', [(ring[p], ring[(p + reach) % n]) for p i...  14.3 us
    convert_element_type x8, other arithmetic, on_ring(): value = value.astype(BF16)  11.8 us
  transfers between devices with their start and end apart: 52, of which 26 were waited for; matrix products, arithmetic and copies ran while one was open for 7% of the time, Pallas kernels for 20%

profile of v3, /device:TPU:0, one launch (start us, length us, event | category | flops | bytes accessed | tf_op | source)
XLA Modules:
  0.0 281.8 jit_solution(13251999913435282842)
XLA Ops:
  16.1 4.7 %project.8 = (bf16[256,1024]{1,0:T(8,128)(2,1)S(1)}, bf16[256,1024]{1,0:T(8,128)(2,1)S(1)}) custom-call(s32[8]{0:T(128)S(1)} %get-tuple-element.77.info_ref, bf16[512,2048]{1,0:T(8,128)(2,1)S(1)} %maximum_maximum_fusion.x_ref, bf16[2048,8192]{1,0:T(8,128)(2,1)} %w_ref.15), custom_call_target="tpu_custom_call" | custom-call | flops 2147483648 | bytes 4194304 | tf_op jit(solution)/shard_map/project/pallas_call | solution.py:91
  24.0 4.7 %project.13 = (bf16[256,1024]{1,0:T(8,128)(2,1)S(1)}, bf16[256,1024]{1,0:T(8,128)(2,1)S(1)}) custom-call(s32[8]{0:T(128)S(1)} %get-tuple-element.77.info_ref, bf16[512,2048]{1,0:T(8,128)(2,1)S(1)} %maximum_maximum_fusion.x_ref, bf16[2048,8192]{1,0:T(8,128)(2,1)} %w_ref.15, bf16[256,1024]{1,0:T(8,128)(2,1)S(1)} %broadcast_select_fusion.10.refs_0_), custom_call_target="tpu_custom_call" | custom-call | flops 2147483648 | bytes 4194304 | tf_op jit(solution)/shard_map/project/pallas_call | solution.py:91
  32.3 4.7 %project.9 = (bf16[256,1024]{1,0:T(8,128)(2,1)S(1)}, bf16[256,1024]{1,0:T(8,128)(2,1)S(1)}) custom-call(s32[8]{0:T(128)S(1)} %get-tuple-element.77.info_ref, bf16[512,2048]{1,0:T(8,128)(2,1)S(1)} %maximum_maximum_fusion.x_ref, bf16[2048,8192]{1,0:T(8,128)(2,1)} %w_ref.15), custom_call_target="tpu_custom_call" | custom-call | flops 2147483648 | bytes 4194304 | tf_op jit(solution)/shard_map/project/pallas_call | solution.py:91
  37.3 6.7 %collective-permute-done.12.refs_1_ = bf16[256,1024]{1,0:T(8,128)(2,1)S(1)} collective-permute-done((bf16[256,1024]{1,0:T(8,128)(2,1)S(1)}, bf16[256,1024]{1,0:T(8,128)(2,1)S(1)}, u32[]{:S(2)}, u32[]{:S(2)}) %collective-permute-start.12) | collective-permute-done | bytes 524320 | tf_op jit(solution)/shard_map/ppermute | solution.py:269
  44.1 4.7 %project.14 = (bf16[256,1024]{1,0:T(8,128)(2,1)S(1)}, bf16[256,1024]{1,0:T(8,128)(2,1)S(1)}) custom-call(s32[8]{0:T(128)S(1)} %get-tuple-element.77.info_ref, bf16[512,2048]{1,0:T(8,128)(2,1)S(1)} %maximum_maximum_fusion.x_ref, bf16[2048,8192]{1,0:T(8,128)(2,1)} %w_ref.15, bf16[256,1024]{1,0:T(8,128)(2,1)S(1)} %broadcast_select_fusion.6.refs_0_, ...), custom_call_target="tpu_custom_call" | custom-call | flops 2147483648 | bytes 4194304 | tf_op jit(solution)/shard_map/project/pallas_call | solution.py:91
  51.9 5.4 %project.10 = (bf16[256,1024]{1,0:T(8,128)(2,1)S(1)}, bf16[256,1024]{1,0:T(8,128)(2,1)}) custom-call(s32[8]{0:T(128)S(1)} %get-tuple-element.77.info_ref, bf16[512,2048]{1,0:T(8,128)(2,1)S(1)} %maximum_maximum_fusion.x_ref, bf16[2048,8192]{1,0:T(8,128)(2,1)} %w_ref.15, bf16[256,1024]{1,0:T(8,128)(2,1)} %broadcast_select_fusion.11.refs_0_), custom_call_target="tpu_custom_call" | custom-call | flops 2147483648 | bytes 4194304 | tf_op jit(solution)/shard_map/project/pallas_call | solution.py:91
  57.7 5.6 %collective-permute-done.19.refs_1_ = bf16[256,1024]{1,0:T(8,128)(2,1)S(1)} collective-permute-done((bf16[256,1024]{1,0:T(8,128)(2,1)S(1)}, bf16[256,1024]{1,0:T(8,128)(2,1)S(1)}, u32[]{:S(2)}, u32[]{:S(2)}) %collective-permute-start.19) | collective-permute-done | bytes 524320 | tf_op jit(solution)/shard_map/ppermute | solution.py:269
  63.2 5.4 %project.15 = (bf16[256,1024]{1,0:T(8,128)(2,1)S(1)}, bf16[256,1024]{1,0:T(8,128)(2,1)}) custom-call(s32[8]{0:T(128)S(1)} %get-tuple-element.77.info_ref, bf16[512,2048]{1,0:T(8,128)(2,1)S(1)} %maximum_maximum_fusion.x_ref, bf16[2048,8192]{1,0:T(8,128)(2,1)} %w_ref.15, bf16[256,1024]{1,0:T(8,128)(2,1)S(1)} %add_convert_fusion.8.refs_0_, ...), custom_call_target="tpu_custom_call" | custom-call | flops 2147483648 | bytes 4194304 | tf_op jit(solution)/shard_map/project/pallas_call | solution.py:91
  71.7 4.7 %project.11 = (bf16[256,1024]{1,0:T(8,128)(2,1)S(1)}, bf16[256,1024]{1,0:T(8,128)(2,1)S(1)}) custom-call(s32[8]{0:T(128)S(1)} %get-tuple-element.77.info_ref, bf16[512,2048]{1,0:T(8,128)(2,1)S(1)} %maximum_maximum_fusion.x_ref, bf16[2048,8192]{1,0:T(8,128)(2,1)} %w_ref.15, bf16[256,1024]{1,0:T(8,128)(2,1)S(1)} %broadcast_select_fusion.7.refs_0_, ...), custom_call_target="tpu_custom_call" | custom-call | flops 2147483648 | bytes 4194304 | tf_op jit(solution)/shard_map/project/pallas_call | solution.py:91
  80.4 11.8 %collective-permute-done.21 = bf16[256,1024]{1,0:T(8,128)(2,1)S(1)} collective-permute-done((bf16[256,1024]{1,0:T(8,128)(2,1)S(1)}, bf16[256,1024]{1,0:T(8,128)(2,1)S(1)}, u32[]{:S(2)}, u32[]{:S(2)}) %collective-permute-start.21) | collective-permute-done | bytes 524320 | tf_op jit(solution)/shard_map/ppermute | solution.py:269
  96.7 5.4 %project.12 = (bf16[256,1024]{1,0:T(8,128)(2,1)S(1)}, bf16[256,1024]{1,0:T(8,128)(2,1)}) custom-call(s32[8]{0:T(128)S(1)} %get-tuple-element.77.info_ref, bf16[512,2048]{1,0:T(8,128)(2,1)S(1)} %maximum_maximum_fusion.x_ref, bf16[2048,8192]{1,0:T(8,128)(2,1)} %w_ref.15, bf16[256,1024]{1,0:T(8,128)(2,1)} %get-tuple-element.75.refs_0_, ...), custom_call_target="tpu_custom_call" | custom-call | flops 2147483648 | bytes 4194304 | tf_op jit(solution)/shard_map/project/pallas_call | solution.py:91
  102.9 5.2 %collective-permute-done.23 = bf16[256,1024]{1,0:T(8,128)(2,1)} collective-permute-done((bf16[256,1024]{1,0:T(8,128)(2,1)}, bf16[256,1024]{1,0:T(8,128)(2,1)}, u32[]{:S(2)}, u32[]{:S(2)}) %collective-permute-start.23) | collective-permute-done | bytes 524320 | tf_op jit(solution)/shard_map/ppermute | solution.py:269
  118.4 7.2 %collective-permute-done.24 = bf16[256,1024]{1,0:T(8,128)(2,1)} collective-permute-done((bf16[256,1024]{1,0:T(8,128)(2,1)}, bf16[256,1024]{1,0:T(8,128)(2,1)}, u32[]{:S(2)}, u32[]{:S(2)}) %collective-permute-start.24) | collective-permute-done | bytes 524320 | tf_op jit(solution)/shard_map/ppermute | solution.py:269
  142.6 5.3 %collective-permute-done.25 = bf16[256,1024]{1,0:T(8,128)(2,1)S(1)} collective-permute-done((bf16[256,1024]{1,0:T(8,128)(2,1)S(1)}, bf16[256,1024]{1,0:T(8,128)(2,1)S(1)}, u32[]{:S(2)}, u32[]{:S(2)}) %collective-permute-start.25) | collective-permute-done | bytes 524320 | tf_op jit(solution)/shard_map/ppermute | solution.py:269
  151.9 5.6 %collective-permute-done.18 = bf16[256,1024]{1,0:T(8,128)(2,1)S(1)} collective-permute-done((bf16[256,1024]{1,0:T(8,128)(2,1)S(1)}, bf16[256,1024]{1,0:T(8,128)(2,1)S(1)}, u32[]{:S(2)}, u32[]{:S(2)}) %collective-permute-start.18) | collective-permute-done | bytes 524320 | tf_op jit(solution)/shard_map/ppermute | solution.py:269
  163.8 9.6 %collective-permute-done.30.refs_1_ = bf16[256,1024]{1,0:T(8,128)(2,1)S(1)} collective-permute-done((bf16[256,1024]{1,0:T(8,128)(2,1)S(1)}, bf16[256,1024]{1,0:T(8,128)(2,1)S(1)}, u32[]{:S(2)}, u32[]{:S(2)}) %collective-permute-start.30) | collective-permute-done | bytes 524320 | tf_op jit(solution)/shard_map/ppermute | solution.py:295
  176.4 10.7 %collective-permute-done.26.refs_2_ = bf16[256,1024]{1,0:T(8,128)(2,1)S(1)} collective-permute-done((bf16[256,1024]{1,0:T(8,128)(2,1)S(1)}, bf16[256,1024]{1,0:T(8,128)(2,1)S(1)}, u32[]{:S(2)}, u32[]{:S(2)}) %collective-permute-start.26) | collective-permute-done | bytes 524320 | tf_op jit(solution)/shard_map/ppermute | solution.py:295
  189.3 6.6 %collective-permute-done.31.refs_1_ = bf16[256,1024]{1,0:T(8,128)(2,1)S(1)} collective-permute-done((bf16[256,1024]{1,0:T(8,128)(2,1)S(1)}, bf16[256,1024]{1,0:T(8,128)(2,1)S(1)}, u32[]{:S(2)}, u32[]{:S(2)}) %collective-permute-start.31) | collective-permute-done | bytes 524320 | tf_op jit(solution)/shard_map/ppermute | solution.py:295
  198.5 9.3 %collective-permute-done.27.refs_2_ = bf16[256,1024]{1,0:T(8,128)(2,1)S(1)} collective-permute-done((bf16[256,1024]{1,0:T(8,128)(2,1)S(1)}, bf16[256,1024]{1,0:T(8,128)(2,1)S(1)}, u32[]{:S(2)}, u32[]{:S(2)}) %collective-permute-start.27) | collective-permute-done | bytes 524320 | tf_op jit(solution)/shard_map/ppermute | solution.py:295
  212.9 11.3 %collective-permute-done.41.refs_8_ = f32[1,256]{1,0:T(1,128)S(1)} collective-permute-done((f32[1,256]{1,0:T(1,128)S(1)}, f32[1,256]{1,0:T(1,128)S(1)}, u32[]{:S(2)}, u32[]{:S(2)}) %collective-permute-start.41) | collective-permute-done | bytes 1056 | tf_op jit(solution)/shard_map/ppermute | solution.py:311
  226.2 8.5 %next_query.4 = (f32[256,2048]{1,0:T(8,128)S(1)}, f32[256,2048]{1,0:T(8,128)S(1)}, s32[8]{0:T(128)S(1)}, f32[1,256]{1,0:T(1,128)S(1)}) custom-call(s32[8]{0:T(128)S(1)} %get-tuple-element.77.info_ref, bf16[256,1024]{1,0:T(8,128)(2,1)S(1)} %collective-permute-done.38.refs_0_, bf16[256,1024]{1,0:T(8,128)(2,1)S(1)} %collective-permute-done.31.refs_1_, ...), custom_call_target="tpu_custom_call" | custom-call | flops 4294967296 | bytes 16777216 | tf_op jit(solution)/shard_map/next_query/pallas_call | solution.py:161
  244.4 8.6 %next_query.5 = (f32[256,2048]{1,0:T(8,128)S(1)}, f32[256,2048]{1,0:T(8,128)S(1)}, s32[8]{0:T(128)S(1)}, f32[1,256]{1,0:T(1,128)S(1)}) custom-call(s32[8]{0:T(128)S(1)} %get-tuple-element.77.info_ref, bf16[256,1024]{1,0:T(8,128)(2,1)S(1)} %collective-permute-done.34.refs_0_, bf16[256,1024]{1,0:T(8,128)(2,1)S(1)} %collective-permute-done.30.refs_1_, ...), custom_call_target="tpu_custom_call" | custom-call | flops 4294967296 | bytes 16777216 | tf_op jit(solution)/shard_map/next_query/pallas_call | solution.py:161
  257.1 8.6 %next_query.6 = (f32[256,2048]{1,0:T(8,128)S(1)}, f32[256,2048]{1,0:T(8,128)S(1)}, s32[8]{0:T(128)}, f32[1,256]{1,0:T(1,128)S(1)}) custom-call(s32[8]{0:T(128)S(1)} %get-tuple-element.77.info_ref, bf16[256,1024]{1,0:T(8,128)(2,1)S(1)} %collective-permute-done.47.refs_0_, bf16[256,1024]{1,0:T(8,128)(2,1)S(1)} %collective-permute-done.32.refs_1_, ...), custom_call_target="tpu_custom_call" | custom-call | flops 4294967296 | bytes 16777216 | tf_op jit(solution)/shard_map/next_query/pallas_call | solution.py:161
  269.3 8.5 %next_query.7 = (f32[256,2048]{1,0:T(8,128)S(1)}, bf16[256,2048]{1,0:T(8,128)(2,1)S(1)}, s32[8]{0:T(128)}, f32[1,256]{1,0:T(1,128)S(1)}) custom-call(s32[8]{0:T(128)S(1)} %get-tuple-element.77.info_ref, bf16[256,1024]{1,0:T(8,128)(2,1)S(1)} %get-tuple-element.68.refs_0_, bf16[256,1024]{1,0:T(8,128)(2,1)S(1)} %get-tuple-element.66.refs_1_, ...), custom_call_target="tpu_custom_call" | custom-call | flops 4294967296 | bytes 16777216 | tf_op jit(solution)/shard_map/next_query/pallas_call | solution.py:161
  (185 shorter events, 107.3 us)
Async XLA Ops:
  28.9 15.2 %collective-permute-start.12 = (bf16[256,1024]{1,0:T(8,128)(2,1)S(1)}, bf16[256,1024]{1,0:T(8,128)(2,1)S(1)}, u32[]{:S(2)}, u32[]{:S(2)}) collective-permute-start(bf16[256,1024]{1,0:T(8,128)(2,1)S(1)} %broadcast_select_fusion.10.refs_0_), channel_id=1, source_target_pairs={{0,4},{4,8},{8,12},{12,14},{14,10},{10,6},{6,2},{2,0},{1,5},{5,9},... | collective-permute-start | bytes 1572872 | tf_op jit(solution)/shard_map/ppermute | solution.py:269
  51.7 19.9 %collective-permute-start.7 = (bf16[256,1024]{1,0:T(8,128)(2,1)}, bf16[256,1024]{1,0:T(8,128)(2,1)}, u32[]{:S(2)}, u32[]{:S(2)}) collective-permute-start(bf16[256,1024]{1,0:T(8,128)(2,1)} %broadcast_select_fusion.11.refs_0_), channel_id=1, source_target_pairs={{4,0},{8,4},{12,8},{14,12},{10,14},{6,10},{2,6},{0,2},{5,1},{9,5},... | collective-permute-start | bytes 1572872 | tf_op jit(solution)/shard_map/ppermute | solution.py:269
  80.2 16.5 %collective-permute-start.9 = (bf16[256,1024]{1,0:T(8,128)(2,1)S(1)}, bf16[256,1024]{1,0:T(8,128)(2,1)S(1)}, u32[]{:S(2)}, u32[]{:S(2)}) collective-permute-start(bf16[256,1024]{1,0:T(8,128)(2,1)S(1)} %broadcast_select_fusion.7.refs_0_), channel_id=1, source_target_pairs={{4,0},{8,4},{12,8},{14,12},{10,14},{6,10},{2,6},{0,2},{5,1},{9,5},... | collective-permute-start | bytes 1572872 | tf_op jit(solution)/shard_map/ppermute | solution.py:269
  96.2 16.7 %collective-permute-start.14 = (bf16[256,1024]{1,0:T(8,128)(2,1)S(1)}, bf16[256,1024]{1,0:T(8,128)(2,1)}, u32[]{:S(2)}, u32[]{:S(2)}) collective-permute-start(bf16[256,1024]{1,0:T(8,128)(2,1)S(1)} %add_convert_fusion.8.refs_0_), channel_id=1, source_target_pairs={{0,4},{4,8},{8,12},{12,14},{14,10},{10,6},{6,2},{2,0},{1,5},{5,9},... | collective-permute-start | bytes 1572872 | tf_op jit(solution)/shard_map/ppermute | solution.py:269
  110.4 15.2 %collective-permute-start.24 = (bf16[256,1024]{1,0:T(8,128)(2,1)}, bf16[256,1024]{1,0:T(8,128)(2,1)}, u32[]{:S(2)}, u32[]{:S(2)}) collective-permute-start(bf16[256,1024]{1,0:T(8,128)(2,1)} %add_convert_fusion.1), channel_id=1, source_target_pairs={{4,0},{8,4},{12,8},{14,12},{10,14},{6,10},{2,6},{0,2},{5,1},{9,5},... | collective-permute-start | bytes 1572872 | tf_op jit(solution)/shard_map/ppermute | solution.py:269
  116.3 15.2 %collective-permute-start.15 = (bf16[256,1024]{1,0:T(8,128)(2,1)}, bf16[256,1024]{1,0:T(8,128)(2,1)}, u32[]{:S(2)}, u32[]{:S(2)}) collective-permute-start(bf16[256,1024]{1,0:T(8,128)(2,1)} %get-tuple-element.72), channel_id=1, source_target_pairs={{0,4},{4,8},{8,12},{12,14},{14,10},{10,6},{6,2},{2,0},{1,5},{5,9},... | collective-permute-start | bytes 1572872 | tf_op jit(solution)/shard_map/ppermute | solution.py:269
  116.3 26.3 %collective-permute-start.22 = (bf16[256,1024]{1,0:T(8,128)(2,1)}, bf16[256,1024]{1,0:T(8,128)(2,1)S(1)}, u32[]{:S(2)}, u32[]{:S(2)}) collective-permute-start(bf16[256,1024]{1,0:T(8,128)(2,1)} %get-tuple-element.74), channel_id=1, source_target_pairs={{0,4},{4,8},{8,12},{12,14},{14,10},{10,6},{6,2},{2,0},{1,5},{5,9},... | collective-permute-start | bytes 1572872 | tf_op jit(solution)/shard_map/ppermute | solution.py:269
  116.9 19.9 %collective-permute-start.17 = (bf16[256,1024]{1,0:T(8,128)(2,1)}, bf16[256,1024]{1,0:T(8,128)(2,1)S(1)}, u32[]{:S(2)}, u32[]{:S(2)}) collective-permute-start(bf16[256,1024]{1,0:T(8,128)(2,1)} %get-tuple-element.73), channel_id=1, source_target_pairs={{4,0},{8,4},{12,8},{14,12},{10,14},{6,10},{2,6},{0,2},{5,1},{9,5},... | collective-permute-start | bytes 1572872 | tf_op jit(solution)/shard_map/ppermute | solution.py:269
  126.9 21.0 %collective-permute-start.25 = (bf16[256,1024]{1,0:T(8,128)(2,1)S(1)}, bf16[256,1024]{1,0:T(8,128)(2,1)S(1)}, u32[]{:S(2)}, u32[]{:S(2)}) collective-permute-start(bf16[256,1024]{1,0:T(8,128)(2,1)S(1)} %add_convert_fusion), channel_id=1, source_target_pairs={{4,0},{8,4},{12,8},{14,12},{10,14},{6,10},{2,6},{0,2},{5,1},{9,5},... | collective-permute-start | bytes 1572872 | tf_op jit(solution)/shard_map/ppermute | solution.py:269
  132.8 19.1 %collective-permute-start.16 = (bf16[256,1024]{1,0:T(8,128)(2,1)S(1)}, bf16[256,1024]{1,0:T(8,128)(2,1)S(1)}, u32[]{:S(2)}, u32[]{:S(2)}) collective-permute-start(bf16[256,1024]{1,0:T(8,128)(2,1)S(1)} %add_convert_fusion.6), channel_id=1, source_target_pairs={{0,4},{4,8},{8,12},{12,14},{14,10},{10,6},{6,2},{2,0},{1,5},{5,9},... | collective-permute-start | bytes 1572872 | tf_op jit(solution)/shard_map/ppermute | solution.py:269
  137.0 20.5 %collective-permute-start.18 = (bf16[256,1024]{1,0:T(8,128)(2,1)S(1)}, bf16[256,1024]{1,0:T(8,128)(2,1)S(1)}, u32[]{:S(2)}, u32[]{:S(2)}) collective-permute-start(bf16[256,1024]{1,0:T(8,128)(2,1)S(1)} %add_convert_fusion.4), channel_id=1, source_target_pairs={{4,0},{8,4},{12,8},{14,12},{10,14},{6,10},{2,6},{0,2},{5,1},{9,5},... | collective-permute-start | bytes 1572872 | tf_op jit(solution)/shard_map/ppermute | solution.py:269
  161.2 26.0 %collective-permute-start.26 = (bf16[256,1024]{1,0:T(8,128)(2,1)S(1)}, bf16[256,1024]{1,0:T(8,128)(2,1)S(1)}, u32[]{:S(2)}, u32[]{:S(2)}) collective-permute-start(bf16[256,1024]{1,0:T(8,128)(2,1)S(1)} %get-tuple-element.68.refs_0_), channel_id=1, source_target_pairs={{0,4},{4,8},{8,12},{12,14},{14,10},{10,6},{6,2},{2,0},{1,5},{5,9},... | collective-permute-start | bytes 1572872 | tf_op jit(solution)/shard_map/ppermute | solution.py:295
  163.8 23.4 %collective-permute-start.34 = (bf16[256,1024]{1,0:T(8,128)(2,1)S(1)}, bf16[256,1024]{1,0:T(8,128)(2,1)S(1)}, u32[]{:S(2)}, u32[]{:S(2)}) collective-permute-start(bf16[256,1024]{1,0:T(8,128)(2,1)S(1)} %get-tuple-element.68.refs_0_), channel_id=1, source_target_pairs={{4,0},{8,4},{12,8},{14,12},{10,14},{6,10},{2,6},{0,2},{5,1},{9,5},... | collective-permute-start | bytes 1572872 | tf_op jit(solution)/shard_map/ppermute | solution.py:295
  173.4 22.5 %collective-permute-start.31 = (bf16[256,1024]{1,0:T(8,128)(2,1)S(1)}, bf16[256,1024]{1,0:T(8,128)(2,1)S(1)}, u32[]{:S(2)}, u32[]{:S(2)}) collective-permute-start(bf16[256,1024]{1,0:T(8,128)(2,1)S(1)} %collective-permute-done.30.refs_1_), channel_id=1, source_target_pairs={{4,0},{8,4},{12,8},{14,12},{10,14},{6,10},{2,6},{0,2},{5,1},{9,5},... | collective-permute-start | bytes 1572872 | tf_op jit(solution)/shard_map/ppermute | solution.py:295
  175.9 22.5 %collective-permute-start.36 = (bf16[256,1024]{1,0:T(8,128)(2,1)S(1)}, bf16[256,1024]{1,0:T(8,128)(2,1)S(1)}, u32[]{:S(2)}, u32[]{:S(2)}) collective-permute-start(bf16[256,1024]{1,0:T(8,128)(2,1)S(1)} %collective-permute-done.35.refs_3_), channel_id=1, source_target_pairs={{0,4},{4,8},{8,12},{12,14},{14,10},{10,6},{6,2},{2,0},{1,5},{5,9},... | collective-permute-start | bytes 1572872 | tf_op jit(solution)/shard_map/ppermute | solution.py:295
  187.1 20.7 %collective-permute-start.27 = (bf16[256,1024]{1,0:T(8,128)(2,1)S(1)}, bf16[256,1024]{1,0:T(8,128)(2,1)S(1)}, u32[]{:S(2)}, u32[]{:S(2)}) collective-permute-start(bf16[256,1024]{1,0:T(8,128)(2,1)S(1)} %collective-permute-done.26.refs_2_), channel_id=1, source_target_pairs={{0,4},{4,8},{8,12},{12,14},{14,10},{10,6},{6,2},{2,0},{1,5},{5,9},... | collective-permute-start | bytes 1572872 | tf_op jit(solution)/shard_map/ppermute | solution.py:295
  187.2 20.6 %collective-permute-start.38 = (bf16[256,1024]{1,0:T(8,128)(2,1)S(1)}, bf16[256,1024]{1,0:T(8,128)(2,1)S(1)}, u32[]{:S(2)}, u32[]{:S(2)}) collective-permute-start(bf16[256,1024]{1,0:T(8,128)(2,1)S(1)} %collective-permute-done.34.refs_0_), channel_id=1, source_target_pairs={{4,0},{8,4},{12,8},{14,12},{10,14},{6,10},{2,6},{0,2},{5,1},{9,5},... | collective-permute-start | bytes 1572872 | tf_op jit(solution)/shard_map/ppermute | solution.py:295
  198.4 25.8 %collective-permute-start.40 = (bf16[256,1024]{1,0:T(8,128)(2,1)S(1)}, bf16[256,1024]{1,0:T(8,128)(2,1)S(1)}, u32[]{:S(2)}, u32[]{:S(2)}) collective-permute-start(bf16[256,1024]{1,0:T(8,128)(2,1)S(1)} %broadcast_select_fusion.8), channel_id=1, source_target_pairs={{0,1},{1,0},{2,3},{3,2},{4,5},{5,4},{6,7},{7,6},{8,9},{9,8},{10,11... | collective-permute-start | bytes 1572872 | tf_op jit(solution)/shard_map/ppermute | solution.py:308
  207.9 18.4 %collective-permute-start.39 = (bf16[256,1024]{1,0:T(8,128)(2,1)S(1)}, bf16[256,1024]{1,0:T(8,128)(2,1)S(1)}, u32[]{:S(2)}, u32[]{:S(2)}) collective-permute-start(bf16[256,1024]{1,0:T(8,128)(2,1)S(1)} %broadcast_select_fusion.9), channel_id=1, source_target_pairs={{0,1},{1,0},{2,3},{3,2},{4,5},{5,4},{6,7},{7,6},{8,9},{9,8},{10,11... | collective-permute-start | bytes 1572872 | tf_op jit(solution)/shard_map/ppermute | solution.py:308
  208.0 28.7 %collective-permute-start.37 = (bf16[256,1024]{1,0:T(8,128)(2,1)S(1)}, bf16[256,1024]{1,0:T(8,128)(2,1)S(1)}, u32[]{:S(2)}, u32[]{:S(2)}) collective-permute-start(bf16[256,1024]{1,0:T(8,128)(2,1)S(1)} %collective-permute-done.36.refs_3_), channel_id=1, source_target_pairs={{0,4},{4,8},{8,12},{12,14},{14,10},{10,6},{6,2},{2,0},{1,5},{5,9},... | collective-permute-start | bytes 1572872 | tf_op jit(solution)/shard_map/ppermute | solution.py:295
  208.3 15.9 %collective-permute-start.41 = (f32[1,256]{1,0:T(1,128)S(1)}, f32[1,256]{1,0:T(1,128)S(1)}, u32[]{:S(2)}, u32[]{:S(2)}) collective-permute-start(f32[1,256]{1,0:T(1,128)S(1)} %bitcast.24), channel_id=1, source_target_pairs={{0,14},{4,10},{8,6},{12,2},{14,0},{10,4},{6,8},{2,12},{1,15},{5,11... | collective-permute-start | bytes 3080 | tf_op jit(solution)/shard_map/ppermute | solution.py:311
  212.0 25.6 %collective-permute-start.32 = (bf16[256,1024]{1,0:T(8,128)(2,1)S(1)}, bf16[256,1024]{1,0:T(8,128)(2,1)S(1)}, u32[]{:S(2)}, u32[]{:S(2)}) collective-permute-start(bf16[256,1024]{1,0:T(8,128)(2,1)S(1)} %collective-permute-done.31.refs_1_), channel_id=1, source_target_pairs={{4,0},{8,4},{12,8},{14,12},{10,14},{6,10},{2,6},{0,2},{5,1},{9,5},... | collective-permute-start | bytes 1572872 | tf_op jit(solution)/shard_map/ppermute | solution.py:295
  224.2 15.4 %collective-permute-start.47 = (bf16[256,1024]{1,0:T(8,128)(2,1)S(1)}, bf16[256,1024]{1,0:T(8,128)(2,1)S(1)}, u32[]{:S(2)}, u32[]{:S(2)}) collective-permute-start(bf16[256,1024]{1,0:T(8,128)(2,1)S(1)} %collective-permute-done.38.refs_0_), channel_id=1, source_target_pairs={{4,0},{8,4},{12,8},{14,12},{10,14},{6,10},{2,6},{0,2},{5,1},{9,5},... | collective-permute-start | bytes 1572872 | tf_op jit(solution)/shard_map/ppermute | solution.py:295
  237.6 19.5 %collective-permute-start.49 = (bf16[256,1024]{1,0:T(8,128)(2,1)S(1)}, bf16[256,1024]{1,0:T(8,128)(2,1)S(1)}, u32[]{:S(2)}, u32[]{:S(2)}) collective-permute-start(bf16[256,1024]{1,0:T(8,128)(2,1)S(1)} %broadcast_select_fusion), channel_id=1, source_target_pairs={{0,1},{1,0},{2,3},{3,2},{4,5},{5,4},{6,7},{7,6},{8,9},{9,8},{10,11... | collective-permute-start | bytes 1572872 | tf_op jit(solution)/shard_map/ppermute | solution.py:308
  (55 other events, 579.7 us)

commit v4 on v3

v4 whole, which is shorter than its diff:
```python
import functools
import math

import jax
import jax.numpy as jnp
import numpy as np
from jax import lax
from jax.experimental import pallas as pl
from jax.experimental.pallas import tpu as pltpu
from jax.sharding import PartitionSpec as P

D = 16384
H = 128
KVH = 8
HD = 128
EPS_NORM = 1e-05
BF16 = jnp.bfloat16
F32 = jnp.float32
RING_LIMIT = 16
MIB = 1024 * 1024


def dot(a, b):
    return jnp.dot(a, b, preferred_element_type=F32)


def attention_kernel(heads, core_ref, q_ref, own_ref, far_ref, *refs):
    o_ref = refs[-1]
    k_ref, v_ref, pk_ref, pv_ref = own_ref.at[0], own_ref.at[1], far_ref.at[0], far_ref.at[1]
    rows = q_ref.shape[0]
    inv_root = 1.0 / math.sqrt(HD)
    query_pos = lax.broadcasted_iota(jnp.int32, (rows, rows), 0)
    key_pos = lax.broadcasted_iota(jnp.int32, (rows, rows), 1)
    visible = key_pos <= query_pos
    peer_visible = core_ref[0] == 1
    contract = (((1,), (1,)), ((), ()))
    for head in range(heads):
        columns = slice(head * HD, (head + 1) * HD)
        query = q_ref[:, columns]
        own = lax.dot_general(query, k_ref[...], contract, preferred_element_type=F32) * inv_root
        far = lax.dot_general(query, pk_ref[...], contract, preferred_element_type=F32) * inv_root
        own = jnp.where(visible, own, -1e30)
        far = jnp.where(peer_visible, far, -1e30)
        top = jnp.maximum(jnp.max(own, axis=1, keepdims=True), jnp.max(far, axis=1, keepdims=True))
        own = jnp.exp(own - top)
        far = jnp.exp(far - top)
        total = jnp.sum(own, axis=1, keepdims=True) + jnp.sum(far, axis=1, keepdims=True)
        mixed = dot(own.astype(BF16), v_ref[...]) + dot(far.astype(BF16), pv_ref[...])
        o_ref[:, columns] = (mixed / total).astype(BF16)


def attention(core, queries, own, far, after=()):
    queries, index, count = queries
    rows, width = queries.shape
    width = width // count
    heads = min(4, width // HD)
    first = index * width // (heads * HD)
    whole = pl.BlockSpec(memory_space=pltpu.VMEM)
    wanted = pl.BlockSpec((rows, heads * HD), lambda h, s: (0, first + h))
    part = pl.BlockSpec((rows, heads * HD), lambda h, s: (0, h))
    return pl.pallas_call(
        functools.partial(attention_kernel, heads),
        grid_spec=pltpu.PrefetchScalarGridSpec(
            num_scalar_prefetch=1,
            grid=(width // (heads * HD),),
            in_specs=[wanted, whole, whole] + [pl.BlockSpec(memory_space=pl.ANY)] * len(after),
            out_specs=part,
        ),
        out_shape=jax.ShapeDtypeStruct((rows, width), BF16),
        compiler_params=pltpu.CompilerParams(vmem_limit_bytes=24 * MIB),
        cost_estimate=pl.CostEstimate(
            flops=8 * rows * rows * width, bytes_accessed=4 * rows * width, transcendentals=2 * rows * rows * width // HD
        ),
        name="attention",
    )(core, queries, own, far, *after)


def project_kernel(info_ref, x_ref, w_ref, *refs):
    own_ref, peer_ref = refs[-2:]
    rows = own_ref.shape[0]
    result = dot(x_ref[...], w_ref[...]).astype(BF16)
    own_ref[...] = result[:rows]
    peer_ref[...] = result[rows:]


def project(info, pair, pieces, piece, both, weight, width, after):
    rows, depth = both.shape
    rows = rows // 2
    tile = min(256, width)
    tiles = width // tile
    out = pl.BlockSpec((rows, tile), lambda j, s: (0, j))
    return pl.pallas_call(
        project_kernel,
        grid_spec=pltpu.PrefetchScalarGridSpec(
            num_scalar_prefetch=1,
            grid=(tiles,),
            in_specs=[
                pl.BlockSpec(memory_space=pltpu.VMEM),
                pl.BlockSpec((depth, tile), lambda j, s: (0, (s[pair] * pieces + piece) * tiles + j)),
            ]
            + [pl.BlockSpec(memory_space=pl.ANY)] * len(after),
            out_specs=[out, out],
        ),
        out_shape=[jax.ShapeDtypeStruct((rows, width), BF16)] * 2,
        compiler_params=pltpu.CompilerParams(vmem_limit_bytes=34 * MIB),
        cost_estimate=pl.CostEstimate(
            flops=4 * rows * depth * width, bytes_accessed=2 * depth * width, transcendentals=0
        ),
        name="project",
    )(info, both, weight, *after)


def query_kernel(sizes, code, first, info_ref, *refs):
    chosen, far = refs[: sizes[0]], refs[sizes[0] : sum(sizes)]
    w_ref = refs[sum(sizes)]
    own_ref, peer_ref, x_ref = refs[-3:]
    rows = own_ref.shape[0]

    @pl.when(pl.program_id(0) == 0)
    def _():
        for blocks, place in ((chosen, slice(0, rows)), (far, slice(rows, 2 * rows))):
            for choice, block in enumerate(blocks):

                @pl.when(info_ref[code] == choice if len(blocks) > 1 else True)
                def _():
                    x_ref[place] = block[...]

    for part, (place, out) in enumerate(((slice(0, rows), own_ref), (slice(rows, 2 * rows), peer_ref))):
        result = dot(x_ref[place], w_ref[...])
        if not first:
            result = result + refs[sum(sizes) + 1 + part][...]
        out[...] = result.astype(out.dtype)


def query_block(info, pair, code, chosen, far, weight, acc, last):
    rows, depth = far[0].shape
    width = weight.shape[1]
    tile = min(512, width)
    whole = pl.BlockSpec(memory_space=pltpu.VMEM)
    out = pl.BlockSpec((rows, tile), lambda j, s: (0, j))
    return pl.pallas_call(
        functools.partial(query_kernel, (len(chosen), len(far)), code, not acc),
        grid_spec=pltpu.PrefetchScalarGridSpec(
            num_scalar_prefetch=1,
            grid=(width // tile,),
            in_specs=[whole] * (len(chosen) + len(far))
            + [pl.BlockSpec((depth, tile), lambda j, s: (s[pair], j))]
            + [out] * len(acc),
            out_specs=[out, out],
            scratch_shapes=[pltpu.VMEM((2 * rows, depth), BF16)],
        ),
        out_shape=[
            jax.ShapeDtypeStruct((rows, width), F32),
            jax.ShapeDtypeStruct((rows, width), BF16 if last else F32),
        ],
        compiler_params=pltpu.CompilerParams(vmem_limit_bytes=34 * MIB),
        cost_estimate=pl.CostEstimate(
            flops=4 * rows * depth * width, bytes_accessed=2 * depth * width + 16 * rows * width, transcendentals=0
        ),
        name="next_query",
    )(info, *chosen, *far, weight, *acc)


def add_kernel(total_ref, more_ref, *refs):
    refs[-1][...] = total_ref[...] + more_ref[...]


def add_in_step(total, more, blocks):
    whole = pl.BlockSpec(memory_space=pltpu.VMEM)
    free = pl.BlockSpec(memory_space=pl.ANY)
    *blocks, total = pl.pallas_call(
        add_kernel,
        in_specs=[whole, whole] + [free] * len(blocks),
        out_specs=[free] * len(blocks) + [whole],
        out_shape=[jax.ShapeDtypeStruct(block.shape, block.dtype) for block in (*blocks, total)],
        input_output_aliases={2 + index: index for index in range(len(blocks))},
        name="add_squares",
    )(total, more, *blocks)
    return total, blocks


def pick_kernel(codes, sizes, info_ref, *refs):
    outs = refs[len(refs) - len(codes) :]
    start = 0
    for code, size, out in zip(codes, sizes, outs):
        for choice in range(size):

            @pl.when(info_ref[code] == choice)
            def _():
                out[...] = refs[start + choice][...]

        start += size


def pick(info, codes, groups, after):
    whole = pl.BlockSpec(memory_space=pltpu.VMEM)
    first = groups[0][0]
    return pl.pallas_call(
        functools.partial(pick_kernel, codes, [len(group) for group in groups]),
        grid_spec=pltpu.PrefetchScalarGridSpec(
            num_scalar_prefetch=1,
            grid=(1,),
            in_specs=[whole] * sum(len(group) for group in groups) + [pl.BlockSpec(memory_space=pl.ANY)] * len(after),
            out_specs=[whole] * len(groups),
        ),
        out_shape=[jax.ShapeDtypeStruct(first.shape, first.dtype)] * len(groups),
        name="pick",
    )(info, *[block for group in groups for block in group], *after)


def ring_of(n):
    return [2 * p for p in range(n // 2)] + [2 * p + 1 for p in reversed(range(n // 2))]


def tables(n):
    half = n // 2
    ring = ring_of(n)
    place = {chip: p for p, chip in enumerate(ring)}
    table = np.zeros((n, 2, 2 * half + n), np.int32)
    for chip in range(n):
        for core in range(2):

            def is_mine(q):
                return ring[(place[chip] + q) % n] // half == core

            for k in range(half):
                near = is_mine(k)
                assert near != is_mine(k - half)
                table[chip, core, k] = ring[(place[chip] + (k if near else k - half)) % n] - core * half
                q = (k if near else k - half) * (1 if core == 0 else -1)
                if k > 0:
                    table[chip, core, half + k] = block_choices(k, half).index(q)
                else:
                    table[chip, core, half] = 0 if near else 1 + core
            for q in range(1 - half, half + 1):
                real = q if core == 0 else -q
                pair = (real % half, 0 if is_mine(real) else 1)
                table[chip, core, 2 * half + q + half - 1] = sum_choices(q, half).index(pair)
    return table.reshape(2 * n, -1)


def block_choices(k, half):
    return list(dict.fromkeys([k, k - half, -k, half - k]))


def sum_choices(q, half):
    return [(k, kind) for k in dict.fromkeys([q % half, -q % half]) for kind in (0, 1)]


def choose(code, arrays):
    result = arrays[-1]
    for index in reversed(range(len(arrays) - 1)):
        result = jnp.where(code == index, arrays[index], result)
    return result


def on_ring(n, att_queries, att_keys, att_values, out_weight, residual, norm_gain, next_weight):
    half = n // 2
    ring = ring_of(n)
    up = [(ring[p], ring[(p + 1) % n]) for p in range(n)]
    swap = [(0, 1), (1, 0)]
    long_way = [(2 * a, 2 * b) for a, b in up] + [(2 * b + 1, 2 * a + 1) for a, b in up]
    short_way = [(2 * b, 2 * a) for a, b in up] + [(2 * a + 1, 2 * b + 1) for a, b in up]
    devices = ("tensor", "tokens")
    chip = lax.axis_index("tensor")
    core = lax.axis_index("tokens")
    rows, width = att_queries.shape
    info = lax.dynamic_index_in_dim(jnp.asarray(tables(n)), chip * 2 + core, 0, keepdims=False)

    heads_here = width // HD
    kv_head = chip * heads_here // (H // KVH)
    own = jnp.stack([lax.dynamic_index_in_dim(array, kv_head, 1, keepdims=False) for array in (att_keys, att_values)])
    far = lax.ppermute(own, "tokens", swap)
    attended, attended_peer = [], []
    for part in range(2):
        queries = (att_queries, part, 2)
        attended.append(attention(core[None], queries, own, far, attended))
        attended_peer.append(lax.ppermute(attended[-1], "tokens", swap))
    both = jnp.concatenate(
        [jnp.concatenate(attended, axis=1), jnp.concatenate(attended_peer, axis=1)], axis=0
    )

    made = {}

    def make(k, after=()):
        made[k, 0], outgoing = project(info, k, 1, 0, both, out_weight, residual.shape[1], after)
        made[k, 1] = lax.ppermute(outgoing, "tokens", swap)

    def partial_sum(q):
        return choose(info[2 * half + q + half - 1], [made[key] for key in sum_choices(q, half)]).astype(F32)

    arrived = {}

    def send(way, step):
        q = half - step + 1 if way == "long" else step - half
        value = partial_sum(q)
        if step > 1:
            value = value + arrived[way].astype(F32)
        value = value.astype(BF16)
        arrived[way] = lax.ppermute(value, devices, long_way if way == "long" else short_way)
        return value

    def need(q, after):
        for k in dict.fromkeys([q % half, -q % half]):
            if (k, 0) not in made:
                make(k, after)

    make(0)
    make(1)
    recent = [send("long", 1)]
    for step in range(1, half):
        need(step - half, recent)
        need(half - step, recent)
        recent = [send("short", step), send("long", step + 1)]

    mixed = residual.astype(F32) + partial_sum(0) + arrived["long"].astype(F32) + arrived["short"].astype(F32)
    resid_out = mixed.astype(BF16)
    scaled = (mixed * norm_gain.astype(F32)).astype(BF16)
    squares = jnp.sum(mixed * mixed, axis=1)[None]

    held = {0: scaled}
    long_block, short_block = scaled, scaled
    reach = half
    for step in range(1, half):
        long_block = lax.ppermute(long_block, devices, long_way)
        short_block = lax.ppermute(short_block, devices, short_way)
        if reach >= 1:
            more = lax.ppermute(squares, "tensor", [(ring[p], ring[(p + reach) % n]) for p in range(n)])
            squares, (long_block, short_block) = add_in_step(squares, more, [long_block, short_block])
            reach //= 2
        held[-step], held[step] = long_block, short_block
    while reach >= 1:
        squares = squares + lax.ppermute(squares, "tensor", [(ring[p], ring[(p + reach) % n]) for p in range(n)])
        reach //= 2
    meets = {b: ring[(p + half) % n] // half for p, b in enumerate(ring)}
    last_hop = [
        lax.ppermute(held[1 - half], devices, [(2 * a, 2 * b + meets[b]) for a, b in up]),
        lax.ppermute(held[1 - half], devices, [(2 * b + 1, 2 * a + meets[a]) for a, b in up]),
    ]
    scaled_peer = lax.ppermute(scaled, "tokens", swap)

    acc, after = (), ()
    groups = {}
    for k in range(1, half):
        groups.setdefault(max(k, half - k), []).append(k)
    for reached in sorted(groups):
        pairs = groups[reached]
        wanted = {k: [held[q] for q in block_choices(k, half)] for k in pairs}
        others = [[wanted[k][index ^ 1] for index in range(len(wanted[k]))] for k in pairs]
        outgoing = pick(info, [half + k for k in pairs], others, after)
        far = [lax.ppermute(block, "tokens", swap) for block in outgoing]
        for k, block in zip(pairs, far):
            acc = query_block(info, k, half + k, wanted[k], [block], next_weight, acc, False)
            after = acc[:1]
    acc = query_block(
        info, 0, half, [scaled, *last_hop], [scaled_peer, *reversed(last_hop)], next_weight, acc, True
    )
    query_sum = acc[0] + lax.ppermute(acc[1], "tokens", swap).astype(F32)
    factor = 1.0 / jnp.sqrt(squares[0] / D + EPS_NORM)
    return (resid_out, (query_sum * factor[:, None]).astype(BF16))


def on_mesh(n, att_queries, att_keys, att_values, out_weight, residual, norm_gain, next_weight):
    rows, width = att_queries.shape
    swap = [(0, 1), (1, 0)]
    chip = lax.axis_index("tensor")
    core = lax.axis_index("tokens")
    kv_head = chip * (width // HD) // (H // KVH)
    own = jnp.stack([lax.dynamic_index_in_dim(array, kv_head, 1, keepdims=False) for array in (att_keys, att_values)])
    far = lax.ppermute(own, "tokens", swap)
    attended = attention(core[None], (att_queries, 0, 1), own, far)
    both = lax.all_gather(attended, "tokens", axis=0, tiled=True)
    partial = dot(both, out_weight).astype(BF16)
    partial = lax.all_to_all(partial, "tokens", split_axis=0, concat_axis=1, tiled=True)
    attn_out = lax.psum_scatter(partial.astype(F32), "tensor", scatter_dimension=1, tiled=True)
    mixed = residual.astype(F32) + attn_out
    total_squares = lax.psum(jnp.sum(mixed * mixed, axis=1), "tensor")
    factor = 1.0 / jnp.sqrt(total_squares / D + EPS_NORM)
    normed = (mixed * factor[:, None] * norm_gain.astype(F32)).astype(BF16)
    gathered = lax.all_gather(normed, "tensor", axis=1, tiled=True)
    halves = lax.all_to_all(gathered, "tokens", split_axis=1, concat_axis=0, tiled=True)
    query_sum = lax.psum_scatter(dot(halves, next_weight), "tokens", scatter_dimension=0, tiled=True)
    return (mixed.astype(BF16), query_sum.astype(BF16))


def solution(mesh):
    n = mesh.shape["tensor"]
    in_specs = (
        P(("groups", "tokens"), "tensor"),
        P(("groups", "tokens"), None, None),
        P(("groups", "tokens"), None, None),
        P("tensor", "tokens"),
        P(("groups", "tokens"), "tensor"),
        P("tensor"),
        P("tokens", "tensor"),
    )
    out_specs = (P(("groups", "tokens"), "tensor"), P(("groups", "tokens"), "tensor"))
    body = functools.partial(on_ring if n <= RING_LIMIT else on_mesh, n)
    return jax.shard_map(body, mesh=mesh, in_specs=in_specs, out_specs=out_specs, check_vma=False)
```

time: 283 us -> 289 us (1.021)
  starting transfers between devices: 46.3 us -> 26.8 us
  waiting for transfers between devices: 121 us -> 135 us
  other arithmetic: 20.3 us -> 7.18 us
  local copies, waits for them, and re-layouts: 9.3 us -> 18.4 us
  Pallas kernels: 79.8 us -> 88.2 us
  between operations: 5.59 us -> 11.4 us
    ppermute x3, waiting for transfers between devices: 14.3 us -> 54.6 us  [on_ring(): lax.ppermute(squares, 'tensor', [(ring[p], ring[(p + reach) % n]) for p i...]
    ppermute x46 -> x24, waiting for transfers between devices: 104 us -> 76.9 us  [the longest x7 73.2 us: send(): lax.ppermute(value, devices, long_way if way == 'long' else short_way)]
    ppermute x46 -> x24, starting transfers between devices: 38.8 us -> 19.8 us  [the longest x7 9.19 us: send(): lax.ppermute(value, devices, long_way if way == 'long' else short_way)]
    pallas_call x4 -> x9, Pallas kernels: 34.2 us -> 44.8 us  [the longest x4 31.9 us: query_block(): pl.pallas_call(functools.partial(query_kernel, (len(chosen), len(far)), c...]
    unnamed x56 -> x62, local copies, waits for them, and re-layouts: 5.52 us -> 15.6 us
    convert_element_type x11 -> x5, other arithmetic: 12.1 us -> 4.48 us  [the longest x3 3.25 us: send(): value = value.astype(BF16)]
    select_n x12 -> x2, other arithmetic: 3.66 us -> 0.3 us  [choose(): result = jnp.where(code == index, arrays[index], result)]
    pallas_call x8 -> x4, Pallas kernels: 39.8 us -> 37.7 us  [project(): pl.pallas_call(project_kernel, grid_spec=pltpu.PrefetchScalarGridSpec(num...]
  transfers between devices with their start and end apart: 52 -> 30, of which waited for: 26 -> 16; matrix products, arithmetic and copies ran while one was open for 7% -> 1% of each run, Pallas kernels for 20% -> 15%
where the time goes in v4:
time: 289 us; the launch traced here: 287 us
  waiting for transfers between devices  135 us (47%)
  Pallas kernels  88.2 us (31%)
  starting transfers between devices  26.8 us (9%)
  local copies, waits for them, and re-layouts  18.4 us (6%)
  between operations  11.4 us (4%)
  other arithmetic  7.18 us (2%)
    ppermute x7, waiting for transfers between devices, send(): lax.ppermute(value, devices, long_way if way == 'long' else short_way)  73.2 us
    ppermute x3, waiting for transfers between devices, on_ring(): lax.ppermute(squares, 'tensor', [(ring[p], ring[(p + reach) % n]) for p i...  54.6 us
    pallas_call x4, Pallas kernels, project(): pl.pallas_call(project_kernel, grid_spec=pltpu.PrefetchScalarGridSpec(num...  37.7 us
    pallas_call x4, Pallas kernels, query_block(): pl.pallas_call(functools.partial(query_kernel, (len(chosen), len(far)), c...  31.9 us
    unnamed x62, local copies, waits for them, and re-layouts  15.6 us
    pallas_call x2, Pallas kernels, pick(): pl.pallas_call(functools.partial(pick_kernel, codes, [len(group) for grou...  9.24 us
    ppermute x7, starting transfers between devices, send(): lax.ppermute(value, devices, long_way if way == 'long' else short_way)  9.19 us
  transfers between devices with their start and end apart: 30, of which 16 were waited for; matrix products, arithmetic and copies ran while one was open for 1% of the time, Pallas kernels for 15%

profile of v4, /device:TPU:0, one launch (start us, length us, event | category | flops | bytes accessed | tf_op | source)
XLA Modules:
  0.0 287.4 jit_solution(9714080209753380280)
XLA Ops:
  4.9 2.9 attention.2.refs_0_
  7.8 2.9 %attention.3 = bf16[256,1024]{1,0:T(8,128)(2,1)S(1)} custom-call(s32[1]{0:T(128)} %bitcast.2.core_ref, bf16[256,2048]{1,0:T(8,128)(2,1)S(1)} %copy-done.18, bf16[2,256,128]{2,1,0:T(8,128)(2,1)S(1)} %pad_maximum_fusion.own_ref, bf16[2,256,128]{2,1,0:T(8,128)(2,1)S(1)} %collective-permute-done.far_ref, bf16[256,1024]{1,0:T(8,128)(2,1)S(1)} %attention.2.refs_0_), custom_call_target="tpu_custom_call" | custom-call | flops 536870912 | bytes 1048576 | tf_op jit(solution)/shard_map/attention/pallas_call | solution.py:61
  13.6 9.4 %project.4 = (bf16[256,2048]{1,0:T(8,128)(2,1)S(1)}, bf16[256,2048]{1,0:T(8,128)(2,1)S(1)}) custom-call(s32[16]{0:T(128)S(1)} %get-tuple-element.65.info_ref, bf16[512,2048]{1,0:T(8,128)(2,1)S(1)} %maximum_maximum_fusion.x_ref, bf16[2048,8192]{1,0:T(8,128)(2,1)} %w_ref.7), custom_call_target="tpu_custom_call" | custom-call | flops 4294967296 | bytes 8388608 | tf_op jit(solution)/shard_map/project/pallas_call | solution.py:92
  24.8 9.4 %project.5 = (bf16[256,2048]{1,0:T(8,128)(2,1)S(1)}, bf16[256,2048]{1,0:T(8,128)(2,1)S(1)}) custom-call(s32[16]{0:T(128)S(1)} %get-tuple-element.65.info_ref, bf16[512,2048]{1,0:T(8,128)(2,1)S(1)} %maximum_maximum_fusion.x_ref, bf16[2048,8192]{1,0:T(8,128)(2,1)} %w_ref.7), custom_call_target="tpu_custom_call" | custom-call | flops 4294967296 | bytes 8388608 | tf_op jit(solution)/shard_map/project/pallas_call | solution.py:92
  34.6 9.4 %project.6 = (bf16[256,2048]{1,0:T(8,128)(2,1)S(1)}, bf16[256,2048]{1,0:T(8,128)(2,1)S(1)}) custom-call(s32[16]{0:T(128)S(1)} %get-tuple-element.65.info_ref, bf16[512,2048]{1,0:T(8,128)(2,1)S(1)} %maximum_maximum_fusion.x_ref, bf16[2048,8192]{1,0:T(8,128)(2,1)} %w_ref.7, bf16[256,2048]{1,0:T(8,128)(2,1)S(1)} %broadcast_select_fusion.refs_0_), custom_call_target="tpu_custom_call" | custom-call | flops 4294967296 | bytes 8388608 | tf_op jit(solution)/shard_map/project/pallas_call | solution.py:92
  44.4 2.7 collective-permute-start.6
  51.1 8.7 %collective-permute-done.6 = bf16[256,2048]{1,0:T(8,128)(2,1)S(1)} collective-permute-done((bf16[256,2048]{1,0:T(8,128)(2,1)S(1)}, bf16[256,2048]{1,0:T(8,128)(2,1)S(1)}, u32[]{:S(2)}, u32[]{:S(2)}) %collective-permute-start.6) | collective-permute-done | bytes 1048608 | tf_op jit(solution)/shard_map/ppermute | solution.py:300
  60.8 9.4 %project.7 = (bf16[256,2048]{1,0:T(8,128)(2,1)S(1)}, bf16[256,2048]{1,0:T(8,128)(2,1)S(1)}) custom-call(s32[16]{0:T(128)S(1)} %get-tuple-element.65.info_ref, bf16[512,2048]{1,0:T(8,128)(2,1)S(1)} %maximum_maximum_fusion.x_ref, bf16[2048,8192]{1,0:T(8,128)(2,1)} %w_ref.7, bf16[256,2048]{1,0:T(8,128)(2,1)S(1)} %select_select_fusion.refs_0_, ...), custom_call_target="tpu_custom_call" | custom-call | flops 4294967296 | bytes 8388608 | tf_op jit(solution)/shard_map/project/pallas_call | solution.py:92
  70.3 2.1 collective-permute-start.11
  73.8 21.7 %collective-permute-done.11 = bf16[256,2048]{1,0:T(8,128)(2,1)S(1)} collective-permute-done((bf16[256,2048]{1,0:T(8,128)(2,1)S(1)}, bf16[256,2048]{1,0:T(8,128)(2,1)S(1)}, u32[]{:S(2)}, u32[]{:S(2)}) %collective-permute-start.11) | collective-permute-done | bytes 1048608 | tf_op jit(solution)/shard_map/ppermute | solution.py:300
  103.0 19.1 %collective-permute-done.12 = bf16[256,2048]{1,0:T(8,128)(2,1)S(1)} collective-permute-done((bf16[256,2048]{1,0:T(8,128)(2,1)S(1)}, bf16[256,2048]{1,0:T(8,128)(2,1)S(1)}, u32[]{:S(2)}, u32[]{:S(2)}) %collective-permute-start.12) | collective-permute-done | bytes 1048608 | tf_op jit(solution)/shard_map/ppermute | solution.py:300
  123.7 2.1 collective-permute-start.10
  126.6 23.0 %collective-permute-done.10 = bf16[256,2048]{1,0:T(8,128)(2,1)S(1)} collective-permute-done((bf16[256,2048]{1,0:T(8,128)(2,1)S(1)}, bf16[256,2048]{1,0:T(8,128)(2,1)S(1)}, u32[]{:S(2)}, u32[]{:S(2)}) %collective-permute-start.10) | collective-permute-done | bytes 1048608 | tf_op jit(solution)/shard_map/ppermute | solution.py:300
  153.8 5.0 %collective-permute-start.14 = (f32[1,256]{1,0:T(1,128)S(1)}, f32[1,256]{1,0:T(1,128)S(1)}, u32[]{:S(2)}, u32[]{:S(2)}) collective-permute-start(f32[1,256]{1,0:T(1,128)S(1)} %bitcast.29), channel_id=1, source_target_pairs={{0,14},{4,10},{8,6},{12,2},{14,0},{10,4},{6,8},{2,12},{1,15},{5,11... | collective-permute-start | bytes 3080 | tf_op jit(solution)/shard_map/ppermute | solution.py:328
  158.8 21.8 %collective-permute-done.14.more_ref = f32[1,256]{1,0:T(1,128)S(1)} collective-permute-done((f32[1,256]{1,0:T(1,128)S(1)}, f32[1,256]{1,0:T(1,128)S(1)}, u32[]{:S(2)}, u32[]{:S(2)}) %collective-permute-start.14) | collective-permute-done | bytes 1056 | tf_op jit(solution)/shard_map/ppermute | solution.py:328
  186.0 21.6 %collective-permute-done.17.more_ref = f32[1,256]{1,0:T(1,128)S(1)} collective-permute-done((f32[1,256]{1,0:T(1,128)}, f32[1,256]{1,0:T(1,128)S(1)}, u32[]{:S(2)}, u32[]{:S(2)}) %collective-permute-start.17) | collective-permute-done | bytes 1056 | tf_op jit(solution)/shard_map/ppermute | solution.py:328
  212.7 3.4 %pick.2 = bf16[256,2048]{1,0:T(8,128)(2,1)} custom-call(s32[16]{0:T(128)} %copy-done.19, bf16[256,2048]{1,0:T(8,128)(2,1)} %get-tuple-element.41.refs_0_.refs_1_, bf16[256,2048]{1,0:T(8,128)(2,1)} %get-tuple-element.42.refs_1_.refs_0_), custom_call_target="tpu_custom_call" | custom-call | tf_op jit(solution)/shard_map/pick/pallas_call | solution.py:198
  220.2 7.9 %next_query.4 = (f32[256,2048]{1,0:T(8,128)S(1)}, f32[256,2048]{1,0:T(8,128)S(1)}) custom-call(s32[16]{0:T(128)S(1)} %copy-done.20, bf16[256,2048]{1,0:T(8,128)(2,1)S(1)} %copy-done.11, bf16[256,2048]{1,0:T(8,128)(2,1)S(1)} %copy-done.9, bf16[256,2048]{1,0:T(8,128)(2,1)S(1)} %collective-permute-done.26.refs_2_, bf16[8192,2048]{1,0:T(8,128)(2,1)} %refs_6_.1), custom_call_target="tpu_custom_call" | custom-call | flops 4294967296 | bytes 16777216 | tf_op jit(solution)/shard_map/next_query/pallas_call | solution.py:141
  230.8 11.2 %collective-permute-done.20.more_ref = f32[1,256]{1,0:T(1,128)S(1)} collective-permute-done((f32[1,256]{1,0:T(1,128)S(1)}, f32[1,256]{1,0:T(1,128)S(1)}, u32[]{:S(2)}, u32[]{:S(2)}) %collective-permute-start.20) | collective-permute-done | bytes 1056 | tf_op jit(solution)/shard_map/ppermute | solution.py:328
  245.1 5.9 %pick.3 = (bf16[256,2048]{1,0:T(8,128)(2,1)}, bf16[256,2048]{1,0:T(8,128)(2,1)}) custom-call(s32[16]{0:T(128)} %copy-done.19, bf16[256,2048]{1,0:T(8,128)(2,1)} %get-tuple-element.43.refs_0_.refs_7_.refs_1_.refs_2_, bf16[256,2048]{1,0:T(8,128)(2,1)} %get-tuple-element.39.refs_1_.refs_6_.refs_0_.refs_3_, ...), custom_call_target="tpu_custom_call" | custom-call | tf_op jit(solution)/shard_map/pick/pallas_call | solution.py:198
  258.3 8.0 %next_query.5 = (f32[256,2048]{1,0:T(8,128)S(1)}, f32[256,2048]{1,0:T(8,128)S(1)}) custom-call(s32[16]{0:T(128)S(1)} %copy-done.21, bf16[256,2048]{1,0:T(8,128)(2,1)S(1)} %copy-done.7, bf16[256,2048]{1,0:T(8,128)(2,1)S(1)} %copy-done.1, bf16[256,2048]{1,0:T(8,128)(2,1)S(1)} %copy-done.5, bf16[256,2048]{1,0:T(8,128)(2,1)S(1)} %copy-done.3, ...), custom_call_target="tpu_custom_call" | custom-call | flops 4294967296 | bytes 16777216 | tf_op jit(solution)/shard_map/next_query/pallas_call | solution.py:141
  266.4 8.0 %next_query.6 = (f32[256,2048]{1,0:T(8,128)S(1)}, f32[256,2048]{1,0:T(8,128)S(1)}) custom-call(s32[16]{0:T(128)S(1)} %copy-done.21, bf16[256,2048]{1,0:T(8,128)(2,1)S(1)} %copy-done.3, bf16[256,2048]{1,0:T(8,128)(2,1)S(1)} %copy-done.5, bf16[256,2048]{1,0:T(8,128)(2,1)S(1)} %copy-done.1, bf16[256,2048]{1,0:T(8,128)(2,1)S(1)} %copy-done.7, ...), custom_call_target="tpu_custom_call" | custom-call | flops 4294967296 | bytes 16777216 | tf_op jit(solution)/shard_map/next_query/pallas_call | solution.py:141
  274.4 8.0 %next_query.7 = (f32[256,2048]{1,0:T(8,128)S(1)}, bf16[256,2048]{1,0:T(8,128)(2,1)S(1)}) custom-call(s32[16]{0:T(128)S(1)} %copy-done.21, bf16[256,2048]{1,0:T(8,128)(2,1)S(1)} %copy-done.15, bf16[256,2048]{1,0:T(8,128)(2,1)S(1)} %collective-permute-done.23.refs_1_.refs_5_, bf16[256,2048]{1,0:T(8,128)(2,1)S(1)} %collective-permute-done.24.refs_2_.refs_4_, ...), custom_call_target="tpu_custom_call" | custom-call | flops 4294967296 | bytes 16777216 | tf_op jit(solution)/shard_map/next_query/pallas_call | solution.py:141
  283.8 2.3 collective-permute-done.29
  (128 shorter events, 50.2 us)
Async XLA Ops:
  23.0 11.4 %collective-permute-start.3 = (bf16[256,2048]{1,0:T(8,128)(2,1)S(1)}, bf16[256,2048]{1,0:T(8,128)(2,1)S(1)}, u32[]{:S(2)}, u32[]{:S(2)}) collective-permute-start(bf16[256,2048]{1,0:T(8,128)(2,1)S(1)} %get-tuple-element.30), channel_id=1, source_target_pairs={{0,1},{1,0},{2,3},{3,2},{4,5},{5,4},{6,7},{7,6},{8,9},{9,8},{10,11... | collective-permute-start | bytes 3145736 | tf_op jit(solution)/shard_map/ppermute | solution.py:287
  34.2 16.7 %collective-permute-start.4 = (bf16[256,2048]{1,0:T(8,128)(2,1)S(1)}, bf16[256,2048]{1,0:T(8,128)(2,1)S(1)}, u32[]{:S(2)}, u32[]{:S(2)}) collective-permute-start(bf16[256,2048]{1,0:T(8,128)(2,1)S(1)} %get-tuple-element.32), channel_id=1, source_target_pairs={{0,1},{1,0},{2,3},{3,2},{4,5},{5,4},{6,7},{7,6},{8,9},{9,8},{10,11... | collective-permute-start | bytes 3145736 | tf_op jit(solution)/shard_map/ppermute | solution.py:287
  44.0 6.9 %collective-permute-start.5 = (bf16[256,2048]{1,0:T(8,128)(2,1)S(1)}, bf16[256,2048]{1,0:T(8,128)(2,1)S(1)}, u32[]{:S(2)}, u32[]{:S(2)}) collective-permute-start(bf16[256,2048]{1,0:T(8,128)(2,1)S(1)} %get-tuple-element.34), channel_id=1, source_target_pairs={{0,1},{1,0},{2,3},{3,2},{4,5},{5,4},{6,7},{7,6},{8,9},{9,8},{10,11... | collective-permute-start | bytes 3145736 | tf_op jit(solution)/shard_map/ppermute | solution.py:287
  44.4 15.4 %collective-permute-start.6 = (bf16[256,2048]{1,0:T(8,128)(2,1)S(1)}, bf16[256,2048]{1,0:T(8,128)(2,1)S(1)}, u32[]{:S(2)}, u32[]{:S(2)}) collective-permute-start(bf16[256,2048]{1,0:T(8,128)(2,1)S(1)} %broadcast_select_fusion.refs_0_), channel_id=1, source_target_pairs={{0,4},{4,8},{8,12},{12,14},{14,10},{10,6},{6,2},{2,0},{5,1},{9,5},... | collective-permute-start | bytes 3145736 | tf_op jit(solution)/shard_map/ppermute | solution.py:300
  70.3 25.2 %collective-permute-start.11 = (bf16[256,2048]{1,0:T(8,128)(2,1)S(1)}, bf16[256,2048]{1,0:T(8,128)(2,1)S(1)}, u32[]{:S(2)}, u32[]{:S(2)}) collective-permute-start(bf16[256,2048]{1,0:T(8,128)(2,1)S(1)} %select_select_fusion.refs_0_), channel_id=1, source_target_pairs={{4,0},{8,4},{12,8},{14,12},{10,14},{6,10},{2,6},{0,2},{1,5},{5,9},... | collective-permute-start | bytes 3145736 | tf_op jit(solution)/shard_map/ppermute | solution.py:300
  72.3 23.8 %collective-permute-start.8 = (bf16[256,2048]{1,0:T(8,128)(2,1)S(1)}, bf16[256,2048]{1,0:T(8,128)(2,1)S(1)}, u32[]{:S(2)}, u32[]{:S(2)}) collective-permute-start(bf16[256,2048]{1,0:T(8,128)(2,1)S(1)} %add_convert_fusion.4.refs_1_), channel_id=1, source_target_pairs={{0,4},{4,8},{8,12},{12,14},{14,10},{10,6},{6,2},{2,0},{5,1},{9,5},... | collective-permute-start | bytes 3145736 | tf_op jit(solution)/shard_map/ppermute | solution.py:300
  96.9 25.2 %collective-permute-start.12 = (bf16[256,2048]{1,0:T(8,128)(2,1)S(1)}, bf16[256,2048]{1,0:T(8,128)(2,1)S(1)}, u32[]{:S(2)}, u32[]{:S(2)}) collective-permute-start(bf16[256,2048]{1,0:T(8,128)(2,1)S(1)} %get-tuple-element.63), channel_id=1, source_target_pairs={{4,0},{8,4},{12,8},{14,12},{10,14},{6,10},{2,6},{0,2},{1,5},{5,9},... | collective-permute-start | bytes 3145736 | tf_op jit(solution)/shard_map/ppermute | solution.py:300
  98.8 23.4 %collective-permute-start.9 = (bf16[256,2048]{1,0:T(8,128)(2,1)S(1)}, bf16[256,2048]{1,0:T(8,128)(2,1)S(1)}, u32[]{:S(2)}, u32[]{:S(2)}) collective-permute-start(bf16[256,2048]{1,0:T(8,128)(2,1)S(1)} %get-tuple-element.62), channel_id=1, source_target_pairs={{0,4},{4,8},{8,12},{12,14},{14,10},{10,6},{6,2},{2,0},{5,1},{9,5},... | collective-permute-start | bytes 3145736 | tf_op jit(solution)/shard_map/ppermute | solution.py:300
  123.7 25.8 %collective-permute-start.10 = (bf16[256,2048]{1,0:T(8,128)(2,1)S(1)}, bf16[256,2048]{1,0:T(8,128)(2,1)S(1)}, u32[]{:S(2)}, u32[]{:S(2)}) collective-permute-start(bf16[256,2048]{1,0:T(8,128)(2,1)S(1)} %get-tuple-element.58), channel_id=1, source_target_pairs={{0,4},{4,8},{8,12},{12,14},{14,10},{10,6},{6,2},{2,0},{5,1},{9,5},... | collective-permute-start | bytes 3145736 | tf_op jit(solution)/shard_map/ppermute | solution.py:300
  125.8 23.8 %collective-permute-start.13 = (bf16[256,2048]{1,0:T(8,128)(2,1)S(1)}, bf16[256,2048]{1,0:T(8,128)(2,1)S(1)}, u32[]{:S(2)}, u32[]{:S(2)}) collective-permute-start(bf16[256,2048]{1,0:T(8,128)(2,1)S(1)} %get-tuple-element.59), channel_id=1, source_target_pairs={{4,0},{8,4},{12,8},{14,12},{10,14},{6,10},{2,6},{0,2},{1,5},{5,9},... | collective-permute-start | bytes 3145736 | tf_op jit(solution)/shard_map/ppermute | solution.py:300
  151.7 28.8 %collective-permute-start.15 = (bf16[256,2048]{1,0:T(8,128)(2,1)S(1)}, bf16[256,2048]{1,0:T(8,128)(2,1)S(1)}, u32[]{:S(2)}, u32[]{:S(2)}) collective-permute-start(bf16[256,2048]{1,0:T(8,128)(2,1)S(1)} %get-tuple-element.60.refs_0_), channel_id=1, source_target_pairs={{0,4},{4,8},{8,12},{12,14},{14,10},{10,6},{6,2},{2,0},{5,1},{9,5},... | collective-permute-start | bytes 3145736 | tf_op jit(solution)/shard_map/ppermute | solution.py:325
  153.6 27.0 %collective-permute-start.16 = (bf16[256,2048]{1,0:T(8,128)(2,1)S(1)}, bf16[256,2048]{1,0:T(8,128)(2,1)S(1)}, u32[]{:S(2)}, u32[]{:S(2)}) collective-permute-start(bf16[256,2048]{1,0:T(8,128)(2,1)S(1)} %get-tuple-element.60.refs_0_), channel_id=1, source_target_pairs={{4,0},{8,4},{12,8},{14,12},{10,14},{6,10},{2,6},{0,2},{1,5},{5,9},... | collective-permute-start | bytes 3145736 | tf_op jit(solution)/shard_map/ppermute | solution.py:326
  153.8 26.8 %collective-permute-start.14 = (f32[1,256]{1,0:T(1,128)S(1)}, f32[1,256]{1,0:T(1,128)S(1)}, u32[]{:S(2)}, u32[]{:S(2)}) collective-permute-start(f32[1,256]{1,0:T(1,128)S(1)} %bitcast.29), channel_id=1, source_target_pairs={{0,14},{4,10},{8,6},{12,2},{14,0},{10,4},{6,8},{2,12},{1,15},{5,11... | collective-permute-start | bytes 3080 | tf_op jit(solution)/shard_map/ppermute | solution.py:328
  183.9 25.6 %collective-permute-start.18 = (bf16[256,2048]{1,0:T(8,128)(2,1)}, bf16[256,2048]{1,0:T(8,128)(2,1)S(1)}, u32[]{:S(2)}, u32[]{:S(2)}) collective-permute-start(bf16[256,2048]{1,0:T(8,128)(2,1)} %get-tuple-element.38.refs_3_.refs_4_.refs_2_.refs_1_), channel_id=1, source_target_pairs={{0,4},{4,8},{8,12},{12,14},{14,10},{10,6},{6,2},{2,0},{5,1},{9,5},... | collective-permute-start | bytes 3145736 | tf_op jit(solution)/shard_map/ppermute | solution.py:325
  183.9 25.6 %collective-permute-start.19 = (bf16[256,2048]{1,0:T(8,128)(2,1)}, bf16[256,2048]{1,0:T(8,128)(2,1)S(1)}, u32[]{:S(2)}, u32[]{:S(2)}) collective-permute-start(bf16[256,2048]{1,0:T(8,128)(2,1)} %get-tuple-element.39.refs_1_.refs_6_.refs_0_.refs_3_), channel_id=1, source_target_pairs={{4,0},{8,4},{12,8},{14,12},{10,14},{6,10},{2,6},{0,2},{1,5},{5,9},... | collective-permute-start | bytes 3145736 | tf_op jit(solution)/shard_map/ppermute | solution.py:326
  185.9 21.6 %collective-permute-start.17 = (f32[1,256]{1,0:T(1,128)}, f32[1,256]{1,0:T(1,128)S(1)}, u32[]{:S(2)}, u32[]{:S(2)}) collective-permute-start(f32[1,256]{1,0:T(1,128)} %get-tuple-element.37.total_ref), channel_id=1, source_target_pairs={{0,8},{4,12},{8,14},{12,10},{14,6},{10,2},{6,0},{2,4},{1,9},{5,13}... | collective-permute-start | bytes 3080 | tf_op jit(solution)/shard_map/ppermute | solution.py:328
  216.1 25.9 %collective-permute-start.21 = (bf16[256,2048]{1,0:T(8,128)(2,1)S(1)}, bf16[256,2048]{1,0:T(8,128)(2,1)S(1)}, u32[]{:S(2)}, u32[]{:S(2)}) collective-permute-start(bf16[256,2048]{1,0:T(8,128)(2,1)S(1)} %copy-done.9), channel_id=1, source_target_pairs={{0,4},{4,8},{8,12},{12,14},{14,10},{10,6},{6,2},{2,0},{5,1},{9,5},... | collective-permute-start | bytes 3145736 | tf_op jit(solution)/shard_map/ppermute | solution.py:325
  216.1 25.8 %collective-permute-start.22 = (bf16[256,2048]{1,0:T(8,128)(2,1)}, bf16[256,2048]{1,0:T(8,128)(2,1)S(1)}, u32[]{:S(2)}, u32[]{:S(2)}) collective-permute-start(bf16[256,2048]{1,0:T(8,128)(2,1)} %get-tuple-element.42.refs_1_.refs_0_), channel_id=1, source_target_pairs={{4,0},{8,4},{12,8},{14,12},{10,14},{6,10},{2,6},{0,2},{1,5},{5,9},... | collective-permute-start | bytes 3145736 | tf_op jit(solution)/shard_map/ppermute | solution.py:326
  218.1 23.8 %collective-permute-start.20 = (f32[1,256]{1,0:T(1,128)S(1)}, f32[1,256]{1,0:T(1,128)S(1)}, u32[]{:S(2)}, u32[]{:S(2)}) collective-permute-start(f32[1,256]{1,0:T(1,128)S(1)} %copy-done.25), channel_id=1, source_target_pairs={{0,4},{4,8},{8,12},{12,14},{14,10},{10,6},{6,2},{2,0},{1,5},{5,9},... | collective-permute-start | bytes 3080 | tf_op jit(solution)/shard_map/ppermute | solution.py:328
  251.0 15.4 %collective-permute-start.27 = (bf16[256,2048]{1,0:T(8,128)(2,1)}, bf16[256,2048]{1,0:T(8,128)(2,1)S(1)}, u32[]{:S(2)}, u32[]{:S(2)}) collective-permute-start(bf16[256,2048]{1,0:T(8,128)(2,1)} %get-tuple-element.46), channel_id=1, source_target_pairs={{0,1},{1,0},{2,3},{3,2},{4,5},{5,4},{6,7},{7,6},{8,9},{9,8},{10,11... | collective-permute-start | bytes 3145736 | tf_op jit(solution)/shard_map/ppermute | solution.py:351
  251.5 22.9 %collective-permute-start.25 = (bf16[256,2048]{1,0:T(8,128)(2,1)}, bf16[256,2048]{1,0:T(8,128)(2,1)S(1)}, u32[]{:S(2)}, u32[]{:S(2)}) collective-permute-start(bf16[256,2048]{1,0:T(8,128)(2,1)} %copy-done.14), channel_id=1, source_target_pairs={{0,1},{1,0},{2,3},{3,2},{4,5},{5,4},{6,7},{7,6},{8,9},{9,8},{10,11... | collective-permute-start | bytes 3145736 | tf_op jit(solution)/shard_map/ppermute | solution.py:340
  251.5 22.9 %collective-permute-start.23 = (bf16[256,2048]{1,0:T(8,128)(2,1)S(1)}, bf16[256,2048]{1,0:T(8,128)(2,1)S(1)}, u32[]{:S(2)}, u32[]{:S(2)}) collective-permute-start(bf16[256,2048]{1,0:T(8,128)(2,1)S(1)} %copy-done.1), channel_id=1, source_target_pairs={{0,5},{4,8},{8,12},{12,14},{14,10},{10,7},{6,3},{2,1},{16,21},{20,... | collective-permute-start | bytes 3145736 | tf_op jit(solution)/shard_map/ppermute | solution.py:337
  253.1 21.3 %collective-permute-start.24 = (bf16[256,2048]{1,0:T(8,128)(2,1)S(1)}, bf16[256,2048]{1,0:T(8,128)(2,1)S(1)}, u32[]{:S(2)}, u32[]{:S(2)}) collective-permute-start(bf16[256,2048]{1,0:T(8,128)(2,1)S(1)} %copy-done.1), channel_id=1, source_target_pairs={{5,1},{9,5},{13,8},{15,12},{11,14},{7,10},{3,7},{1,3},{21,17},{25,... | collective-permute-start | bytes 3145736 | tf_op jit(solution)/shard_map/ppermute | solution.py:338
  282.4 3.7 %collective-permute-start.29 = (bf16[256,2048]{1,0:T(8,128)(2,1)S(1)}, bf16[256,2048]{1,0:T(8,128)(2,1)S(1)}, u32[]{:S(2)}, u32[]{:S(2)}) collective-permute-start(bf16[256,2048]{1,0:T(8,128)(2,1)S(1)} %get-tuple-element.54), channel_id=1, source_target_pairs={{0,1},{1,0},{2,3},{3,2},{4,5},{5,4},{6,7},{7,6},{8,9},{9,8},{10,11... | collective-permute-start | bytes 3145736 | tf_op jit(solution)/shard_map/ppermute | solution.py:358
  (36 other events, 211.6 us)

commit v5 on v4

--- a/solution.py
+++ b/solution.py
@@ -86,7 +86,7 @@
 def project(info, pair, pieces, piece, both, weight, width, after):
     rows, depth = both.shape
     rows = rows // 2
-    tile = min(256, width)
+    tile = min(512, width)
     tiles = width // tile
     out = pl.BlockSpec((rows, tile), lambda j, s: (0, j))
     return pl.pallas_call(
@@ -98,7 +98,7 @@
                 pl.BlockSpec(memory_space=pltpu.VMEM),
                 pl.BlockSpec((depth, tile), lambda j, s: (0, (s[pair] * pieces + piece) * tiles + j)),
             ]
-            + [pl.BlockSpec(memory_space=pl.ANY)] * len(after),
+            + [pl.BlockSpec(memory_space=pltpu.VMEM)] * len(after),
             out_specs=[out, out],
         ),
         out_shape=[jax.ShapeDtypeStruct((rows, width), BF16)] * 2,
@@ -153,7 +153,7 @@
             jax.ShapeDtypeStruct((rows, width), F32),
             jax.ShapeDtypeStruct((rows, width), BF16 if last else F32),
         ],
-        compiler_params=pltpu.CompilerParams(vmem_limit_bytes=34 * MIB),
+        compiler_params=pltpu.CompilerParams(vmem_limit_bytes=24 * MIB),
         cost_estimate=pl.CostEstimate(
             flops=4 * rows * depth * width, bytes_accessed=2 * depth * width + 16 * rows * width, transcendentals=0
         ),
@@ -165,17 +165,17 @@
     refs[-1][...] = total_ref[...] + more_ref[...]
 
 
-def add_in_step(total, more, blocks):
+def add_in_step(total, more, blocks, after):
     whole = pl.BlockSpec(memory_space=pltpu.VMEM)
-    free = pl.BlockSpec(memory_space=pl.ANY)
     *blocks, total = pl.pallas_call(
         add_kernel,
-        in_specs=[whole, whole] + [free] * len(blocks),
-        out_specs=[free] * len(blocks) + [whole],
+        in_specs=[whole] * (2 + len(blocks) + len(after)),
+        out_specs=[whole] * (len(blocks) + 1),
         out_shape=[jax.ShapeDtypeStruct(block.shape, block.dtype) for block in (*blocks, total)],
         input_output_aliases={2 + index: index for index in range(len(blocks))},
+        compiler_params=pltpu.CompilerParams(vmem_limit_bytes=4 * MIB),
         name="add_squares",
-    )(total, more, *blocks)
+    )(total, more, *blocks, *after)
     return total, blocks
 
 
@@ -200,10 +200,11 @@
         grid_spec=pltpu.PrefetchScalarGridSpec(
             num_scalar_prefetch=1,
             grid=(1,),
-            in_specs=[whole] * sum(len(group) for group in groups) + [pl.BlockSpec(memory_space=pl.ANY)] * len(after),
+            in_specs=[whole] * (sum(len(group) for group in groups) + len(after)),
             out_specs=[whole] * len(groups),
         ),
         out_shape=[jax.ShapeDtypeStruct(first.shape, first.dtype)] * len(groups),
+        compiler_params=pltpu.CompilerParams(vmem_limit_bytes=4 * MIB),
         name="pick",
     )(info, *[block for group in groups for block in group], *after)
 
@@ -291,27 +292,25 @@
 
     arrived = {}
 
-    def send(way, step):
+    def send(way, step, previous):
         q = half - step + 1 if way == "long" else step - half
         value = partial_sum(q)
         if step > 1:
-            value = value + arrived[way].astype(F32)
+            value = value + lax.optimization_barrier((arrived[way], previous))[0].astype(F32)
         value = value.astype(BF16)
         arrived[way] = lax.ppermute(value, devices, long_way if way == "long" else short_way)
         return value
 
-    def need(q, after):
-        for k in dict.fromkeys([q % half, -q % half]):
-            if (k, 0) not in made:
-                make(k, after)
-
     make(0)
-    make(1)
-    recent = [send("long", 1)]
+    for k in range(1, half):
+        if k != half - k:
+            make(k)
+    value = send("long", 1, None)
+    if half % 2 == 0:
+        make(half // 2, [value])
     for step in range(1, half):
-        need(step - half, recent)
-        need(half - step, recent)
-        recent = [send("short", step), send("long", step + 1)]
+        value = send("short", step, value)
+        value = send("long", step + 1, value)
 
     mixed = residual.astype(F32) + partial_sum(0) + arrived["long"].astype(F32) + arrived["short"].astype(F32)
     resid_out = mixed.astype(BF16)
@@ -320,38 +319,37 @@
 
     held = {0: scaled}
     long_block, short_block = scaled, scaled
-    reach = half
+    scaled_peer = lax.ppermute(scaled, "tokens", swap)
+    groups = {}
+    for k in range(1, half):
+        groups.setdefault(max(k, half - k), []).append(k)
+    reach = 1
+    acc, after = (), ()
     for step in range(1, half):
         long_block = lax.ppermute(long_block, devices, long_way)
         short_block = lax.ppermute(short_block, devices, short_way)
-        if reach >= 1:
-            more = lax.ppermute(squares, "tensor", [(ring[p], ring[(p + reach) % n]) for p in range(n)])
-            squares, (long_block, short_block) = add_in_step(squares, more, [long_block, short_block])
-            reach //= 2
+        if reach < n:
+            more = lax.ppermute(squares, "tensor", [(c, c ^ reach) for c in range(n)])
+            squares, (long_block,) = add_in_step(squares, more, [long_block], after)
+            reach *= 2
         held[-step], held[step] = long_block, short_block
-    while reach >= 1:
-        squares = squares + lax.ppermute(squares, "tensor", [(ring[p], ring[(p + reach) % n]) for p in range(n)])
-        reach //= 2
+        pairs = groups.get(step, [])
+        if pairs:
+            wanted = {k: [held[q] for q in block_choices(k, half)] for k in pairs}
+            others = [[wanted[k][index ^ 1] for index in range(len(wanted[k]))] for k in pairs]
+            outgoing = pick(info, [half + k for k in pairs], others, after)
+            far = [lax.ppermute(block, "tokens", swap) for block in outgoing]
+            for k, block in zip(pairs, far):
+                acc = query_block(info, k, half + k, wanted[k], [block], next_weight, acc, False)
+            after = acc[:1]
+    while reach < n:
+        squares = squares + lax.ppermute(squares, "tensor", [(c, c ^ reach) for c in range(n)])
+        reach *= 2
     meets = {b: ring[(p + half) % n] // half for p, b in enumerate(ring)}
     last_hop = [
         lax.ppermute(held[1 - half], devices, [(2 * a, 2 * b + meets[b]) for a, b in up]),
         lax.ppermute(held[1 - half], devices, [(2 * b + 1, 2 * a + meets[a]) for a, b in up]),
     ]
-    scaled_peer = lax.ppermute(scaled, "tokens", swap)
-
-    acc, after = (), ()
-    groups = {}
-    for k in range(1, half):
-        groups.setdefault(max(k, half - k), []).append(k)
-    for reached in sorted(groups):
-        pairs = groups[reached]
-        wanted = {k: [held[q] for q in block_choices(k, half)] for k in pairs}
-        others = [[wanted[k][index ^ 1] for index in range(len(wanted[k]))] for k in pairs]
-        outgoing = pick(info, [half + k for k in pairs], others, after)
-        far = [lax.ppermute(block, "tokens", swap) for block in outgoing]
-        for k, block in zip(pairs, far):
-            acc = query_block(info, k, half + k, wanted[k], [block], next_weight, acc, False)
-            after = acc[:1]
     acc = query_block(
         info, 0, half, [scaled, *last_hop], [scaled_peer, *reversed(last_hop)], next_weight, acc, True
     )

time: 289 us -> 246 us (0.85)
  Pallas kernels: 88.2 us -> 69.7 us
  local copies, waits for them, and re-layouts: 18.4 us -> 4.09 us
  waiting for transfers between devices: 135 us -> 123 us
    unnamed x62 -> x8, local copies, waits for them, and re-layouts: 15.6 us -> 1.25 us
    ppermute x7, waiting for transfers between devices: 73.2 us -> 61.4 us  [send(): lax.ppermute(value, devices, long_way if way == 'long' else short_way)]
    pallas_call x2, Pallas kernels: 9.24 us -> 1.35 us  [pick(): pl.pallas_call(functools.partial(pick_kernel, codes, [len(group) for grou...]
    pallas_call x4, Pallas kernels: 37.7 us -> 30.7 us  [project(): pl.pallas_call(project_kernel, grid_spec=pltpu.PrefetchScalarGridSpec(num...]
    pallas_call x3, Pallas kernels: 3.68 us -> 0.01 us  [add_in_step(): pl.pallas_call(add_kernel, in_specs=[whole] * (2 + len(blocks) + len(afte...]
    ppermute x3, starting transfers between devices: 1.82 us -> 4.72 us  [on_ring(): long_block = lax.ppermute(long_block, devices, long_way)]
  transfers between devices with their start and end apart: 30 -> 30, of which waited for: 16 -> 11; matrix products, arithmetic and copies ran while one was open for 1% -> 2% of each run, Pallas kernels for 15% -> 19%
where the time goes in v5:
time: 246 us; the launch traced here: 244 us
  waiting for transfers between devices  123 us (50%)
  Pallas kernels  69.7 us (28%)
  starting transfers between devices  28.8 us (12%)
  between operations  10.9 us (4%)
  other arithmetic  7.95 us (3%)
  local copies, waits for them, and re-layouts  4.09 us (2%)
    ppermute x7, waiting for transfers between devices, send(): lax.ppermute(value, devices, long_way if way == 'long' else short_way)  61.4 us
    ppermute x3, waiting for transfers between devices, on_ring(): more = lax.ppermute(squares, 'tensor', [(c, c ^ reach) for c in range(n)])  56.6 us
    pallas_call x4, Pallas kernels, query_block(): pl.pallas_call(functools.partial(query_kernel, (len(chosen), len(far)), c...  31.9 us
    pallas_call x4, Pallas kernels, project(): pl.pallas_call(project_kernel, grid_spec=pltpu.PrefetchScalarGridSpec(num...  30.7 us
    ppermute x7, starting transfers between devices, send(): lax.ppermute(value, devices, long_way if way == 'long' else short_way)  9.46 us
    pallas_call x2, Pallas kernels, attention(): pl.pallas_call(functools.partial(attention_kernel, heads), grid_spec=pltp...  5.73 us
  transfers between devices with their start and end apart: 30, of which 11 were waited for; matrix products, arithmetic and copies ran while one was open for 2% of the time, Pallas kernels for 19%

profile of v5, /device:TPU:0, one launch (start us, length us, event | category | flops | bytes accessed | tf_op | source)
XLA Modules:
  0.0 244.2 jit_solution(12318859529926554959)
XLA Ops:
  4.9 2.9 %attention.2.refs_0_ = bf16[256,1024]{1,0:T(8,128)(2,1)S(1)} custom-call(s32[1]{0:T(128)} %bitcast.2.core_ref, bf16[256,2048]{1,0:T(8,128)(2,1)S(1)} %copy-done, bf16[2,256,128]{2,1,0:T(8,128)(2,1)S(1)} %pad_maximum_fusion.own_ref, bf16[2,256,128]{2,1,0:T(8,128)(2,1)S(1)} %collective-permute-done.far_ref), custom_call_target="tpu_custom_call" | custom-call | flops 536870912 | bytes 1048576 | tf_op jit(solution)/shard_map/attention/pallas_call | solution.py:61
  7.8 2.9 %attention.3 = bf16[256,1024]{1,0:T(8,128)(2,1)S(1)} custom-call(s32[1]{0:T(128)} %bitcast.2.core_ref, bf16[256,2048]{1,0:T(8,128)(2,1)S(1)} %copy-done, bf16[2,256,128]{2,1,0:T(8,128)(2,1)S(1)} %pad_maximum_fusion.own_ref, bf16[2,256,128]{2,1,0:T(8,128)(2,1)S(1)} %collective-permute-done.far_ref, bf16[256,1024]{1,0:T(8,128)(2,1)S(1)} %attention.2.refs_0_), custom_call_target="tpu_custom_call" | custom-call | flops 536870912 | bytes 1048576 | tf_op jit(solution)/shard_map/attention/pallas_call | solution.py:61
  13.6 7.7 %project.4 = (bf16[256,2048]{1,0:T(8,128)(2,1)S(1)}, bf16[256,2048]{1,0:T(8,128)(2,1)S(1)}) custom-call(s32[16]{0:T(128)S(1)} %get-tuple-element.65.info_ref, bf16[512,2048]{1,0:T(8,128)(2,1)S(1)} %maximum_maximum_fusion.x_ref, bf16[2048,8192]{1,0:T(8,128)(2,1)} %w_ref.7), custom_call_target="tpu_custom_call" | custom-call | flops 4294967296 | bytes 8388608 | tf_op jit(solution)/shard_map/project/pallas_call | solution.py:92
  21.7 7.7 %project.6 = (bf16[256,2048]{1,0:T(8,128)(2,1)S(1)}, bf16[256,2048]{1,0:T(8,128)(2,1)S(1)}) custom-call(s32[16]{0:T(128)S(1)} %get-tuple-element.65.info_ref, bf16[512,2048]{1,0:T(8,128)(2,1)S(1)} %maximum_maximum_fusion.x_ref, bf16[2048,8192]{1,0:T(8,128)(2,1)} %w_ref.7), custom_call_target="tpu_custom_call" | custom-call | flops 4294967296 | bytes 8388608 | tf_op jit(solution)/shard_map/project/pallas_call | solution.py:92
  29.6 7.7 %project.5 = (bf16[256,2048]{1,0:T(8,128)(2,1)S(1)}, bf16[256,2048]{1,0:T(8,128)(2,1)S(1)}) custom-call(s32[16]{0:T(128)S(1)} %get-tuple-element.65.info_ref, bf16[512,2048]{1,0:T(8,128)(2,1)S(1)} %maximum_maximum_fusion.x_ref, bf16[2048,8192]{1,0:T(8,128)(2,1)} %w_ref.7), custom_call_target="tpu_custom_call" | custom-call | flops 4294967296 | bytes 8388608 | tf_op jit(solution)/shard_map/project/pallas_call | solution.py:92
  39.2 2.8 %collective-permute-start.7 = (bf16[256,2048]{1,0:T(8,128)(2,1)S(1)}, bf16[256,2048]{1,0:T(8,128)(2,1)S(1)}, u32[]{:S(2)}, u32[]{:S(2)}) collective-permute-start(bf16[256,2048]{1,0:T(8,128)(2,1)S(1)} %broadcast_select_fusion.refs_0_), channel_id=1, source_target_pairs={{0,4},{4,8},{8,12},{12,14},{14,10},{10,6},{6,2},{2,0},{5,1},{9,5},... | collective-permute-start | bytes 3145736 | tf_op jit(solution)/shard_map/ppermute | solution.py:301
  45.7 7.7 %project.7 = (bf16[256,2048]{1,0:T(8,128)(2,1)S(1)}, bf16[256,2048]{1,0:T(8,128)(2,1)S(1)}) custom-call(s32[16]{0:T(128)S(1)} %get-tuple-element.65.info_ref, bf16[512,2048]{1,0:T(8,128)(2,1)S(1)} %maximum_maximum_fusion.x_ref, bf16[2048,8192]{1,0:T(8,128)(2,1)} %w_ref.7, bf16[256,2048]{1,0:T(8,128)(2,1)S(1)} %broadcast_select_fusion.refs_0_), custom_call_target="tpu_custom_call" | custom-call | flops 4294967296 | bytes 8388608 | tf_op jit(solution)/shard_map/project/pallas_call | solution.py:92
  55.6 2.2 collective-permute-start.8
  58.4 20.5 %collective-permute-done.9 = bf16[256,2048]{1,0:T(8,128)(2,1)S(1)} collective-permute-done((bf16[256,2048]{1,0:T(8,128)(2,1)S(1)}, bf16[256,2048]{1,0:T(8,128)(2,1)S(1)}, u32[]{:S(2)}, u32[]{:S(2)}) %collective-permute-start.9) | collective-permute-done | bytes 1048608 | tf_op jit(solution)/shard_map/ppermute | solution.py:301
  80.8 2.1 collective-permute-start.10
  86.4 18.8 %collective-permute-done.11 = bf16[256,2048]{1,0:T(8,128)(2,1)S(1)} collective-permute-done((bf16[256,2048]{1,0:T(8,128)(2,1)S(1)}, bf16[256,2048]{1,0:T(8,128)(2,1)S(1)}, u32[]{:S(2)}, u32[]{:S(2)}) %collective-permute-start.11) | collective-permute-done | bytes 1048608 | tf_op jit(solution)/shard_map/ppermute | solution.py:301
  107.6 2.0 collective-permute-start.12
  110.2 21.2 %collective-permute-done.13 = bf16[256,2048]{1,0:T(8,128)(2,1)S(1)} collective-permute-done((bf16[256,2048]{1,0:T(8,128)(2,1)S(1)}, bf16[256,2048]{1,0:T(8,128)(2,1)S(1)}, u32[]{:S(2)}, u32[]{:S(2)}) %collective-permute-start.13) | collective-permute-done | bytes 1048608 | tf_op jit(solution)/shard_map/ppermute | solution.py:301
  136.1 22.2 %collective-permute-done.14.more_ref = f32[1,256]{1,0:T(1,128)S(1)} collective-permute-done((f32[1,256]{1,0:T(1,128)S(1)}, f32[1,256]{1,0:T(1,128)S(1)}, u32[]{:S(2)}, u32[]{:S(2)}) %collective-permute-start.14) | collective-permute-done | bytes 1056 | tf_op jit(solution)/shard_map/ppermute | solution.py:332
  161.6 20.5 %collective-permute-done.16.more_ref = f32[1,256]{1,0:T(1,128)S(1)} collective-permute-done((f32[1,256]{1,0:T(1,128)S(1)}, f32[1,256]{1,0:T(1,128)S(1)}, u32[]{:S(2)}, u32[]{:S(2)}) %collective-permute-start.16) | collective-permute-done | bytes 1056 | tf_op jit(solution)/shard_map/ppermute | solution.py:332
  182.9 1.8 collective-permute-start.19
  184.9 2.9 %collective-permute-start.18 = (f32[1,256]{1,0:T(1,128)S(1)}, f32[1,256]{1,0:T(1,128)S(1)}, u32[]{:S(2)}, u32[]{:S(2)}) collective-permute-start(f32[1,256]{1,0:T(1,128)S(1)} %get-tuple-element.46.total_ref), channel_id=1, source_target_pairs={{0,8},{2,10},{4,12},{6,14},{8,0},{10,2},{12,4},{14,6},{1,9},{3,11}... | collective-permute-start | bytes 3080 | tf_op jit(solution)/shard_map/ppermute | solution.py:332
  187.9 7.9 %next_query.4 = (f32[256,2048]{1,0:T(8,128)S(1)}, f32[256,2048]{1,0:T(8,128)S(1)}) custom-call(s32[16]{0:T(128)S(1)} %get-tuple-element.65.info_ref, bf16[256,2048]{1,0:T(8,128)(2,1)S(1)} %collective-permute-done.21.refs_1_.refs_0_, bf16[256,2048]{1,0:T(8,128)(2,1)S(1)} %get-tuple-element.47.refs_0_.refs_1_, ...), custom_call_target="tpu_custom_call" | custom-call | flops 4294967296 | bytes 16777216 | tf_op jit(solution)/shard_map/next_query/pallas_call | solution.py:141
  195.8 13.8 %collective-permute-done.18.more_ref = f32[1,256]{1,0:T(1,128)S(1)} collective-permute-done((f32[1,256]{1,0:T(1,128)S(1)}, f32[1,256]{1,0:T(1,128)S(1)}, u32[]{:S(2)}, u32[]{:S(2)}) %collective-permute-start.18) | collective-permute-done | bytes 1056 | tf_op jit(solution)/shard_map/ppermute | solution.py:332
  211.1 4.0 %collective-permute-start.23 = (bf16[256,2048]{1,0:T(8,128)(2,1)S(1)}, bf16[256,2048]{1,0:T(8,128)(2,1)S(1)}, u32[]{:S(2)}, u32[]{:S(2)}) collective-permute-start(bf16[256,2048]{1,0:T(8,128)(2,1)S(1)} %get-tuple-element.49.refs_0_.refs_7_.refs_1_.refs_2_), channel_id=1, source_target_pairs={{0,5},{4,8},{8,12},{12,14},{14,10},{10,7},{6,3},{2,1},{16,21},{20,... | collective-permute-start | bytes 3145736 | tf_op jit(solution)/shard_map/ppermute | solution.py:350
  215.8 8.0 %next_query.5 = (f32[256,2048]{1,0:T(8,128)S(1)}, f32[256,2048]{1,0:T(8,128)S(1)}) custom-call(s32[16]{0:T(128)S(1)} %get-tuple-element.65.info_ref, bf16[256,2048]{1,0:T(8,128)(2,1)S(1)} %collective-permute-done.20.refs_1_.refs_6_.refs_0_.refs_3_, bf16[256,2048]{1,0:T(8,128)(2,1)S(1)} %get-tuple-element.49.refs_0_.refs_7_.refs_1_.refs_2_, ...), custom_call_target="tpu_custom_call" | custom-call | flops 4294967296 | bytes 16777216 | tf_op jit(solution)/shard_map/next_query/pallas_call | solution.py:141
  223.9 8.0 %next_query.6 = (f32[256,2048]{1,0:T(8,128)S(1)}, f32[256,2048]{1,0:T(8,128)S(1)}) custom-call(s32[16]{0:T(128)S(1)} %get-tuple-element.65.info_ref, bf16[256,2048]{1,0:T(8,128)(2,1)S(1)} %collective-permute-done.26.refs_2_.refs_5_.refs_3_.refs_0_, bf16[256,2048]{1,0:T(8,128)(2,1)S(1)} %get-tuple-element.45.refs_3_.refs_4_.refs_2_.refs_1_, ...), custom_call_target="tpu_custom_call" | custom-call | flops 4294967296 | bytes 16777216 | tf_op jit(solution)/shard_map/next_query/pallas_call | solution.py:141
  231.9 8.0 %next_query.7 = (f32[256,2048]{1,0:T(8,128)S(1)}, bf16[256,2048]{1,0:T(8,128)(2,1)S(1)}) custom-call(s32[16]{0:T(128)S(1)} %get-tuple-element.65.info_ref, bf16[256,2048]{1,0:T(8,128)(2,1)S(1)} %get-tuple-element.62.refs_0_, bf16[256,2048]{1,0:T(8,128)(2,1)S(1)} %collective-permute-done.23.refs_1_.refs_5_, ...), custom_call_target="tpu_custom_call" | custom-call | flops 4294967296 | bytes 16777216 | tf_op jit(solution)/shard_map/next_query/pallas_call | solution.py:141
  240.7 2.3 collective-permute-done.29
  (76 shorter events, 27.8 us)
Async XLA Ops:
  21.3 17.7 %collective-permute-start.3 = (bf16[256,2048]{1,0:T(8,128)(2,1)S(1)}, bf16[256,2048]{1,0:T(8,128)(2,1)S(1)}, u32[]{:S(2)}, u32[]{:S(2)}) collective-permute-start(bf16[256,2048]{1,0:T(8,128)(2,1)S(1)} %get-tuple-element.32), channel_id=1, source_target_pairs={{0,1},{1,0},{2,3},{3,2},{4,5},{5,4},{6,7},{7,6},{8,9},{9,8},{10,11... | collective-permute-start | bytes 3145736 | tf_op jit(solution)/shard_map/ppermute | solution.py:288
  29.4 24.0 %collective-permute-start.5 = (bf16[256,2048]{1,0:T(8,128)(2,1)S(1)}, bf16[256,2048]{1,0:T(8,128)(2,1)S(1)}, u32[]{:S(2)}, u32[]{:S(2)}) collective-permute-start(bf16[256,2048]{1,0:T(8,128)(2,1)S(1)} %get-tuple-element.36), channel_id=1, source_target_pairs={{0,1},{1,0},{2,3},{3,2},{4,5},{5,4},{6,7},{7,6},{8,9},{9,8},{10,11... | collective-permute-start | bytes 3145736 | tf_op jit(solution)/shard_map/ppermute | solution.py:288
  37.3 16.1 %collective-permute-start.4 = (bf16[256,2048]{1,0:T(8,128)(2,1)S(1)}, bf16[256,2048]{1,0:T(8,128)(2,1)S(1)}, u32[]{:S(2)}, u32[]{:S(2)}) collective-permute-start(bf16[256,2048]{1,0:T(8,128)(2,1)S(1)} %get-tuple-element.34), channel_id=1, source_target_pairs={{0,1},{1,0},{2,3},{3,2},{4,5},{5,4},{6,7},{7,6},{8,9},{9,8},{10,11... | collective-permute-start | bytes 3145736 | tf_op jit(solution)/shard_map/ppermute | solution.py:288
  39.2 15.5 %collective-permute-start.7 = (bf16[256,2048]{1,0:T(8,128)(2,1)S(1)}, bf16[256,2048]{1,0:T(8,128)(2,1)S(1)}, u32[]{:S(2)}, u32[]{:S(2)}) collective-permute-start(bf16[256,2048]{1,0:T(8,128)(2,1)S(1)} %broadcast_select_fusion.refs_0_), channel_id=1, source_target_pairs={{0,4},{4,8},{8,12},{12,14},{14,10},{10,6},{6,2},{2,0},{5,1},{9,5},... | collective-permute-start | bytes 3145736 | tf_op jit(solution)/shard_map/ppermute | solution.py:301
  53.6 25.3 %collective-permute-start.9 = (bf16[256,2048]{1,0:T(8,128)(2,1)S(1)}, bf16[256,2048]{1,0:T(8,128)(2,1)S(1)}, u32[]{:S(2)}, u32[]{:S(2)}) collective-permute-start(bf16[256,2048]{1,0:T(8,128)(2,1)S(1)} %select_select_fusion), channel_id=1, source_target_pairs={{4,0},{8,4},{12,8},{14,12},{10,14},{6,10},{2,6},{0,2},{1,5},{5,9},... | collective-permute-start | bytes 3145736 | tf_op jit(solution)/shard_map/ppermute | solution.py:301
  53.7 25.2 %collective-permute-start.6 = (bf16[256,2048]{1,0:T(8,128)(2,1)S(1)}, bf16[256,2048]{1,0:T(8,128)(2,1)S(1)}, u32[]{:S(2)}, u32[]{:S(2)}) collective-permute-start(bf16[256,2048]{1,0:T(8,128)(2,1)S(1)} %get-tuple-element.38), channel_id=1, source_target_pairs={{0,1},{1,0},{2,3},{3,2},{4,5},{5,4},{6,7},{7,6},{8,9},{9,8},{10,11... | collective-permute-start | bytes 3145736 | tf_op jit(solution)/shard_map/ppermute | solution.py:288
  55.6 24.7 %collective-permute-start.8 = (bf16[256,2048]{1,0:T(8,128)(2,1)S(1)}, bf16[256,2048]{1,0:T(8,128)(2,1)S(1)}, u32[]{:S(2)}, u32[]{:S(2)}) collective-permute-start(bf16[256,2048]{1,0:T(8,128)(2,1)S(1)} %add_convert_fusion.4), channel_id=1, source_target_pairs={{0,4},{4,8},{8,12},{12,14},{14,10},{10,6},{6,2},{2,0},{5,1},{9,5},... | collective-permute-start | bytes 3145736 | tf_op jit(solution)/shard_map/ppermute | solution.py:301
  79.5 25.7 %collective-permute-start.11 = (bf16[256,2048]{1,0:T(8,128)(2,1)S(1)}, bf16[256,2048]{1,0:T(8,128)(2,1)S(1)}, u32[]{:S(2)}, u32[]{:S(2)}) collective-permute-start(bf16[256,2048]{1,0:T(8,128)(2,1)S(1)} %add_convert_fusion.3), channel_id=1, source_target_pairs={{4,0},{8,4},{12,8},{14,12},{10,14},{6,10},{2,6},{0,2},{1,5},{5,9},... | collective-permute-start | bytes 3145736 | tf_op jit(solution)/shard_map/ppermute | solution.py:301
  80.8 25.8 %collective-permute-start.10 = (bf16[256,2048]{1,0:T(8,128)(2,1)S(1)}, bf16[256,2048]{1,0:T(8,128)(2,1)S(1)}, u32[]{:S(2)}, u32[]{:S(2)}) collective-permute-start(bf16[256,2048]{1,0:T(8,128)(2,1)S(1)} %add_convert_fusion.2), channel_id=1, source_target_pairs={{0,4},{4,8},{8,12},{12,14},{14,10},{10,6},{6,2},{2,0},{5,1},{9,5},... | collective-permute-start | bytes 3145736 | tf_op jit(solution)/shard_map/ppermute | solution.py:301
  106.2 25.2 %collective-permute-start.13 = (bf16[256,2048]{1,0:T(8,128)(2,1)S(1)}, bf16[256,2048]{1,0:T(8,128)(2,1)S(1)}, u32[]{:S(2)}, u32[]{:S(2)}) collective-permute-start(bf16[256,2048]{1,0:T(8,128)(2,1)S(1)} %add_convert_fusion.1), channel_id=1, source_target_pairs={{4,0},{8,4},{12,8},{14,12},{10,14},{6,10},{2,6},{0,2},{1,5},{5,9},... | collective-permute-start | bytes 3145736 | tf_op jit(solution)/shard_map/ppermute | solution.py:301
  107.6 23.8 %collective-permute-start.12 = (bf16[256,2048]{1,0:T(8,128)(2,1)S(1)}, bf16[256,2048]{1,0:T(8,128)(2,1)S(1)}, u32[]{:S(2)}, u32[]{:S(2)}) collective-permute-start(bf16[256,2048]{1,0:T(8,128)(2,1)S(1)} %add_convert_fusion), channel_id=1, source_target_pairs={{0,4},{4,8},{8,12},{12,14},{14,10},{10,6},{6,2},{2,0},{5,1},{9,5},... | collective-permute-start | bytes 3145736 | tf_op jit(solution)/shard_map/ppermute | solution.py:301
  133.6 24.8 %collective-permute-start.15 = (bf16[256,2048]{1,0:T(8,128)(2,1)S(1)}, bf16[256,2048]{1,0:T(8,128)(2,1)S(1)}, u32[]{:S(2)}, u32[]{:S(2)}) collective-permute-start(bf16[256,2048]{1,0:T(8,128)(2,1)S(1)} %get-tuple-element.62.refs_0_), channel_id=1, source_target_pairs={{0,4},{4,8},{8,12},{12,14},{14,10},{10,6},{6,2},{2,0},{5,1},{9,5},... | collective-permute-start | bytes 3145736 | tf_op jit(solution)/shard_map/ppermute | solution.py:329
  135.2 24.4 %collective-permute-start.20 = (bf16[256,2048]{1,0:T(8,128)(2,1)S(1)}, bf16[256,2048]{1,0:T(8,128)(2,1)S(1)}, u32[]{:S(2)}, u32[]{:S(2)}) collective-permute-start(bf16[256,2048]{1,0:T(8,128)(2,1)S(1)} %get-tuple-element.62.refs_0_), channel_id=1, source_target_pairs={{4,0},{8,4},{12,8},{14,12},{10,14},{6,10},{2,6},{0,2},{1,5},{5,9},... | collective-permute-start | bytes 3145736 | tf_op jit(solution)/shard_map/ppermute | solution.py:330
  135.6 22.7 %collective-permute-start.14 = (f32[1,256]{1,0:T(1,128)S(1)}, f32[1,256]{1,0:T(1,128)S(1)}, u32[]{:S(2)}, u32[]{:S(2)}) collective-permute-start(f32[1,256]{1,0:T(1,128)S(1)} %bitcast.27), channel_id=1, source_target_pairs={{0,2},{2,0},{4,6},{6,4},{8,10},{10,8},{12,14},{14,12},{1,3},{3,1},... | collective-permute-start | bytes 3080 | tf_op jit(solution)/shard_map/ppermute | solution.py:332
  158.3 23.8 %collective-permute-start.17 = (bf16[256,2048]{1,0:T(8,128)(2,1)S(1)}, bf16[256,2048]{1,0:T(8,128)(2,1)S(1)}, u32[]{:S(2)}, u32[]{:S(2)}) collective-permute-start(bf16[256,2048]{1,0:T(8,128)(2,1)S(1)} %get-tuple-element.45.refs_3_.refs_4_.refs_2_.refs_1_), channel_id=1, source_target_pairs={{0,4},{4,8},{8,12},{12,14},{14,10},{10,6},{6,2},{2,0},{5,1},{9,5},... | collective-permute-start | bytes 3145736 | tf_op jit(solution)/shard_map/ppermute | solution.py:329
  159.6 22.6 %collective-permute-start.21 = (bf16[256,2048]{1,0:T(8,128)(2,1)S(1)}, bf16[256,2048]{1,0:T(8,128)(2,1)S(1)}, u32[]{:S(2)}, u32[]{:S(2)}) collective-permute-start(bf16[256,2048]{1,0:T(8,128)(2,1)S(1)} %collective-permute-done.20.refs_1_.refs_6_.refs_0_.refs_3_), channel_id=1, source_target_pairs={{4,0},{8,4},{12,8},{14,12},{10,14},{6,10},{2,6},{0,2},{1,5},{5,9},... | collective-permute-start | bytes 3145736 | tf_op jit(solution)/shard_map/ppermute | solution.py:330
  160.4 21.8 %collective-permute-start.16 = (f32[1,256]{1,0:T(1,128)S(1)}, f32[1,256]{1,0:T(1,128)S(1)}, u32[]{:S(2)}, u32[]{:S(2)}) collective-permute-start(f32[1,256]{1,0:T(1,128)S(1)} %get-tuple-element.44.total_ref), channel_id=1, source_target_pairs={{0,4},{2,6},{4,0},{6,2},{8,12},{10,14},{12,8},{14,10},{1,5},{3,7},... | collective-permute-start | bytes 3080 | tf_op jit(solution)/shard_map/ppermute | solution.py:332
  182.9 26.8 %collective-permute-start.19 = (bf16[256,2048]{1,0:T(8,128)(2,1)S(1)}, bf16[256,2048]{1,0:T(8,128)(2,1)S(1)}, u32[]{:S(2)}, u32[]{:S(2)}) collective-permute-start(bf16[256,2048]{1,0:T(8,128)(2,1)S(1)} %get-tuple-element.47.refs_0_.refs_1_), channel_id=1, source_target_pairs={{0,4},{4,8},{8,12},{12,14},{14,10},{10,6},{6,2},{2,0},{5,1},{9,5},... | collective-permute-start | bytes 3145736 | tf_op jit(solution)/shard_map/ppermute | solution.py:329
  184.7 25.0 %collective-permute-start.26 = (bf16[256,2048]{1,0:T(8,128)(2,1)S(1)}, bf16[256,2048]{1,0:T(8,128)(2,1)S(1)}, u32[]{:S(2)}, u32[]{:S(2)}) collective-permute-start(bf16[256,2048]{1,0:T(8,128)(2,1)S(1)} %collective-permute-done.21.refs_1_.refs_0_), channel_id=1, source_target_pairs={{4,0},{8,4},{12,8},{14,12},{10,14},{6,10},{2,6},{0,2},{1,5},{5,9},... | collective-permute-start | bytes 3145736 | tf_op jit(solution)/shard_map/ppermute | solution.py:330
  184.9 24.7 %collective-permute-start.18 = (f32[1,256]{1,0:T(1,128)S(1)}, f32[1,256]{1,0:T(1,128)S(1)}, u32[]{:S(2)}, u32[]{:S(2)}) collective-permute-start(f32[1,256]{1,0:T(1,128)S(1)} %get-tuple-element.46.total_ref), channel_id=1, source_target_pairs={{0,8},{2,10},{4,12},{6,14},{8,0},{10,2},{12,4},{14,6},{1,9},{3,11}... | collective-permute-start | bytes 3080 | tf_op jit(solution)/shard_map/ppermute | solution.py:332
  210.5 13.4 %collective-permute-start.27 = (bf16[256,2048]{1,0:T(8,128)(2,1)S(1)}, bf16[256,2048]{1,0:T(8,128)(2,1)S(1)}, u32[]{:S(2)}, u32[]{:S(2)}) collective-permute-start(bf16[256,2048]{1,0:T(8,128)(2,1)S(1)} %get-tuple-element.50), channel_id=1, source_target_pairs={{0,1},{1,0},{2,3},{3,2},{4,5},{5,4},{6,7},{7,6},{8,9},{9,8},{10,11... | collective-permute-start | bytes 3145736 | tf_op jit(solution)/shard_map/ppermute | solution.py:341
  211.0 20.9 %collective-permute-start.25 = (bf16[256,2048]{1,0:T(8,128)(2,1)S(1)}, bf16[256,2048]{1,0:T(8,128)(2,1)S(1)}, u32[]{:S(2)}, u32[]{:S(2)}) collective-permute-start(bf16[256,2048]{1,0:T(8,128)(2,1)S(1)} %get-tuple-element.62.refs_0_), channel_id=1, source_target_pairs={{0,1},{1,0},{2,3},{3,2},{4,5},{5,4},{6,7},{7,6},{8,9},{9,8},{10,11... | collective-permute-start | bytes 3145736 | tf_op jit(solution)/shard_map/ppermute | solution.py:322
  211.1 20.9 %collective-permute-start.23 = (bf16[256,2048]{1,0:T(8,128)(2,1)S(1)}, bf16[256,2048]{1,0:T(8,128)(2,1)S(1)}, u32[]{:S(2)}, u32[]{:S(2)}) collective-permute-start(bf16[256,2048]{1,0:T(8,128)(2,1)S(1)} %get-tuple-element.49.refs_0_.refs_7_.refs_1_.refs_2_), channel_id=1, source_target_pairs={{0,5},{4,8},{8,12},{12,14},{14,10},{10,7},{6,3},{2,1},{16,21},{20,... | collective-permute-start | bytes 3145736 | tf_op jit(solution)/shard_map/ppermute | solution.py:350
  215.1 16.8 %collective-permute-start.24 = (bf16[256,2048]{1,0:T(8,128)(2,1)S(1)}, bf16[256,2048]{1,0:T(8,128)(2,1)S(1)}, u32[]{:S(2)}, u32[]{:S(2)}) collective-permute-start(bf16[256,2048]{1,0:T(8,128)(2,1)S(1)} %get-tuple-element.49.refs_0_.refs_7_.refs_1_.refs_2_), channel_id=1, source_target_pairs={{5,1},{9,5},{13,8},{15,12},{11,14},{7,10},{3,7},{1,3},{21,17},{25,... | collective-permute-start | bytes 3145736 | tf_op jit(solution)/shard_map/ppermute | solution.py:351
  (9 other events, 49.0 us)

commit v6 on v5

--- a/solution.py
+++ b/solution.py
@@ -179,6 +179,23 @@
     return total, blocks
 
 
+def hold_kernel(*refs):
+    pass
+
+
+def hold(array, after):
+    whole = pl.BlockSpec(memory_space=pltpu.VMEM)
+    return pl.pallas_call(
+        hold_kernel,
+        in_specs=[whole] * (1 + len(after)),
+        out_specs=whole,
+        out_shape=jax.ShapeDtypeStruct(array.shape, array.dtype),
+        input_output_aliases={0: 0},
+        compiler_params=pltpu.CompilerParams(vmem_limit_bytes=4 * MIB),
+        name="hold",
+    )(array, *after)
+
+
 def pick_kernel(codes, sizes, info_ref, *refs):
     outs = refs[len(refs) - len(codes) :]
     start = 0
@@ -283,8 +300,10 @@
 
     made = {}
 
-    def make(k, after=()):
+    def make(k, after=(), arrivals=()):
         made[k, 0], outgoing = project(info, k, 1, 0, both, out_weight, residual.shape[1], after)
+        if arrivals:
+            outgoing = hold(outgoing, arrivals)
         made[k, 1] = lax.ppermute(outgoing, "tokens", swap)
 
     def partial_sum(q):
@@ -302,13 +321,15 @@
         return value
 
     make(0)
-    for k in range(1, half):
-        if k != half - k:
-            make(k)
-    value = send("long", 1, None)
-    if half % 2 == 0:
-        make(half // 2, [value])
-    for step in range(1, half):
+    make(1)
+    long_value = send("long", 1, None)
+    for k in range(half - 1, half // 2, -1):
+        make(k, [long_value], [arrived["long"]])
+    value = send("short", 1, long_value)
+    for k in range(2, half // 2 + 1):
+        make(k, [value], [arrived["short"]])
+    value = send("long", 2, value)
+    for step in range(2, half):
         value = send("short", step, value)
         value = send("long", step + 1, value)
 
@@ -318,8 +339,8 @@
     squares = jnp.sum(mixed * mixed, axis=1)[None]
 
     held = {0: scaled}
-    long_block, short_block = scaled, scaled
     scaled_peer = lax.ppermute(scaled, "tokens", swap)
+    long_block, short_block = scaled, hold(scaled, [scaled_peer])
     groups = {}
     for k in range(1, half):
         groups.setdefault(max(k, half - k), []).append(k)

time: 246 us -> 240 us (0.976)
  waiting for transfers between devices: 123 us -> 119 us
    ppermute x7, waiting for transfers between devices: 61.4 us -> 53.6 us  [send(): lax.ppermute(value, devices, long_way if way == 'long' else short_way)]
    ppermute x3, starting transfers between devices: 4.72 us -> 0.39 us  [on_ring(): long_block = lax.ppermute(long_block, devices, long_way)]
    ppermute x3, starting transfers between devices: 1.41 us -> 5.31 us  [on_ring(): short_block = lax.ppermute(short_block, devices, short_way)]
  transfers between devices with their start and end apart: 30 -> 30, of which waited for: 11 -> 17; matrix products, arithmetic and copies ran while one was open for 2% -> 2% of each run, Pallas kernels for 19% -> 20%
where the time goes in v6:
time: 240 us; the launch traced here: 239 us
  waiting for transfers between devices  119 us (50%)
  Pallas kernels  69.7 us (29%)
  starting transfers between devices  27.1 us (11%)
  between operations  10.9 us (5%)
  other arithmetic  8.07 us (3%)
  local copies, waits for them, and re-layouts  4.19 us (2%)
    ppermute x3, waiting for transfers between devices, on_ring(): more = lax.ppermute(squares, 'tensor', [(c, c ^ reach) for c in range(n)])  55.8 us
    ppermute x7, waiting for transfers between devices, send(): lax.ppermute(value, devices, long_way if way == 'long' else short_way)  53.6 us
    pallas_call x4, Pallas kernels, query_block(): pl.pallas_call(functools.partial(query_kernel, (len(chosen), len(far)), c...  31.9 us
    pallas_call x4, Pallas kernels, project(): pl.pallas_call(project_kernel, grid_spec=pltpu.PrefetchScalarGridSpec(num...  30.7 us
    ppermute x7, starting transfers between devices, send(): lax.ppermute(value, devices, long_way if way == 'long' else short_way)  10.6 us
    pallas_call x2, Pallas kernels, attention(): pl.pallas_call(functools.partial(attention_kernel, heads), grid_spec=pltp...  5.73 us
    ppermute x3, starting transfers between devices, on_ring(): short_block = lax.ppermute(short_block, devices, short_way)  5.31 us
  transfers between devices with their start and end apart: 30, of which 17 were waited for; matrix products, arithmetic and copies ran while one was open for 2% of the time, Pallas kernels for 20%

profile of v6, /device:TPU:0, one launch (start us, length us, event | category | flops | bytes accessed | tf_op | source)
XLA Modules:
  0.0 239.4 jit_solution(17211472171933576367)
XLA Ops:
  4.9 2.9 %attention.2.refs_0_ = bf16[256,1024]{1,0:T(8,128)(2,1)S(1)} custom-call(s32[1]{0:T(128)} %bitcast.2.core_ref, bf16[256,2048]{1,0:T(8,128)(2,1)S(1)} %copy-done, bf16[2,256,128]{2,1,0:T(8,128)(2,1)S(1)} %pad_maximum_fusion.own_ref, bf16[2,256,128]{2,1,0:T(8,128)(2,1)S(1)} %collective-permute-done.far_ref), custom_call_target="tpu_custom_call" | custom-call | flops 536870912 | bytes 1048576 | tf_op jit(solution)/shard_map/attention/pallas_call | solution.py:61
  7.8 2.9 %attention.3 = bf16[256,1024]{1,0:T(8,128)(2,1)S(1)} custom-call(s32[1]{0:T(128)} %bitcast.2.core_ref, bf16[256,2048]{1,0:T(8,128)(2,1)S(1)} %copy-done, bf16[2,256,128]{2,1,0:T(8,128)(2,1)S(1)} %pad_maximum_fusion.own_ref, bf16[2,256,128]{2,1,0:T(8,128)(2,1)S(1)} %collective-permute-done.far_ref, bf16[256,1024]{1,0:T(8,128)(2,1)S(1)} %attention.2.refs_0_), custom_call_target="tpu_custom_call" | custom-call | flops 536870912 | bytes 1048576 | tf_op jit(solution)/shard_map/attention/pallas_call | solution.py:61
  13.6 7.7 %project.4 = (bf16[256,2048]{1,0:T(8,128)(2,1)S(1)}, bf16[256,2048]{1,0:T(8,128)(2,1)S(1)}) custom-call(s32[16]{0:T(128)S(1)} %get-tuple-element.65.info_ref, bf16[512,2048]{1,0:T(8,128)(2,1)S(1)} %maximum_maximum_fusion.x_ref, bf16[2048,8192]{1,0:T(8,128)(2,1)} %w_ref.7), custom_call_target="tpu_custom_call" | custom-call | flops 4294967296 | bytes 8388608 | tf_op jit(solution)/shard_map/project/pallas_call | solution.py:92
  24.1 3.0 %collective-permute-start.5 = (bf16[256,2048]{1,0:T(8,128)(2,1)S(1)}, bf16[256,2048]{1,0:T(8,128)(2,1)S(1)}, u32[]{:S(2)}, u32[]{:S(2)}) collective-permute-start(bf16[256,2048]{1,0:T(8,128)(2,1)S(1)} %broadcast_select_fusion.refs_0_), channel_id=1, source_target_pairs={{0,4},{4,8},{8,12},{12,14},{14,10},{10,6},{6,2},{2,0},{5,1},{9,5},... | collective-permute-start | bytes 3145736 | tf_op jit(solution)/shard_map/ppermute | solution.py:320
  27.1 7.7 %project.5 = (bf16[256,2048]{1,0:T(8,128)(2,1)S(1)}, bf16[256,2048]{1,0:T(8,128)(2,1)S(1)}) custom-call(s32[16]{0:T(128)S(1)} %get-tuple-element.65.info_ref, bf16[512,2048]{1,0:T(8,128)(2,1)S(1)} %maximum_maximum_fusion.x_ref, bf16[2048,8192]{1,0:T(8,128)(2,1)} %w_ref.7), custom_call_target="tpu_custom_call" | custom-call | flops 4294967296 | bytes 8388608 | tf_op jit(solution)/shard_map/project/pallas_call | solution.py:92
  34.9 7.7 %project.6 = (bf16[256,2048]{1,0:T(8,128)(2,1)S(1)}, bf16[256,2048]{1,0:T(8,128)(2,1)S(1)}) custom-call(s32[16]{0:T(128)S(1)} %get-tuple-element.65.info_ref, bf16[512,2048]{1,0:T(8,128)(2,1)S(1)} %maximum_maximum_fusion.x_ref, bf16[2048,8192]{1,0:T(8,128)(2,1)} %w_ref.7, bf16[256,2048]{1,0:T(8,128)(2,1)S(1)} %broadcast_select_fusion.refs_0_), custom_call_target="tpu_custom_call" | custom-call | flops 4294967296 | bytes 8388608 | tf_op jit(solution)/shard_map/project/pallas_call | solution.py:92
  48.8 7.7 %project.7 = (bf16[256,2048]{1,0:T(8,128)(2,1)S(1)}, bf16[256,2048]{1,0:T(8,128)(2,1)S(1)}) custom-call(s32[16]{0:T(128)S(1)} %get-tuple-element.65.info_ref, bf16[512,2048]{1,0:T(8,128)(2,1)S(1)} %maximum_maximum_fusion.x_ref, bf16[2048,8192]{1,0:T(8,128)(2,1)} %w_ref.7, bf16[256,2048]{1,0:T(8,128)(2,1)S(1)} %select_select_fusion.refs_0_), custom_call_target="tpu_custom_call" | custom-call | flops 4294967296 | bytes 8388608 | tf_op jit(solution)/shard_map/project/pallas_call | solution.py:92
  56.5 4.0 %collective-permute-done.7.refs_1_ = bf16[256,2048]{1,0:T(8,128)(2,1)S(1)} collective-permute-done((bf16[256,2048]{1,0:T(8,128)(2,1)S(1)}, bf16[256,2048]{1,0:T(8,128)(2,1)S(1)}, u32[]{:S(2)}, u32[]{:S(2)}) %collective-permute-start.7) | collective-permute-done | bytes 1048608 | tf_op jit(solution)/shard_map/ppermute | solution.py:320
  65.6 20.1 %collective-permute-done.9 = bf16[256,2048]{1,0:T(8,128)(2,1)S(1)} collective-permute-done((bf16[256,2048]{1,0:T(8,128)(2,1)S(1)}, bf16[256,2048]{1,0:T(8,128)(2,1)S(1)}, u32[]{:S(2)}, u32[]{:S(2)}) %collective-permute-start.9) | collective-permute-done | bytes 1048608 | tf_op jit(solution)/shard_map/ppermute | solution.py:320
  86.3 2.0 collective-permute-start.10
  92.9 8.3 %collective-permute-done.10 = bf16[256,2048]{1,0:T(8,128)(2,1)S(1)} collective-permute-done((bf16[256,2048]{1,0:T(8,128)(2,1)S(1)}, bf16[256,2048]{1,0:T(8,128)(2,1)S(1)}, u32[]{:S(2)}, u32[]{:S(2)}) %collective-permute-start.10) | collective-permute-done | bytes 1048608 | tf_op jit(solution)/shard_map/ppermute | solution.py:320
  102.1 2.0 collective-permute-start.12
  104.9 21.2 %collective-permute-done.12 = bf16[256,2048]{1,0:T(8,128)(2,1)S(1)} collective-permute-done((bf16[256,2048]{1,0:T(8,128)(2,1)S(1)}, bf16[256,2048]{1,0:T(8,128)(2,1)S(1)}, u32[]{:S(2)}, u32[]{:S(2)}) %collective-permute-start.12) | collective-permute-done | bytes 1048608 | tf_op jit(solution)/shard_map/ppermute | solution.py:320
  128.7 2.2 collective-permute-done.20.refs_1_.refs_3_
  134.1 18.9 %collective-permute-done.14.more_ref = f32[1,256]{1,0:T(1,128)S(1)} collective-permute-done((f32[1,256]{1,0:T(1,128)S(1)}, f32[1,256]{1,0:T(1,128)S(1)}, u32[]{:S(2)}, u32[]{:S(2)}) %collective-permute-start.14) | collective-permute-done | bytes 1056 | tf_op jit(solution)/shard_map/ppermute | solution.py:353
  155.8 23.4 %collective-permute-done.16.more_ref = f32[1,256]{1,0:T(1,128)S(1)} collective-permute-done((f32[1,256]{1,0:T(1,128)S(1)}, f32[1,256]{1,0:T(1,128)S(1)}, u32[]{:S(2)}, u32[]{:S(2)}) %collective-permute-start.16) | collective-permute-done | bytes 1056 | tf_op jit(solution)/shard_map/ppermute | solution.py:353
  180.1 2.0 collective-permute-start.26
  183.4 7.9 %next_query.4 = (f32[256,2048]{1,0:T(8,128)S(1)}, f32[256,2048]{1,0:T(8,128)S(1)}) custom-call(s32[16]{0:T(128)S(1)} %get-tuple-element.65.info_ref, bf16[256,2048]{1,0:T(8,128)(2,1)S(1)} %collective-permute-done.22.refs_1_.refs_0_, bf16[256,2048]{1,0:T(8,128)(2,1)S(1)} %get-tuple-element.47.refs_0_.refs_1_, ...), custom_call_target="tpu_custom_call" | custom-call | flops 4294967296 | bytes 16777216 | tf_op jit(solution)/shard_map/next_query/pallas_call | solution.py:141
  191.3 13.5 %collective-permute-done.18.more_ref = f32[1,256]{1,0:T(1,128)S(1)} collective-permute-done((f32[1,256]{1,0:T(1,128)S(1)}, f32[1,256]{1,0:T(1,128)S(1)}, u32[]{:S(2)}, u32[]{:S(2)}) %collective-permute-start.18) | collective-permute-done | bytes 1056 | tf_op jit(solution)/shard_map/ppermute | solution.py:353
  206.9 3.2 %collective-permute-start.24 = (bf16[256,2048]{1,0:T(8,128)(2,1)S(1)}, bf16[256,2048]{1,0:T(8,128)(2,1)S(1)}, u32[]{:S(2)}, u32[]{:S(2)}) collective-permute-start(bf16[256,2048]{1,0:T(8,128)(2,1)S(1)} %get-tuple-element.49.refs_0_.refs_7_.refs_1_.refs_2_), channel_id=1, source_target_pairs={{0,5},{4,8},{8,12},{12,14},{14,10},{10,7},{6,3},{2,1},{16,21},{20,... | collective-permute-start | bytes 3145736 | tf_op jit(solution)/shard_map/ppermute | solution.py:371
  210.9 8.0 %next_query.5 = (f32[256,2048]{1,0:T(8,128)S(1)}, f32[256,2048]{1,0:T(8,128)S(1)}) custom-call(s32[16]{0:T(128)S(1)} %get-tuple-element.65.info_ref, bf16[256,2048]{1,0:T(8,128)(2,1)S(1)} %collective-permute-done.21.refs_1_.refs_6_.refs_0_.refs_3_, bf16[256,2048]{1,0:T(8,128)(2,1)S(1)} %get-tuple-element.49.refs_0_.refs_7_.refs_1_.refs_2_, ...), custom_call_target="tpu_custom_call" | custom-call | flops 4294967296 | bytes 16777216 | tf_op jit(solution)/shard_map/next_query/pallas_call | solution.py:141
  218.9 8.0 %next_query.6 = (f32[256,2048]{1,0:T(8,128)S(1)}, f32[256,2048]{1,0:T(8,128)S(1)}) custom-call(s32[16]{0:T(128)S(1)} %get-tuple-element.65.info_ref, bf16[256,2048]{1,0:T(8,128)(2,1)S(1)} %collective-permute-done.26.refs_2_.refs_5_.refs_3_.refs_0_, bf16[256,2048]{1,0:T(8,128)(2,1)S(1)} %get-tuple-element.45.refs_3_.refs_4_.refs_2_.refs_1_, ...), custom_call_target="tpu_custom_call" | custom-call | flops 4294967296 | bytes 16777216 | tf_op jit(solution)/shard_map/next_query/pallas_call | solution.py:141
  227.0 8.0 %next_query.7 = (f32[256,2048]{1,0:T(8,128)S(1)}, bf16[256,2048]{1,0:T(8,128)(2,1)S(1)}) custom-call(s32[16]{0:T(128)S(1)} %get-tuple-element.65.info_ref, bf16[256,2048]{1,0:T(8,128)(2,1)S(1)} %get-tuple-element.62.refs_0_, bf16[256,2048]{1,0:T(8,128)(2,1)S(1)} %collective-permute-done.24.refs_1_.refs_5_, ...), custom_call_target="tpu_custom_call" | custom-call | flops 4294967296 | bytes 16777216 | tf_op jit(solution)/shard_map/next_query/pallas_call | solution.py:141
  235.8 2.3 collective-permute-done.29
  (80 shorter events, 34.0 us)
Async XLA Ops:
  24.1 18.4 %collective-permute-start.5 = (bf16[256,2048]{1,0:T(8,128)(2,1)S(1)}, bf16[256,2048]{1,0:T(8,128)(2,1)S(1)}, u32[]{:S(2)}, u32[]{:S(2)}) collective-permute-start(bf16[256,2048]{1,0:T(8,128)(2,1)S(1)} %broadcast_select_fusion.refs_0_), channel_id=1, source_target_pairs={{0,4},{4,8},{8,12},{12,14},{14,10},{10,6},{6,2},{2,0},{5,1},{9,5},... | collective-permute-start | bytes 3145736 | tf_op jit(solution)/shard_map/ppermute | solution.py:320
  34.8 10.3 %collective-permute-start.4 = (bf16[256,2048]{1,0:T(8,128)(2,1)S(1)}, bf16[256,2048]{1,0:T(8,128)(2,1)S(1)}, u32[]{:S(2)}, u32[]{:S(2)}) collective-permute-start(bf16[256,2048]{1,0:T(8,128)(2,1)S(1)} %get-tuple-element.34), channel_id=1, source_target_pairs={{0,1},{1,0},{2,3},{3,2},{4,5},{5,4},{6,7},{7,6},{8,9},{9,8},{10,11... | collective-permute-start | bytes 3145736 | tf_op jit(solution)/shard_map/ppermute | solution.py:307
  45.6 14.9 %collective-permute-start.7 = (bf16[256,2048]{1,0:T(8,128)(2,1)S(1)}, bf16[256,2048]{1,0:T(8,128)(2,1)S(1)}, u32[]{:S(2)}, u32[]{:S(2)}) collective-permute-start(bf16[256,2048]{1,0:T(8,128)(2,1)S(1)} %select_select_fusion.refs_0_), channel_id=1, source_target_pairs={{4,0},{8,4},{12,8},{14,12},{10,14},{6,10},{2,6},{0,2},{1,5},{5,9},... | collective-permute-start | bytes 3145736 | tf_op jit(solution)/shard_map/ppermute | solution.py:320
  60.5 3.3 %collective-permute-start.8 = (bf16[256,2048]{1,0:T(8,128)(2,1)S(1)}, bf16[256,2048]{1,0:T(8,128)(2,1)S(1)}, u32[]{:S(2)}, u32[]{:S(2)}) collective-permute-start(bf16[256,2048]{1,0:T(8,128)(2,1)S(1)} %hold.4), channel_id=1, source_target_pairs={{0,1},{1,0},{2,3},{3,2},{4,5},{5,4},{6,7},{7,6},{8,9},{9,8},{10,11... | collective-permute-start | bytes 3145736 | tf_op jit(solution)/shard_map/ppermute | solution.py:307
  61.5 24.2 %collective-permute-start.9 = (bf16[256,2048]{1,0:T(8,128)(2,1)S(1)}, bf16[256,2048]{1,0:T(8,128)(2,1)S(1)}, u32[]{:S(2)}, u32[]{:S(2)}) collective-permute-start(bf16[256,2048]{1,0:T(8,128)(2,1)S(1)} %add_convert_fusion.4), channel_id=1, source_target_pairs={{0,4},{4,8},{8,12},{12,14},{14,10},{10,6},{6,2},{2,0},{5,1},{9,5},... | collective-permute-start | bytes 3145736 | tf_op jit(solution)/shard_map/ppermute | solution.py:320
  64.4 27.5 %collective-permute-start.11 = (bf16[256,2048]{1,0:T(8,128)(2,1)S(1)}, bf16[256,2048]{1,0:T(8,128)(2,1)S(1)}, u32[]{:S(2)}, u32[]{:S(2)}) collective-permute-start(bf16[256,2048]{1,0:T(8,128)(2,1)S(1)} %add_convert_fusion.3), channel_id=1, source_target_pairs={{4,0},{8,4},{12,8},{14,12},{10,14},{6,10},{2,6},{0,2},{1,5},{5,9},... | collective-permute-start | bytes 3145736 | tf_op jit(solution)/shard_map/ppermute | solution.py:320
  86.3 14.9 %collective-permute-start.10 = (bf16[256,2048]{1,0:T(8,128)(2,1)S(1)}, bf16[256,2048]{1,0:T(8,128)(2,1)S(1)}, u32[]{:S(2)}, u32[]{:S(2)}) collective-permute-start(bf16[256,2048]{1,0:T(8,128)(2,1)S(1)} %add_convert_fusion.2), channel_id=1, source_target_pairs={{0,4},{4,8},{8,12},{12,14},{14,10},{10,6},{6,2},{2,0},{5,1},{9,5},... | collective-permute-start | bytes 3145736 | tf_op jit(solution)/shard_map/ppermute | solution.py:320
  102.1 23.9 %collective-permute-start.12 = (bf16[256,2048]{1,0:T(8,128)(2,1)S(1)}, bf16[256,2048]{1,0:T(8,128)(2,1)S(1)}, u32[]{:S(2)}, u32[]{:S(2)}) collective-permute-start(bf16[256,2048]{1,0:T(8,128)(2,1)S(1)} %add_convert_fusion), channel_id=1, source_target_pairs={{0,4},{4,8},{8,12},{12,14},{14,10},{10,6},{6,2},{2,0},{5,1},{9,5},... | collective-permute-start | bytes 3145736 | tf_op jit(solution)/shard_map/ppermute | solution.py:320
  104.1 21.9 %collective-permute-start.13 = (bf16[256,2048]{1,0:T(8,128)(2,1)S(1)}, bf16[256,2048]{1,0:T(8,128)(2,1)S(1)}, u32[]{:S(2)}, u32[]{:S(2)}) collective-permute-start(bf16[256,2048]{1,0:T(8,128)(2,1)S(1)} %add_convert_fusion.1), channel_id=1, source_target_pairs={{4,0},{8,4},{12,8},{14,12},{10,14},{6,10},{2,6},{0,2},{1,5},{5,9},... | collective-permute-start | bytes 3145736 | tf_op jit(solution)/shard_map/ppermute | solution.py:320
  128.2 24.7 %collective-permute-start.15 = (bf16[256,2048]{1,0:T(8,128)(2,1)S(1)}, bf16[256,2048]{1,0:T(8,128)(2,1)S(1)}, u32[]{:S(2)}, u32[]{:S(2)}) collective-permute-start(bf16[256,2048]{1,0:T(8,128)(2,1)S(1)} %get-tuple-element.62.refs_0_), channel_id=1, source_target_pairs={{0,4},{4,8},{8,12},{12,14},{14,10},{10,6},{6,2},{2,0},{5,1},{9,5},... | collective-permute-start | bytes 3145736 | tf_op jit(solution)/shard_map/ppermute | solution.py:350
  130.9 22.9 %collective-permute-start.21 = (bf16[256,2048]{1,0:T(8,128)(2,1)S(1)}, bf16[256,2048]{1,0:T(8,128)(2,1)S(1)}, u32[]{:S(2)}, u32[]{:S(2)}) collective-permute-start(bf16[256,2048]{1,0:T(8,128)(2,1)S(1)} %hold.5), channel_id=1, source_target_pairs={{4,0},{8,4},{12,8},{14,12},{10,14},{6,10},{2,6},{0,2},{1,5},{5,9},... | collective-permute-start | bytes 3145736 | tf_op jit(solution)/shard_map/ppermute | solution.py:351
  132.5 20.5 %collective-permute-start.14 = (f32[1,256]{1,0:T(1,128)S(1)}, f32[1,256]{1,0:T(1,128)S(1)}, u32[]{:S(2)}, u32[]{:S(2)}) collective-permute-start(f32[1,256]{1,0:T(1,128)S(1)} %bitcast.27), channel_id=1, source_target_pairs={{0,2},{2,0},{4,6},{6,4},{8,10},{10,8},{12,14},{14,12},{1,3},{3,1},... | collective-permute-start | bytes 3080 | tf_op jit(solution)/shard_map/ppermute | solution.py:353
  153.0 26.3 %collective-permute-start.17 = (bf16[256,2048]{1,0:T(8,128)(2,1)S(1)}, bf16[256,2048]{1,0:T(8,128)(2,1)S(1)}, u32[]{:S(2)}, u32[]{:S(2)}) collective-permute-start(bf16[256,2048]{1,0:T(8,128)(2,1)S(1)} %get-tuple-element.45.refs_3_.refs_4_.refs_2_.refs_1_), channel_id=1, source_target_pairs={{0,4},{4,8},{8,12},{12,14},{14,10},{10,6},{6,2},{2,0},{5,1},{9,5},... | collective-permute-start | bytes 3145736 | tf_op jit(solution)/shard_map/ppermute | solution.py:350
  153.8 25.5 %collective-permute-start.22 = (bf16[256,2048]{1,0:T(8,128)(2,1)S(1)}, bf16[256,2048]{1,0:T(8,128)(2,1)S(1)}, u32[]{:S(2)}, u32[]{:S(2)}) collective-permute-start(bf16[256,2048]{1,0:T(8,128)(2,1)S(1)} %collective-permute-done.21.refs_1_.refs_6_.refs_0_.refs_3_), channel_id=1, source_target_pairs={{4,0},{8,4},{12,8},{14,12},{10,14},{6,10},{2,6},{0,2},{1,5},{5,9},... | collective-permute-start | bytes 3145736 | tf_op jit(solution)/shard_map/ppermute | solution.py:351
  155.5 23.8 %collective-permute-start.16 = (f32[1,256]{1,0:T(1,128)S(1)}, f32[1,256]{1,0:T(1,128)S(1)}, u32[]{:S(2)}, u32[]{:S(2)}) collective-permute-start(f32[1,256]{1,0:T(1,128)S(1)} %get-tuple-element.44.total_ref), channel_id=1, source_target_pairs={{0,4},{2,6},{4,0},{6,2},{8,12},{10,14},{12,8},{14,10},{1,5},{3,7},... | collective-permute-start | bytes 3080 | tf_op jit(solution)/shard_map/ppermute | solution.py:353
  179.9 3.5 %collective-permute-start.23 = (bf16[256,2048]{1,0:T(8,128)(2,1)S(1)}, bf16[256,2048]{1,0:T(8,128)(2,1)S(1)}, u32[]{:S(2)}, u32[]{:S(2)}) collective-permute-start(bf16[256,2048]{1,0:T(8,128)(2,1)S(1)} %pick.2), channel_id=1, source_target_pairs={{0,1},{1,0},{2,3},{3,2},{4,5},{5,4},{6,7},{7,6},{8,9},{9,8},{10,11... | collective-permute-start | bytes 3145736 | tf_op jit(solution)/shard_map/ppermute | solution.py:362
  180.0 25.4 %collective-permute-start.19 = (bf16[256,2048]{1,0:T(8,128)(2,1)S(1)}, bf16[256,2048]{1,0:T(8,128)(2,1)S(1)}, u32[]{:S(2)}, u32[]{:S(2)}) collective-permute-start(bf16[256,2048]{1,0:T(8,128)(2,1)S(1)} %get-tuple-element.47.refs_0_.refs_1_), channel_id=1, source_target_pairs={{0,4},{4,8},{8,12},{12,14},{14,10},{10,6},{6,2},{2,0},{5,1},{9,5},... | collective-permute-start | bytes 3145736 | tf_op jit(solution)/shard_map/ppermute | solution.py:350
  180.1 25.5 %collective-permute-start.26 = (bf16[256,2048]{1,0:T(8,128)(2,1)S(1)}, bf16[256,2048]{1,0:T(8,128)(2,1)S(1)}, u32[]{:S(2)}, u32[]{:S(2)}) collective-permute-start(bf16[256,2048]{1,0:T(8,128)(2,1)S(1)} %collective-permute-done.22.refs_1_.refs_0_), channel_id=1, source_target_pairs={{4,0},{8,4},{12,8},{14,12},{10,14},{6,10},{2,6},{0,2},{1,5},{5,9},... | collective-permute-start | bytes 3145736 | tf_op jit(solution)/shard_map/ppermute | solution.py:351
  182.1 22.7 %collective-permute-start.18 = (f32[1,256]{1,0:T(1,128)S(1)}, f32[1,256]{1,0:T(1,128)S(1)}, u32[]{:S(2)}, u32[]{:S(2)}) collective-permute-start(f32[1,256]{1,0:T(1,128)S(1)} %get-tuple-element.46.total_ref), channel_id=1, source_target_pairs={{0,8},{2,10},{4,12},{6,14},{8,0},{10,2},{12,4},{14,6},{1,9},{3,11}... | collective-permute-start | bytes 3080 | tf_op jit(solution)/shard_map/ppermute | solution.py:353
  206.3 4.5 %collective-permute-start.28 = (bf16[256,2048]{1,0:T(8,128)(2,1)S(1)}, bf16[256,2048]{1,0:T(8,128)(2,1)S(1)}, u32[]{:S(2)}, u32[]{:S(2)}) collective-permute-start(bf16[256,2048]{1,0:T(8,128)(2,1)S(1)} %get-tuple-element.51), channel_id=1, source_target_pairs={{0,1},{1,0},{2,3},{3,2},{4,5},{5,4},{6,7},{7,6},{8,9},{9,8},{10,11... | collective-permute-start | bytes 3145736 | tf_op jit(solution)/shard_map/ppermute | solution.py:362
  206.7 12.2 %collective-permute-start.27 = (bf16[256,2048]{1,0:T(8,128)(2,1)S(1)}, bf16[256,2048]{1,0:T(8,128)(2,1)S(1)}, u32[]{:S(2)}, u32[]{:S(2)}) collective-permute-start(bf16[256,2048]{1,0:T(8,128)(2,1)S(1)} %get-tuple-element.50), channel_id=1, source_target_pairs={{0,1},{1,0},{2,3},{3,2},{4,5},{5,4},{6,7},{7,6},{8,9},{9,8},{10,11... | collective-permute-start | bytes 3145736 | tf_op jit(solution)/shard_map/ppermute | solution.py:362
  206.9 20.0 %collective-permute-start.24 = (bf16[256,2048]{1,0:T(8,128)(2,1)S(1)}, bf16[256,2048]{1,0:T(8,128)(2,1)S(1)}, u32[]{:S(2)}, u32[]{:S(2)}) collective-permute-start(bf16[256,2048]{1,0:T(8,128)(2,1)S(1)} %get-tuple-element.49.refs_0_.refs_7_.refs_1_.refs_2_), channel_id=1, source_target_pairs={{0,5},{4,8},{8,12},{12,14},{14,10},{10,7},{6,3},{2,1},{16,21},{20,... | collective-permute-start | bytes 3145736 | tf_op jit(solution)/shard_map/ppermute | solution.py:371
  210.1 16.8 %collective-permute-start.25 = (bf16[256,2048]{1,0:T(8,128)(2,1)S(1)}, bf16[256,2048]{1,0:T(8,128)(2,1)S(1)}, u32[]{:S(2)}, u32[]{:S(2)}) collective-permute-start(bf16[256,2048]{1,0:T(8,128)(2,1)S(1)} %get-tuple-element.49.refs_0_.refs_7_.refs_1_.refs_2_), channel_id=1, source_target_pairs={{5,1},{9,5},{13,8},{15,12},{11,14},{7,10},{3,7},{1,3},{21,17},{25,... | collective-permute-start | bytes 3145736 | tf_op jit(solution)/shard_map/ppermute | solution.py:372
  235.0 3.1 %collective-permute-start.29 = (bf16[256,2048]{1,0:T(8,128)(2,1)S(1)}, bf16[256,2048]{1,0:T(8,128)(2,1)S(1)}, u32[]{:S(2)}, u32[]{:S(2)}) collective-permute-start(bf16[256,2048]{1,0:T(8,128)(2,1)S(1)} %get-tuple-element.58), channel_id=1, source_target_pairs={{0,1},{1,0},{2,3},{3,2},{4,5},{5,4},{6,7},{7,6},{8,9},{9,8},{10,11... | collective-permute-start | bytes 3145736 | tf_op jit(solution)/shard_map/ppermute | solution.py:377
  (9 other events, 43.9 us)

commit v7 on v6

--- a/solution.py
+++ b/solution.py
@@ -17,6 +17,7 @@
 BF16 = jnp.bfloat16
 F32 = jnp.float32
 RING_LIMIT = 16
+EXTRA = 8
 MIB = 1024 * 1024
 
 
@@ -123,7 +124,7 @@
 
                 @pl.when(info_ref[code] == choice if len(blocks) > 1 else True)
                 def _():
-                    x_ref[place] = block[...]
+                    x_ref[place] = block[:rows]
 
     for part, (place, out) in enumerate(((slice(0, rows), own_ref), (slice(rows, 2 * rows), peer_ref))):
         result = dot(x_ref[place], w_ref[...])
@@ -132,8 +133,8 @@
         out[...] = result.astype(out.dtype)
 
 
-def query_block(info, pair, code, chosen, far, weight, acc, last):
-    rows, depth = far[0].shape
+def query_block(info, pair, code, chosen, far, weight, acc, rows, last):
+    depth = far[0].shape[1]
     width = weight.shape[1]
     tile = min(512, width)
     whole = pl.BlockSpec(memory_space=pltpu.VMEM)
@@ -161,24 +162,6 @@
     )(info, *chosen, *far, weight, *acc)
 
 
-def add_kernel(total_ref, more_ref, *refs):
-    refs[-1][...] = total_ref[...] + more_ref[...]
-
-
-def add_in_step(total, more, blocks, after):
-    whole = pl.BlockSpec(memory_space=pltpu.VMEM)
-    *blocks, total = pl.pallas_call(
-        add_kernel,
-        in_specs=[whole] * (2 + len(blocks) + len(after)),
-        out_specs=[whole] * (len(blocks) + 1),
-        out_shape=[jax.ShapeDtypeStruct(block.shape, block.dtype) for block in (*blocks, total)],
-        input_output_aliases={2 + index: index for index in range(len(blocks))},
-        compiler_params=pltpu.CompilerParams(vmem_limit_bytes=4 * MIB),
-        name="add_squares",
-    )(total, more, *blocks, *after)
-    return total, blocks
-
-
 def hold_kernel(*refs):
     pass
 
@@ -204,14 +187,14 @@
 
             @pl.when(info_ref[code] == choice)
             def _():
-                out[...] = refs[start + choice][...]
+                out[...] = refs[start + choice][: out.shape[0]]
 
         start += size
 
 
-def pick(info, codes, groups, after):
+def pick(info, codes, groups, rows, after):
     whole = pl.BlockSpec(memory_space=pltpu.VMEM)
-    first = groups[0][0]
+    shape = jax.ShapeDtypeStruct((rows, groups[0][0].shape[1]), groups[0][0].dtype)
     return pl.pallas_call(
         functools.partial(pick_kernel, codes, [len(group) for group in groups]),
         grid_spec=pltpu.PrefetchScalarGridSpec(
@@ -220,7 +203,7 @@
             in_specs=[whole] * (sum(len(group) for group in groups) + len(after)),
             out_specs=[whole] * len(groups),
         ),
-        out_shape=[jax.ShapeDtypeStruct(first.shape, first.dtype)] * len(groups),
+        out_shape=[shape] * len(groups),
         compiler_params=pltpu.CompilerParams(vmem_limit_bytes=4 * MIB),
         name="pick",
     )(info, *[block for group in groups for block in group], *after)
@@ -325,10 +308,10 @@
     long_value = send("long", 1, None)
     for k in range(half - 1, half // 2, -1):
         make(k, [long_value], [arrived["long"]])
-    value = send("short", 1, long_value)
+    short_value = send("short", 1, long_value)
+    value = send("long", 2, short_value)
     for k in range(2, half // 2 + 1):
-        make(k, [value], [arrived["short"]])
-    value = send("long", 2, value)
+        make(k, [short_value, value], [arrived["short"], arrived["long"]])
     for step in range(2, half):
         value = send("short", step, value)
         value = send("long", step + 1, value)
@@ -336,46 +319,54 @@
     mixed = residual.astype(F32) + partial_sum(0) + arrived["long"].astype(F32) + arrived["short"].astype(F32)
     resid_out = mixed.astype(BF16)
     scaled = (mixed * norm_gain.astype(F32)).astype(BF16)
-    squares = jnp.sum(mixed * mixed, axis=1)[None]
-
-    held = {0: scaled}
-    scaled_peer = lax.ppermute(scaled, "tokens", swap)
-    long_block, short_block = scaled, hold(scaled, [scaled_peer])
+    squares = jnp.sum(mixed * mixed, axis=1)
+    high = lax.reduce_precision(squares, 8, 7)
+    middle = lax.reduce_precision(squares - high, 8, 7)
+    digits = jnp.stack([high, middle, squares - high - middle]).astype(BF16)
+    digits = jnp.pad(digits, ((0, EXTRA - 3), (0, scaled.shape[1] - rows)))
+    message = jnp.concatenate([scaled, digits], axis=0)
+
+    def squares_in(block):
+        return block[rows : rows + 3, :rows].astype(F32)
+
+    held = {0: message}
+    message_peer = lax.ppermute(message, "tokens", swap)
+    long_block, short_block = message, hold(message, [message_peer])
     groups = {}
     for k in range(1, half):
         groups.setdefault(max(k, half - k), []).append(k)
-    reach = 1
     acc, after = (), ()
     for step in range(1, half):
         long_block = lax.ppermute(long_block, devices, long_way)
         short_block = lax.ppermute(short_block, devices, short_way)
-        if reach < n:
-            more = lax.ppermute(squares, "tensor", [(c, c ^ reach) for c in range(n)])
-            squares, (long_block,) = add_in_step(squares, more, [long_block], after)
-            reach *= 2
+        if after:
+            long_block = hold(long_block, after)
         held[-step], held[step] = long_block, short_block
         pairs = groups.get(step, [])
         if pairs:
             wanted = {k: [held[q] for q in block_choices(k, half)] for k in pairs}
             others = [[wanted[k][index ^ 1] for index in range(len(wanted[k]))] for k in pairs]
-            outgoing = pick(info, [half + k for k in pairs], others, after)
+            outgoing = pick(info, [half + k for k in pairs], others, rows, after)
             far = [lax.ppermute(block, "tokens", swap) for block in outgoing]
             for k, block in zip(pairs, far):
-                acc = query_block(info, k, half + k, wanted[k], [block], next_weight, acc, False)
+                acc = query_block(info, k, half + k, wanted[k], [block], next_weight, acc, rows, False)
             after = acc[:1]
-    while reach < n:
-        squares = squares + lax.ppermute(squares, "tensor", [(c, c ^ reach) for c in range(n)])
-        reach *= 2
     meets = {b: ring[(p + half) % n] // half for p, b in enumerate(ring)}
     last_hop = [
         lax.ppermute(held[1 - half], devices, [(2 * a, 2 * b + meets[b]) for a, b in up]),
         lax.ppermute(held[1 - half], devices, [(2 * b + 1, 2 * a + meets[a]) for a, b in up]),
     ]
     acc = query_block(
-        info, 0, half, [scaled, *last_hop], [scaled_peer, *reversed(last_hop)], next_weight, acc, True
+        info, 0, half, [message, *last_hop], [message_peer, *reversed(last_hop)], next_weight, acc, rows, True
     )
     query_sum = acc[0] + lax.ppermute(acc[1], "tokens", swap).astype(F32)
-    factor = 1.0 / jnp.sqrt(squares[0] / D + EPS_NORM)
+    last = [squares_in(block) for block in last_hop]
+    digits = lax.ppermute(jnp.where(core == 0, last[1], last[0]), "tokens", swap)
+    digits = digits + jnp.where(core == 0, last[0], last[1])
+    for step in range(1, half):
+        digits = digits + squares_in(held[step]) + squares_in(held[-step])
+    squares = squares + jnp.sum(digits, axis=0)
+    factor = 1.0 / jnp.sqrt(squares / D + EPS_NORM)
     return (resid_out, (query_sum * factor[:, None]).astype(BF16))
 
 

time: 240 us -> 251 us (1.046)
  waiting for transfers between devices: 119 us -> 127 us
  other arithmetic: 8.07 us -> 11.3 us
    ppermute x3, waiting for transfers between devices: 0.66 us -> 60.8 us  [on_ring(): long_block = lax.ppermute(long_block, devices, long_way)]
    ppermute x4 -> x2, waiting for transfers between devices: 58.1 us -> 3.13 us  [the longest x1 1.66 us: on_ring(): message_peer = lax.ppermute(message, 'tokens', swap)]
    ppermute x7, waiting for transfers between devices: 53.6 us -> 57 us  [send(): lax.ppermute(value, devices, long_way if way == 'long' else short_way)]
    ppermute x4 -> x2, starting transfers between devices: 3.18 us -> 0.58 us  [the longest x1 0.51 us: on_ring(): lax.ppermute(jnp.where(core == 0, last[1], last[0]), 'tokens', swap)]
  transfers between devices with their start and end apart: 30 -> 28, of which waited for: 17 -> 15; matrix products, arithmetic and copies ran while one was open for 2% -> 2% of each run, Pallas kernels for 20% -> 19%
where the time goes in v7:
time: 251 us; the launch traced here: 250 us
  waiting for transfers between devices  127 us (51%)
  Pallas kernels  70.5 us (28%)
  starting transfers between devices  24.9 us (10%)
  other arithmetic  11.3 us (5%)
  between operations  10.9 us (4%)
  local copies, waits for them, and re-layouts  5.57 us (2%)
    ppermute x3, waiting for transfers between devices, on_ring(): long_block = lax.ppermute(long_block, devices, long_way)  60.8 us
    ppermute x7, waiting for transfers between devices, send(): lax.ppermute(value, devices, long_way if way == 'long' else short_way)  57 us
    pallas_call x4, Pallas kernels, query_block(): pl.pallas_call(functools.partial(query_kernel, (len(chosen), len(far)), c...  32.8 us
    pallas_call x4, Pallas kernels, project(): pl.pallas_call(project_kernel, grid_spec=pltpu.PrefetchScalarGridSpec(num...  30.6 us
    ppermute x7, starting transfers between devices, send(): lax.ppermute(value, devices, long_way if way == 'long' else short_way)  9.27 us
    pallas_call x2, Pallas kernels, attention(): pl.pallas_call(functools.partial(attention_kernel, heads), grid_spec=pltp...  5.73 us
  transfers between devices with their start and end apart: 28, of which 15 were waited for; matrix products, arithmetic and copies ran while one was open for 2% of the time, Pallas kernels for 19%

profile of v7, /device:TPU:0, one launch (start us, length us, event | category | flops | bytes accessed | tf_op | source)
XLA Modules:
  0.0 250.3 jit_solution(6982444902295471488)
XLA Ops:
  4.9 2.9 %attention.2.refs_0_ = bf16[256,1024]{1,0:T(8,128)(2,1)S(1)} custom-call(s32[1]{0:T(128)} %bitcast.2.core_ref, bf16[256,2048]{1,0:T(8,128)(2,1)S(1)} %copy-done.6, bf16[2,256,128]{2,1,0:T(8,128)(2,1)S(1)} %pad_maximum_fusion.1.own_ref, bf16[2,256,128]{2,1,0:T(8,128)(2,1)S(1)} %collective-permute-done.far_ref), custom_call_target="tpu_custom_call" | custom-call | flops 536870912 | bytes 1048576 | tf_op jit(solution)/shard_map/attention/pallas_call | solution.py:62
  7.8 2.9 %attention.3 = bf16[256,1024]{1,0:T(8,128)(2,1)S(1)} custom-call(s32[1]{0:T(128)} %bitcast.2.core_ref, bf16[256,2048]{1,0:T(8,128)(2,1)S(1)} %copy-done.6, bf16[2,256,128]{2,1,0:T(8,128)(2,1)S(1)} %pad_maximum_fusion.1.own_ref, bf16[2,256,128]{2,1,0:T(8,128)(2,1)S(1)} %collective-permute-done.far_ref, bf16[256,1024]{1,0:T(8,128)(2,1)S(1)} %attention.2.refs_0_), custom_call_target="tpu_custom_call" | custom-call | flops 536870912 | bytes 1048576 | tf_op jit(solution)/shard_map/attention/pallas_call | solution.py:62
  13.6 7.7 %project.4 = (bf16[256,2048]{1,0:T(8,128)(2,1)S(1)}, bf16[256,2048]{1,0:T(8,128)(2,1)S(1)}) custom-call(s32[16]{0:T(128)S(1)} %get-tuple-element.53.info_ref, bf16[512,2048]{1,0:T(8,128)(2,1)S(1)} %maximum_maximum_fusion.x_ref, bf16[2048,8192]{1,0:T(8,128)(2,1)} %w_ref.7), custom_call_target="tpu_custom_call" | custom-call | flops 4294967296 | bytes 8388608 | tf_op jit(solution)/shard_map/project/pallas_call | solution.py:93
  24.1 3.0 %collective-permute-start.5 = (bf16[256,2048]{1,0:T(8,128)(2,1)S(1)}, bf16[256,2048]{1,0:T(8,128)(2,1)S(1)}, u32[]{:S(2)}, u32[]{:S(2)}) collective-permute-start(bf16[256,2048]{1,0:T(8,128)(2,1)S(1)} %broadcast_select_fusion.refs_0_), channel_id=1, source_target_pairs={{0,4},{4,8},{8,12},{12,14},{14,10},{10,6},{6,2},{2,0},{5,1},{9,5},... | collective-permute-start | bytes 3145736 | tf_op jit(solution)/shard_map/ppermute | solution.py:303
  27.1 7.7 %project.5 = (bf16[256,2048]{1,0:T(8,128)(2,1)S(1)}, bf16[256,2048]{1,0:T(8,128)(2,1)S(1)}) custom-call(s32[16]{0:T(128)S(1)} %get-tuple-element.53.info_ref, bf16[512,2048]{1,0:T(8,128)(2,1)S(1)} %maximum_maximum_fusion.x_ref, bf16[2048,8192]{1,0:T(8,128)(2,1)} %w_ref.7), custom_call_target="tpu_custom_call" | custom-call | flops 4294967296 | bytes 8388608 | tf_op jit(solution)/shard_map/project/pallas_call | solution.py:93
  34.8 7.7 %project.6 = (bf16[256,2048]{1,0:T(8,128)(2,1)S(1)}, bf16[256,2048]{1,0:T(8,128)(2,1)S(1)}) custom-call(s32[16]{0:T(128)S(1)} %get-tuple-element.53.info_ref, bf16[512,2048]{1,0:T(8,128)(2,1)S(1)} %maximum_maximum_fusion.x_ref, bf16[2048,8192]{1,0:T(8,128)(2,1)} %w_ref.7, bf16[256,2048]{1,0:T(8,128)(2,1)S(1)} %broadcast_select_fusion.refs_0_), custom_call_target="tpu_custom_call" | custom-call | flops 4294967296 | bytes 8388608 | tf_op jit(solution)/shard_map/project/pallas_call | solution.py:93
  48.1 1.6 collective-permute-start.8
  50.2 7.7 %project.7 = (bf16[256,2048]{1,0:T(8,128)(2,1)S(1)}, bf16[256,2048]{1,0:T(8,128)(2,1)S(1)}) custom-call(s32[16]{0:T(128)S(1)} %get-tuple-element.53.info_ref, bf16[512,2048]{1,0:T(8,128)(2,1)S(1)} %maximum_maximum_fusion.x_ref, bf16[2048,8192]{1,0:T(8,128)(2,1)} %w_ref.7, bf16[256,2048]{1,0:T(8,128)(2,1)S(1)} %select_select_fusion.refs_0_, ...), custom_call_target="tpu_custom_call" | custom-call | flops 4294967296 | bytes 8388608 | tf_op jit(solution)/shard_map/project/pallas_call | solution.py:93
  57.8 16.2 %collective-permute-done.8.refs_2_ = bf16[256,2048]{1,0:T(8,128)(2,1)S(1)} collective-permute-done((bf16[256,2048]{1,0:T(8,128)(2,1)S(1)}, bf16[256,2048]{1,0:T(8,128)(2,1)S(1)}, u32[]{:S(2)}, u32[]{:S(2)}) %collective-permute-start.8) | collective-permute-done | bytes 1048608 | tf_op jit(solution)/shard_map/ppermute | solution.py:303
  74.8 1.9 collective-permute-done.9
  78.9 1.6 collective-permute-start.10
  84.0 18.4 %collective-permute-done.11 = bf16[256,2048]{1,0:T(8,128)(2,1)S(1)} collective-permute-done((bf16[256,2048]{1,0:T(8,128)(2,1)S(1)}, bf16[256,2048]{1,0:T(8,128)(2,1)S(1)}, u32[]{:S(2)}, u32[]{:S(2)}) %collective-permute-start.11) | collective-permute-done | bytes 1048608 | tf_op jit(solution)/shard_map/ppermute | solution.py:303
  104.5 1.9 collective-permute-start.13
  107.0 22.4 %collective-permute-done.12 = bf16[256,2048]{1,0:T(8,128)(2,1)S(1)} collective-permute-done((bf16[256,2048]{1,0:T(8,128)(2,1)S(1)}, bf16[256,2048]{1,0:T(8,128)(2,1)S(1)}, u32[]{:S(2)}, u32[]{:S(2)}) %collective-permute-start.12) | collective-permute-done | bytes 1048608 | tf_op jit(solution)/shard_map/ppermute | solution.py:303
  132.9 1.7 collective-permute-done.17.refs_1_.refs_3_
  135.6 21.5 %collective-permute-done.14.refs_3_.refs_4_.refs_2_.refs_1_ = bf16[264,2048]{1,0:T(8,128)(2,1)S(1)} collective-permute-done((bf16[264,2048]{1,0:T(8,128)(2,1)S(1)}, bf16[264,2048]{1,0:T(8,128)(2,1)S(1)}, u32[]{:S(2)}, u32[]{:S(2)}) %collective-permute-start.14) | collective-permute-done | bytes 1081376 | tf_op jit(solution)/shard_map/ppermute | solution.py:340
  159.6 23.5 %collective-permute-done.15.refs_0_.refs_1_ = bf16[264,2048]{1,0:T(8,128)(2,1)S(1)} collective-permute-done((bf16[264,2048]{1,0:T(8,128)(2,1)S(1)}, bf16[264,2048]{1,0:T(8,128)(2,1)S(1)}, u32[]{:S(2)}, u32[]{:S(2)}) %collective-permute-start.15) | collective-permute-done | bytes 1081376 | tf_op jit(solution)/shard_map/ppermute | solution.py:340
  186.6 7.9 %next_query.4 = (f32[256,2048]{1,0:T(8,128)S(1)}, f32[256,2048]{1,0:T(8,128)S(1)}) custom-call(s32[16]{0:T(128)S(1)} %get-tuple-element.53.info_ref, bf16[264,2048]{1,0:T(8,128)(2,1)S(1)} %collective-permute-done.19.refs_1_.refs_0_, bf16[264,2048]{1,0:T(8,128)(2,1)S(1)} %collective-permute-done.15.refs_0_.refs_1_, ...), custom_call_target="tpu_custom_call" | custom-call | flops 4294967296 | bytes 16777216 | tf_op jit(solution)/shard_map/next_query/pallas_call | solution.py:142
  194.5 15.8 %collective-permute-done.16.refs_0_ = bf16[264,2048]{1,0:T(8,128)(2,1)S(1)} collective-permute-done((bf16[264,2048]{1,0:T(8,128)(2,1)S(1)}, bf16[264,2048]{1,0:T(8,128)(2,1)S(1)}, u32[]{:S(2)}, u32[]{:S(2)}) %collective-permute-start.16) | collective-permute-done | bytes 1081376 | tf_op jit(solution)/shard_map/ppermute | solution.py:340
  212.5 4.9 %collective-permute-start.21 = (bf16[264,2048]{1,0:T(8,128)(2,1)S(1)}, bf16[264,2048]{1,0:T(8,128)(2,1)S(1)}, u32[]{:S(2)}, u32[]{:S(2)}) collective-permute-start(bf16[264,2048]{1,0:T(8,128)(2,1)S(1)} %hold.7.refs_0_.refs_7_.refs_1_.refs_2_), channel_id=1, source_target_pairs={{0,5},{4,8},{8,12},{12,14},{14,10},{10,7},{6,3},{2,1},{16,21},{20,... | collective-permute-start | bytes 3244040 | tf_op jit(solution)/shard_map/ppermute | solution.py:356
  217.4 8.0 %next_query.5 = (f32[256,2048]{1,0:T(8,128)S(1)}, f32[256,2048]{1,0:T(8,128)S(1)}) custom-call(s32[16]{0:T(128)S(1)} %get-tuple-element.53.info_ref, bf16[264,2048]{1,0:T(8,128)(2,1)S(1)} %collective-permute-done.18.refs_1_.refs_6_.refs_0_.refs_3_, bf16[264,2048]{1,0:T(8,128)(2,1)S(1)} %hold.7.refs_0_.refs_7_.refs_1_.refs_2_, ...), custom_call_target="tpu_custom_call" | custom-call | flops 4294967296 | bytes 16777216 | tf_op jit(solution)/shard_map/next_query/pallas_call | solution.py:142
  225.5 8.0 %next_query.6 = (f32[256,2048]{1,0:T(8,128)S(1)}, f32[256,2048]{1,0:T(8,128)S(1)}) custom-call(s32[16]{0:T(128)S(1)} %get-tuple-element.53.info_ref, bf16[264,2048]{1,0:T(8,128)(2,1)S(1)} %collective-permute-done.23.refs_2_.refs_5_.refs_3_.refs_0_, bf16[264,2048]{1,0:T(8,128)(2,1)S(1)} %collective-permute-done.14.refs_3_.refs_4_.refs_2_.refs_1_, ...), custom_call_target="tpu_custom_call" | custom-call | flops 4294967296 | bytes 16777216 | tf_op jit(solution)/shard_map/next_query/pallas_call | solution.py:142
  233.5 8.9 %next_query.7 = (f32[256,2048]{1,0:T(8,128)S(1)}, bf16[256,2048]{1,0:T(8,128)(2,1)}) custom-call(s32[16]{0:T(128)S(1)} %get-tuple-element.53.info_ref, bf16[264,2048]{1,0:T(8,128)(2,1)S(1)} %pad_maximum_fusion.refs_0_, bf16[264,2048]{1,0:T(8,128)(2,1)S(1)} %collective-permute-done.21.refs_1_.refs_5_, ...), custom_call_target="tpu_custom_call" | custom-call | flops 4294967296 | bytes 16777216 | tf_op jit(solution)/shard_map/next_query/pallas_call | solution.py:142
  247.2 3.1 %multiply_convert_fusion = bf16[256,2048]{1,0:T(8,128)(2,1)} fusion(f32[256,2048]{1,0:T(8,128)} %copy-done.5, bf16[256,2048]{1,0:T(8,128)(2,1)} %collective-permute-done.26, f32[256]{0:T(256)S(1)} %add_rsqrt_fusion), kind=kLoop, calls=%fused_computation.1 | loop fusion | flops 2097152 | bytes 4195328 | tf_op jit(solution)/shard_map/convert_element_type | solution.py:370
  (91 shorter events, 32.8 us)
Async XLA Ops:
  21.2 2.7 %collective-permute-start.3 = (bf16[256,2048]{1,0:T(8,128)(2,1)S(1)}, bf16[256,2048]{1,0:T(8,128)(2,1)S(1)}, u32[]{:S(2)}, u32[]{:S(2)}) collective-permute-start(bf16[256,2048]{1,0:T(8,128)(2,1)S(1)} %get-tuple-element.26), channel_id=1, source_target_pairs={{0,1},{1,0},{2,3},{3,2},{4,5},{5,4},{6,7},{7,6},{8,9},{9,8},{10,11... | collective-permute-start | bytes 3145736 | tf_op jit(solution)/shard_map/ppermute | solution.py:290
  24.1 18.4 %collective-permute-start.5 = (bf16[256,2048]{1,0:T(8,128)(2,1)S(1)}, bf16[256,2048]{1,0:T(8,128)(2,1)S(1)}, u32[]{:S(2)}, u32[]{:S(2)}) collective-permute-start(bf16[256,2048]{1,0:T(8,128)(2,1)S(1)} %broadcast_select_fusion.refs_0_), channel_id=1, source_target_pairs={{0,4},{4,8},{8,12},{12,14},{14,10},{10,6},{6,2},{2,0},{5,1},{9,5},... | collective-permute-start | bytes 3145736 | tf_op jit(solution)/shard_map/ppermute | solution.py:303
  34.8 12.1 %collective-permute-start.4 = (bf16[256,2048]{1,0:T(8,128)(2,1)S(1)}, bf16[256,2048]{1,0:T(8,128)(2,1)S(1)}, u32[]{:S(2)}, u32[]{:S(2)}) collective-permute-start(bf16[256,2048]{1,0:T(8,128)(2,1)S(1)} %get-tuple-element.28), channel_id=1, source_target_pairs={{0,1},{1,0},{2,3},{3,2},{4,5},{5,4},{6,7},{7,6},{8,9},{9,8},{10,11... | collective-permute-start | bytes 3145736 | tf_op jit(solution)/shard_map/ppermute | solution.py:290
  42.5 4.4 %collective-permute-start.6 = (bf16[256,2048]{1,0:T(8,128)(2,1)S(1)}, bf16[256,2048]{1,0:T(8,128)(2,1)S(1)}, u32[]{:S(2)}, u32[]{:S(2)}) collective-permute-start(bf16[256,2048]{1,0:T(8,128)(2,1)S(1)} %hold.4), channel_id=1, source_target_pairs={{0,1},{1,0},{2,3},{3,2},{4,5},{5,4},{6,7},{7,6},{8,9},{9,8},{10,11... | collective-permute-start | bytes 3145736 | tf_op jit(solution)/shard_map/ppermute | solution.py:290
  48.1 26.0 %collective-permute-start.8 = (bf16[256,2048]{1,0:T(8,128)(2,1)S(1)}, bf16[256,2048]{1,0:T(8,128)(2,1)S(1)}, u32[]{:S(2)}, u32[]{:S(2)}) collective-permute-start(bf16[256,2048]{1,0:T(8,128)(2,1)S(1)} %add_convert_fusion.4.refs_1_), channel_id=1, source_target_pairs={{0,4},{4,8},{8,12},{12,14},{14,10},{10,6},{6,2},{2,0},{5,1},{9,5},... | collective-permute-start | bytes 3145736 | tf_op jit(solution)/shard_map/ppermute | solution.py:303
  49.7 24.3 %collective-permute-start.7 = (bf16[256,2048]{1,0:T(8,128)(2,1)S(1)}, bf16[256,2048]{1,0:T(8,128)(2,1)S(1)}, u32[]{:S(2)}, u32[]{:S(2)}) collective-permute-start(bf16[256,2048]{1,0:T(8,128)(2,1)S(1)} %select_select_fusion.refs_0_), channel_id=1, source_target_pairs={{4,0},{8,4},{12,8},{14,12},{10,14},{6,10},{2,6},{0,2},{1,5},{5,9},... | collective-permute-start | bytes 3145736 | tf_op jit(solution)/shard_map/ppermute | solution.py:303
  74.1 2.7 %collective-permute-start.9 = (bf16[256,2048]{1,0:T(8,128)(2,1)S(1)}, bf16[256,2048]{1,0:T(8,128)(2,1)S(1)}, u32[]{:S(2)}, u32[]{:S(2)}) collective-permute-start(bf16[256,2048]{1,0:T(8,128)(2,1)S(1)} %hold.5), channel_id=1, source_target_pairs={{0,1},{1,0},{2,3},{3,2},{4,5},{5,4},{6,7},{7,6},{8,9},{9,8},{10,11... | collective-permute-start | bytes 3145736 | tf_op jit(solution)/shard_map/ppermute | solution.py:290
  77.3 25.2 %collective-permute-start.11 = (bf16[256,2048]{1,0:T(8,128)(2,1)S(1)}, bf16[256,2048]{1,0:T(8,128)(2,1)S(1)}, u32[]{:S(2)}, u32[]{:S(2)}) collective-permute-start(bf16[256,2048]{1,0:T(8,128)(2,1)S(1)} %add_convert_fusion.3), channel_id=1, source_target_pairs={{4,0},{8,4},{12,8},{14,12},{10,14},{6,10},{2,6},{0,2},{1,5},{5,9},... | collective-permute-start | bytes 3145736 | tf_op jit(solution)/shard_map/ppermute | solution.py:303
  78.9 24.4 %collective-permute-start.10 = (bf16[256,2048]{1,0:T(8,128)(2,1)S(1)}, bf16[256,2048]{1,0:T(8,128)(2,1)S(1)}, u32[]{:S(2)}, u32[]{:S(2)}) collective-permute-start(bf16[256,2048]{1,0:T(8,128)(2,1)S(1)} %add_convert_fusion.2), channel_id=1, source_target_pairs={{0,4},{4,8},{8,12},{12,14},{14,10},{10,6},{6,2},{2,0},{5,1},{9,5},... | collective-permute-start | bytes 3145736 | tf_op jit(solution)/shard_map/ppermute | solution.py:303
  104.3 25.2 %collective-permute-start.12 = (bf16[256,2048]{1,0:T(8,128)(2,1)S(1)}, bf16[256,2048]{1,0:T(8,128)(2,1)S(1)}, u32[]{:S(2)}, u32[]{:S(2)}) collective-permute-start(bf16[256,2048]{1,0:T(8,128)(2,1)S(1)} %add_convert_fusion), channel_id=1, source_target_pairs={{0,4},{4,8},{8,12},{12,14},{14,10},{10,6},{6,2},{2,0},{5,1},{9,5},... | collective-permute-start | bytes 3145736 | tf_op jit(solution)/shard_map/ppermute | solution.py:303
  104.5 25.0 %collective-permute-start.13 = (bf16[256,2048]{1,0:T(8,128)(2,1)S(1)}, bf16[256,2048]{1,0:T(8,128)(2,1)S(1)}, u32[]{:S(2)}, u32[]{:S(2)}) collective-permute-start(bf16[256,2048]{1,0:T(8,128)(2,1)S(1)} %add_convert_fusion.1), channel_id=1, source_target_pairs={{4,0},{8,4},{12,8},{14,12},{10,14},{6,10},{2,6},{0,2},{1,5},{5,9},... | collective-permute-start | bytes 3145736 | tf_op jit(solution)/shard_map/ppermute | solution.py:303
  131.8 2.8 %collective-permute-start.17 = (bf16[264,2048]{1,0:T(8,128)(2,1)S(1)}, bf16[264,2048]{1,0:T(8,128)(2,1)S(1)}, u32[]{:S(2)}, u32[]{:S(2)}) collective-permute-start(bf16[264,2048]{1,0:T(8,128)(2,1)S(1)} %pad_maximum_fusion.refs_0_), channel_id=1, source_target_pairs={{0,1},{1,0},{2,3},{3,2},{4,5},{5,4},{6,7},{7,6},{8,9},{9,8},{10,11... | collective-permute-start | bytes 3244040 | tf_op jit(solution)/shard_map/ppermute | solution.py:333
  132.0 25.0 %collective-permute-start.14 = (bf16[264,2048]{1,0:T(8,128)(2,1)S(1)}, bf16[264,2048]{1,0:T(8,128)(2,1)S(1)}, u32[]{:S(2)}, u32[]{:S(2)}) collective-permute-start(bf16[264,2048]{1,0:T(8,128)(2,1)S(1)} %pad_maximum_fusion.refs_0_), channel_id=1, source_target_pairs={{0,4},{4,8},{8,12},{12,14},{14,10},{10,6},{6,2},{2,0},{5,1},{9,5},... | collective-permute-start | bytes 3244040 | tf_op jit(solution)/shard_map/ppermute | solution.py:340
  134.6 24.0 %collective-permute-start.18 = (bf16[264,2048]{1,0:T(8,128)(2,1)S(1)}, bf16[264,2048]{1,0:T(8,128)(2,1)S(1)}, u32[]{:S(2)}, u32[]{:S(2)}) collective-permute-start(bf16[264,2048]{1,0:T(8,128)(2,1)S(1)} %hold.6), channel_id=1, source_target_pairs={{4,0},{8,4},{12,8},{14,12},{10,14},{6,10},{2,6},{0,2},{1,5},{5,9},... | collective-permute-start | bytes 3244040 | tf_op jit(solution)/shard_map/ppermute | solution.py:341
  157.0 26.0 %collective-permute-start.15 = (bf16[264,2048]{1,0:T(8,128)(2,1)S(1)}, bf16[264,2048]{1,0:T(8,128)(2,1)S(1)}, u32[]{:S(2)}, u32[]{:S(2)}) collective-permute-start(bf16[264,2048]{1,0:T(8,128)(2,1)S(1)} %collective-permute-done.14.refs_3_.refs_4_.refs_2_.refs_1_), channel_id=1, source_target_pairs={{0,4},{4,8},{8,12},{12,14},{14,10},{10,6},{6,2},{2,0},{5,1},{9,5},... | collective-permute-start | bytes 3244040 | tf_op jit(solution)/shard_map/ppermute | solution.py:340
  158.6 24.5 %collective-permute-start.19 = (bf16[264,2048]{1,0:T(8,128)(2,1)S(1)}, bf16[264,2048]{1,0:T(8,128)(2,1)S(1)}, u32[]{:S(2)}, u32[]{:S(2)}) collective-permute-start(bf16[264,2048]{1,0:T(8,128)(2,1)S(1)} %collective-permute-done.18.refs_1_.refs_6_.refs_0_.refs_3_), channel_id=1, source_target_pairs={{4,0},{8,4},{12,8},{14,12},{10,14},{6,10},{2,6},{0,2},{1,5},{5,9},... | collective-permute-start | bytes 3244040 | tf_op jit(solution)/shard_map/ppermute | solution.py:341
  183.7 2.9 %collective-permute-start.20 = (bf16[256,2048]{1,0:T(8,128)(2,1)S(1)}, bf16[256,2048]{1,0:T(8,128)(2,1)S(1)}, u32[]{:S(2)}, u32[]{:S(2)}) collective-permute-start(bf16[256,2048]{1,0:T(8,128)(2,1)S(1)} %pick.2), channel_id=1, source_target_pairs={{0,1},{1,0},{2,3},{3,2},{4,5},{5,4},{6,7},{7,6},{8,9},{9,8},{10,11... | collective-permute-start | bytes 3145736 | tf_op jit(solution)/shard_map/ppermute | solution.py:350
  184.3 26.0 %collective-permute-start.16 = (bf16[264,2048]{1,0:T(8,128)(2,1)S(1)}, bf16[264,2048]{1,0:T(8,128)(2,1)S(1)}, u32[]{:S(2)}, u32[]{:S(2)}) collective-permute-start(bf16[264,2048]{1,0:T(8,128)(2,1)S(1)} %collective-permute-done.15.refs_0_.refs_1_), channel_id=1, source_target_pairs={{0,4},{4,8},{8,12},{12,14},{14,10},{10,6},{6,2},{2,0},{5,1},{9,5},... | collective-permute-start | bytes 3244040 | tf_op jit(solution)/shard_map/ppermute | solution.py:340
  185.3 25.0 %collective-permute-start.23 = (bf16[264,2048]{1,0:T(8,128)(2,1)S(1)}, bf16[264,2048]{1,0:T(8,128)(2,1)S(1)}, u32[]{:S(2)}, u32[]{:S(2)}) collective-permute-start(bf16[264,2048]{1,0:T(8,128)(2,1)S(1)} %collective-permute-done.19.refs_1_.refs_0_), channel_id=1, source_target_pairs={{4,0},{8,4},{12,8},{14,12},{10,14},{6,10},{2,6},{0,2},{1,5},{5,9},... | collective-permute-start | bytes 3244040 | tf_op jit(solution)/shard_map/ppermute | solution.py:341
  211.0 6.4 %collective-permute-start.25 = (bf16[256,2048]{1,0:T(8,128)(2,1)S(1)}, bf16[256,2048]{1,0:T(8,128)(2,1)S(1)}, u32[]{:S(2)}, u32[]{:S(2)}) collective-permute-start(bf16[256,2048]{1,0:T(8,128)(2,1)S(1)} %get-tuple-element.40), channel_id=1, source_target_pairs={{0,1},{1,0},{2,3},{3,2},{4,5},{5,4},{6,7},{7,6},{8,9},{9,8},{10,11... | collective-permute-start | bytes 3145736 | tf_op jit(solution)/shard_map/ppermute | solution.py:350
  211.7 13.8 %collective-permute-start.24 = (bf16[256,2048]{1,0:T(8,128)(2,1)S(1)}, bf16[256,2048]{1,0:T(8,128)(2,1)S(1)}, u32[]{:S(2)}, u32[]{:S(2)}) collective-permute-start(bf16[256,2048]{1,0:T(8,128)(2,1)S(1)} %get-tuple-element.39), channel_id=1, source_target_pairs={{0,1},{1,0},{2,3},{3,2},{4,5},{5,4},{6,7},{7,6},{8,9},{9,8},{10,11... | collective-permute-start | bytes 3145736 | tf_op jit(solution)/shard_map/ppermute | solution.py:350
  211.7 21.8 %collective-permute-start.22 = (bf16[264,2048]{1,0:T(8,128)(2,1)S(1)}, bf16[264,2048]{1,0:T(8,128)(2,1)S(1)}, u32[]{:S(2)}, u32[]{:S(2)}) collective-permute-start(bf16[264,2048]{1,0:T(8,128)(2,1)S(1)} %hold.7.refs_0_.refs_7_.refs_1_.refs_2_), channel_id=1, source_target_pairs={{5,1},{9,5},{13,8},{15,12},{11,14},{7,10},{3,7},{1,3},{21,17},{25,... | collective-permute-start | bytes 3244040 | tf_op jit(solution)/shard_map/ppermute | solution.py:357
  212.5 21.0 %collective-permute-start.21 = (bf16[264,2048]{1,0:T(8,128)(2,1)S(1)}, bf16[264,2048]{1,0:T(8,128)(2,1)S(1)}, u32[]{:S(2)}, u32[]{:S(2)}) collective-permute-start(bf16[264,2048]{1,0:T(8,128)(2,1)S(1)} %hold.7.refs_0_.refs_7_.refs_1_.refs_2_), channel_id=1, source_target_pairs={{0,5},{4,8},{8,12},{12,14},{14,10},{10,7},{6,3},{2,1},{16,21},{20,... | collective-permute-start | bytes 3244040 | tf_op jit(solution)/shard_map/ppermute | solution.py:356
  243.8 3.4 %collective-permute-start.26 = (bf16[256,2048]{1,0:T(8,128)(2,1)}, bf16[256,2048]{1,0:T(8,128)(2,1)}, u32[]{:S(2)}, u32[]{:S(2)}) collective-permute-start(bf16[256,2048]{1,0:T(8,128)(2,1)} %get-tuple-element.47), channel_id=1, source_target_pairs={{0,1},{1,0},{2,3},{3,2},{4,5},{5,4},{6,7},{7,6},{8,9},{9,8},{10,11... | collective-permute-start | bytes 3145736 | tf_op jit(solution)/shard_map/ppermute | solution.py:362
  (13 other events, 95.9 us)

commit v8 on v6

--- a/solution.py
+++ b/solution.py
@@ -110,55 +110,73 @@
     )(info, both, weight, *after)
 
 
-def query_kernel(sizes, code, first, info_ref, *refs):
-    chosen, far = refs[: sizes[0]], refs[sizes[0] : sum(sizes)]
-    w_ref = refs[sum(sizes)]
+def query_kernel(codes, sizes, first, info_ref, *refs):
     own_ref, peer_ref, x_ref = refs[-3:]
     rows = own_ref.shape[0]
+    start = 0
+    fills = []
+    for index, (code, groups) in enumerate(zip(codes, sizes)):
+        for half_index, (choices, parts) in enumerate(groups):
+            fills.append((index, half_index, code, refs[start : start + choices * parts], parts))
+            start += choices * parts
+    weights = refs[start : start + len(codes)]
+    depth = weights[0].shape[0]
 
     @pl.when(pl.program_id(0) == 0)
     def _():
-        for blocks, place in ((chosen, slice(0, rows)), (far, slice(rows, 2 * rows))):
-            for choice, block in enumerate(blocks):
-
-                @pl.when(info_ref[code] == choice if len(blocks) > 1 else True)
+        for index, half_index, code, blocks, parts in fills:
+            place = slice(half_index * rows, (half_index + 1) * rows)
+            width = depth // parts
+            for choice in range(len(blocks) // parts):
+
+                @pl.when(info_ref[code] == choice if len(blocks) > parts else True)
                 def _():
-                    x_ref[place] = block[...]
-
-    for part, (place, out) in enumerate(((slice(0, rows), own_ref), (slice(rows, 2 * rows), peer_ref))):
-        result = dot(x_ref[place], w_ref[...])
-        if not first:
-            result = result + refs[sum(sizes) + 1 + part][...]
+                    for part in range(parts):
+                        columns = slice(index * depth + part * width, index * depth + (part + 1) * width)
+                        x_ref[place, columns] = blocks[choice * parts + part][...]
+
+    for half_index, out in enumerate((own_ref, peer_ref)):
+        place = slice(half_index * rows, (half_index + 1) * rows)
+        result = None if first else refs[start + len(codes) + half_index][...]
+        for index, w_ref in enumerate(weights):
+            product = dot(x_ref[place, index * depth : (index + 1) * depth], w_ref[...])
+            result = product if result is None else result + product
         out[...] = result.astype(out.dtype)
 
 
-def query_block(info, pair, code, chosen, far, weight, acc, last):
-    rows, depth = far[0].shape
+def query_block(info, half, blocks, weight, acc, last):
+    rows = blocks[0][1][0][0].shape[0]
+    depth = sum(piece.shape[1] for piece in blocks[0][1][0])
     width = weight.shape[1]
     tile = min(512, width)
     whole = pl.BlockSpec(memory_space=pltpu.VMEM)
     out = pl.BlockSpec((rows, tile), lambda j, s: (0, j))
+    sizes = [[(len(choices), len(choices[0])) for choices in (own, far)] for _, own, far in blocks]
+    arrays = [piece for _, own, far in blocks for choices in (own, far) for choice in choices for piece in choice]
+    weight_specs = [
+        pl.BlockSpec((depth, tile), functools.partial(lambda pair, j, s: (s[pair], j), pair)) for pair, _, _ in blocks
+    ]
     return pl.pallas_call(
-        functools.partial(query_kernel, (len(chosen), len(far)), code, not acc),
+        functools.partial(query_kernel, [half + pair for pair, _, _ in blocks], sizes, not acc),
         grid_spec=pltpu.PrefetchScalarGridSpec(
             num_scalar_prefetch=1,
             grid=(width // tile,),
-            in_specs=[whole] * (len(chosen) + len(far))
-            + [pl.BlockSpec((depth, tile), lambda j, s: (s[pair], j))]
-            + [out] * len(acc),
+            in_specs=[whole] * len(arrays) + weight_specs + [out] * len(acc),
             out_specs=[out, out],
-            scratch_shapes=[pltpu.VMEM((2 * rows, depth), BF16)],
+            scratch_shapes=[pltpu.VMEM((2 * rows, depth * len(blocks)), BF16)],
         ),
         out_shape=[
             jax.ShapeDtypeStruct((rows, width), F32),
             jax.ShapeDtypeStruct((rows, width), BF16 if last else F32),
         ],
-        compiler_params=pltpu.CompilerParams(vmem_limit_bytes=24 * MIB),
+        compiler_params=pltpu.CompilerParams(vmem_limit_bytes=26 * MIB),
         cost_estimate=pl.CostEstimate(
-            flops=4 * rows * depth * width, bytes_accessed=2 * depth * width + 16 * rows * width, transcendentals=0
+            flops=4 * rows * depth * width * len(blocks),
+            bytes_accessed=2 * depth * width * len(blocks) + 16 * rows * width,
+            transcendentals=0,
         ),
         name="next_query",
-    )(info, *chosen, *far, weight, *acc)
+    )(info, *arrays, *[weight] * len(blocks), *acc)
 
 
 def add_kernel(total_ref, more_ref, *refs):
@@ -199,31 +217,35 @@
 def pick_kernel(codes, sizes, info_ref, *refs):
     outs = refs[len(refs) - len(codes) :]
     start = 0
-    for code, size, out in zip(codes, sizes, outs):
-        for choice in range(size):
+    for code, (choices, parts), out in zip(codes, sizes, outs):
+        width = out.shape[1] // parts
+        for choice in range(choices):
 
             @pl.when(info_ref[code] == choice)
             def _():
-                out[...] = refs[start + choice][...]
-
-        start += size
+                for part in range(parts):
+                    out[:, part * width : (part + 1) * width] = refs[start + choice * parts + part][...]
+
+        start += choices * parts
 
 
 def pick(info, codes, groups, after):
     whole = pl.BlockSpec(memory_space=pltpu.VMEM)
-    first = groups[0][0]
+    arrays = [piece for group in groups for choice in group for piece in choice]
+    rows, piece_width = arrays[0].shape
+    shape = jax.ShapeDtypeStruct((rows, piece_width * len(groups[0][0])), arrays[0].dtype)
     return pl.pallas_call(
-        functools.partial(pick_kernel, codes, [len(group) for group in groups]),
+        functools.partial(pick_kernel, codes, [(len(group), len(group[0])) for group in groups]),
         grid_spec=pltpu.PrefetchScalarGridSpec(
             num_scalar_prefetch=1,
             grid=(1,),
-            in_specs=[whole] * (sum(len(group) for group in groups) + len(after)),
+            in_specs=[whole] * (len(arrays) + len(after)),
             out_specs=[whole] * len(groups),
         ),
-        out_shape=[jax.ShapeDtypeStruct(first.shape, first.dtype)] * len(groups),
+        out_shape=[shape] * len(groups),
         compiler_params=pltpu.CompilerParams(vmem_limit_bytes=4 * MIB),
         name="pick",
-    )(info, *[block for group in groups for block in group], *after)
+    )(info, *arrays, *after)
 
 
 def ring_of(n):
@@ -333,35 +355,34 @@
         value = send("short", step, value)
         value = send("long", step + 1, value)
 
+    arrived["short"] = hold(arrived["short"], [])
     mixed = residual.astype(F32) + partial_sum(0) + arrived["long"].astype(F32) + arrived["short"].astype(F32)
     resid_out = mixed.astype(BF16)
     scaled = (mixed * norm_gain.astype(F32)).astype(BF16)
     squares = jnp.sum(mixed * mixed, axis=1)[None]
 
+    scaled_peer = lax.ppermute(scaled, "tokens", swap)
     held = {0: scaled}
-    scaled_peer = lax.ppermute(scaled, "tokens", swap)
-    long_block, short_block = scaled, hold(scaled, [scaled_peer])
     groups = {}
     for k in range(1, half):
         groups.setdefault(max(k, half - k), []).append(k)
     reach = 1
     acc, after = (), ()
     for step in range(1, half):
-        long_block = lax.ppermute(long_block, devices, long_way)
-        short_block = lax.ppermute(short_block, devices, short_way)
+        held[-step] = lax.ppermute(held[1 - step], devices, long_way)
+        held[step] = lax.ppermute(held[step - 1], devices, short_way)
         if reach < n:
             more = lax.ppermute(squares, "tensor", [(c, c ^ reach) for c in range(n)])
-            squares, (long_block,) = add_in_step(squares, more, [long_block], after)
+            squares, (held[-step],) = add_in_step(squares, more, [held[-step]], after)
             reach *= 2
-        held[-step], held[step] = long_block, short_block
         pairs = groups.get(step, [])
         if pairs:
-            wanted = {k: [held[q] for q in block_choices(k, half)] for k in pairs}
+            wanted = {k: [[held[q]] for q in block_choices(k, half)] for k in pairs}
             others = [[wanted[k][index ^ 1] for index in range(len(wanted[k]))] for k in pairs]
             outgoing = pick(info, [half + k for k in pairs], others, after)
             far = [lax.ppermute(block, "tokens", swap) for block in outgoing]
-            for k, block in zip(pairs, far):
-                acc = query_block(info, k, half + k, wanted[k], [block], next_weight, acc, False)
+            blocks = [(k, wanted[k], [[block]]) for k, block in zip(pairs, far)]
+            acc = query_block(info, half, blocks, next_weight, acc, False)
             after = acc[:1]
     while reach < n:
         squares = squares + lax.ppermute(squares, "tensor", [(c, c ^ reach) for c in range(n)])
@@ -371,9 +392,9 @@
         lax.ppermute(held[1 - half], devices, [(2 * a, 2 * b + meets[b]) for a, b in up]),
         lax.ppermute(held[1 - half], devices, [(2 * b + 1, 2 * a + meets[a]) for a, b in up]),
     ]
-    acc = query_block(
-        info, 0, half, [scaled, *last_hop], [scaled_peer, *reversed(last_hop)], next_weight, acc, True
-    )
+    own = [[scaled], *[[block] for block in last_hop]]
+    far = [[scaled_peer], *[[block] for block in reversed(last_hop)]]
+    acc = query_block(info, half, [(0, own, far)], next_weight, acc, True)
     query_sum = acc[0] + lax.ppermute(acc[1], "tokens", swap).astype(F32)
     factor = 1.0 / jnp.sqrt(squares[0] / D + EPS_NORM)
     return (resid_out, (query_sum * factor[:, None]).astype(BF16))

time: 240 us -> 231 us (0.963)
  waiting for transfers between devices: 119 us -> 109 us
  starting transfers between devices: 27.1 us -> 32.1 us
  Pallas kernels: 69.7 us -> 66.7 us
    ppermute x3, waiting for transfers between devices: 55.8 us -> 47.1 us  [on_ring(): more = lax.ppermute(squares, 'tensor', [(c, c ^ reach) for c in range(n)])]
    pallas_call x6 -> x5, Pallas kernels: 33.3 us -> 30.2 us  [the longest x3 28.9 us: query_block(): pl.pallas_call(functools.partial(query_kernel, [half + pair for pair, _,...]
  transfers between devices with their start and end apart: 30 -> 30, of which waited for: 17 -> 15; matrix products, arithmetic and copies ran while one was open for 2% -> 2% of each run, Pallas kernels for 20% -> 19%
where the time goes in v8:
time: 231 us
  waiting for transfers between devices  109 us (47%)
  Pallas kernels  66.7 us (29%)
  starting transfers between devices  32.1 us (14%)
  between operations  10.8 us (5%)
  other arithmetic  7.97 us (3%)
  local copies, waits for them, and re-layouts  4.1 us (2%)
    ppermute x7, waiting for transfers between devices, send(): lax.ppermute(value, devices, long_way if way == 'long' else short_way)  54.1 us
    ppermute x3, waiting for transfers between devices, on_ring(): more = lax.ppermute(squares, 'tensor', [(c, c ^ reach) for c in range(n)])  47.1 us
    pallas_call x4, Pallas kernels, project(): pl.pallas_call(project_kernel, grid_spec=pltpu.PrefetchScalarGridSpec(num...  30.7 us
    pallas_call x3, Pallas kernels, query_block(): pl.pallas_call(functools.partial(query_kernel, [half + pair for pair, _,...  28.9 us
    ppermute x7, starting transfers between devices, send(): lax.ppermute(value, devices, long_way if way == 'long' else short_way)  11.4 us
    ppermute x3, starting transfers between devices, on_ring(): held[-step] = lax.ppermute(held[1 - step], devices, long_way)  6.99 us
    pallas_call x2, Pallas kernels, attention(): pl.pallas_call(functools.partial(attention_kernel, heads), grid_spec=pltp...  5.73 us
    ppermute x3, starting transfers between devices, on_ring(): more = lax.ppermute(squares, 'tensor', [(c, c ^ reach) for c in range(n)])  5.09 us
  transfers between devices with their start and end apart: 30, of which 15 were waited for; matrix products, arithmetic and copies ran while one was open for 2% of the time, Pallas kernels for 19%

profile of v8, /device:TPU:0, one launch (start us, length us, event | category | flops | bytes accessed | tf_op | source)
XLA Modules:
  0.0 230.7 jit_solution(11702075079828503709)
XLA Ops:
  4.9 2.9 %attention.2.refs_0_ = bf16[256,1024]{1,0:T(8,128)(2,1)S(1)} custom-call(s32[1]{0:T(128)} %bitcast.2.core_ref, bf16[256,2048]{1,0:T(8,128)(2,1)S(1)} %copy-done, bf16[2,256,128]{2,1,0:T(8,128)(2,1)S(1)} %pad_maximum_fusion.own_ref, bf16[2,256,128]{2,1,0:T(8,128)(2,1)S(1)} %collective-permute-done.far_ref), custom_call_target="tpu_custom_call" | custom-call | flops 536870912 | bytes 1048576 | tf_op jit(solution)/shard_map/attention/pallas_call | solution.py:61
  7.8 2.9 %attention.3 = bf16[256,1024]{1,0:T(8,128)(2,1)S(1)} custom-call(s32[1]{0:T(128)} %bitcast.2.core_ref, bf16[256,2048]{1,0:T(8,128)(2,1)S(1)} %copy-done, bf16[2,256,128]{2,1,0:T(8,128)(2,1)S(1)} %pad_maximum_fusion.own_ref, bf16[2,256,128]{2,1,0:T(8,128)(2,1)S(1)} %collective-permute-done.far_ref, bf16[256,1024]{1,0:T(8,128)(2,1)S(1)} %attention.2.refs_0_), custom_call_target="tpu_custom_call" | custom-call | flops 536870912 | bytes 1048576 | tf_op jit(solution)/shard_map/attention/pallas_call | solution.py:61
  13.6 7.7 %project.4 = (bf16[256,2048]{1,0:T(8,128)(2,1)S(1)}, bf16[256,2048]{1,0:T(8,128)(2,1)S(1)}) custom-call(s32[16]{0:T(128)S(1)} %get-tuple-element.61.info_ref, bf16[512,2048]{1,0:T(8,128)(2,1)S(1)} %maximum_maximum_fusion.x_ref, bf16[2048,8192]{1,0:T(8,128)(2,1)} %w_ref.7), custom_call_target="tpu_custom_call" | custom-call | flops 4294967296 | bytes 8388608 | tf_op jit(solution)/shard_map/project/pallas_call | solution.py:92
  24.1 3.0 %collective-permute-start.5 = (bf16[256,2048]{1,0:T(8,128)(2,1)S(1)}, bf16[256,2048]{1,0:T(8,128)(2,1)S(1)}, u32[]{:S(2)}, u32[]{:S(2)}) collective-permute-start(bf16[256,2048]{1,0:T(8,128)(2,1)S(1)} %broadcast_select_fusion.refs_0_), channel_id=1, source_target_pairs={{0,4},{4,8},{8,12},{12,14},{14,10},{10,6},{6,2},{2,0},{5,1},{9,5},... | collective-permute-start | bytes 3145736 | tf_op jit(solution)/shard_map/ppermute | solution.py:342
  27.1 7.7 %project.5 = (bf16[256,2048]{1,0:T(8,128)(2,1)S(1)}, bf16[256,2048]{1,0:T(8,128)(2,1)S(1)}) custom-call(s32[16]{0:T(128)S(1)} %get-tuple-element.61.info_ref, bf16[512,2048]{1,0:T(8,128)(2,1)S(1)} %maximum_maximum_fusion.x_ref, bf16[2048,8192]{1,0:T(8,128)(2,1)} %w_ref.7), custom_call_target="tpu_custom_call" | custom-call | flops 4294967296 | bytes 8388608 | tf_op jit(solution)/shard_map/project/pallas_call | solution.py:92
  34.9 7.7 %project.6 = (bf16[256,2048]{1,0:T(8,128)(2,1)S(1)}, bf16[256,2048]{1,0:T(8,128)(2,1)S(1)}) custom-call(s32[16]{0:T(128)S(1)} %get-tuple-element.61.info_ref, bf16[512,2048]{1,0:T(8,128)(2,1)S(1)} %maximum_maximum_fusion.x_ref, bf16[2048,8192]{1,0:T(8,128)(2,1)} %w_ref.7, bf16[256,2048]{1,0:T(8,128)(2,1)S(1)} %broadcast_select_fusion.refs_0_), custom_call_target="tpu_custom_call" | custom-call | flops 4294967296 | bytes 8388608 | tf_op jit(solution)/shard_map/project/pallas_call | solution.py:92
  48.8 7.7 %project.7 = (bf16[256,2048]{1,0:T(8,128)(2,1)S(1)}, bf16[256,2048]{1,0:T(8,128)(2,1)S(1)}) custom-call(s32[16]{0:T(128)S(1)} %get-tuple-element.61.info_ref, bf16[512,2048]{1,0:T(8,128)(2,1)S(1)} %maximum_maximum_fusion.x_ref, bf16[2048,8192]{1,0:T(8,128)(2,1)} %w_ref.7, bf16[256,2048]{1,0:T(8,128)(2,1)S(1)} %select_select_fusion.refs_0_), custom_call_target="tpu_custom_call" | custom-call | flops 4294967296 | bytes 8388608 | tf_op jit(solution)/shard_map/project/pallas_call | solution.py:92
  56.5 4.0 %collective-permute-done.7.refs_1_ = bf16[256,2048]{1,0:T(8,128)(2,1)S(1)} collective-permute-done((bf16[256,2048]{1,0:T(8,128)(2,1)S(1)}, bf16[256,2048]{1,0:T(8,128)(2,1)S(1)}, u32[]{:S(2)}, u32[]{:S(2)}) %collective-permute-start.7) | collective-permute-done | bytes 1048608 | tf_op jit(solution)/shard_map/ppermute | solution.py:342
  65.5 20.2 %collective-permute-done.9 = bf16[256,2048]{1,0:T(8,128)(2,1)S(1)} collective-permute-done((bf16[256,2048]{1,0:T(8,128)(2,1)S(1)}, bf16[256,2048]{1,0:T(8,128)(2,1)S(1)}, u32[]{:S(2)}, u32[]{:S(2)}) %collective-permute-start.9) | collective-permute-done | bytes 1048608 | tf_op jit(solution)/shard_map/ppermute | solution.py:342
  93.0 17.2 %collective-permute-done.10 = bf16[256,2048]{1,0:T(8,128)(2,1)S(1)} collective-permute-done((bf16[256,2048]{1,0:T(8,128)(2,1)S(1)}, bf16[256,2048]{1,0:T(8,128)(2,1)S(1)}, u32[]{:S(2)}, u32[]{:S(2)}) %collective-permute-start.10) | collective-permute-done | bytes 1048608 | tf_op jit(solution)/shard_map/ppermute | solution.py:342
  111.2 2.7 %collective-permute-start.12 = (bf16[256,2048]{1,0:T(8,128)(2,1)S(1)}, bf16[256,2048]{1,0:T(8,128)(2,1)S(1)}, u32[]{:S(2)}, u32[]{:S(2)}) collective-permute-start(bf16[256,2048]{1,0:T(8,128)(2,1)S(1)} %add_convert_fusion), channel_id=1, source_target_pairs={{0,4},{4,8},{8,12},{12,14},{14,10},{10,6},{6,2},{2,0},{5,1},{9,5},... | collective-permute-start | bytes 3145736 | tf_op jit(solution)/shard_map/ppermute | solution.py:342
  114.6 12.8 %collective-permute-done.12 = bf16[256,2048]{1,0:T(8,128)(2,1)S(1)} collective-permute-done((bf16[256,2048]{1,0:T(8,128)(2,1)S(1)}, bf16[256,2048]{1,0:T(8,128)(2,1)S(1)}, u32[]{:S(2)}, u32[]{:S(2)}) %collective-permute-start.12) | collective-permute-done | bytes 1048608 | tf_op jit(solution)/shard_map/ppermute | solution.py:342
  129.5 2.5 %collective-permute-start.15 = (bf16[256,2048]{1,0:T(8,128)(2,1)S(1)}, bf16[256,2048]{1,0:T(8,128)(2,1)S(1)}, u32[]{:S(2)}, u32[]{:S(2)}) collective-permute-start(bf16[256,2048]{1,0:T(8,128)(2,1)S(1)} %get-tuple-element.58.refs_0_), channel_id=1, source_target_pairs={{0,4},{4,8},{8,12},{12,14},{14,10},{10,6},{6,2},{2,0},{5,1},{9,5},... | collective-permute-start | bytes 3145736 | tf_op jit(solution)/shard_map/ppermute | solution.py:372
  132.0 18.9 %collective-permute-done.14.more_ref = f32[1,256]{1,0:T(1,128)S(1)} collective-permute-done((f32[1,256]{1,0:T(1,128)S(1)}, f32[1,256]{1,0:T(1,128)S(1)}, u32[]{:S(2)}, u32[]{:S(2)}) %collective-permute-start.14) | collective-permute-done | bytes 1056 | tf_op jit(solution)/shard_map/ppermute | solution.py:375
  151.6 2.9 %collective-permute-start.17 = (bf16[256,2048]{1,0:T(8,128)(2,1)S(1)}, bf16[256,2048]{1,0:T(8,128)(2,1)S(1)}, u32[]{:S(2)}, u32[]{:S(2)}) collective-permute-start(bf16[256,2048]{1,0:T(8,128)(2,1)S(1)} %get-tuple-element.43.refs_3_.refs_4_.refs_2_.refs_6_), channel_id=1, source_target_pairs={{0,4},{4,8},{8,12},{12,14},{14,10},{10,6},{6,2},{2,0},{5,1},{9,5},... | collective-permute-start | bytes 3145736 | tf_op jit(solution)/shard_map/ppermute | solution.py:372
  154.5 2.5 %collective-permute-start.16 = (f32[1,256]{1,0:T(1,128)S(1)}, f32[1,256]{1,0:T(1,128)S(1)}, u32[]{:S(2)}, u32[]{:S(2)}) collective-permute-start(f32[1,256]{1,0:T(1,128)S(1)} %get-tuple-element.42.total_ref), channel_id=1, source_target_pairs={{0,4},{2,6},{4,0},{6,2},{8,12},{10,14},{12,8},{14,10},{1,5},{3,7},... | collective-permute-start | bytes 3080 | tf_op jit(solution)/shard_map/ppermute | solution.py:375
  157.0 14.2 %collective-permute-done.16.more_ref = f32[1,256]{1,0:T(1,128)S(1)} collective-permute-done((f32[1,256]{1,0:T(1,128)S(1)}, f32[1,256]{1,0:T(1,128)S(1)}, u32[]{:S(2)}, u32[]{:S(2)}) %collective-permute-start.16) | collective-permute-done | bytes 1056 | tf_op jit(solution)/shard_map/ppermute | solution.py:375
  174.9 2.6 %collective-permute-start.18 = (f32[1,256]{1,0:T(1,128)S(1)}, f32[1,256]{1,0:T(1,128)S(1)}, u32[]{:S(2)}, u32[]{:S(2)}) collective-permute-start(f32[1,256]{1,0:T(1,128)S(1)} %get-tuple-element.44.total_ref), channel_id=1, source_target_pairs={{0,8},{2,10},{4,12},{6,14},{8,0},{10,2},{12,4},{14,6},{1,9},{3,11}... | collective-permute-start | bytes 3080 | tf_op jit(solution)/shard_map/ppermute | solution.py:375
  177.5 7.9 %next_query.3 = (f32[256,2048]{1,0:T(8,128)S(1)}, f32[256,2048]{1,0:T(8,128)S(1)}) custom-call(s32[16]{0:T(128)S(1)} %get-tuple-element.61.info_ref, bf16[256,2048]{1,0:T(8,128)(2,1)S(1)} %collective-permute-done.21.refs_1_.refs_0_, bf16[256,2048]{1,0:T(8,128)(2,1)S(1)} %get-tuple-element.45.refs_0_.refs_1_, ...), custom_call_target="tpu_custom_call" | custom-call | flops 4294967296 | bytes 16777216 | tf_op jit(solution)/shard_map/next_query/pallas_call | solution.py:159
  185.4 14.0 %collective-permute-done.18.more_ref = f32[1,256]{1,0:T(1,128)S(1)} collective-permute-done((f32[1,256]{1,0:T(1,128)S(1)}, f32[1,256]{1,0:T(1,128)S(1)}, u32[]{:S(2)}, u32[]{:S(2)}) %collective-permute-start.18) | collective-permute-done | bytes 1056 | tf_op jit(solution)/shard_map/ppermute | solution.py:375
  200.8 3.6 %collective-permute-start.23 = (bf16[256,2048]{1,0:T(8,128)(2,1)S(1)}, bf16[256,2048]{1,0:T(8,128)(2,1)S(1)}, u32[]{:S(2)}, u32[]{:S(2)}) collective-permute-start(bf16[256,2048]{1,0:T(8,128)(2,1)S(1)} %get-tuple-element.47.refs_0_.refs_7_.refs_1_), channel_id=1, source_target_pairs={{0,5},{4,8},{8,12},{12,14},{14,10},{10,7},{6,3},{2,1},{16,21},{20,... | collective-permute-start | bytes 3145736 | tf_op jit(solution)/shard_map/ppermute | solution.py:392
  205.2 13.0 %next_query.4 = (f32[256,2048]{1,0:T(8,128)S(1)}, f32[256,2048]{1,0:T(8,128)S(1)}) custom-call(s32[16]{0:T(128)S(1)} %get-tuple-element.61.info_ref, bf16[256,2048]{1,0:T(8,128)(2,1)S(1)} %collective-permute-done.20.refs_1_.refs_6_.refs_0_.refs_8_, bf16[256,2048]{1,0:T(8,128)(2,1)S(1)} %get-tuple-element.47.refs_0_.refs_7_.refs_1_, ...), custom_call_target="tpu_custom_call" | custom-call | flops 8589934592 | bytes 25165824 | tf_op jit(solution)/shard_map/next_query/pallas_call | solution.py:159
  218.2 8.0 %next_query.5 = (f32[256,2048]{1,0:T(8,128)S(1)}, bf16[256,2048]{1,0:T(8,128)(2,1)S(1)}) custom-call(s32[16]{0:T(128)S(1)} %get-tuple-element.61.info_ref, bf16[256,2048]{1,0:T(8,128)(2,1)S(1)} %get-tuple-element.58.refs_0_, bf16[256,2048]{1,0:T(8,128)(2,1)S(1)} %collective-permute-done.23.refs_1_.refs_5_, ...), custom_call_target="tpu_custom_call" | custom-call | flops 4294967296 | bytes 16777216 | tf_op jit(solution)/shard_map/next_query/pallas_call | solution.py:159
  227.2 2.3 collective-permute-done.29
  (78 shorter events, 31.2 us)
Async XLA Ops:
  24.1 18.4 %collective-permute-start.5 = (bf16[256,2048]{1,0:T(8,128)(2,1)S(1)}, bf16[256,2048]{1,0:T(8,128)(2,1)S(1)}, u32[]{:S(2)}, u32[]{:S(2)}) collective-permute-start(bf16[256,2048]{1,0:T(8,128)(2,1)S(1)} %broadcast_select_fusion.refs_0_), channel_id=1, source_target_pairs={{0,4},{4,8},{8,12},{12,14},{14,10},{10,6},{6,2},{2,0},{5,1},{9,5},... | collective-permute-start | bytes 3145736 | tf_op jit(solution)/shard_map/ppermute | solution.py:342
  34.8 10.2 %collective-permute-start.4 = (bf16[256,2048]{1,0:T(8,128)(2,1)S(1)}, bf16[256,2048]{1,0:T(8,128)(2,1)S(1)}, u32[]{:S(2)}, u32[]{:S(2)}) collective-permute-start(bf16[256,2048]{1,0:T(8,128)(2,1)S(1)} %get-tuple-element.32), channel_id=1, source_target_pairs={{0,1},{1,0},{2,3},{3,2},{4,5},{5,4},{6,7},{7,6},{8,9},{9,8},{10,11... | collective-permute-start | bytes 3145736 | tf_op jit(solution)/shard_map/ppermute | solution.py:329
  45.6 14.9 %collective-permute-start.7 = (bf16[256,2048]{1,0:T(8,128)(2,1)S(1)}, bf16[256,2048]{1,0:T(8,128)(2,1)S(1)}, u32[]{:S(2)}, u32[]{:S(2)}) collective-permute-start(bf16[256,2048]{1,0:T(8,128)(2,1)S(1)} %select_select_fusion.refs_0_), channel_id=1, source_target_pairs={{4,0},{8,4},{12,8},{14,12},{10,14},{6,10},{2,6},{0,2},{1,5},{5,9},... | collective-permute-start | bytes 3145736 | tf_op jit(solution)/shard_map/ppermute | solution.py:342
  60.5 3.3 %collective-permute-start.8 = (bf16[256,2048]{1,0:T(8,128)(2,1)S(1)}, bf16[256,2048]{1,0:T(8,128)(2,1)S(1)}, u32[]{:S(2)}, u32[]{:S(2)}) collective-permute-start(bf16[256,2048]{1,0:T(8,128)(2,1)S(1)} %hold.4), channel_id=1, source_target_pairs={{0,1},{1,0},{2,3},{3,2},{4,5},{5,4},{6,7},{7,6},{8,9},{9,8},{10,11... | collective-permute-start | bytes 3145736 | tf_op jit(solution)/shard_map/ppermute | solution.py:329
  61.5 24.2 %collective-permute-start.9 = (bf16[256,2048]{1,0:T(8,128)(2,1)S(1)}, bf16[256,2048]{1,0:T(8,128)(2,1)S(1)}, u32[]{:S(2)}, u32[]{:S(2)}) collective-permute-start(bf16[256,2048]{1,0:T(8,128)(2,1)S(1)} %add_convert_fusion.4), channel_id=1, source_target_pairs={{0,4},{4,8},{8,12},{12,14},{14,10},{10,6},{6,2},{2,0},{5,1},{9,5},... | collective-permute-start | bytes 3145736 | tf_op jit(solution)/shard_map/ppermute | solution.py:342
  64.3 27.5 %collective-permute-start.11 = (bf16[256,2048]{1,0:T(8,128)(2,1)S(1)}, bf16[256,2048]{1,0:T(8,128)(2,1)S(1)}, u32[]{:S(2)}, u32[]{:S(2)}) collective-permute-start(bf16[256,2048]{1,0:T(8,128)(2,1)S(1)} %add_convert_fusion.3), channel_id=1, source_target_pairs={{4,0},{8,4},{12,8},{14,12},{10,14},{6,10},{2,6},{0,2},{1,5},{5,9},... | collective-permute-start | bytes 3145736 | tf_op jit(solution)/shard_map/ppermute | solution.py:342
  86.3 23.9 %collective-permute-start.10 = (bf16[256,2048]{1,0:T(8,128)(2,1)S(1)}, bf16[256,2048]{1,0:T(8,128)(2,1)S(1)}, u32[]{:S(2)}, u32[]{:S(2)}) collective-permute-start(bf16[256,2048]{1,0:T(8,128)(2,1)S(1)} %add_convert_fusion.2), channel_id=1, source_target_pairs={{0,4},{4,8},{8,12},{12,14},{14,10},{10,6},{6,2},{2,0},{5,1},{9,5},... | collective-permute-start | bytes 3145736 | tf_op jit(solution)/shard_map/ppermute | solution.py:342
  92.8 21.7 %collective-permute-start.13 = (bf16[256,2048]{1,0:T(8,128)(2,1)S(1)}, bf16[256,2048]{1,0:T(8,128)(2,1)S(1)}, u32[]{:S(2)}, u32[]{:S(2)}) collective-permute-start(bf16[256,2048]{1,0:T(8,128)(2,1)S(1)} %add_convert_fusion.1), channel_id=1, source_target_pairs={{4,0},{8,4},{12,8},{14,12},{10,14},{6,10},{2,6},{0,2},{1,5},{5,9},... | collective-permute-start | bytes 3145736 | tf_op jit(solution)/shard_map/ppermute | solution.py:342
  111.2 16.2 %collective-permute-start.12 = (bf16[256,2048]{1,0:T(8,128)(2,1)S(1)}, bf16[256,2048]{1,0:T(8,128)(2,1)S(1)}, u32[]{:S(2)}, u32[]{:S(2)}) collective-permute-start(bf16[256,2048]{1,0:T(8,128)(2,1)S(1)} %add_convert_fusion), channel_id=1, source_target_pairs={{0,4},{4,8},{8,12},{12,14},{14,10},{10,6},{6,2},{2,0},{5,1},{9,5},... | collective-permute-start | bytes 3145736 | tf_op jit(solution)/shard_map/ppermute | solution.py:342
  129.5 22.1 %collective-permute-start.15 = (bf16[256,2048]{1,0:T(8,128)(2,1)S(1)}, bf16[256,2048]{1,0:T(8,128)(2,1)S(1)}, u32[]{:S(2)}, u32[]{:S(2)}) collective-permute-start(bf16[256,2048]{1,0:T(8,128)(2,1)S(1)} %get-tuple-element.58.refs_0_), channel_id=1, source_target_pairs={{0,4},{4,8},{8,12},{12,14},{14,10},{10,6},{6,2},{2,0},{5,1},{9,5},... | collective-permute-start | bytes 3145736 | tf_op jit(solution)/shard_map/ppermute | solution.py:372
  132.0 22.5 %collective-permute-start.20 = (bf16[256,2048]{1,0:T(8,128)(2,1)S(1)}, bf16[256,2048]{1,0:T(8,128)(2,1)S(1)}, u32[]{:S(2)}, u32[]{:S(2)}) collective-permute-start(bf16[256,2048]{1,0:T(8,128)(2,1)S(1)} %get-tuple-element.58.refs_0_), channel_id=1, source_target_pairs={{4,0},{8,4},{12,8},{14,12},{10,14},{6,10},{2,6},{0,2},{1,5},{5,9},... | collective-permute-start | bytes 3145736 | tf_op jit(solution)/shard_map/ppermute | solution.py:373
  132.0 18.9 %collective-permute-start.14 = (f32[1,256]{1,0:T(1,128)S(1)}, f32[1,256]{1,0:T(1,128)S(1)}, u32[]{:S(2)}, u32[]{:S(2)}) collective-permute-start(f32[1,256]{1,0:T(1,128)S(1)} %bitcast.27), channel_id=1, source_target_pairs={{0,2},{2,0},{4,6},{6,4},{8,10},{10,8},{12,14},{14,12},{1,3},{3,1},... | collective-permute-start | bytes 3080 | tf_op jit(solution)/shard_map/ppermute | solution.py:375
  151.6 20.5 %collective-permute-start.17 = (bf16[256,2048]{1,0:T(8,128)(2,1)S(1)}, bf16[256,2048]{1,0:T(8,128)(2,1)S(1)}, u32[]{:S(2)}, u32[]{:S(2)}) collective-permute-start(bf16[256,2048]{1,0:T(8,128)(2,1)S(1)} %get-tuple-element.43.refs_3_.refs_4_.refs_2_.refs_6_), channel_id=1, source_target_pairs={{0,4},{4,8},{8,12},{12,14},{14,10},{10,6},{6,2},{2,0},{5,1},{9,5},... | collective-permute-start | bytes 3145736 | tf_op jit(solution)/shard_map/ppermute | solution.py:372
  154.5 17.6 %collective-permute-start.21 = (bf16[256,2048]{1,0:T(8,128)(2,1)S(1)}, bf16[256,2048]{1,0:T(8,128)(2,1)S(1)}, u32[]{:S(2)}, u32[]{:S(2)}) collective-permute-start(bf16[256,2048]{1,0:T(8,128)(2,1)S(1)} %collective-permute-done.20.refs_1_.refs_6_.refs_0_.refs_8_), channel_id=1, source_target_pairs={{4,0},{8,4},{12,8},{14,12},{10,14},{6,10},{2,6},{0,2},{1,5},{5,9},... | collective-permute-start | bytes 3145736 | tf_op jit(solution)/shard_map/ppermute | solution.py:373
  154.5 16.6 %collective-permute-start.16 = (f32[1,256]{1,0:T(1,128)S(1)}, f32[1,256]{1,0:T(1,128)S(1)}, u32[]{:S(2)}, u32[]{:S(2)}) collective-permute-start(f32[1,256]{1,0:T(1,128)S(1)} %get-tuple-element.42.total_ref), channel_id=1, source_target_pairs={{0,4},{2,6},{4,0},{6,2},{8,12},{10,14},{12,8},{14,10},{1,5},{3,7},... | collective-permute-start | bytes 3080 | tf_op jit(solution)/shard_map/ppermute | solution.py:375
  172.8 4.8 %collective-permute-start.22 = (bf16[256,2048]{1,0:T(8,128)(2,1)S(1)}, bf16[256,2048]{1,0:T(8,128)(2,1)S(1)}, u32[]{:S(2)}, u32[]{:S(2)}) collective-permute-start(bf16[256,2048]{1,0:T(8,128)(2,1)S(1)} %pick.2), channel_id=1, source_target_pairs={{0,1},{1,0},{2,3},{3,2},{4,5},{5,4},{6,7},{7,6},{8,9},{9,8},{10,11... | collective-permute-start | bytes 3145736 | tf_op jit(solution)/shard_map/ppermute | solution.py:383
  172.8 26.6 %collective-permute-start.19 = (bf16[256,2048]{1,0:T(8,128)(2,1)S(1)}, bf16[256,2048]{1,0:T(8,128)(2,1)S(1)}, u32[]{:S(2)}, u32[]{:S(2)}) collective-permute-start(bf16[256,2048]{1,0:T(8,128)(2,1)S(1)} %get-tuple-element.45.refs_0_.refs_1_), channel_id=1, source_target_pairs={{0,4},{4,8},{8,12},{12,14},{14,10},{10,6},{6,2},{2,0},{5,1},{9,5},... | collective-permute-start | bytes 3145736 | tf_op jit(solution)/shard_map/ppermute | solution.py:372
  174.4 25.0 %collective-permute-start.26 = (bf16[256,2048]{1,0:T(8,128)(2,1)S(1)}, bf16[256,2048]{1,0:T(8,128)(2,1)S(1)}, u32[]{:S(2)}, u32[]{:S(2)}) collective-permute-start(bf16[256,2048]{1,0:T(8,128)(2,1)S(1)} %collective-permute-done.21.refs_1_.refs_0_), channel_id=1, source_target_pairs={{4,0},{8,4},{12,8},{14,12},{10,14},{6,10},{2,6},{0,2},{1,5},{5,9},... | collective-permute-start | bytes 3145736 | tf_op jit(solution)/shard_map/ppermute | solution.py:373
  174.9 24.5 %collective-permute-start.18 = (f32[1,256]{1,0:T(1,128)S(1)}, f32[1,256]{1,0:T(1,128)S(1)}, u32[]{:S(2)}, u32[]{:S(2)}) collective-permute-start(f32[1,256]{1,0:T(1,128)S(1)} %get-tuple-element.44.total_ref), channel_id=1, source_target_pairs={{0,8},{2,10},{4,12},{6,14},{8,0},{10,2},{12,4},{14,6},{1,9},{3,11}... | collective-permute-start | bytes 3080 | tf_op jit(solution)/shard_map/ppermute | solution.py:375
  200.2 5.0 %collective-permute-start.27 = (bf16[256,2048]{1,0:T(8,128)(2,1)S(1)}, bf16[256,2048]{1,0:T(8,128)(2,1)S(1)}, u32[]{:S(2)}, u32[]{:S(2)}) collective-permute-start(bf16[256,2048]{1,0:T(8,128)(2,1)S(1)} %get-tuple-element.48), channel_id=1, source_target_pairs={{0,1},{1,0},{2,3},{3,2},{4,5},{5,4},{6,7},{7,6},{8,9},{9,8},{10,11... | collective-permute-start | bytes 3145736 | tf_op jit(solution)/shard_map/ppermute | solution.py:383
  200.2 4.9 %collective-permute-start.28 = (bf16[256,2048]{1,0:T(8,128)(2,1)S(1)}, bf16[256,2048]{1,0:T(8,128)(2,1)S(1)}, u32[]{:S(2)}, u32[]{:S(2)}) collective-permute-start(bf16[256,2048]{1,0:T(8,128)(2,1)S(1)} %get-tuple-element.49), channel_id=1, source_target_pairs={{0,1},{1,0},{2,3},{3,2},{4,5},{5,4},{6,7},{7,6},{8,9},{9,8},{10,11... | collective-permute-start | bytes 3145736 | tf_op jit(solution)/shard_map/ppermute | solution.py:383
  200.7 17.5 %collective-permute-start.25 = (bf16[256,2048]{1,0:T(8,128)(2,1)S(1)}, bf16[256,2048]{1,0:T(8,128)(2,1)S(1)}, u32[]{:S(2)}, u32[]{:S(2)}) collective-permute-start(bf16[256,2048]{1,0:T(8,128)(2,1)S(1)} %get-tuple-element.58.refs_0_), channel_id=1, source_target_pairs={{0,1},{1,0},{2,3},{3,2},{4,5},{5,4},{6,7},{7,6},{8,9},{9,8},{10,11... | collective-permute-start | bytes 3145736 | tf_op jit(solution)/shard_map/ppermute | solution.py:364
  200.8 17.4 %collective-permute-start.23 = (bf16[256,2048]{1,0:T(8,128)(2,1)S(1)}, bf16[256,2048]{1,0:T(8,128)(2,1)S(1)}, u32[]{:S(2)}, u32[]{:S(2)}) collective-permute-start(bf16[256,2048]{1,0:T(8,128)(2,1)S(1)} %get-tuple-element.47.refs_0_.refs_7_.refs_1_), channel_id=1, source_target_pairs={{0,5},{4,8},{8,12},{12,14},{14,10},{10,7},{6,3},{2,1},{16,21},{20,... | collective-permute-start | bytes 3145736 | tf_op jit(solution)/shard_map/ppermute | solution.py:392
  204.4 13.8 %collective-permute-start.24 = (bf16[256,2048]{1,0:T(8,128)(2,1)S(1)}, bf16[256,2048]{1,0:T(8,128)(2,1)S(1)}, u32[]{:S(2)}, u32[]{:S(2)}) collective-permute-start(bf16[256,2048]{1,0:T(8,128)(2,1)S(1)} %get-tuple-element.47.refs_0_.refs_7_.refs_1_), channel_id=1, source_target_pairs={{5,1},{9,5},{13,8},{15,12},{11,14},{7,10},{3,7},{1,3},{21,17},{25,... | collective-permute-start | bytes 3145736 | tf_op jit(solution)/shard_map/ppermute | solution.py:393
  (9 other events, 36.4 us)

commit v9 on v8

--- a/solution.py
+++ b/solution.py
@@ -28,7 +28,7 @@
     o_ref = refs[-1]
     k_ref, v_ref, pk_ref, pv_ref = own_ref.at[0], own_ref.at[1], far_ref.at[0], far_ref.at[1]
     rows = q_ref.shape[0]
-    inv_root = 1.0 / math.sqrt(HD)
+    scale = math.log2(math.e) / math.sqrt(HD)
     query_pos = lax.broadcasted_iota(jnp.int32, (rows, rows), 0)
     key_pos = lax.broadcasted_iota(jnp.int32, (rows, rows), 1)
     visible = key_pos <= query_pos
@@ -37,13 +37,13 @@
     for head in range(heads):
         columns = slice(head * HD, (head + 1) * HD)
         query = q_ref[:, columns]
-        own = lax.dot_general(query, k_ref[...], contract, preferred_element_type=F32) * inv_root
-        far = lax.dot_general(query, pk_ref[...], contract, preferred_element_type=F32) * inv_root
+        own = lax.dot_general(query, k_ref[...], contract, preferred_element_type=F32)
+        far = lax.dot_general(query, pk_ref[...], contract, preferred_element_type=F32)
         own = jnp.where(visible, own, -1e30)
         far = jnp.where(peer_visible, far, -1e30)
         top = jnp.maximum(jnp.max(own, axis=1, keepdims=True), jnp.max(far, axis=1, keepdims=True))
-        own = jnp.exp(own - top)
-        far = jnp.exp(far - top)
+        own = jnp.exp2((own - top) * scale)
+        far = jnp.exp2((far - top) * scale)
         total = jnp.sum(own, axis=1, keepdims=True) + jnp.sum(far, axis=1, keepdims=True)
         mixed = dot(own.astype(BF16), v_ref[...]) + dot(far.astype(BF16), pv_ref[...])
         o_ref[:, columns] = (mixed / total).astype(BF16)
@@ -337,7 +337,10 @@
         q = half - step + 1 if way == "long" else step - half
         value = partial_sum(q)
         if step > 1:
-            value = value + lax.optimization_barrier((arrived[way], previous))[0].astype(F32)
+            before = arrived[way]
+            if (way, step) == ("short", 2):
+                before = hold(before, [arrived["long"]])
+            value = value + lax.optimization_barrier((before, previous))[0].astype(F32)
         value = value.astype(BF16)
         arrived[way] = lax.ppermute(value, devices, long_way if way == "long" else short_way)
         return value
@@ -347,18 +350,23 @@
     long_value = send("long", 1, None)
     for k in range(half - 1, half // 2, -1):
         make(k, [long_value], [arrived["long"]])
-    value = send("short", 1, long_value)
+    short_value = send("short", 1, long_value)
+    value = send("long", 2, short_value)
     for k in range(2, half // 2 + 1):
-        make(k, [value], [arrived["short"]])
-    value = send("long", 2, value)
+        make(k, [short_value, value])
     for step in range(2, half):
         value = send("short", step, value)
         value = send("long", step + 1, value)
 
     arrived["short"] = hold(arrived["short"], [])
-    mixed = residual.astype(F32) + partial_sum(0) + arrived["long"].astype(F32) + arrived["short"].astype(F32)
+    own_sum = partial_sum(0)
+
+    def mix(long_sum, short_sum):
+        return residual.astype(F32) + own_sum + long_sum.astype(F32) + short_sum.astype(F32)
+
+    scaled = (mix(arrived["long"], arrived["short"]) * norm_gain.astype(F32)).astype(BF16)
+    mixed = mix(*lax.optimization_barrier((arrived["long"], arrived["short"], scaled))[:2])
     resid_out = mixed.astype(BF16)
-    scaled = (mixed * norm_gain.astype(F32)).astype(BF16)
     squares = jnp.sum(mixed * mixed, axis=1)[None]
 
     scaled_peer = lax.ppermute(scaled, "tokens", swap)

time: 231 us -> 237 us (1.026)
    ppermute x3, waiting for transfers between devices: 47.1 us -> 53.5 us  [on_ring(): more = lax.ppermute(squares, 'tensor', [(c, c ^ reach) for c in range(n)])]
    ppermute x7, waiting for transfers between devices: 54.1 us -> 51.4 us  [send(): lax.ppermute(value, devices, long_way if way == 'long' else short_way)]
  transfers between devices with their start and end apart: 30 -> 30, of which waited for: 15 -> 12; matrix products, arithmetic and copies ran while one was open for 2% -> 3% of each run, Pallas kernels for 19% -> 19%
where the time goes in v9:
time: 237 us; the launch traced here: 236 us
  waiting for transfers between devices  111 us (47%)
  Pallas kernels  66.7 us (28%)
  starting transfers between devices  34.3 us (14%)
  between operations  10.8 us (5%)
  other arithmetic  8.56 us (4%)
  local copies, waits for them, and re-layouts  4.1 us (2%)
    ppermute x3, waiting for transfers between devices, on_ring(): more = lax.ppermute(squares, 'tensor', [(c, c ^ reach) for c in range(n)])  53.5 us
    ppermute x7, waiting for transfers between devices, send(): lax.ppermute(value, devices, long_way if way == 'long' else short_way)  51.4 us
    pallas_call x4, Pallas kernels, project(): pl.pallas_call(project_kernel, grid_spec=pltpu.PrefetchScalarGridSpec(num...  30.7 us
    pallas_call x3, Pallas kernels, query_block(): pl.pallas_call(functools.partial(query_kernel, [half + pair for pair, _,...  28.9 us
    ppermute x7, starting transfers between devices, send(): lax.ppermute(value, devices, long_way if way == 'long' else short_way)  10.3 us
    ppermute x3, starting transfers between devices, on_ring(): more = lax.ppermute(squares, 'tensor', [(c, c ^ reach) for c in range(n)])  6.45 us
    ppermute x3, starting transfers between devices, on_ring(): held[-step] = lax.ppermute(held[1 - step], devices, long_way)  5.74 us
    pallas_call x2, Pallas kernels, attention(): pl.pallas_call(functools.partial(attention_kernel, heads), grid_spec=pltp...  5.68 us
  transfers between devices with their start and end apart: 30, of which 12 were waited for; matrix products, arithmetic and copies ran while one was open for 3% of the time, Pallas kernels for 19%

profile of v9, /device:TPU:0, one launch (start us, length us, event | category | flops | bytes accessed | tf_op | source)
XLA Modules:
  0.0 235.6 jit_solution(7788199443340765875)
XLA Ops:
  4.9 2.8 %attention.2.refs_0_ = bf16[256,1024]{1,0:T(8,128)(2,1)S(1)} custom-call(s32[1]{0:T(128)} %bitcast.2.core_ref, bf16[256,2048]{1,0:T(8,128)(2,1)S(1)} %copy-done, bf16[2,256,128]{2,1,0:T(8,128)(2,1)S(1)} %pad_maximum_fusion.own_ref, bf16[2,256,128]{2,1,0:T(8,128)(2,1)S(1)} %collective-permute-done.far_ref), custom_call_target="tpu_custom_call" | custom-call | flops 536870912 | bytes 1048576 | tf_op jit(solution)/shard_map/attention/pallas_call | solution.py:61
  7.8 2.9 %attention.3 = bf16[256,1024]{1,0:T(8,128)(2,1)S(1)} custom-call(s32[1]{0:T(128)} %bitcast.2.core_ref, bf16[256,2048]{1,0:T(8,128)(2,1)S(1)} %copy-done, bf16[2,256,128]{2,1,0:T(8,128)(2,1)S(1)} %pad_maximum_fusion.own_ref, bf16[2,256,128]{2,1,0:T(8,128)(2,1)S(1)} %collective-permute-done.far_ref, bf16[256,1024]{1,0:T(8,128)(2,1)S(1)} %attention.2.refs_0_), custom_call_target="tpu_custom_call" | custom-call | flops 536870912 | bytes 1048576 | tf_op jit(solution)/shard_map/attention/pallas_call | solution.py:61
  13.5 7.7 %project.4 = (bf16[256,2048]{1,0:T(8,128)(2,1)S(1)}, bf16[256,2048]{1,0:T(8,128)(2,1)S(1)}) custom-call(s32[16]{0:T(128)S(1)} %get-tuple-element.65.info_ref, bf16[512,2048]{1,0:T(8,128)(2,1)S(1)} %maximum_maximum_fusion.x_ref, bf16[2048,8192]{1,0:T(8,128)(2,1)} %w_ref.7), custom_call_target="tpu_custom_call" | custom-call | flops 4294967296 | bytes 8388608 | tf_op jit(solution)/shard_map/project/pallas_call | solution.py:92
  24.1 3.0 %collective-permute-start.5 = (bf16[256,2048]{1,0:T(8,128)(2,1)S(1)}, bf16[256,2048]{1,0:T(8,128)(2,1)S(1)}, u32[]{:S(2)}, u32[]{:S(2)}) collective-permute-start(bf16[256,2048]{1,0:T(8,128)(2,1)S(1)} %broadcast_select_fusion.refs_0_), channel_id=1, source_target_pairs={{0,4},{4,8},{8,12},{12,14},{14,10},{10,6},{6,2},{2,0},{5,1},{9,5},... | collective-permute-start | bytes 3145736 | tf_op jit(solution)/shard_map/ppermute | solution.py:345
  27.1 7.7 %project.5 = (bf16[256,2048]{1,0:T(8,128)(2,1)S(1)}, bf16[256,2048]{1,0:T(8,128)(2,1)S(1)}) custom-call(s32[16]{0:T(128)S(1)} %get-tuple-element.65.info_ref, bf16[512,2048]{1,0:T(8,128)(2,1)S(1)} %maximum_maximum_fusion.x_ref, bf16[2048,8192]{1,0:T(8,128)(2,1)} %w_ref.7), custom_call_target="tpu_custom_call" | custom-call | flops 4294967296 | bytes 8388608 | tf_op jit(solution)/shard_map/project/pallas_call | solution.py:92
  34.9 7.7 %project.6 = (bf16[256,2048]{1,0:T(8,128)(2,1)S(1)}, bf16[256,2048]{1,0:T(8,128)(2,1)S(1)}) custom-call(s32[16]{0:T(128)S(1)} %get-tuple-element.65.info_ref, bf16[512,2048]{1,0:T(8,128)(2,1)S(1)} %maximum_maximum_fusion.x_ref, bf16[2048,8192]{1,0:T(8,128)(2,1)} %w_ref.7, bf16[256,2048]{1,0:T(8,128)(2,1)S(1)} %broadcast_select_fusion.refs_0_), custom_call_target="tpu_custom_call" | custom-call | flops 4294967296 | bytes 8388608 | tf_op jit(solution)/shard_map/project/pallas_call | solution.py:92
  50.3 7.7 %project.7 = (bf16[256,2048]{1,0:T(8,128)(2,1)S(1)}, bf16[256,2048]{1,0:T(8,128)(2,1)S(1)}) custom-call(s32[16]{0:T(128)S(1)} %get-tuple-element.65.info_ref, bf16[512,2048]{1,0:T(8,128)(2,1)S(1)} %maximum_maximum_fusion.x_ref, bf16[2048,8192]{1,0:T(8,128)(2,1)} %w_ref.7, bf16[256,2048]{1,0:T(8,128)(2,1)S(1)} %select_select_fusion.refs_0_, ...), custom_call_target="tpu_custom_call" | custom-call | flops 4294967296 | bytes 8388608 | tf_op jit(solution)/shard_map/project/pallas_call | solution.py:92
  58.7 13.7 %collective-permute-done.8.refs_1_ = bf16[256,2048]{1,0:T(8,128)(2,1)S(1)} collective-permute-done((bf16[256,2048]{1,0:T(8,128)(2,1)S(1)}, bf16[256,2048]{1,0:T(8,128)(2,1)S(1)}, u32[]{:S(2)}, u32[]{:S(2)}) %collective-permute-start.8) | collective-permute-done | bytes 1048608 | tf_op jit(solution)/shard_map/ppermute | solution.py:345
  79.7 16.9 %collective-permute-done.11 = bf16[256,2048]{1,0:T(8,128)(2,1)S(1)} collective-permute-done((bf16[256,2048]{1,0:T(8,128)(2,1)S(1)}, bf16[256,2048]{1,0:T(8,128)(2,1)S(1)}, u32[]{:S(2)}, u32[]{:S(2)}) %collective-permute-start.11) | collective-permute-done | bytes 1048608 | tf_op jit(solution)/shard_map/ppermute | solution.py:345
  97.6 2.3 collective-permute-start.13
  102.2 20.8 %collective-permute-done.13.refs_0_ = bf16[256,2048]{1,0:T(8,128)(2,1)S(1)} collective-permute-done((bf16[256,2048]{1,0:T(8,128)(2,1)S(1)}, bf16[256,2048]{1,0:T(8,128)(2,1)S(1)}, u32[]{:S(2)}, u32[]{:S(2)}) %collective-permute-start.13) | collective-permute-done | bytes 1048608 | tf_op jit(solution)/shard_map/ppermute | solution.py:345
  128.4 2.5 %collective-permute-start.14 = (f32[1,256]{1,0:T(1,128)S(1)}, f32[1,256]{1,0:T(1,128)S(1)}, u32[]{:S(2)}, u32[]{:S(2)}) collective-permute-start(f32[1,256]{1,0:T(1,128)S(1)} %bitcast.27), channel_id=1, source_target_pairs={{0,2},{2,0},{4,6},{6,4},{8,10},{10,8},{12,14},{14,12},{1,3},{3,1},... | collective-permute-start | bytes 3080 | tf_op jit(solution)/shard_map/ppermute | solution.py:383
  130.9 18.6 %collective-permute-done.14.more_ref = f32[1,256]{1,0:T(1,128)S(1)} collective-permute-done((f32[1,256]{1,0:T(1,128)S(1)}, f32[1,256]{1,0:T(1,128)S(1)}, u32[]{:S(2)}, u32[]{:S(2)}) %collective-permute-start.14) | collective-permute-done | bytes 1056 | tf_op jit(solution)/shard_map/ppermute | solution.py:383
  149.5 2.9 %collective-permute-start.17 = (bf16[256,2048]{1,0:T(8,128)(2,1)S(1)}, bf16[256,2048]{1,0:T(8,128)(2,1)S(1)}, u32[]{:S(2)}, u32[]{:S(2)}) collective-permute-start(bf16[256,2048]{1,0:T(8,128)(2,1)S(1)} %get-tuple-element.47.refs_3_.refs_4_.refs_2_.refs_6_), channel_id=1, source_target_pairs={{0,4},{4,8},{8,12},{12,14},{14,10},{10,6},{6,2},{2,0},{5,1},{9,5},... | collective-permute-start | bytes 3145736 | tf_op jit(solution)/shard_map/ppermute | solution.py:380
  152.7 2.2 collective-permute-start.16
  154.9 20.8 %collective-permute-done.16.more_ref = f32[1,256]{1,0:T(1,128)S(1)} collective-permute-done((f32[1,256]{1,0:T(1,128)S(1)}, f32[1,256]{1,0:T(1,128)S(1)}, u32[]{:S(2)}, u32[]{:S(2)}) %collective-permute-start.16) | collective-permute-done | bytes 1056 | tf_op jit(solution)/shard_map/ppermute | solution.py:383
  179.4 1.8 collective-permute-start.18
  181.2 7.9 %next_query.3 = (f32[256,2048]{1,0:T(8,128)S(1)}, f32[256,2048]{1,0:T(8,128)S(1)}) custom-call(s32[16]{0:T(128)S(1)} %get-tuple-element.65.info_ref, bf16[256,2048]{1,0:T(8,128)(2,1)S(1)} %collective-permute-done.21.refs_1_.refs_0_, bf16[256,2048]{1,0:T(8,128)(2,1)S(1)} %get-tuple-element.49.refs_0_.refs_1_, ...), custom_call_target="tpu_custom_call" | custom-call | flops 4294967296 | bytes 16777216 | tf_op jit(solution)/shard_map/next_query/pallas_call | solution.py:159
  189.1 14.1 %collective-permute-done.18.more_ref = f32[1,256]{1,0:T(1,128)S(1)} collective-permute-done((f32[1,256]{1,0:T(1,128)S(1)}, f32[1,256]{1,0:T(1,128)S(1)}, u32[]{:S(2)}, u32[]{:S(2)}) %collective-permute-start.18) | collective-permute-done | bytes 1056 | tf_op jit(solution)/shard_map/ppermute | solution.py:383
  204.6 3.6 %collective-permute-start.23 = (bf16[256,2048]{1,0:T(8,128)(2,1)S(1)}, bf16[256,2048]{1,0:T(8,128)(2,1)S(1)}, u32[]{:S(2)}, u32[]{:S(2)}) collective-permute-start(bf16[256,2048]{1,0:T(8,128)(2,1)S(1)} %get-tuple-element.51.refs_0_.refs_7_.refs_1_), channel_id=1, source_target_pairs={{0,5},{4,8},{8,12},{12,14},{14,10},{10,7},{6,3},{2,1},{16,21},{20,... | collective-permute-start | bytes 3145736 | tf_op jit(solution)/shard_map/ppermute | solution.py:400
  209.0 13.0 %next_query.4 = (f32[256,2048]{1,0:T(8,128)S(1)}, f32[256,2048]{1,0:T(8,128)S(1)}) custom-call(s32[16]{0:T(128)S(1)} %get-tuple-element.65.info_ref, bf16[256,2048]{1,0:T(8,128)(2,1)S(1)} %collective-permute-done.20.refs_1_.refs_6_.refs_0_.refs_8_, bf16[256,2048]{1,0:T(8,128)(2,1)S(1)} %get-tuple-element.51.refs_0_.refs_7_.refs_1_, ...), custom_call_target="tpu_custom_call" | custom-call | flops 8589934592 | bytes 25165824 | tf_op jit(solution)/shard_map/next_query/pallas_call | solution.py:159
  222.0 8.0 %next_query.5 = (f32[256,2048]{1,0:T(8,128)S(1)}, bf16[256,2048]{1,0:T(8,128)(2,1)S(1)}) custom-call(s32[16]{0:T(128)S(1)} %get-tuple-element.65.info_ref, bf16[256,2048]{1,0:T(8,128)(2,1)S(1)} %get-tuple-element.60.refs_0_, bf16[256,2048]{1,0:T(8,128)(2,1)S(1)} %collective-permute-done.23.refs_1_.refs_5_, ...), custom_call_target="tpu_custom_call" | custom-call | flops 4294967296 | bytes 16777216 | tf_op jit(solution)/shard_map/next_query/pallas_call | solution.py:159
  230.0 2.0 collective-permute-start.29
  232.1 2.3 collective-permute-done.29
  (78 shorter events, 32.1 us)
Async XLA Ops:
  24.1 18.4 %collective-permute-start.5 = (bf16[256,2048]{1,0:T(8,128)(2,1)S(1)}, bf16[256,2048]{1,0:T(8,128)(2,1)S(1)}, u32[]{:S(2)}, u32[]{:S(2)}) collective-permute-start(bf16[256,2048]{1,0:T(8,128)(2,1)S(1)} %broadcast_select_fusion.refs_0_), channel_id=1, source_target_pairs={{0,4},{4,8},{8,12},{12,14},{14,10},{10,6},{6,2},{2,0},{5,1},{9,5},... | collective-permute-start | bytes 3145736 | tf_op jit(solution)/shard_map/ppermute | solution.py:345
  34.8 12.1 %collective-permute-start.4 = (bf16[256,2048]{1,0:T(8,128)(2,1)S(1)}, bf16[256,2048]{1,0:T(8,128)(2,1)S(1)}, u32[]{:S(2)}, u32[]{:S(2)}) collective-permute-start(bf16[256,2048]{1,0:T(8,128)(2,1)S(1)} %get-tuple-element.34), channel_id=1, source_target_pairs={{0,1},{1,0},{2,3},{3,2},{4,5},{5,4},{6,7},{7,6},{8,9},{9,8},{10,11... | collective-permute-start | bytes 3145736 | tf_op jit(solution)/shard_map/ppermute | solution.py:329
  42.6 4.4 %collective-permute-start.6 = (bf16[256,2048]{1,0:T(8,128)(2,1)S(1)}, bf16[256,2048]{1,0:T(8,128)(2,1)S(1)}, u32[]{:S(2)}, u32[]{:S(2)}) collective-permute-start(bf16[256,2048]{1,0:T(8,128)(2,1)S(1)} %hold.3), channel_id=1, source_target_pairs={{0,1},{1,0},{2,3},{3,2},{4,5},{5,4},{6,7},{7,6},{8,9},{9,8},{10,11... | collective-permute-start | bytes 3145736 | tf_op jit(solution)/shard_map/ppermute | solution.py:329
  47.2 25.1 %collective-permute-start.9 = (bf16[256,2048]{1,0:T(8,128)(2,1)S(1)}, bf16[256,2048]{1,0:T(8,128)(2,1)S(1)}, u32[]{:S(2)}, u32[]{:S(2)}) collective-permute-start(bf16[256,2048]{1,0:T(8,128)(2,1)S(1)} %select_select_fusion.refs_0_), channel_id=1, source_target_pairs={{4,0},{8,4},{12,8},{14,12},{10,14},{6,10},{2,6},{0,2},{1,5},{5,9},... | collective-permute-start | bytes 3145736 | tf_op jit(solution)/shard_map/ppermute | solution.py:345
  49.0 23.3 %collective-permute-start.8 = (bf16[256,2048]{1,0:T(8,128)(2,1)S(1)}, bf16[256,2048]{1,0:T(8,128)(2,1)S(1)}, u32[]{:S(2)}, u32[]{:S(2)}) collective-permute-start(bf16[256,2048]{1,0:T(8,128)(2,1)S(1)} %add_convert_fusion.4.refs_1_), channel_id=1, source_target_pairs={{0,4},{4,8},{8,12},{12,14},{14,10},{10,6},{6,2},{2,0},{5,1},{9,5},... | collective-permute-start | bytes 3145736 | tf_op jit(solution)/shard_map/ppermute | solution.py:345
  57.9 14.4 %collective-permute-start.7 = (bf16[256,2048]{1,0:T(8,128)(2,1)S(1)}, bf16[256,2048]{1,0:T(8,128)(2,1)S(1)}, u32[]{:S(2)}, u32[]{:S(2)}) collective-permute-start(bf16[256,2048]{1,0:T(8,128)(2,1)S(1)} %get-tuple-element.39), channel_id=1, source_target_pairs={{0,1},{1,0},{2,3},{3,2},{4,5},{5,4},{6,7},{7,6},{8,9},{9,8},{10,11... | collective-permute-start | bytes 3145736 | tf_op jit(solution)/shard_map/ppermute | solution.py:329
  72.9 23.7 %collective-permute-start.11 = (bf16[256,2048]{1,0:T(8,128)(2,1)S(1)}, bf16[256,2048]{1,0:T(8,128)(2,1)S(1)}, u32[]{:S(2)}, u32[]{:S(2)}) collective-permute-start(bf16[256,2048]{1,0:T(8,128)(2,1)S(1)} %add_convert_fusion.3), channel_id=1, source_target_pairs={{4,0},{8,4},{12,8},{14,12},{10,14},{6,10},{2,6},{0,2},{1,5},{5,9},... | collective-permute-start | bytes 3145736 | tf_op jit(solution)/shard_map/ppermute | solution.py:345
  75.5 24.4 %collective-permute-start.10 = (bf16[256,2048]{1,0:T(8,128)(2,1)S(1)}, bf16[256,2048]{1,0:T(8,128)(2,1)S(1)}, u32[]{:S(2)}, u32[]{:S(2)}) collective-permute-start(bf16[256,2048]{1,0:T(8,128)(2,1)S(1)} %add_convert_fusion.2), channel_id=1, source_target_pairs={{0,4},{4,8},{8,12},{12,14},{14,10},{10,6},{6,2},{2,0},{5,1},{9,5},... | collective-permute-start | bytes 3145736 | tf_op jit(solution)/shard_map/ppermute | solution.py:345
  97.6 25.4 %collective-permute-start.13 = (bf16[256,2048]{1,0:T(8,128)(2,1)S(1)}, bf16[256,2048]{1,0:T(8,128)(2,1)S(1)}, u32[]{:S(2)}, u32[]{:S(2)}) collective-permute-start(bf16[256,2048]{1,0:T(8,128)(2,1)S(1)} %add_convert_fusion.1), channel_id=1, source_target_pairs={{4,0},{8,4},{12,8},{14,12},{10,14},{6,10},{2,6},{0,2},{1,5},{5,9},... | collective-permute-start | bytes 3145736 | tf_op jit(solution)/shard_map/ppermute | solution.py:345
  100.8 22.2 %collective-permute-start.12 = (bf16[256,2048]{1,0:T(8,128)(2,1)S(1)}, bf16[256,2048]{1,0:T(8,128)(2,1)S(1)}, u32[]{:S(2)}, u32[]{:S(2)}) collective-permute-start(bf16[256,2048]{1,0:T(8,128)(2,1)S(1)} %add_convert_fusion), channel_id=1, source_target_pairs={{0,4},{4,8},{8,12},{12,14},{14,10},{10,6},{6,2},{2,0},{5,1},{9,5},... | collective-permute-start | bytes 3145736 | tf_op jit(solution)/shard_map/ppermute | solution.py:345
  124.1 25.4 %collective-permute-start.15 = (bf16[256,2048]{1,0:T(8,128)(2,1)S(1)}, bf16[256,2048]{1,0:T(8,128)(2,1)S(1)}, u32[]{:S(2)}, u32[]{:S(2)}) collective-permute-start(bf16[256,2048]{1,0:T(8,128)(2,1)S(1)} %get-tuple-element.60.refs_0_), channel_id=1, source_target_pairs={{0,4},{4,8},{8,12},{12,14},{14,10},{10,6},{6,2},{2,0},{5,1},{9,5},... | collective-permute-start | bytes 3145736 | tf_op jit(solution)/shard_map/ppermute | solution.py:380
  125.8 26.6 %collective-permute-start.20 = (bf16[256,2048]{1,0:T(8,128)(2,1)S(1)}, bf16[256,2048]{1,0:T(8,128)(2,1)S(1)}, u32[]{:S(2)}, u32[]{:S(2)}) collective-permute-start(bf16[256,2048]{1,0:T(8,128)(2,1)S(1)} %get-tuple-element.60.refs_0_), channel_id=1, source_target_pairs={{4,0},{8,4},{12,8},{14,12},{10,14},{6,10},{2,6},{0,2},{1,5},{5,9},... | collective-permute-start | bytes 3145736 | tf_op jit(solution)/shard_map/ppermute | solution.py:381
  128.4 21.1 %collective-permute-start.14 = (f32[1,256]{1,0:T(1,128)S(1)}, f32[1,256]{1,0:T(1,128)S(1)}, u32[]{:S(2)}, u32[]{:S(2)}) collective-permute-start(f32[1,256]{1,0:T(1,128)S(1)} %bitcast.27), channel_id=1, source_target_pairs={{0,2},{2,0},{4,6},{6,4},{8,10},{10,8},{12,14},{14,12},{1,3},{3,1},... | collective-permute-start | bytes 3080 | tf_op jit(solution)/shard_map/ppermute | solution.py:383
  149.5 26.8 %collective-permute-start.17 = (bf16[256,2048]{1,0:T(8,128)(2,1)S(1)}, bf16[256,2048]{1,0:T(8,128)(2,1)S(1)}, u32[]{:S(2)}, u32[]{:S(2)}) collective-permute-start(bf16[256,2048]{1,0:T(8,128)(2,1)S(1)} %get-tuple-element.47.refs_3_.refs_4_.refs_2_.refs_6_), channel_id=1, source_target_pairs={{0,4},{4,8},{8,12},{12,14},{14,10},{10,6},{6,2},{2,0},{5,1},{9,5},... | collective-permute-start | bytes 3145736 | tf_op jit(solution)/shard_map/ppermute | solution.py:380
  152.4 23.9 %collective-permute-start.21 = (bf16[256,2048]{1,0:T(8,128)(2,1)S(1)}, bf16[256,2048]{1,0:T(8,128)(2,1)S(1)}, u32[]{:S(2)}, u32[]{:S(2)}) collective-permute-start(bf16[256,2048]{1,0:T(8,128)(2,1)S(1)} %collective-permute-done.20.refs_1_.refs_6_.refs_0_.refs_8_), channel_id=1, source_target_pairs={{4,0},{8,4},{12,8},{14,12},{10,14},{6,10},{2,6},{0,2},{1,5},{5,9},... | collective-permute-start | bytes 3145736 | tf_op jit(solution)/shard_map/ppermute | solution.py:381
  152.7 23.0 %collective-permute-start.16 = (f32[1,256]{1,0:T(1,128)S(1)}, f32[1,256]{1,0:T(1,128)S(1)}, u32[]{:S(2)}, u32[]{:S(2)}) collective-permute-start(f32[1,256]{1,0:T(1,128)S(1)} %get-tuple-element.46.total_ref), channel_id=1, source_target_pairs={{0,4},{2,6},{4,0},{6,2},{8,12},{10,14},{12,8},{14,10},{1,5},{3,7},... | collective-permute-start | bytes 3080 | tf_op jit(solution)/shard_map/ppermute | solution.py:383
  177.0 26.2 %collective-permute-start.19 = (bf16[256,2048]{1,0:T(8,128)(2,1)S(1)}, bf16[256,2048]{1,0:T(8,128)(2,1)S(1)}, u32[]{:S(2)}, u32[]{:S(2)}) collective-permute-start(bf16[256,2048]{1,0:T(8,128)(2,1)S(1)} %get-tuple-element.49.refs_0_.refs_1_), channel_id=1, source_target_pairs={{0,4},{4,8},{8,12},{12,14},{14,10},{10,6},{6,2},{2,0},{5,1},{9,5},... | collective-permute-start | bytes 3145736 | tf_op jit(solution)/shard_map/ppermute | solution.py:380
  178.2 25.0 %collective-permute-start.26 = (bf16[256,2048]{1,0:T(8,128)(2,1)S(1)}, bf16[256,2048]{1,0:T(8,128)(2,1)S(1)}, u32[]{:S(2)}, u32[]{:S(2)}) collective-permute-start(bf16[256,2048]{1,0:T(8,128)(2,1)S(1)} %collective-permute-done.21.refs_1_.refs_0_), channel_id=1, source_target_pairs={{4,0},{8,4},{12,8},{14,12},{10,14},{6,10},{2,6},{0,2},{1,5},{5,9},... | collective-permute-start | bytes 3145736 | tf_op jit(solution)/shard_map/ppermute | solution.py:381
  179.4 23.8 %collective-permute-start.18 = (f32[1,256]{1,0:T(1,128)S(1)}, f32[1,256]{1,0:T(1,128)S(1)}, u32[]{:S(2)}, u32[]{:S(2)}) collective-permute-start(f32[1,256]{1,0:T(1,128)S(1)} %get-tuple-element.48.total_ref), channel_id=1, source_target_pairs={{0,8},{2,10},{4,12},{6,14},{8,0},{10,2},{12,4},{14,6},{1,9},{3,11}... | collective-permute-start | bytes 3080 | tf_op jit(solution)/shard_map/ppermute | solution.py:383
  203.9 5.1 %collective-permute-start.27 = (bf16[256,2048]{1,0:T(8,128)(2,1)S(1)}, bf16[256,2048]{1,0:T(8,128)(2,1)S(1)}, u32[]{:S(2)}, u32[]{:S(2)}) collective-permute-start(bf16[256,2048]{1,0:T(8,128)(2,1)S(1)} %get-tuple-element.52), channel_id=1, source_target_pairs={{0,1},{1,0},{2,3},{3,2},{4,5},{5,4},{6,7},{7,6},{8,9},{9,8},{10,11... | collective-permute-start | bytes 3145736 | tf_op jit(solution)/shard_map/ppermute | solution.py:391
  204.1 4.9 %collective-permute-start.28 = (bf16[256,2048]{1,0:T(8,128)(2,1)S(1)}, bf16[256,2048]{1,0:T(8,128)(2,1)S(1)}, u32[]{:S(2)}, u32[]{:S(2)}) collective-permute-start(bf16[256,2048]{1,0:T(8,128)(2,1)S(1)} %get-tuple-element.53), channel_id=1, source_target_pairs={{0,1},{1,0},{2,3},{3,2},{4,5},{5,4},{6,7},{7,6},{8,9},{9,8},{10,11... | collective-permute-start | bytes 3145736 | tf_op jit(solution)/shard_map/ppermute | solution.py:391
  204.5 17.5 %collective-permute-start.25 = (bf16[256,2048]{1,0:T(8,128)(2,1)S(1)}, bf16[256,2048]{1,0:T(8,128)(2,1)S(1)}, u32[]{:S(2)}, u32[]{:S(2)}) collective-permute-start(bf16[256,2048]{1,0:T(8,128)(2,1)S(1)} %get-tuple-element.60.refs_0_), channel_id=1, source_target_pairs={{0,1},{1,0},{2,3},{3,2},{4,5},{5,4},{6,7},{7,6},{8,9},{9,8},{10,11... | collective-permute-start | bytes 3145736 | tf_op jit(solution)/shard_map/ppermute | solution.py:372
  204.6 17.4 %collective-permute-start.23 = (bf16[256,2048]{1,0:T(8,128)(2,1)S(1)}, bf16[256,2048]{1,0:T(8,128)(2,1)S(1)}, u32[]{:S(2)}, u32[]{:S(2)}) collective-permute-start(bf16[256,2048]{1,0:T(8,128)(2,1)S(1)} %get-tuple-element.51.refs_0_.refs_7_.refs_1_), channel_id=1, source_target_pairs={{0,5},{4,8},{8,12},{12,14},{14,10},{10,7},{6,3},{2,1},{16,21},{20,... | collective-permute-start | bytes 3145736 | tf_op jit(solution)/shard_map/ppermute | solution.py:400
  208.2 13.8 %collective-permute-start.24 = (bf16[256,2048]{1,0:T(8,128)(2,1)S(1)}, bf16[256,2048]{1,0:T(8,128)(2,1)S(1)}, u32[]{:S(2)}, u32[]{:S(2)}) collective-permute-start(bf16[256,2048]{1,0:T(8,128)(2,1)S(1)} %get-tuple-element.51.refs_0_.refs_7_.refs_1_), channel_id=1, source_target_pairs={{5,1},{9,5},{13,8},{15,12},{11,14},{7,10},{3,7},{1,3},{21,17},{25,... | collective-permute-start | bytes 3145736 | tf_op jit(solution)/shard_map/ppermute | solution.py:401
  (9 other events, 42.9 us)

commit v10 on v9

--- a/solution.py
+++ b/solution.py
@@ -256,7 +256,8 @@
     half = n // 2
     ring = ring_of(n)
     place = {chip: p for p, chip in enumerate(ring)}
-    table = np.zeros((n, 2, 2 * half + n), np.int32)
+    table = np.zeros((n, 2, 2 * half), np.int32)
+    flags = np.zeros((n, 2, 4 * n), bool)
     for chip in range(n):
         for core in range(2):
 
@@ -275,8 +276,8 @@
             for q in range(1 - half, half + 1):
                 real = q if core == 0 else -q
                 pair = (real % half, 0 if is_mine(real) else 1)
-                table[chip, core, 2 * half + q + half - 1] = sum_choices(q, half).index(pair)
-    return table.reshape(2 * n, -1)
+                flags[chip, core, 4 * (q + half - 1) + sum_choices(q, half).index(pair)] = True
+    return table.reshape(2 * n, -1), flags.reshape(2 * n, -1)
 
 
 def block_choices(k, half):
@@ -287,10 +288,10 @@
     return [(k, kind) for k in dict.fromkeys([q % half, -q % half]) for kind in (0, 1)]
 
 
-def choose(code, arrays):
+def choose(flags, arrays):
     result = arrays[-1]
     for index in reversed(range(len(arrays) - 1)):
-        result = jnp.where(code == index, arrays[index], result)
+        result = jnp.where(flags[index], arrays[index], result)
     return result
 
 
@@ -305,7 +306,9 @@
     chip = lax.axis_index("tensor")
     core = lax.axis_index("tokens")
     rows, width = att_queries.shape
-    info = lax.dynamic_index_in_dim(jnp.asarray(tables(n)), chip * 2 + core, 0, keepdims=False)
+    info, flags = (
+        lax.dynamic_index_in_dim(jnp.asarray(table), chip * 2 + core, 0, keepdims=False) for table in tables(n)
+    )
 
     heads_here = width // HD
     kv_head = chip * heads_here // (H // KVH)
@@ -329,7 +332,7 @@
         made[k, 1] = lax.ppermute(outgoing, "tokens", swap)
 
     def partial_sum(q):
-        return choose(info[2 * half + q + half - 1], [made[key] for key in sum_choices(q, half)]).astype(F32)
+        return choose(flags[4 * (q + half - 1) :], [made[key] for key in sum_choices(q, half)]).astype(F32)
 
     arrived = {}
 
@@ -359,14 +362,9 @@
         value = send("long", step + 1, value)
 
     arrived["short"] = hold(arrived["short"], [])
-    own_sum = partial_sum(0)
-
-    def mix(long_sum, short_sum):
-        return residual.astype(F32) + own_sum + long_sum.astype(F32) + short_sum.astype(F32)
-
-    scaled = (mix(arrived["long"], arrived["short"]) * norm_gain.astype(F32)).astype(BF16)
-    mixed = mix(*lax.optimization_barrier((arrived["long"], arrived["short"], scaled))[:2])
+    mixed = residual.astype(F32) + partial_sum(0) + arrived["long"].astype(F32) + arrived["short"].astype(F32)
     resid_out = mixed.astype(BF16)
+    scaled = (mixed * norm_gain.astype(F32)).astype(BF16)
     squares = jnp.sum(mixed * mixed, axis=1)[None]
 
     scaled_peer = lax.ppermute(scaled, "tokens", swap)

time: 237 us -> 242 us (1.021)
  between operations: 10.8 us -> 0.95 us
  other arithmetic: 8.56 us -> 17.9 us
  waiting for transfers between devices: 111 us -> 116 us
    convert_element_type x5, other arithmetic: 3.89 us -> 10.8 us  [send(): value = value.astype(BF16)]
    ppermute x3, waiting for transfers between devices: 53.5 us -> 56.2 us  [on_ring(): more = lax.ppermute(squares, 'tensor', [(c, c ^ reach) for c in range(n)])]
  transfers between devices with their start and end apart: 30 -> 30, of which waited for: 12 -> 14; matrix products, arithmetic and copies ran while one was open for 3% -> 5% of each run, Pallas kernels for 19% -> 18%
where the time goes in v10:
time: 242 us; the launch traced here: 240 us
  waiting for transfers between devices  116 us (48%)
  Pallas kernels  66.7 us (28%)
  starting transfers between devices  33.4 us (14%)
  other arithmetic  17.9 us (7%)
  local copies, waits for them, and re-layouts  4.82 us (2%)
    ppermute x3, waiting for transfers between devices, on_ring(): more = lax.ppermute(squares, 'tensor', [(c, c ^ reach) for c in range(n)])  56.2 us
    ppermute x7, waiting for transfers between devices, send(): lax.ppermute(value, devices, long_way if way == 'long' else short_way)  52.2 us
    pallas_call x4, Pallas kernels, project(): pl.pallas_call(project_kernel, grid_spec=pltpu.PrefetchScalarGridSpec(num...  30.7 us
    pallas_call x3, Pallas kernels, query_block(): pl.pallas_call(functools.partial(query_kernel, [half + pair for pair, _,...  28.9 us
    convert_element_type x5, other arithmetic, send(): value = value.astype(BF16)  10.8 us
    ppermute x7, starting transfers between devices, send(): lax.ppermute(value, devices, long_way if way == 'long' else short_way)  9.56 us
    ppermute x3, starting transfers between devices, on_ring(): more = lax.ppermute(squares, 'tensor', [(c, c ^ reach) for c in range(n)])  6.71 us
    pallas_call x2, Pallas kernels, attention(): pl.pallas_call(functools.partial(attention_kernel, heads), grid_spec=pltp...  5.68 us
  transfers between devices with their start and end apart: 30, of which 14 were waited for; matrix products, arithmetic and copies ran while one was open for 5% of the time, Pallas kernels for 18%

profile of v10, /device:TPU:0, one launch (start us, length us, event | category | flops | bytes accessed | tf_op | source)
XLA Modules:
  0.0 240.1 jit_solution(1929389342271869608)
XLA Ops:
  4.9 2.8 %attention.2.refs_0_ = bf16[256,1024]{1,0:T(8,128)(2,1)S(1)} custom-call(s32[1]{0:T(128)} %bitcast.2.core_ref, bf16[256,2048]{1,0:T(8,128)(2,1)S(1)} %copy-done, bf16[2,256,128]{2,1,0:T(8,128)(2,1)S(1)} %pad_maximum_fusion.own_ref, bf16[2,256,128]{2,1,0:T(8,128)(2,1)S(1)} %collective-permute-done.far_ref), custom_call_target="tpu_custom_call" | custom-call | flops 536870912 | bytes 1048576 | tf_op jit(solution)/shard_map/attention/pallas_call | solution.py:61
  7.8 2.9 %attention.3 = bf16[256,1024]{1,0:T(8,128)(2,1)S(1)} custom-call(s32[1]{0:T(128)} %bitcast.2.core_ref, bf16[256,2048]{1,0:T(8,128)(2,1)S(1)} %copy-done, bf16[2,256,128]{2,1,0:T(8,128)(2,1)S(1)} %pad_maximum_fusion.own_ref, bf16[2,256,128]{2,1,0:T(8,128)(2,1)S(1)} %collective-permute-done.far_ref, bf16[256,1024]{1,0:T(8,128)(2,1)S(1)} %attention.2.refs_0_), custom_call_target="tpu_custom_call" | custom-call | flops 536870912 | bytes 1048576 | tf_op jit(solution)/shard_map/attention/pallas_call | solution.py:61
  13.5 7.7 %project.4 = (bf16[256,2048]{1,0:T(8,128)(2,1)S(1)}, bf16[256,2048]{1,0:T(8,128)(2,1)S(1)}) custom-call(s32[8]{0:T(128)S(1)} %fusion.info_ref, bf16[512,2048]{1,0:T(8,128)(2,1)S(1)} %maximum_maximum_fusion.x_ref, bf16[2048,8192]{1,0:T(8,128)(2,1)} %w_ref.7), custom_call_target="tpu_custom_call" | custom-call | flops 4294967296 | bytes 8388608 | tf_op jit(solution)/shard_map/project/pallas_call | solution.py:92
  24.7 3.0 %collective-permute-start.5 = (bf16[256,2048]{1,0:T(8,128)(2,1)S(1)}, bf16[256,2048]{1,0:T(8,128)(2,1)S(1)}, u32[]{:S(2)}, u32[]{:S(2)}) collective-permute-start(bf16[256,2048]{1,0:T(8,128)(2,1)S(1)} %broadcast_select_fusion.refs_0_), channel_id=1, source_target_pairs={{0,4},{4,8},{8,12},{12,14},{14,10},{10,6},{6,2},{2,0},{5,1},{9,5},... | collective-permute-start | bytes 3145736 | tf_op jit(solution)/shard_map/ppermute | solution.py:348
  27.7 7.7 %project.5 = (bf16[256,2048]{1,0:T(8,128)(2,1)S(1)}, bf16[256,2048]{1,0:T(8,128)(2,1)S(1)}) custom-call(s32[8]{0:T(128)S(1)} %fusion.info_ref, bf16[512,2048]{1,0:T(8,128)(2,1)S(1)} %maximum_maximum_fusion.x_ref, bf16[2048,8192]{1,0:T(8,128)(2,1)} %w_ref.7), custom_call_target="tpu_custom_call" | custom-call | flops 4294967296 | bytes 8388608 | tf_op jit(solution)/shard_map/project/pallas_call | solution.py:92
  35.5 7.7 %project.6 = (bf16[256,2048]{1,0:T(8,128)(2,1)S(1)}, bf16[256,2048]{1,0:T(8,128)(2,1)S(1)}) custom-call(s32[8]{0:T(128)S(1)} %fusion.info_ref, bf16[512,2048]{1,0:T(8,128)(2,1)S(1)} %maximum_maximum_fusion.x_ref, bf16[2048,8192]{1,0:T(8,128)(2,1)} %w_ref.7, bf16[256,2048]{1,0:T(8,128)(2,1)S(1)} %broadcast_select_fusion.refs_0_), custom_call_target="tpu_custom_call" | custom-call | flops 4294967296 | bytes 8388608 | tf_op jit(solution)/shard_map/project/pallas_call | solution.py:92
  43.7 2.3 collective-permute-done.6
  49.4 2.7 %add_convert_fusion.4.refs_1_ = bf16[256,2048]{1,0:T(8,128)(2,1)S(1)} fusion(bf16[256,2048]{1,0:T(8,128)(2,1)S(1)} %collective-permute-done.5.refs_1_, bf16[256,2048]{1,0:T(8,128)(2,1)S(1)} %get-tuple-element.33, bf16[256,2048]{1,0:T(8,128)(2,1)S(1)} %collective-permute-done.6, bf16[256,2048]{1,0:T(8,128)(2,1)S(1)} %get-tuple-element.31, ...), kind=kLoop, calls=%fused_computation.9 | loop fusion | flops 3670016 | bytes 6291459 | tf_op jit(solution)/shard_map/convert_element_type | solution.py:347
  53.0 7.7 %project.7 = (bf16[256,2048]{1,0:T(8,128)(2,1)S(1)}, bf16[256,2048]{1,0:T(8,128)(2,1)S(1)}) custom-call(s32[8]{0:T(128)S(1)} %fusion.info_ref, bf16[512,2048]{1,0:T(8,128)(2,1)S(1)} %maximum_maximum_fusion.x_ref, bf16[2048,8192]{1,0:T(8,128)(2,1)} %w_ref.7, bf16[256,2048]{1,0:T(8,128)(2,1)S(1)} %select_select_fusion.refs_0_, ...), custom_call_target="tpu_custom_call" | custom-call | flops 4294967296 | bytes 8388608 | tf_op jit(solution)/shard_map/project/pallas_call | solution.py:92
  60.7 12.9 %collective-permute-done.8.refs_1_ = bf16[256,2048]{1,0:T(8,128)(2,1)S(1)} collective-permute-done((bf16[256,2048]{1,0:T(8,128)(2,1)S(1)}, bf16[256,2048]{1,0:T(8,128)(2,1)S(1)}, u32[]{:S(2)}, u32[]{:S(2)}) %collective-permute-start.8) | collective-permute-done | bytes 1048608 | tf_op jit(solution)/shard_map/ppermute | solution.py:348
  78.2 20.6 %collective-permute-done.11 = bf16[256,2048]{1,0:T(8,128)(2,1)S(1)} collective-permute-done((bf16[256,2048]{1,0:T(8,128)(2,1)S(1)}, bf16[256,2048]{1,0:T(8,128)(2,1)S(1)}, u32[]{:S(2)}, u32[]{:S(2)}) %collective-permute-start.11) | collective-permute-done | bytes 1048608 | tf_op jit(solution)/shard_map/ppermute | solution.py:348
  98.8 2.8 %add_convert_fusion.1 = bf16[256,2048]{1,0:T(8,128)(2,1)S(1)} fusion(bf16[256,2048]{1,0:T(8,128)(2,1)S(1)} %collective-permute-done.11, bf16[256,2048]{1,0:T(8,128)(2,1)S(1)} %get-tuple-element.33, bf16[256,2048]{1,0:T(8,128)(2,1)S(1)} %collective-permute-done.6, bf16[256,2048]{1,0:T(8,128)(2,1)S(1)} %get-tuple-element.31, ...), kind=kLoop, calls=%fused_computation.6 | loop fusion | flops 3670016 | bytes 6291459 | tf_op jit(solution)/shard_map/convert_element_type | solution.py:347
  103.1 2.9 %add_convert_fusion = bf16[256,2048]{1,0:T(8,128)(2,1)S(1)} fusion(bf16[256,2048]{1,0:T(8,128)(2,1)S(1)} %collective-permute-done.10, bf16[256,2048]{1,0:T(8,128)(2,1)S(1)} %get-tuple-element.31, bf16[256,2048]{1,0:T(8,128)(2,1)S(1)} %collective-permute-done.4, bf16[256,2048]{1,0:T(8,128)(2,1)S(1)} %get-tuple-element.33, ...), kind=kLoop, calls=%fused_computation.5 | loop fusion | flops 3670016 | bytes 6291459 | tf_op jit(solution)/shard_map/convert_element_type | solution.py:347
  106.7 18.4 %collective-permute-done.13.refs_0_ = bf16[256,2048]{1,0:T(8,128)(2,1)S(1)} collective-permute-done((bf16[256,2048]{1,0:T(8,128)(2,1)S(1)}, bf16[256,2048]{1,0:T(8,128)(2,1)S(1)}, u32[]{:S(2)}, u32[]{:S(2)}) %collective-permute-start.13) | collective-permute-done | bytes 1048608 | tf_op jit(solution)/shard_map/ppermute | solution.py:348
  131.2 2.5 %collective-permute-start.14 = (f32[1,256]{1,0:T(1,128)S(1)}, f32[1,256]{1,0:T(1,128)S(1)}, u32[]{:S(2)}, u32[]{:S(2)}) collective-permute-start(f32[1,256]{1,0:T(1,128)S(1)} %bitcast.27), channel_id=1, source_target_pairs={{0,2},{2,0},{4,6},{6,4},{8,10},{10,8},{12,14},{14,12},{1,3},{3,1},... | collective-permute-start | bytes 3080 | tf_op jit(solution)/shard_map/ppermute | solution.py:381
  133.6 20.8 %collective-permute-done.14.more_ref = f32[1,256]{1,0:T(1,128)S(1)} collective-permute-done((f32[1,256]{1,0:T(1,128)S(1)}, f32[1,256]{1,0:T(1,128)S(1)}, u32[]{:S(2)}, u32[]{:S(2)}) %collective-permute-start.14) | collective-permute-done | bytes 1056 | tf_op jit(solution)/shard_map/ppermute | solution.py:381
  158.8 21.6 %collective-permute-done.16.more_ref = f32[1,256]{1,0:T(1,128)S(1)} collective-permute-done((f32[1,256]{1,0:T(1,128)S(1)}, f32[1,256]{1,0:T(1,128)S(1)}, u32[]{:S(2)}, u32[]{:S(2)}) %collective-permute-start.16) | collective-permute-done | bytes 1056 | tf_op jit(solution)/shard_map/ppermute | solution.py:381
  183.8 2.4 collective-permute-start.18
  186.2 7.9 %next_query.3 = (f32[256,2048]{1,0:T(8,128)S(1)}, f32[256,2048]{1,0:T(8,128)S(1)}) custom-call(s32[8]{0:T(128)S(1)} %fusion.info_ref, bf16[256,2048]{1,0:T(8,128)(2,1)S(1)} %collective-permute-done.21.refs_1_.refs_0_, bf16[256,2048]{1,0:T(8,128)(2,1)S(1)} %get-tuple-element.45.refs_0_.refs_1_, bf16[256,2048]{1,0:T(8,128)(2,1)S(1)} %collective-permute-done.22.refs_2_, ...), custom_call_target="tpu_custom_call" | custom-call | flops 4294967296 | bytes 16777216 | tf_op jit(solution)/shard_map/next_query/pallas_call | solution.py:159
  194.1 13.9 %collective-permute-done.18.more_ref = f32[1,256]{1,0:T(1,128)S(1)} collective-permute-done((f32[1,256]{1,0:T(1,128)S(1)}, f32[1,256]{1,0:T(1,128)S(1)}, u32[]{:S(2)}, u32[]{:S(2)}) %collective-permute-start.18) | collective-permute-done | bytes 1056 | tf_op jit(solution)/shard_map/ppermute | solution.py:381
  209.4 3.8 %collective-permute-start.23 = (bf16[256,2048]{1,0:T(8,128)(2,1)S(1)}, bf16[256,2048]{1,0:T(8,128)(2,1)S(1)}, u32[]{:S(2)}, u32[]{:S(2)}) collective-permute-start(bf16[256,2048]{1,0:T(8,128)(2,1)S(1)} %get-tuple-element.47.refs_0_.refs_7_.refs_1_), channel_id=1, source_target_pairs={{0,5},{4,8},{8,12},{12,14},{14,10},{10,7},{6,3},{2,1},{16,21},{20,... | collective-permute-start | bytes 3145736 | tf_op jit(solution)/shard_map/ppermute | solution.py:398
  214.0 13.0 %next_query.4 = (f32[256,2048]{1,0:T(8,128)S(1)}, f32[256,2048]{1,0:T(8,128)S(1)}) custom-call(s32[8]{0:T(128)S(1)} %fusion.info_ref, bf16[256,2048]{1,0:T(8,128)(2,1)S(1)} %collective-permute-done.20.refs_1_.refs_6_.refs_0_.refs_8_, bf16[256,2048]{1,0:T(8,128)(2,1)S(1)} %get-tuple-element.47.refs_0_.refs_7_.refs_1_, ...), custom_call_target="tpu_custom_call" | custom-call | flops 8589934592 | bytes 25165824 | tf_op jit(solution)/shard_map/next_query/pallas_call | solution.py:159
  227.0 8.0 %next_query.5 = (f32[256,2048]{1,0:T(8,128)S(1)}, bf16[256,2048]{1,0:T(8,128)(2,1)S(1)}) custom-call(s32[8]{0:T(128)S(1)} %fusion.info_ref, bf16[256,2048]{1,0:T(8,128)(2,1)S(1)} %get-tuple-element.58.refs_0_, bf16[256,2048]{1,0:T(8,128)(2,1)S(1)} %collective-permute-done.23.refs_1_.refs_5_, bf16[256,2048]{1,0:T(8,128)(2,1)S(1)} %collective-permute-done.24.refs_2_.refs_4_, ...), custom_call_target="tpu_custom_call" | custom-call | flops 4294967296 | bytes 16777216 | tf_op jit(solution)/shard_map/next_query/pallas_call | solution.py:159
  236.6 2.3 collective-permute-done.29
  (79 shorter events, 41.2 us)
Async XLA Ops:
  24.7 18.4 %collective-permute-start.5 = (bf16[256,2048]{1,0:T(8,128)(2,1)S(1)}, bf16[256,2048]{1,0:T(8,128)(2,1)S(1)}, u32[]{:S(2)}, u32[]{:S(2)}) collective-permute-start(bf16[256,2048]{1,0:T(8,128)(2,1)S(1)} %broadcast_select_fusion.refs_0_), channel_id=1, source_target_pairs={{0,4},{4,8},{8,12},{12,14},{14,10},{10,6},{6,2},{2,0},{5,1},{9,5},... | collective-permute-start | bytes 3145736 | tf_op jit(solution)/shard_map/ppermute | solution.py:348
  35.4 8.4 %collective-permute-start.4 = (bf16[256,2048]{1,0:T(8,128)(2,1)S(1)}, bf16[256,2048]{1,0:T(8,128)(2,1)S(1)}, u32[]{:S(2)}, u32[]{:S(2)}) collective-permute-start(bf16[256,2048]{1,0:T(8,128)(2,1)S(1)} %get-tuple-element.32), channel_id=1, source_target_pairs={{0,1},{1,0},{2,3},{3,2},{4,5},{5,4},{6,7},{7,6},{8,9},{9,8},{10,11... | collective-permute-start | bytes 3145736 | tf_op jit(solution)/shard_map/ppermute | solution.py:332
  48.1 25.5 %collective-permute-start.9 = (bf16[256,2048]{1,0:T(8,128)(2,1)S(1)}, bf16[256,2048]{1,0:T(8,128)(2,1)S(1)}, u32[]{:S(2)}, u32[]{:S(2)}) collective-permute-start(bf16[256,2048]{1,0:T(8,128)(2,1)S(1)} %select_select_fusion.refs_0_), channel_id=1, source_target_pairs={{4,0},{8,4},{12,8},{14,12},{10,14},{6,10},{2,6},{0,2},{1,5},{5,9},... | collective-permute-start | bytes 3145736 | tf_op jit(solution)/shard_map/ppermute | solution.py:348
  52.1 21.5 %collective-permute-start.8 = (bf16[256,2048]{1,0:T(8,128)(2,1)S(1)}, bf16[256,2048]{1,0:T(8,128)(2,1)S(1)}, u32[]{:S(2)}, u32[]{:S(2)}) collective-permute-start(bf16[256,2048]{1,0:T(8,128)(2,1)S(1)} %add_convert_fusion.4.refs_1_), channel_id=1, source_target_pairs={{0,4},{4,8},{8,12},{12,14},{14,10},{10,6},{6,2},{2,0},{5,1},{9,5},... | collective-permute-start | bytes 3145736 | tf_op jit(solution)/shard_map/ppermute | solution.py:348
  60.6 13.0 %collective-permute-start.7 = (bf16[256,2048]{1,0:T(8,128)(2,1)S(1)}, bf16[256,2048]{1,0:T(8,128)(2,1)S(1)}, u32[]{:S(2)}, u32[]{:S(2)}) collective-permute-start(bf16[256,2048]{1,0:T(8,128)(2,1)S(1)} %get-tuple-element.37), channel_id=1, source_target_pairs={{0,1},{1,0},{2,3},{3,2},{4,5},{5,4},{6,7},{7,6},{8,9},{9,8},{10,11... | collective-permute-start | bytes 3145736 | tf_op jit(solution)/shard_map/ppermute | solution.py:332
  74.8 24.0 %collective-permute-start.11 = (bf16[256,2048]{1,0:T(8,128)(2,1)S(1)}, bf16[256,2048]{1,0:T(8,128)(2,1)S(1)}, u32[]{:S(2)}, u32[]{:S(2)}) collective-permute-start(bf16[256,2048]{1,0:T(8,128)(2,1)S(1)} %add_convert_fusion.3), channel_id=1, source_target_pairs={{4,0},{8,4},{12,8},{14,12},{10,14},{6,10},{2,6},{0,2},{1,5},{5,9},... | collective-permute-start | bytes 3145736 | tf_op jit(solution)/shard_map/ppermute | solution.py:348
  77.1 26.0 %collective-permute-start.10 = (bf16[256,2048]{1,0:T(8,128)(2,1)S(1)}, bf16[256,2048]{1,0:T(8,128)(2,1)S(1)}, u32[]{:S(2)}, u32[]{:S(2)}) collective-permute-start(bf16[256,2048]{1,0:T(8,128)(2,1)S(1)} %add_convert_fusion.2), channel_id=1, source_target_pairs={{0,4},{4,8},{8,12},{12,14},{14,10},{10,6},{6,2},{2,0},{5,1},{9,5},... | collective-permute-start | bytes 3145736 | tf_op jit(solution)/shard_map/ppermute | solution.py:348
  101.6 23.6 %collective-permute-start.13 = (bf16[256,2048]{1,0:T(8,128)(2,1)S(1)}, bf16[256,2048]{1,0:T(8,128)(2,1)S(1)}, u32[]{:S(2)}, u32[]{:S(2)}) collective-permute-start(bf16[256,2048]{1,0:T(8,128)(2,1)S(1)} %add_convert_fusion.1), channel_id=1, source_target_pairs={{4,0},{8,4},{12,8},{14,12},{10,14},{6,10},{2,6},{0,2},{1,5},{5,9},... | collective-permute-start | bytes 3145736 | tf_op jit(solution)/shard_map/ppermute | solution.py:348
  106.0 19.4 %collective-permute-start.12 = (bf16[256,2048]{1,0:T(8,128)(2,1)S(1)}, bf16[256,2048]{1,0:T(8,128)(2,1)S(1)}, u32[]{:S(2)}, u32[]{:S(2)}) collective-permute-start(bf16[256,2048]{1,0:T(8,128)(2,1)S(1)} %add_convert_fusion), channel_id=1, source_target_pairs={{0,4},{4,8},{8,12},{12,14},{14,10},{10,6},{6,2},{2,0},{5,1},{9,5},... | collective-permute-start | bytes 3145736 | tf_op jit(solution)/shard_map/ppermute | solution.py:348
  128.3 26.2 %collective-permute-start.15 = (bf16[256,2048]{1,0:T(8,128)(2,1)S(1)}, bf16[256,2048]{1,0:T(8,128)(2,1)S(1)}, u32[]{:S(2)}, u32[]{:S(2)}) collective-permute-start(bf16[256,2048]{1,0:T(8,128)(2,1)S(1)} %get-tuple-element.58.refs_0_), channel_id=1, source_target_pairs={{0,4},{4,8},{8,12},{12,14},{14,10},{10,6},{6,2},{2,0},{5,1},{9,5},... | collective-permute-start | bytes 3145736 | tf_op jit(solution)/shard_map/ppermute | solution.py:378
  130.4 25.4 %collective-permute-start.20 = (bf16[256,2048]{1,0:T(8,128)(2,1)S(1)}, bf16[256,2048]{1,0:T(8,128)(2,1)S(1)}, u32[]{:S(2)}, u32[]{:S(2)}) collective-permute-start(bf16[256,2048]{1,0:T(8,128)(2,1)S(1)} %get-tuple-element.58.refs_0_), channel_id=1, source_target_pairs={{4,0},{8,4},{12,8},{14,12},{10,14},{6,10},{2,6},{0,2},{1,5},{5,9},... | collective-permute-start | bytes 3145736 | tf_op jit(solution)/shard_map/ppermute | solution.py:379
  131.2 23.3 %collective-permute-start.14 = (f32[1,256]{1,0:T(1,128)S(1)}, f32[1,256]{1,0:T(1,128)S(1)}, u32[]{:S(2)}, u32[]{:S(2)}) collective-permute-start(f32[1,256]{1,0:T(1,128)S(1)} %bitcast.27), channel_id=1, source_target_pairs={{0,2},{2,0},{4,6},{6,4},{8,10},{10,8},{12,14},{14,12},{1,3},{3,1},... | collective-permute-start | bytes 3080 | tf_op jit(solution)/shard_map/ppermute | solution.py:381
  154.4 26.1 %collective-permute-start.17 = (bf16[256,2048]{1,0:T(8,128)(2,1)S(1)}, bf16[256,2048]{1,0:T(8,128)(2,1)S(1)}, u32[]{:S(2)}, u32[]{:S(2)}) collective-permute-start(bf16[256,2048]{1,0:T(8,128)(2,1)S(1)} %get-tuple-element.43.refs_3_.refs_4_.refs_2_.refs_6_), channel_id=1, source_target_pairs={{0,4},{4,8},{8,12},{12,14},{14,10},{10,6},{6,2},{2,0},{5,1},{9,5},... | collective-permute-start | bytes 3145736 | tf_op jit(solution)/shard_map/ppermute | solution.py:378
  155.8 24.7 %collective-permute-start.21 = (bf16[256,2048]{1,0:T(8,128)(2,1)S(1)}, bf16[256,2048]{1,0:T(8,128)(2,1)S(1)}, u32[]{:S(2)}, u32[]{:S(2)}) collective-permute-start(bf16[256,2048]{1,0:T(8,128)(2,1)S(1)} %collective-permute-done.20.refs_1_.refs_6_.refs_0_.refs_8_), channel_id=1, source_target_pairs={{4,0},{8,4},{12,8},{14,12},{10,14},{6,10},{2,6},{0,2},{1,5},{5,9},... | collective-permute-start | bytes 3145736 | tf_op jit(solution)/shard_map/ppermute | solution.py:379
  157.0 23.4 %collective-permute-start.16 = (f32[1,256]{1,0:T(1,128)S(1)}, f32[1,256]{1,0:T(1,128)S(1)}, u32[]{:S(2)}, u32[]{:S(2)}) collective-permute-start(f32[1,256]{1,0:T(1,128)S(1)} %get-tuple-element.42.total_ref), channel_id=1, source_target_pairs={{0,4},{2,6},{4,0},{6,2},{8,12},{10,14},{12,8},{14,10},{1,5},{3,7},... | collective-permute-start | bytes 3080 | tf_op jit(solution)/shard_map/ppermute | solution.py:381
  181.1 5.1 %collective-permute-start.22 = (bf16[256,2048]{1,0:T(8,128)(2,1)S(1)}, bf16[256,2048]{1,0:T(8,128)(2,1)S(1)}, u32[]{:S(2)}, u32[]{:S(2)}) collective-permute-start(bf16[256,2048]{1,0:T(8,128)(2,1)S(1)} %pick.2), channel_id=1, source_target_pairs={{0,1},{1,0},{2,3},{3,2},{4,5},{5,4},{6,7},{7,6},{8,9},{9,8},{10,11... | collective-permute-start | bytes 3145736 | tf_op jit(solution)/shard_map/ppermute | solution.py:389
  181.5 26.5 %collective-permute-start.19 = (bf16[256,2048]{1,0:T(8,128)(2,1)S(1)}, bf16[256,2048]{1,0:T(8,128)(2,1)S(1)}, u32[]{:S(2)}, u32[]{:S(2)}) collective-permute-start(bf16[256,2048]{1,0:T(8,128)(2,1)S(1)} %get-tuple-element.45.refs_0_.refs_1_), channel_id=1, source_target_pairs={{0,4},{4,8},{8,12},{12,14},{14,10},{10,6},{6,2},{2,0},{5,1},{9,5},... | collective-permute-start | bytes 3145736 | tf_op jit(solution)/shard_map/ppermute | solution.py:378
  182.4 25.6 %collective-permute-start.26 = (bf16[256,2048]{1,0:T(8,128)(2,1)S(1)}, bf16[256,2048]{1,0:T(8,128)(2,1)S(1)}, u32[]{:S(2)}, u32[]{:S(2)}) collective-permute-start(bf16[256,2048]{1,0:T(8,128)(2,1)S(1)} %collective-permute-done.21.refs_1_.refs_0_), channel_id=1, source_target_pairs={{4,0},{8,4},{12,8},{14,12},{10,14},{6,10},{2,6},{0,2},{1,5},{5,9},... | collective-permute-start | bytes 3145736 | tf_op jit(solution)/shard_map/ppermute | solution.py:379
  183.8 24.2 %collective-permute-start.18 = (f32[1,256]{1,0:T(1,128)S(1)}, f32[1,256]{1,0:T(1,128)S(1)}, u32[]{:S(2)}, u32[]{:S(2)}) collective-permute-start(f32[1,256]{1,0:T(1,128)S(1)} %get-tuple-element.44.total_ref), channel_id=1, source_target_pairs={{0,8},{2,10},{4,12},{6,14},{8,0},{10,2},{12,4},{14,6},{1,9},{3,11}... | collective-permute-start | bytes 3080 | tf_op jit(solution)/shard_map/ppermute | solution.py:381
  208.7 5.2 %collective-permute-start.27 = (bf16[256,2048]{1,0:T(8,128)(2,1)S(1)}, bf16[256,2048]{1,0:T(8,128)(2,1)S(1)}, u32[]{:S(2)}, u32[]{:S(2)}) collective-permute-start(bf16[256,2048]{1,0:T(8,128)(2,1)S(1)} %get-tuple-element.48), channel_id=1, source_target_pairs={{0,1},{1,0},{2,3},{3,2},{4,5},{5,4},{6,7},{7,6},{8,9},{9,8},{10,11... | collective-permute-start | bytes 3145736 | tf_op jit(solution)/shard_map/ppermute | solution.py:389
  208.8 5.1 %collective-permute-start.28 = (bf16[256,2048]{1,0:T(8,128)(2,1)S(1)}, bf16[256,2048]{1,0:T(8,128)(2,1)S(1)}, u32[]{:S(2)}, u32[]{:S(2)}) collective-permute-start(bf16[256,2048]{1,0:T(8,128)(2,1)S(1)} %get-tuple-element.49), channel_id=1, source_target_pairs={{0,1},{1,0},{2,3},{3,2},{4,5},{5,4},{6,7},{7,6},{8,9},{9,8},{10,11... | collective-permute-start | bytes 3145736 | tf_op jit(solution)/shard_map/ppermute | solution.py:389
  209.3 17.7 %collective-permute-start.25 = (bf16[256,2048]{1,0:T(8,128)(2,1)S(1)}, bf16[256,2048]{1,0:T(8,128)(2,1)S(1)}, u32[]{:S(2)}, u32[]{:S(2)}) collective-permute-start(bf16[256,2048]{1,0:T(8,128)(2,1)S(1)} %get-tuple-element.58.refs_0_), channel_id=1, source_target_pairs={{0,1},{1,0},{2,3},{3,2},{4,5},{5,4},{6,7},{7,6},{8,9},{9,8},{10,11... | collective-permute-start | bytes 3145736 | tf_op jit(solution)/shard_map/ppermute | solution.py:370
  209.4 17.6 %collective-permute-start.23 = (bf16[256,2048]{1,0:T(8,128)(2,1)S(1)}, bf16[256,2048]{1,0:T(8,128)(2,1)S(1)}, u32[]{:S(2)}, u32[]{:S(2)}) collective-permute-start(bf16[256,2048]{1,0:T(8,128)(2,1)S(1)} %get-tuple-element.47.refs_0_.refs_7_.refs_1_), channel_id=1, source_target_pairs={{0,5},{4,8},{8,12},{12,14},{14,10},{10,7},{6,3},{2,1},{16,21},{20,... | collective-permute-start | bytes 3145736 | tf_op jit(solution)/shard_map/ppermute | solution.py:398
  213.2 13.8 %collective-permute-start.24 = (bf16[256,2048]{1,0:T(8,128)(2,1)S(1)}, bf16[256,2048]{1,0:T(8,128)(2,1)S(1)}, u32[]{:S(2)}, u32[]{:S(2)}) collective-permute-start(bf16[256,2048]{1,0:T(8,128)(2,1)S(1)} %get-tuple-element.47.refs_0_.refs_7_.refs_1_), channel_id=1, source_target_pairs={{5,1},{9,5},{13,8},{15,12},{11,14},{7,10},{3,7},{1,3},{21,17},{25,... | collective-permute-start | bytes 3145736 | tf_op jit(solution)/shard_map/ppermute | solution.py:399
  (9 other events, 39.5 us)

commit v11 on v9

--- a/solution.py
+++ b/solution.py
@@ -359,14 +359,9 @@
         value = send("long", step + 1, value)
 
     arrived["short"] = hold(arrived["short"], [])
-    own_sum = partial_sum(0)
-
-    def mix(long_sum, short_sum):
-        return residual.astype(F32) + own_sum + long_sum.astype(F32) + short_sum.astype(F32)
-
-    scaled = (mix(arrived["long"], arrived["short"]) * norm_gain.astype(F32)).astype(BF16)
-    mixed = mix(*lax.optimization_barrier((arrived["long"], arrived["short"], scaled))[:2])
+    mixed = residual.astype(F32) + partial_sum(0) + arrived["long"].astype(F32) + arrived["short"].astype(F32)
     resid_out = mixed.astype(BF16)
+    scaled = (mixed * norm_gain.astype(F32)).astype(BF16)
     squares = jnp.sum(mixed * mixed, axis=1)[None]
 
     scaled_peer = lax.ppermute(scaled, "tokens", swap)

time: 237 us -> 238 us (level)
  transfers between devices with their start and end apart: 30 -> 30, of which waited for: 12 -> 12; matrix products, arithmetic and copies ran while one was open for 3% -> 2% of each run, Pallas kernels for 19% -> 19%
where the time goes in v11:
time: 238 us; the launch traced here: 237 us
  waiting for transfers between devices  113 us (47%)
  Pallas kernels  66.7 us (28%)
  starting transfers between devices  34 us (14%)
  between operations  10.8 us (5%)
  other arithmetic  7.91 us (3%)
  local copies, waits for them, and re-layouts  4.1 us (2%)
    ppermute x3, waiting for transfers between devices, on_ring(): more = lax.ppermute(squares, 'tensor', [(c, c ^ reach) for c in range(n)])  55.4 us
    ppermute x7, waiting for transfers between devices, send(): lax.ppermute(value, devices, long_way if way == 'long' else short_way)  51.4 us
    pallas_call x4, Pallas kernels, project(): pl.pallas_call(project_kernel, grid_spec=pltpu.PrefetchScalarGridSpec(num...  30.7 us
    pallas_call x3, Pallas kernels, query_block(): pl.pallas_call(functools.partial(query_kernel, [half + pair for pair, _,...  28.9 us
    ppermute x7, starting transfers between devices, send(): lax.ppermute(value, devices, long_way if way == 'long' else short_way)  10.3 us
    ppermute x3, starting transfers between devices, on_ring(): more = lax.ppermute(squares, 'tensor', [(c, c ^ reach) for c in range(n)])  6.26 us
    pallas_call x2, Pallas kernels, attention(): pl.pallas_call(functools.partial(attention_kernel, heads), grid_spec=pltp...  5.68 us
    ppermute x3, starting transfers between devices, on_ring(): held[-step] = lax.ppermute(held[1 - step], devices, long_way)  5.62 us
  transfers between devices with their start and end apart: 30, of which 12 were waited for; matrix products, arithmetic and copies ran while one was open for 2% of the time, Pallas kernels for 19%

profile of v11, /device:TPU:0, one launch (start us, length us, event | category | flops | bytes accessed | tf_op | source)
XLA Modules:
  0.0 236.6 jit_solution(5799205339759954683)
XLA Ops:
  4.9 2.8 %attention.2.refs_0_ = bf16[256,1024]{1,0:T(8,128)(2,1)S(1)} custom-call(s32[1]{0:T(128)} %bitcast.2.core_ref, bf16[256,2048]{1,0:T(8,128)(2,1)S(1)} %copy-done, bf16[2,256,128]{2,1,0:T(8,128)(2,1)S(1)} %pad_maximum_fusion.own_ref, bf16[2,256,128]{2,1,0:T(8,128)(2,1)S(1)} %collective-permute-done.far_ref), custom_call_target="tpu_custom_call" | custom-call | flops 536870912 | bytes 1048576 | tf_op jit(solution)/shard_map/attention/pallas_call | solution.py:61
  7.8 2.9 %attention.3 = bf16[256,1024]{1,0:T(8,128)(2,1)S(1)} custom-call(s32[1]{0:T(128)} %bitcast.2.core_ref, bf16[256,2048]{1,0:T(8,128)(2,1)S(1)} %copy-done, bf16[2,256,128]{2,1,0:T(8,128)(2,1)S(1)} %pad_maximum_fusion.own_ref, bf16[2,256,128]{2,1,0:T(8,128)(2,1)S(1)} %collective-permute-done.far_ref, bf16[256,1024]{1,0:T(8,128)(2,1)S(1)} %attention.2.refs_0_), custom_call_target="tpu_custom_call" | custom-call | flops 536870912 | bytes 1048576 | tf_op jit(solution)/shard_map/attention/pallas_call | solution.py:61
  13.5 7.7 %project.4 = (bf16[256,2048]{1,0:T(8,128)(2,1)S(1)}, bf16[256,2048]{1,0:T(8,128)(2,1)S(1)}) custom-call(s32[16]{0:T(128)S(1)} %get-tuple-element.61.info_ref, bf16[512,2048]{1,0:T(8,128)(2,1)S(1)} %maximum_maximum_fusion.x_ref, bf16[2048,8192]{1,0:T(8,128)(2,1)} %w_ref.7), custom_call_target="tpu_custom_call" | custom-call | flops 4294967296 | bytes 8388608 | tf_op jit(solution)/shard_map/project/pallas_call | solution.py:92
  24.1 3.0 %collective-permute-start.5 = (bf16[256,2048]{1,0:T(8,128)(2,1)S(1)}, bf16[256,2048]{1,0:T(8,128)(2,1)S(1)}, u32[]{:S(2)}, u32[]{:S(2)}) collective-permute-start(bf16[256,2048]{1,0:T(8,128)(2,1)S(1)} %broadcast_select_fusion.refs_0_), channel_id=1, source_target_pairs={{0,4},{4,8},{8,12},{12,14},{14,10},{10,6},{6,2},{2,0},{5,1},{9,5},... | collective-permute-start | bytes 3145736 | tf_op jit(solution)/shard_map/ppermute | solution.py:345
  27.1 7.7 %project.5 = (bf16[256,2048]{1,0:T(8,128)(2,1)S(1)}, bf16[256,2048]{1,0:T(8,128)(2,1)S(1)}) custom-call(s32[16]{0:T(128)S(1)} %get-tuple-element.61.info_ref, bf16[512,2048]{1,0:T(8,128)(2,1)S(1)} %maximum_maximum_fusion.x_ref, bf16[2048,8192]{1,0:T(8,128)(2,1)} %w_ref.7), custom_call_target="tpu_custom_call" | custom-call | flops 4294967296 | bytes 8388608 | tf_op jit(solution)/shard_map/project/pallas_call | solution.py:92
  34.9 7.7 %project.6 = (bf16[256,2048]{1,0:T(8,128)(2,1)S(1)}, bf16[256,2048]{1,0:T(8,128)(2,1)S(1)}) custom-call(s32[16]{0:T(128)S(1)} %get-tuple-element.61.info_ref, bf16[512,2048]{1,0:T(8,128)(2,1)S(1)} %maximum_maximum_fusion.x_ref, bf16[2048,8192]{1,0:T(8,128)(2,1)} %w_ref.7, bf16[256,2048]{1,0:T(8,128)(2,1)S(1)} %broadcast_select_fusion.refs_0_), custom_call_target="tpu_custom_call" | custom-call | flops 4294967296 | bytes 8388608 | tf_op jit(solution)/shard_map/project/pallas_call | solution.py:92
  50.3 7.7 %project.7 = (bf16[256,2048]{1,0:T(8,128)(2,1)S(1)}, bf16[256,2048]{1,0:T(8,128)(2,1)S(1)}) custom-call(s32[16]{0:T(128)S(1)} %get-tuple-element.61.info_ref, bf16[512,2048]{1,0:T(8,128)(2,1)S(1)} %maximum_maximum_fusion.x_ref, bf16[2048,8192]{1,0:T(8,128)(2,1)} %w_ref.7, bf16[256,2048]{1,0:T(8,128)(2,1)S(1)} %select_select_fusion.refs_0_, ...), custom_call_target="tpu_custom_call" | custom-call | flops 4294967296 | bytes 8388608 | tf_op jit(solution)/shard_map/project/pallas_call | solution.py:92
  58.7 13.7 %collective-permute-done.8.refs_1_ = bf16[256,2048]{1,0:T(8,128)(2,1)S(1)} collective-permute-done((bf16[256,2048]{1,0:T(8,128)(2,1)S(1)}, bf16[256,2048]{1,0:T(8,128)(2,1)S(1)}, u32[]{:S(2)}, u32[]{:S(2)}) %collective-permute-start.8) | collective-permute-done | bytes 1048608 | tf_op jit(solution)/shard_map/ppermute | solution.py:345
  79.7 16.9 %collective-permute-done.11 = bf16[256,2048]{1,0:T(8,128)(2,1)S(1)} collective-permute-done((bf16[256,2048]{1,0:T(8,128)(2,1)S(1)}, bf16[256,2048]{1,0:T(8,128)(2,1)S(1)}, u32[]{:S(2)}, u32[]{:S(2)}) %collective-permute-start.11) | collective-permute-done | bytes 1048608 | tf_op jit(solution)/shard_map/ppermute | solution.py:345
  97.6 2.3 collective-permute-start.13
  102.2 20.8 %collective-permute-done.13.refs_0_ = bf16[256,2048]{1,0:T(8,128)(2,1)S(1)} collective-permute-done((bf16[256,2048]{1,0:T(8,128)(2,1)S(1)}, bf16[256,2048]{1,0:T(8,128)(2,1)S(1)}, u32[]{:S(2)}, u32[]{:S(2)}) %collective-permute-start.13) | collective-permute-done | bytes 1048608 | tf_op jit(solution)/shard_map/ppermute | solution.py:345
  127.7 2.5 %collective-permute-start.14 = (f32[1,256]{1,0:T(1,128)S(1)}, f32[1,256]{1,0:T(1,128)S(1)}, u32[]{:S(2)}, u32[]{:S(2)}) collective-permute-start(f32[1,256]{1,0:T(1,128)S(1)} %bitcast.27), channel_id=1, source_target_pairs={{0,2},{2,0},{4,6},{6,4},{8,10},{10,8},{12,14},{14,12},{1,3},{3,1},... | collective-permute-start | bytes 3080 | tf_op jit(solution)/shard_map/ppermute | solution.py:378
  130.2 20.4 %collective-permute-done.14.more_ref = f32[1,256]{1,0:T(1,128)S(1)} collective-permute-done((f32[1,256]{1,0:T(1,128)S(1)}, f32[1,256]{1,0:T(1,128)S(1)}, u32[]{:S(2)}, u32[]{:S(2)}) %collective-permute-start.14) | collective-permute-done | bytes 1056 | tf_op jit(solution)/shard_map/ppermute | solution.py:378
  150.5 2.8 %collective-permute-start.17 = (bf16[256,2048]{1,0:T(8,128)(2,1)S(1)}, bf16[256,2048]{1,0:T(8,128)(2,1)S(1)}, u32[]{:S(2)}, u32[]{:S(2)}) collective-permute-start(bf16[256,2048]{1,0:T(8,128)(2,1)S(1)} %get-tuple-element.43.refs_3_.refs_4_.refs_2_.refs_6_), channel_id=1, source_target_pairs={{0,4},{4,8},{8,12},{12,14},{14,10},{10,6},{6,2},{2,0},{5,1},{9,5},... | collective-permute-start | bytes 3145736 | tf_op jit(solution)/shard_map/ppermute | solution.py:375
  153.7 2.1 collective-permute-start.16
  155.8 20.9 %collective-permute-done.16.more_ref = f32[1,256]{1,0:T(1,128)S(1)} collective-permute-done((f32[1,256]{1,0:T(1,128)S(1)}, f32[1,256]{1,0:T(1,128)S(1)}, u32[]{:S(2)}, u32[]{:S(2)}) %collective-permute-start.16) | collective-permute-done | bytes 1056 | tf_op jit(solution)/shard_map/ppermute | solution.py:378
  180.4 1.7 collective-permute-start.18
  182.1 7.9 %next_query.3 = (f32[256,2048]{1,0:T(8,128)S(1)}, f32[256,2048]{1,0:T(8,128)S(1)}) custom-call(s32[16]{0:T(128)S(1)} %get-tuple-element.61.info_ref, bf16[256,2048]{1,0:T(8,128)(2,1)S(1)} %collective-permute-done.21.refs_1_.refs_0_, bf16[256,2048]{1,0:T(8,128)(2,1)S(1)} %get-tuple-element.45.refs_0_.refs_1_, ...), custom_call_target="tpu_custom_call" | custom-call | flops 4294967296 | bytes 16777216 | tf_op jit(solution)/shard_map/next_query/pallas_call | solution.py:159
  190.0 14.2 %collective-permute-done.18.more_ref = f32[1,256]{1,0:T(1,128)S(1)} collective-permute-done((f32[1,256]{1,0:T(1,128)S(1)}, f32[1,256]{1,0:T(1,128)S(1)}, u32[]{:S(2)}, u32[]{:S(2)}) %collective-permute-start.18) | collective-permute-done | bytes 1056 | tf_op jit(solution)/shard_map/ppermute | solution.py:378
  205.6 3.6 %collective-permute-start.23 = (bf16[256,2048]{1,0:T(8,128)(2,1)S(1)}, bf16[256,2048]{1,0:T(8,128)(2,1)S(1)}, u32[]{:S(2)}, u32[]{:S(2)}) collective-permute-start(bf16[256,2048]{1,0:T(8,128)(2,1)S(1)} %get-tuple-element.47.refs_0_.refs_7_.refs_1_), channel_id=1, source_target_pairs={{0,5},{4,8},{8,12},{12,14},{14,10},{10,7},{6,3},{2,1},{16,21},{20,... | collective-permute-start | bytes 3145736 | tf_op jit(solution)/shard_map/ppermute | solution.py:395
  210.0 13.0 %next_query.4 = (f32[256,2048]{1,0:T(8,128)S(1)}, f32[256,2048]{1,0:T(8,128)S(1)}) custom-call(s32[16]{0:T(128)S(1)} %get-tuple-element.61.info_ref, bf16[256,2048]{1,0:T(8,128)(2,1)S(1)} %collective-permute-done.20.refs_1_.refs_6_.refs_0_.refs_8_, bf16[256,2048]{1,0:T(8,128)(2,1)S(1)} %get-tuple-element.47.refs_0_.refs_7_.refs_1_, ...), custom_call_target="tpu_custom_call" | custom-call | flops 8589934592 | bytes 25165824 | tf_op jit(solution)/shard_map/next_query/pallas_call | solution.py:159
  223.1 8.0 %next_query.5 = (f32[256,2048]{1,0:T(8,128)S(1)}, bf16[256,2048]{1,0:T(8,128)(2,1)S(1)}) custom-call(s32[16]{0:T(128)S(1)} %get-tuple-element.61.info_ref, bf16[256,2048]{1,0:T(8,128)(2,1)S(1)} %get-tuple-element.58.refs_0_, bf16[256,2048]{1,0:T(8,128)(2,1)S(1)} %collective-permute-done.23.refs_1_.refs_5_, ...), custom_call_target="tpu_custom_call" | custom-call | flops 4294967296 | bytes 16777216 | tf_op jit(solution)/shard_map/next_query/pallas_call | solution.py:159
  231.1 2.0 collective-permute-start.29
  233.1 2.3 collective-permute-done.29
  (78 shorter events, 31.4 us)
Async XLA Ops:
  24.1 18.4 %collective-permute-start.5 = (bf16[256,2048]{1,0:T(8,128)(2,1)S(1)}, bf16[256,2048]{1,0:T(8,128)(2,1)S(1)}, u32[]{:S(2)}, u32[]{:S(2)}) collective-permute-start(bf16[256,2048]{1,0:T(8,128)(2,1)S(1)} %broadcast_select_fusion.refs_0_), channel_id=1, source_target_pairs={{0,4},{4,8},{8,12},{12,14},{14,10},{10,6},{6,2},{2,0},{5,1},{9,5},... | collective-permute-start | bytes 3145736 | tf_op jit(solution)/shard_map/ppermute | solution.py:345
  34.8 12.1 %collective-permute-start.4 = (bf16[256,2048]{1,0:T(8,128)(2,1)S(1)}, bf16[256,2048]{1,0:T(8,128)(2,1)S(1)}, u32[]{:S(2)}, u32[]{:S(2)}) collective-permute-start(bf16[256,2048]{1,0:T(8,128)(2,1)S(1)} %get-tuple-element.32), channel_id=1, source_target_pairs={{0,1},{1,0},{2,3},{3,2},{4,5},{5,4},{6,7},{7,6},{8,9},{9,8},{10,11... | collective-permute-start | bytes 3145736 | tf_op jit(solution)/shard_map/ppermute | solution.py:329
  42.6 4.4 %collective-permute-start.6 = (bf16[256,2048]{1,0:T(8,128)(2,1)S(1)}, bf16[256,2048]{1,0:T(8,128)(2,1)S(1)}, u32[]{:S(2)}, u32[]{:S(2)}) collective-permute-start(bf16[256,2048]{1,0:T(8,128)(2,1)S(1)} %hold.3), channel_id=1, source_target_pairs={{0,1},{1,0},{2,3},{3,2},{4,5},{5,4},{6,7},{7,6},{8,9},{9,8},{10,11... | collective-permute-start | bytes 3145736 | tf_op jit(solution)/shard_map/ppermute | solution.py:329
  47.2 25.1 %collective-permute-start.9 = (bf16[256,2048]{1,0:T(8,128)(2,1)S(1)}, bf16[256,2048]{1,0:T(8,128)(2,1)S(1)}, u32[]{:S(2)}, u32[]{:S(2)}) collective-permute-start(bf16[256,2048]{1,0:T(8,128)(2,1)S(1)} %select_select_fusion.refs_0_), channel_id=1, source_target_pairs={{4,0},{8,4},{12,8},{14,12},{10,14},{6,10},{2,6},{0,2},{1,5},{5,9},... | collective-permute-start | bytes 3145736 | tf_op jit(solution)/shard_map/ppermute | solution.py:345
  49.0 23.3 %collective-permute-start.8 = (bf16[256,2048]{1,0:T(8,128)(2,1)S(1)}, bf16[256,2048]{1,0:T(8,128)(2,1)S(1)}, u32[]{:S(2)}, u32[]{:S(2)}) collective-permute-start(bf16[256,2048]{1,0:T(8,128)(2,1)S(1)} %add_convert_fusion.4.refs_1_), channel_id=1, source_target_pairs={{0,4},{4,8},{8,12},{12,14},{14,10},{10,6},{6,2},{2,0},{5,1},{9,5},... | collective-permute-start | bytes 3145736 | tf_op jit(solution)/shard_map/ppermute | solution.py:345
  57.9 14.4 %collective-permute-start.7 = (bf16[256,2048]{1,0:T(8,128)(2,1)S(1)}, bf16[256,2048]{1,0:T(8,128)(2,1)S(1)}, u32[]{:S(2)}, u32[]{:S(2)}) collective-permute-start(bf16[256,2048]{1,0:T(8,128)(2,1)S(1)} %get-tuple-element.37), channel_id=1, source_target_pairs={{0,1},{1,0},{2,3},{3,2},{4,5},{5,4},{6,7},{7,6},{8,9},{9,8},{10,11... | collective-permute-start | bytes 3145736 | tf_op jit(solution)/shard_map/ppermute | solution.py:329
  72.9 23.7 %collective-permute-start.11 = (bf16[256,2048]{1,0:T(8,128)(2,1)S(1)}, bf16[256,2048]{1,0:T(8,128)(2,1)S(1)}, u32[]{:S(2)}, u32[]{:S(2)}) collective-permute-start(bf16[256,2048]{1,0:T(8,128)(2,1)S(1)} %add_convert_fusion.3), channel_id=1, source_target_pairs={{4,0},{8,4},{12,8},{14,12},{10,14},{6,10},{2,6},{0,2},{1,5},{5,9},... | collective-permute-start | bytes 3145736 | tf_op jit(solution)/shard_map/ppermute | solution.py:345
  75.5 24.4 %collective-permute-start.10 = (bf16[256,2048]{1,0:T(8,128)(2,1)S(1)}, bf16[256,2048]{1,0:T(8,128)(2,1)S(1)}, u32[]{:S(2)}, u32[]{:S(2)}) collective-permute-start(bf16[256,2048]{1,0:T(8,128)(2,1)S(1)} %add_convert_fusion.2), channel_id=1, source_target_pairs={{0,4},{4,8},{8,12},{12,14},{14,10},{10,6},{6,2},{2,0},{5,1},{9,5},... | collective-permute-start | bytes 3145736 | tf_op jit(solution)/shard_map/ppermute | solution.py:345
  97.6 25.4 %collective-permute-start.13 = (bf16[256,2048]{1,0:T(8,128)(2,1)S(1)}, bf16[256,2048]{1,0:T(8,128)(2,1)S(1)}, u32[]{:S(2)}, u32[]{:S(2)}) collective-permute-start(bf16[256,2048]{1,0:T(8,128)(2,1)S(1)} %add_convert_fusion.1), channel_id=1, source_target_pairs={{4,0},{8,4},{12,8},{14,12},{10,14},{6,10},{2,6},{0,2},{1,5},{5,9},... | collective-permute-start | bytes 3145736 | tf_op jit(solution)/shard_map/ppermute | solution.py:345
  100.8 22.2 %collective-permute-start.12 = (bf16[256,2048]{1,0:T(8,128)(2,1)S(1)}, bf16[256,2048]{1,0:T(8,128)(2,1)S(1)}, u32[]{:S(2)}, u32[]{:S(2)}) collective-permute-start(bf16[256,2048]{1,0:T(8,128)(2,1)S(1)} %add_convert_fusion), channel_id=1, source_target_pairs={{0,4},{4,8},{8,12},{12,14},{14,10},{10,6},{6,2},{2,0},{5,1},{9,5},... | collective-permute-start | bytes 3145736 | tf_op jit(solution)/shard_map/ppermute | solution.py:345
  125.2 25.3 %collective-permute-start.15 = (bf16[256,2048]{1,0:T(8,128)(2,1)S(1)}, bf16[256,2048]{1,0:T(8,128)(2,1)S(1)}, u32[]{:S(2)}, u32[]{:S(2)}) collective-permute-start(bf16[256,2048]{1,0:T(8,128)(2,1)S(1)} %get-tuple-element.58.refs_0_), channel_id=1, source_target_pairs={{0,4},{4,8},{8,12},{12,14},{14,10},{10,6},{6,2},{2,0},{5,1},{9,5},... | collective-permute-start | bytes 3145736 | tf_op jit(solution)/shard_map/ppermute | solution.py:375
  126.8 26.5 %collective-permute-start.20 = (bf16[256,2048]{1,0:T(8,128)(2,1)S(1)}, bf16[256,2048]{1,0:T(8,128)(2,1)S(1)}, u32[]{:S(2)}, u32[]{:S(2)}) collective-permute-start(bf16[256,2048]{1,0:T(8,128)(2,1)S(1)} %get-tuple-element.58.refs_0_), channel_id=1, source_target_pairs={{4,0},{8,4},{12,8},{14,12},{10,14},{6,10},{2,6},{0,2},{1,5},{5,9},... | collective-permute-start | bytes 3145736 | tf_op jit(solution)/shard_map/ppermute | solution.py:376
  127.7 22.9 %collective-permute-start.14 = (f32[1,256]{1,0:T(1,128)S(1)}, f32[1,256]{1,0:T(1,128)S(1)}, u32[]{:S(2)}, u32[]{:S(2)}) collective-permute-start(f32[1,256]{1,0:T(1,128)S(1)} %bitcast.27), channel_id=1, source_target_pairs={{0,2},{2,0},{4,6},{6,4},{8,10},{10,8},{12,14},{14,12},{1,3},{3,1},... | collective-permute-start | bytes 3080 | tf_op jit(solution)/shard_map/ppermute | solution.py:378
  150.5 26.8 %collective-permute-start.17 = (bf16[256,2048]{1,0:T(8,128)(2,1)S(1)}, bf16[256,2048]{1,0:T(8,128)(2,1)S(1)}, u32[]{:S(2)}, u32[]{:S(2)}) collective-permute-start(bf16[256,2048]{1,0:T(8,128)(2,1)S(1)} %get-tuple-element.43.refs_3_.refs_4_.refs_2_.refs_6_), channel_id=1, source_target_pairs={{0,4},{4,8},{8,12},{12,14},{14,10},{10,6},{6,2},{2,0},{5,1},{9,5},... | collective-permute-start | bytes 3145736 | tf_op jit(solution)/shard_map/ppermute | solution.py:375
  153.3 24.0 %collective-permute-start.21 = (bf16[256,2048]{1,0:T(8,128)(2,1)S(1)}, bf16[256,2048]{1,0:T(8,128)(2,1)S(1)}, u32[]{:S(2)}, u32[]{:S(2)}) collective-permute-start(bf16[256,2048]{1,0:T(8,128)(2,1)S(1)} %collective-permute-done.20.refs_1_.refs_6_.refs_0_.refs_8_), channel_id=1, source_target_pairs={{4,0},{8,4},{12,8},{14,12},{10,14},{6,10},{2,6},{0,2},{1,5},{5,9},... | collective-permute-start | bytes 3145736 | tf_op jit(solution)/shard_map/ppermute | solution.py:376
  153.7 23.0 %collective-permute-start.16 = (f32[1,256]{1,0:T(1,128)S(1)}, f32[1,256]{1,0:T(1,128)S(1)}, u32[]{:S(2)}, u32[]{:S(2)}) collective-permute-start(f32[1,256]{1,0:T(1,128)S(1)} %get-tuple-element.42.total_ref), channel_id=1, source_target_pairs={{0,4},{2,6},{4,0},{6,2},{8,12},{10,14},{12,8},{14,10},{1,5},{3,7},... | collective-permute-start | bytes 3080 | tf_op jit(solution)/shard_map/ppermute | solution.py:378
  178.0 26.2 %collective-permute-start.19 = (bf16[256,2048]{1,0:T(8,128)(2,1)S(1)}, bf16[256,2048]{1,0:T(8,128)(2,1)S(1)}, u32[]{:S(2)}, u32[]{:S(2)}) collective-permute-start(bf16[256,2048]{1,0:T(8,128)(2,1)S(1)} %get-tuple-element.45.refs_0_.refs_1_), channel_id=1, source_target_pairs={{0,4},{4,8},{8,12},{12,14},{14,10},{10,6},{6,2},{2,0},{5,1},{9,5},... | collective-permute-start | bytes 3145736 | tf_op jit(solution)/shard_map/ppermute | solution.py:375
  179.2 25.0 %collective-permute-start.26 = (bf16[256,2048]{1,0:T(8,128)(2,1)S(1)}, bf16[256,2048]{1,0:T(8,128)(2,1)S(1)}, u32[]{:S(2)}, u32[]{:S(2)}) collective-permute-start(bf16[256,2048]{1,0:T(8,128)(2,1)S(1)} %collective-permute-done.21.refs_1_.refs_0_), channel_id=1, source_target_pairs={{4,0},{8,4},{12,8},{14,12},{10,14},{6,10},{2,6},{0,2},{1,5},{5,9},... | collective-permute-start | bytes 3145736 | tf_op jit(solution)/shard_map/ppermute | solution.py:376
  180.4 23.8 %collective-permute-start.18 = (f32[1,256]{1,0:T(1,128)S(1)}, f32[1,256]{1,0:T(1,128)S(1)}, u32[]{:S(2)}, u32[]{:S(2)}) collective-permute-start(f32[1,256]{1,0:T(1,128)S(1)} %get-tuple-element.44.total_ref), channel_id=1, source_target_pairs={{0,8},{2,10},{4,12},{6,14},{8,0},{10,2},{12,4},{14,6},{1,9},{3,11}... | collective-permute-start | bytes 3080 | tf_op jit(solution)/shard_map/ppermute | solution.py:378
  204.9 5.1 %collective-permute-start.27 = (bf16[256,2048]{1,0:T(8,128)(2,1)S(1)}, bf16[256,2048]{1,0:T(8,128)(2,1)S(1)}, u32[]{:S(2)}, u32[]{:S(2)}) collective-permute-start(bf16[256,2048]{1,0:T(8,128)(2,1)S(1)} %get-tuple-element.48), channel_id=1, source_target_pairs={{0,1},{1,0},{2,3},{3,2},{4,5},{5,4},{6,7},{7,6},{8,9},{9,8},{10,11... | collective-permute-start | bytes 3145736 | tf_op jit(solution)/shard_map/ppermute | solution.py:386
  205.1 4.9 %collective-permute-start.28 = (bf16[256,2048]{1,0:T(8,128)(2,1)S(1)}, bf16[256,2048]{1,0:T(8,128)(2,1)S(1)}, u32[]{:S(2)}, u32[]{:S(2)}) collective-permute-start(bf16[256,2048]{1,0:T(8,128)(2,1)S(1)} %get-tuple-element.49), channel_id=1, source_target_pairs={{0,1},{1,0},{2,3},{3,2},{4,5},{5,4},{6,7},{7,6},{8,9},{9,8},{10,11... | collective-permute-start | bytes 3145736 | tf_op jit(solution)/shard_map/ppermute | solution.py:386
  205.5 17.5 %collective-permute-start.25 = (bf16[256,2048]{1,0:T(8,128)(2,1)S(1)}, bf16[256,2048]{1,0:T(8,128)(2,1)S(1)}, u32[]{:S(2)}, u32[]{:S(2)}) collective-permute-start(bf16[256,2048]{1,0:T(8,128)(2,1)S(1)} %get-tuple-element.58.refs_0_), channel_id=1, source_target_pairs={{0,1},{1,0},{2,3},{3,2},{4,5},{5,4},{6,7},{7,6},{8,9},{9,8},{10,11... | collective-permute-start | bytes 3145736 | tf_op jit(solution)/shard_map/ppermute | solution.py:367
  205.6 17.4 %collective-permute-start.23 = (bf16[256,2048]{1,0:T(8,128)(2,1)S(1)}, bf16[256,2048]{1,0:T(8,128)(2,1)S(1)}, u32[]{:S(2)}, u32[]{:S(2)}) collective-permute-start(bf16[256,2048]{1,0:T(8,128)(2,1)S(1)} %get-tuple-element.47.refs_0_.refs_7_.refs_1_), channel_id=1, source_target_pairs={{0,5},{4,8},{8,12},{12,14},{14,10},{10,7},{6,3},{2,1},{16,21},{20,... | collective-permute-start | bytes 3145736 | tf_op jit(solution)/shard_map/ppermute | solution.py:395
  209.3 13.8 %collective-permute-start.24 = (bf16[256,2048]{1,0:T(8,128)(2,1)S(1)}, bf16[256,2048]{1,0:T(8,128)(2,1)S(1)}, u32[]{:S(2)}, u32[]{:S(2)}) collective-permute-start(bf16[256,2048]{1,0:T(8,128)(2,1)S(1)} %get-tuple-element.47.refs_0_.refs_7_.refs_1_), channel_id=1, source_target_pairs={{5,1},{9,5},{13,8},{15,12},{11,14},{7,10},{3,7},{1,3},{21,17},{25,... | collective-permute-start | bytes 3145736 | tf_op jit(solution)/shard_map/ppermute | solution.py:396
  (9 other events, 42.7 us)
